TPU v7x, 32 devices: a whole 2x2x4 slice. The times are simulated.
32 devices in a mesh: cells: 8 (over z, core), genes: 4 (over y, x).
Axes of the slice: x: 2, y: 2, z: 4, core: 2. Of those that a mesh axis runs over, the one named last changes fastest.
Arguments:
- sketch: bfloat16 [8192, 256], P('cells'), may hold values from -6 to 6
- tiles: bfloat16 [3072, 128, 128], P(('cells', 'genes')), may hold values from -0.0546875 to 0.0546875
- tile_rows: int32 [3072], P(('cells', 'genes')), may hold values from 0 to 7, as said below
- tile_cols: int32 [3072], P(('cells', 'genes')), may hold values from 0 to 15
- tile_counts: int32 [32], P(('cells', 'genes')), may hold values from 16 to 96, as said below
Outputs:
- projected: float32 [8192, 256], P(('cells', 'genes'))
Inputs may be any that keep to these rules, and one draw needn't show every extreme that they name: Within one device's slots the pairs (tile_rows, tile_cols) are distinct. `tile_counts`: some device holds 96 tiles and the device half the cells axis away from it holds 16.
All inputs are finite; a program needn't handle non-finite values.
Results may differ from a plain program's by a relative error of at most 0.0021.
Values may be sent and summed in bfloat16 or wider, within the bound.
No kernel may reach another device: no remote copies, remote signals or barrier semaphores. Data moves between devices by JAX's collectives and lax.ppermute only.
A program may use at most 128 MiB of HBM per device.

v0:
```python
import jax
import jax.numpy as jnp
from jax import lax
from jax.sharding import PartitionSpec as P

GENE_BLOCKS = 16


def selector(index_ids, slot_live, width):
    hits = (index_ids[:, None] == jnp.arange(width, dtype=jnp.int32)[None, :]).astype(jnp.float32)
    return hits * slot_live[:, None]


def local(sketch, tiles, tile_rows, tile_cols, tile_counts):
    tile_size = tiles.shape[1]
    sketch_width = sketch.shape[1]
    slot_total = tiles.shape[0]
    row_blocks = sketch.shape[0] // tile_size
    sketch_blocks = sketch.reshape(row_blocks, tile_size, sketch_width)
    slot_live = (jnp.arange(slot_total, dtype=jnp.int32) < tile_counts[0]).astype(jnp.float32)
    col_select = selector(tile_cols, slot_live, GENE_BLOCKS)
    row_select = selector(tile_rows, slot_live, row_blocks)
    picked_rows = sketch_blocks[tile_rows]
    first_terms = jnp.einsum("ski,skr->sir", tiles, picked_rows, preferred_element_type=jnp.float32)
    gene_acc = jnp.einsum("sg,sir->gir", col_select, first_terms, precision=lax.Precision.HIGHEST)
    shared = lax.psum_scatter(
        gene_acc.reshape(GENE_BLOCKS * tile_size, sketch_width),
        "cells",
        scatter_dimension=0,
        tiled=True,
    )
    gene_cast = lax.all_gather(shared.astype(jnp.bfloat16), "cells", axis=0, tiled=True).reshape(
        GENE_BLOCKS, tile_size, sketch_width
    )
    picked_genes = gene_cast[tile_cols]
    second_terms = jnp.einsum(
        "sik,skr->sir", tiles, picked_genes, preferred_element_type=jnp.float32
    )
    cell_acc = jnp.einsum("sb,sir->bir", row_select, second_terms, precision=lax.Precision.HIGHEST)
    return lax.psum_scatter(
        cell_acc.reshape(row_blocks * tile_size, sketch_width),
        "genes",
        scatter_dimension=0,
        tiled=True,
    )


def solution(mesh):
    in_specs = (
        P("cells", None),
        P(("cells", "genes"), None, None),
        P(("cells", "genes")),
        P(("cells", "genes")),
        P(("cells", "genes")),
    )
    out_specs = P(("cells", "genes"), None)
    return jax.shard_map(local, mesh=mesh, in_specs=in_specs, out_specs=out_specs, check_vma=False)
```

profile of v0, /device:TPU:0, one launch (start us, length us, event | category | flops | bytes accessed | tf_op | source)
XLA Modules:
  0.0 182.9 jit_solution(10448779680807705465)
XLA Ops:
  6.5 0.0 copy-start
  6.5 0.0 reduce-scatter.3.cloned.1.call-start
  7.4 0.8 compare_select_fusion.1
  8.2 6.9 %gather_fusion = bf16[96,128,256]{2,1,0:T(8,128)(2,1)} fusion(bf16[8,128,256]{2,1,0:T(8,128)(2,1)} %bitcast.22, s32[1024]{0:T(1024)S(1)} %pad_clamp_fusion.1), kind=kCustom, calls=%fused_computation | custom fusion | bytes 12583296 | tf_op jit(solution)/shard_map/gather | solution.py:23
  15.1 0.0 copy-done
  15.1 9.2 %fusion.16 = f32[96,256,128]{2,1,0:T(8,128)} fusion(bf16[96,128,256]{2,1,0:T(8,128)(2,1)} %gather_fusion, bf16[96,128,128]{2,1,0:T(8,128)(2,1)S(1)} %copy-done), kind=kOutput, calls=%fused_computation.25 | convolution fusion | flops 805306368 | bytes 22020096 | tf_op jit(solution)/shard_map/ski,skr->sir/dot_general | solution.py:24
  24.3 0.0 copy-start.1
  24.3 12.7 %copy.8 = f32[96,256,128]{1,0,2:T(8,128)} copy(f32[96,256,128]{2,1,0:T(8,128)} %fusion.16) | data formatting | bytes 25165824 | tf_op jit(solution)/shard_map/ski,skr->sir/dot_general | solution.py:24
  37.0 0.0 copy-done.1
  37.0 8.9 %fusion.2 = f32[16,128,256]{2,0,1:T(8,128)S(1)} fusion(f32[96,256,128]{1,0,2:T(8,128)} %copy.8, f32[96]{0:T(128)S(1)} %compare_convert_fusion, s32[96]{0:T(128)S(1)} %copy-done.1), kind=kOutput, calls=%fused_computation.4 | convolution fusion | flops 603982848 | bytes 14680832 | tf_op jit(solution)/shard_map/sg,sir->gir/dot_general | solution.py:25
  45.9 2.6 %copy.6 = f32[16,128,256]{2,1,0:T(8,128)} copy(f32[16,128,256]{2,0,1:T(8,128)S(1)} %fusion.2) | data formatting | bytes 4194304 | tf_op jit(solution)/shard_map/sg,sir->gir/dot_general | solution.py:25
  48.5 0.0 reduce-scatter.3.cloned.1.call-update
  48.5 0.0 all-gather.2.cloned.1.call-start
  48.6 38.7 %reduce-scatter.3.cloned.1.call-done = f32[256,256]{1,0:T(8,128)} async-done(((f32[2048,256]{1,0:T(8,128)}), f32[256,256]{1,0:T(8,128)}) %reduce-scatter.3.cloned.1.call-update) | async-done | bytes 262160 | tf_op jit(solution)/shard_map/reduce_scatter | solution.py:26
  87.3 1.6 convert_element_type.13
  88.9 0.0 all-gather.2.cloned.1.call-update
  88.9 0.2 reduce-scatter.5.cloned.1.call-start
  89.2 20.4 %all-gather.2.cloned.1.call-done = bf16[2048,256]{1,0:T(8,128)(2,1)} async-done(((bf16[256,256]{1,0:T(8,128)(2,1)}), bf16[2048,256]{1,0:T(8,128)(2,1)}) %all-gather.2.cloned.1.call-update) | async-done | bytes 1048592 | tf_op jit(solution)/shard_map/all_gather | solution.py:32
  109.6 7.2 %gather_fusion.1 = bf16[96,128,256]{2,1,0:T(8,128)(2,1)} fusion(bf16[16,128,256]{2,1,0:T(8,128)(2,1)} %bitcast.23, s32[1024]{0:T(1024)S(1)} %pad_clamp_fusion), kind=kCustom, calls=%fused_computation.1 | custom fusion | bytes 12583296 | tf_op jit(solution)/shard_map/gather | solution.py:35
  116.8 9.2 %fusion.17 = f32[96,256,128]{2,1,0:T(8,128)} fusion(bf16[96,128,256]{2,1,0:T(8,128)(2,1)} %gather_fusion.1, bf16[96,128,128]{2,1,0:T(8,128)(2,1)S(1)} %copy-done), kind=kOutput, calls=%fused_computation.26 | convolution fusion | flops 805306368 | bytes 22020096 | tf_op jit(solution)/shard_map/sik,skr->sir/dot_general | solution.py:36
  125.9 0.0 copy-start.2
  125.9 12.7 %copy.9 = f32[96,256,128]{1,0,2:T(8,128)} copy(f32[96,256,128]{2,1,0:T(8,128)} %fusion.17) | data formatting | bytes 25165824 | tf_op jit(solution)/shard_map/sik,skr->sir/dot_general | solution.py:36
  138.7 0.0 copy-done.2
  138.7 8.9 %fusion = f32[8,128,256]{2,0,1:T(8,128)S(1)} fusion(f32[96,256,128]{1,0,2:T(8,128)} %copy.9, f32[96]{0:T(128)S(1)} %compare_convert_fusion, s32[96]{0:T(128)S(1)} %copy-done.2), kind=kOutput, calls=%fused_computation.2 | convolution fusion | flops 301991424 | bytes 13632256 | tf_op jit(solution)/shard_map/sb,sir->bir/dot_general | solution.py:39
  147.6 1.3 copy.7
  148.9 0.0 reduce-scatter.5.cloned.1.call-update
  148.9 27.5 %reduce-scatter.5.cloned.1.call-done = f32[256,256]{1,0:T(8,128)} async-done(((f32[1024,256]{1,0:T(8,128)}), f32[256,256]{1,0:T(8,128)}) %reduce-scatter.5.cloned.1.call-update) | async-done | bytes 262160 | tf_op jit(solution)/shard_map/reduce_scatter | solution.py:40
  (4 shorter events, 0.0 us)
Async XLA Ops:
  6.5 8.6 %copy-start = (bf16[96,128,128]{2,1,0:T(8,128)(2,1)S(1)}, bf16[96,128,128]{2,1,0:T(8,128)(2,1)}, u32[]{:S(2)}) copy-start(bf16[96,128,128]{2,1,0:T(8,128)(2,1)} %param.6) | copy-start | bytes 9437188
  6.5 80.8 %reduce-scatter.3.cloned.1.call-start = ((), (), s32[]{:S(2)}) async-start(), calls=%async_computation.2 | async-start | bytes 2359296 | tf_op jit(solution)/shard_map/reduce_scatter | solution.py:26
  24.3 12.7 %copy-start.1 = (s32[96]{0:T(128)S(1)}, s32[96]{0:T(128)}, u32[]{:S(2)}) copy-start(s32[96]{0:T(128)} %param.8) | copy-start | bytes 1156
  48.5 61.1 %all-gather.2.cloned.1.call-start = ((), (), s32[]{:S(2)}) async-start(), calls=%async_computation.3 | async-start | bytes 1179648 | tf_op jit(solution)/shard_map/all_gather | solution.py:32
  88.9 87.4 %reduce-scatter.5.cloned.1.call-start = ((), (), s32[]{:S(2)}) async-start(), calls=%async_computation.4 | async-start | bytes 1310720 | tf_op jit(solution)/shard_map/reduce_scatter | solution.py:40
  125.9 12.7 %copy-start.2 = (s32[96]{0:T(128)S(1)}, s32[96]{0:T(128)}, u32[]{:S(2)}) copy-start(s32[96]{0:T(128)} %param.7) | copy-start | bytes 1156
Sparse Core Ops, SparseCore 0:
  48.6 38.6 reduce-scatter.2
  89.1 20.4 all-gather.1
  149.0 27.3 reduce-scatter.4
where the time goes:
time: 184 us; the launch traced here: 183 us
  waiting for transfers between devices  86.7 us (47%)
  local copies, waits for them, and re-layouts  43.4 us (24%)
  matrix products  36.2 us (20%)
  between operations  14 us (8%)
  other arithmetic  2.44 us (1%)
    reduce_scatter x1, waiting for transfers between devices, local(): lax.psum_scatter(gene_acc.reshape(GENE_BLOCKS * tile_size, sketch_width),...  38.7 us
    reduce_scatter x1, waiting for transfers between devices, local(): lax.psum_scatter(cell_acc.reshape(row_blocks * tile_size, sketch_width),...  27.5 us
    all_gather x1, waiting for transfers between devices, local(): lax.all_gather(shared.astype(jnp.bfloat16), 'cells', axis=0, tiled=True)  20.4 us
    dot_general x1, local copies, waits for them, and re-layouts, local(): jnp.einsum('ski,skr->sir', tiles, picked_rows, preferred_element_type=jnp...  12.7 us
    dot_general x1, local copies, waits for them, and re-layouts, local(): jnp.einsum('sik,skr->sir', tiles, picked_genes, preferred_element_type=jn...  12.7 us
    dot_general x1, matrix products, local(): jnp.einsum('sik,skr->sir', tiles, picked_genes, preferred_element_type=jn...  9.16 us
    dot_general x1, matrix products, local(): jnp.einsum('ski,skr->sir', tiles, picked_rows, preferred_element_type=jnp...  9.16 us
    dot_general x1, matrix products, local(): jnp.einsum('sg,sir->gir', col_select, first_terms, precision=lax.Precisio...  8.93 us
  transfers between devices with their start and end apart: 3, of which 3 were waited for; matrix products, arithmetic and copies ran while one was open for 0% of the time, Pallas kernels for 0%

commit v1 on v0

v1 whole, which is shorter than its diff:
```python
import functools

import jax
import jax.numpy as jnp
from jax import lax
from jax.experimental import pallas as pl
from jax.experimental.pallas import tpu as pltpu
from jax.sharding import PartitionSpec as P

GENE_BLOCKS = 16
CORES = 2
MIB = 1 << 20

VMEM = pl.BlockSpec(memory_space=pltpu.VMEM)
SMEM = pl.BlockSpec(memory_space=pltpu.SMEM)
ANY = pl.BlockSpec(memory_space=pl.ANY)
f32, bf16, i16, i32 = jnp.float32, jnp.bfloat16, jnp.int16, jnp.int32


def encode(x, out, at=()):
    peak = jnp.max(jnp.abs(x), axis=0, keepdims=True)
    expo = jnp.ceil(jnp.log2(jnp.maximum(peak, 2.0**-100)))
    expo = jnp.clip(expo, -100.0, 126.0)
    code = jnp.round(x * jnp.exp2(14.0 - expo)).astype(i32)
    top = code[:16]
    row = lax.broadcasted_iota(i32, top.shape, 0)
    word = jnp.broadcast_to(expo.astype(i32) + 128, top.shape)
    marked = (top & ~1) | ((word >> jnp.minimum(row, 7)) & 1)
    top = jnp.where(row < 8, marked, top)
    out[at + (pl.ds(0, 16),)] = top.astype(i16)
    out[at + (pl.ds(16, x.shape[0] - 16),)] = code[16:].astype(i16)


def decode(code):
    code = code.astype(i32)
    head = code[:8]
    row = lax.broadcasted_iota(i32, head.shape, 0)
    word = jnp.sum((head & 1) << row, axis=0, keepdims=True)
    scale = jnp.exp2((word - (128 + 14)).astype(f32))
    return code.astype(f32) * scale


def core_and_chip():
    place = lax.axis_index("cells")
    return lax.rem(place, CORES), lax.div(place, CORES)


def call(body, outs, in_specs, scratch=(), mib=32, flops=0, nbytes=0):
    return pl.pallas_call(
        body,
        out_shape=outs,
        in_specs=in_specs,
        out_specs=jax.tree.map(lambda _: VMEM, outs),
        scratch_shapes=list(scratch),
        compiler_params=pltpu.CompilerParams(vmem_limit_bytes=mib * MIB),
        cost_estimate=pl.CostEstimate(flops=flops, bytes_accessed=nbytes, transcendentals=0),
    )


def dense_kernel(count, rows, cols, sketch, tiles, dense, turned, theirs, sems):
    tile = tiles.shape[1]
    core, _ = core_and_chip()

    def clear(i, _):
        dense[pl.ds(pl.multiple_of(i * 16, 16), 16), :] = jnp.zeros((16, dense.shape[1]), bf16)
        return 0

    lax.fori_loop(0, dense.shape[0] // 16, clear, 0)

    def copy(s):
        r = pl.multiple_of(rows[s] * tile, tile)
        c = pl.multiple_of(cols[s] * tile, tile)
        return pltpu.make_async_copy(tiles.at[s], dense.at[pl.ds(r, tile), pl.ds(c, tile)], sems.at[s])

    def start(s, _):
        copy(s).start()
        return 0

    def wait(s, _):
        copy(s).wait()
        return 0

    lax.fori_loop(0, count[0], start, 0)
    turned[...] = sketch[...].T
    lax.fori_loop(0, count[0], wait, 0)
    half = theirs.shape[0]
    left = turned[pl.ds(pl.multiple_of((1 - core) * half, half), half), :]
    width = 512
    for j in range(dense.shape[1] // width):
        part = jnp.dot(left, dense[:, j * width : (j + 1) * width], preferred_element_type=f32)
        encode_columns(part, theirs, j * width)


def encode_columns(x, out, at):
    encode(x, out.at[:, pl.ds(at, x.shape[1])])


def own_kernel(turned, dense, mine):
    core, _ = core_and_chip()
    half = mine.shape[0]
    left = turned[pl.ds(pl.multiple_of(core * half, half), half), :]
    mine[...] = jnp.dot(left, dense[...], preferred_element_type=f32)


def pair_kernel(mine, got, *outs):
    _, chip = core_and_chip()
    width = outs[0].shape[1]
    for k, out in enumerate(outs):
        cut = pl.ds(pl.multiple_of((chip ^ k) * width, width), width)
        total = mine[:, cut] + decode(got[:, cut])
        if k == 0:
            out[...] = total
        else:
            encode(total, out)


def gene_kernel(own, *refs):
    *got, out = refs
    total = own[...]
    for ref in got:
        total = total + decode(ref[...])
    out[...] = total.astype(bf16)


def cell_kernel(chips, dense, *refs):
    ours, theirs = refs[:chips], refs[chips : 2 * chips]
    outs, gene = refs[2 * chips : -1], refs[-1]
    core, chip = core_and_chip()
    half, width = ours[0].shape
    for k in range(chips):
        cut = pl.ds(pl.multiple_of((chip ^ k) * width, width), width)
        gene[pl.ds(pl.multiple_of(core * half, half), half), cut] = ours[k][...]
        gene[pl.ds(pl.multiple_of((1 - core) * half, half), half), cut] = theirs[k][...]
    me = lax.axis_index("genes")
    height = outs[0].shape[0]
    for k, out in enumerate(outs):
        left = dense[pl.ds(pl.multiple_of((me ^ k) * height, height), height), :]
        part = lax.dot_general(left, gene[...], (((1,), (1,)), ((), ())), preferred_element_type=f32)
        if k == 0:
            out[...] = part
        else:
            encode(part, out)


def last_kernel(own, *refs):
    *got, out = refs
    total = own[...]
    for ref in got:
        total = total + decode(ref[...])
    out[...] = total


def local(n_cells, n_genes, sketch, tiles, tile_rows, tile_cols, tile_counts):
    cells, rank = sketch.shape
    slots, tile, _ = tiles.shape
    genes = GENE_BLOCKS * tile
    chips = n_cells // CORES
    half = rank // CORES
    width = genes // chips
    height = cells // n_genes
    flops = 2 * cells * genes * rank
    shape = jax.ShapeDtypeStruct

    def to_core(x):
        return lax.ppermute(x, "cells", [(i, i ^ 1) for i in range(n_cells)])

    def to_chip(x, k):
        return lax.ppermute(x, "cells", [(i, i ^ (k * CORES)) for i in range(n_cells)])

    def to_gene(x, k):
        return lax.ppermute(x, "genes", [(i, i ^ k) for i in range(n_genes)])

    dense, turned, theirs = call(
        dense_kernel,
        (shape((cells, genes), bf16), shape((rank, cells), bf16), shape((half, genes), i16)),
        [SMEM, SMEM, SMEM, VMEM, ANY],
        scratch=[pltpu.SemaphoreType.DMA((slots,))],
        flops=flops // 2,
        nbytes=8 * MIB,
    )(tile_counts, tile_rows, tile_cols, sketch, tiles)
    got = to_core(theirs)
    mine = call(own_kernel, shape((half, genes), f32), [VMEM, VMEM], flops=flops // 2, nbytes=5 * MIB)(turned, dense)
    pieces = call(
        pair_kernel,
        (shape((half, width), f32),) + (shape((half, width), i16),) * (chips - 1),
        [VMEM, VMEM],
        nbytes=2 * MIB,
    )(mine, got)
    sums = [to_chip(pieces[k], k) for k in range(1, chips)]
    chunk = call(gene_kernel, shape((half, width), bf16), [VMEM] * chips, nbytes=MIB)(pieces[0], *sums)
    ours = [chunk] + [to_chip(chunk, k) for k in range(1, chips)]
    partners = [to_core(x) for x in ours]
    parts = call(
        functools.partial(cell_kernel, chips),
        (shape((height, rank), f32),) + (shape((height, rank), i16),) * (n_genes - 1),
        [VMEM] * (1 + 2 * chips),
        scratch=[pltpu.VMEM((rank, genes), bf16)],
        flops=flops,
        nbytes=6 * MIB,
    )(dense, *ours, *partners)
    rest = [to_gene(parts[k], k) for k in range(1, n_genes)]
    return call(last_kernel, shape((height, rank), f32), [VMEM] * n_genes, nbytes=MIB)(parts[0], *rest)


def solution(mesh):
    in_specs = (
        P("cells", None),
        P(("cells", "genes"), None, None),
        P(("cells", "genes")),
        P(("cells", "genes")),
        P(("cells", "genes")),
    )
    out_specs = P(("cells", "genes"), None)
    body = functools.partial(local, mesh.shape["cells"], mesh.shape["genes"])
    return jax.shard_map(body, mesh=mesh, in_specs=in_specs, out_specs=out_specs, check_vma=False)
```

time: 184 us -> 54.9 us (0.30)
  waiting for transfers between devices: 86.7 us -> 28.5 us
  local copies, waits for them, and re-layouts: 43.4 us -> 4.23 us
  matrix products: 36.2 us -> 0 us
  between operations: 14 us -> 0.72 us
  starting transfers between devices: 0.27 us -> 13.1 us
  Pallas kernels: 0 us -> 8.43 us
  other arithmetic: 2.44 us -> 0 us
    reduce_scatter x2 -> x0, waiting for transfers between devices: 66.2 us -> none  [the longest x1 38.7 us: local(): lax.psum_scatter(gene_acc.reshape(GENE_BLOCKS * tile_size, sketch_width),...]
    dot_general x4 -> x0, matrix products: 36.2 us -> none  [the longest x1 9.16 us: local(): jnp.einsum('sik,skr->sir', tiles, picked_genes, preferred_element_type=jn...]
    dot_general x4 -> x0, local copies, waits for them, and re-layouts: 29.3 us -> none  [the longest x1 12.7 us: local(): jnp.einsum('ski,skr->sir', tiles, picked_rows, preferred_element_type=jnp...]
    ppermute x0 -> x14, waiting for transfers between devices: none -> 28.5 us  [the longest x6 19.7 us: to_chip(): lax.ppermute(x, 'cells', [(i, i ^ k * CORES) for i in range(n_cells)])]
    all_gather x1 -> x0, waiting for transfers between devices: 20.4 us -> none  [local(): lax.all_gather(shared.astype(jnp.bfloat16), 'cells', axis=0, tiled=True)]
    gather x2 -> x0, local copies, waits for them, and re-layouts: 14.1 us -> none  [the longest x1 7.16 us: local(): picked_genes = gene_cast[tile_cols]]
    ppermute x0 -> x14, starting transfers between devices: none -> 13.1 us  [the longest x6 8.9 us: to_chip(): lax.ppermute(x, 'cells', [(i, i ^ k * CORES) for i in range(n_cells)])]
    pallas_call x0 -> x6, Pallas kernels: none -> 8.43 us  [the longest x1 4.99 us: local(): call(dense_kernel, (shape((cells, genes), bf16), shape((rank, cells), bf1...]
  transfers between devices with their start and end apart: 3 -> 14, of which waited for: 3 -> 10; matrix products, arithmetic and copies ran while one was open for 0% -> 0% of each run, Pallas kernels for 0% -> 1%
where the time goes in v1:
time: 54.9 us
  waiting for transfers between devices  28.5 us (52%)
  starting transfers between devices  13.1 us (24%)
  Pallas kernels  8.43 us (15%)
  local copies, waits for them, and re-layouts  4.23 us (8%)
  between operations  0.72 us (1%)
    ppermute x6, waiting for transfers between devices, to_chip(): lax.ppermute(x, 'cells', [(i, i ^ k * CORES) for i in range(n_cells)])  19.7 us
    ppermute x6, starting transfers between devices, to_chip(): lax.ppermute(x, 'cells', [(i, i ^ k * CORES) for i in range(n_cells)])  8.9 us
    ppermute x3, waiting for transfers between devices, to_gene(): return lax.ppermute(x, 'genes', [(i, i ^ k) for i in range(n_genes)])  6.52 us
    pallas_call x1, Pallas kernels, local(): call(dense_kernel, (shape((cells, genes), bf16), shape((rank, cells), bf1...  4.99 us
    unnamed x8, local copies, waits for them, and re-layouts  4.23 us
    ppermute x3, starting transfers between devices, to_gene(): return lax.ppermute(x, 'genes', [(i, i ^ k) for i in range(n_genes)])  3.56 us
    ppermute x5, waiting for transfers between devices, to_core(): return lax.ppermute(x, 'cells', [(i, i ^ 1) for i in range(n_cells)])  2.19 us
    pallas_call x1, Pallas kernels, local(): call(functools.partial(cell_kernel, chips), (shape((height, rank), f32),)...  1.47 us
  transfers between devices with their start and end apart: 14, of which 10 were waited for; matrix products, arithmetic and copies ran while one was open for 0% of the time, Pallas kernels for 1%

profile of v1, /device:TPU:0, one launch (start us, length us, event | category | flops | bytes accessed | tf_op | source)
XLA Modules:
  0.0 54.9 jit_solution(13691865586515774228)
XLA Ops:
  0.7 1.9 %copy-done = bf16[96,128,128]{2,1,0:T(8,128)(2,1)S(1)} copy-done((bf16[96,128,128]{2,1,0:T(8,128)(2,1)S(1)}, bf16[96,128,128]{2,1,0:T(8,128)(2,1)}, u32[]{:S(2)}) %copy-start) | copy-done | bytes 3145752
  2.5 1.0 %copy-done.1 = bf16[1024,256]{1,0:T(8,128)(2,1)S(1)} copy-done((bf16[1024,256]{1,0:T(8,128)(2,1)S(1)}, bf16[1024,256]{1,0:T(8,128)(2,1)}, u32[]{:S(2)}) %copy-start.1) | copy-done | bytes 524312
  3.6 0.7 %copy-done.2 = s32[96]{0:T(128)S(1)} copy-done((s32[96]{0:T(128)S(1)}, s32[96]{0:T(128)}, u32[]{:S(2)}) %copy-start.2) | copy-done | bytes 408
  4.2 0.7 %copy-done.3 = s32[96]{0:T(128)S(1)} copy-done((s32[96]{0:T(128)S(1)}, s32[96]{0:T(128)}, u32[]{:S(2)}) %copy-start.3) | copy-done | bytes 408
  4.9 5.0 %shard_map.55 = (bf16[1024,2048]{1,0:T(8,128)(2,1)S(1)}, bf16[256,1024]{1,0:T(8,128)(2,1)S(1)}, s16[128,2048]{1,0:T(8,128)(2,1)S(1)}) custom-call(s32[1]{0:T(128)S(6)} %copy.6.count, s32[96]{0:T(128)S(1)} %copy-done.2, s32[96]{0:T(128)S(1)} %copy-done.3, bf16[1024,256]{1,0:T(8,128)(2,1)S(1)} %copy-done.1, bf16[96,128,128]{2,1,0:T(8,128)(2,1)S(1)} %copy-done), custom_call_target="tpu_custom_call" | custom-call | flops 536870912 | bytes 8388608 | tf_op jit(solution)/shard_map/pallas_call | solution.py:173
  9.9 0.1 collective-permute-start
  10.0 0.7 %shard_map.56.mine = f32[128,2048]{1,0:T(8,128)S(1)} custom-call(bf16[256,1024]{1,0:T(8,128)(2,1)S(1)} %get-tuple-element.17.turned, bf16[1024,2048]{1,0:T(8,128)(2,1)S(1)} %get-tuple-element.16.dense), custom_call_target="tpu_custom_call" | custom-call | flops 536870912 | bytes 5242880 | tf_op jit(solution)/shard_map/pallas_call | solution.py:182
  10.7 1.2 %collective-permute-done.got = s16[128,2048]{1,0:T(8,128)(2,1)S(1)} collective-permute-done((s16[128,2048]{1,0:T(8,128)(2,1)S(1)}, s16[128,2048]{1,0:T(8,128)(2,1)S(1)}, u32[]{:S(2)}, u32[]{:S(2)}) %collective-permute-start) | collective-permute-done | bytes 524320 | tf_op jit(solution)/shard_map/ppermute | solution.py:165
  11.9 0.3 shard_map.57
  12.2 1.7 %collective-permute-start.1 = (s16[128,512]{1,0:T(8,128)(2,1)S(1)}, s16[128,512]{1,0:T(8,128)(2,1)S(1)}, u32[]{:S(2)}, u32[]{:S(2)}) collective-permute-start(s16[128,512]{1,0:T(8,128)(2,1)S(1)} %get-tuple-element.20), channel_id=1, source_target_pairs={{0,8},{4,12},{8,0},{12,4},{16,24},{20,28},{24,16},{28,20},{1,9},{5... | collective-permute-start | bytes 393224 | tf_op jit(solution)/shard_map/ppermute | solution.py:168
  13.8 2.8 %collective-permute-start.2 = (s16[128,512]{1,0:T(8,128)(2,1)S(1)}, s16[128,512]{1,0:T(8,128)(2,1)S(1)}, u32[]{:S(2)}, u32[]{:S(2)}) collective-permute-start(s16[128,512]{1,0:T(8,128)(2,1)S(1)} %get-tuple-element.21), channel_id=1, source_target_pairs={{0,16},{4,20},{8,24},{12,28},{16,0},{20,4},{24,8},{28,12},{1,17},{... | collective-permute-start | bytes 393224 | tf_op jit(solution)/shard_map/ppermute | solution.py:168
  16.6 0.0 collective-permute-start.3
  16.6 3.2 %collective-permute-done.1.refs_0_ = s16[128,512]{1,0:T(8,128)(2,1)S(1)} collective-permute-done((s16[128,512]{1,0:T(8,128)(2,1)S(1)}, s16[128,512]{1,0:T(8,128)(2,1)S(1)}, u32[]{:S(2)}, u32[]{:S(2)}) %collective-permute-start.1) | collective-permute-done | bytes 131104 | tf_op jit(solution)/shard_map/ppermute | solution.py:168
  19.8 6.9 %collective-permute-done.2.refs_1_ = s16[128,512]{1,0:T(8,128)(2,1)S(1)} collective-permute-done((s16[128,512]{1,0:T(8,128)(2,1)S(1)}, s16[128,512]{1,0:T(8,128)(2,1)S(1)}, u32[]{:S(2)}, u32[]{:S(2)}) %collective-permute-start.2) | collective-permute-done | bytes 131104 | tf_op jit(solution)/shard_map/ppermute | solution.py:168
  26.8 0.1 shard_map.58.refs_0_
  26.9 2.3 %collective-permute-start.6 = (bf16[128,512]{1,0:T(8,128)(2,1)S(1)}, bf16[128,512]{1,0:T(8,128)(2,1)S(1)}, u32[]{:S(2)}, u32[]{:S(2)}) collective-permute-start(bf16[128,512]{1,0:T(8,128)(2,1)S(1)} %shard_map.58.refs_0_), channel_id=1, source_target_pairs={{0,24},{4,28},{8,16},{12,20},{16,8},{20,12},{24,0},{28,4},{1,25},{... | collective-permute-start | bytes 393224 | tf_op jit(solution)/shard_map/ppermute | solution.py:168
  29.2 1.6 %collective-permute-start.5 = (bf16[128,512]{1,0:T(8,128)(2,1)S(1)}, bf16[128,512]{1,0:T(8,128)(2,1)S(1)}, u32[]{:S(2)}, u32[]{:S(2)}) collective-permute-start(bf16[128,512]{1,0:T(8,128)(2,1)S(1)} %shard_map.58.refs_0_), channel_id=1, source_target_pairs={{0,16},{4,20},{8,24},{12,28},{16,0},{20,4},{24,8},{28,12},{1,17},{... | collective-permute-start | bytes 393224 | tf_op jit(solution)/shard_map/ppermute | solution.py:168
  30.8 0.5 collective-permute-start.4
  31.4 0.0 collective-permute-start.7
  31.4 3.4 %collective-permute-done.6.refs_3_ = bf16[128,512]{1,0:T(8,128)(2,1)S(1)} collective-permute-done((bf16[128,512]{1,0:T(8,128)(2,1)S(1)}, bf16[128,512]{1,0:T(8,128)(2,1)S(1)}, u32[]{:S(2)}, u32[]{:S(2)}) %collective-permute-start.6) | collective-permute-done | bytes 131104 | tf_op jit(solution)/shard_map/ppermute | solution.py:168
  34.8 6.2 %collective-permute-done.5.refs_2_ = bf16[128,512]{1,0:T(8,128)(2,1)S(1)} collective-permute-done((bf16[128,512]{1,0:T(8,128)(2,1)S(1)}, bf16[128,512]{1,0:T(8,128)(2,1)S(1)}, u32[]{:S(2)}, u32[]{:S(2)}) %collective-permute-start.5) | collective-permute-done | bytes 131104 | tf_op jit(solution)/shard_map/ppermute | solution.py:168
  41.0 0.5 collective-permute-start.8
  41.5 0.8 %collective-permute-done.9.refs_6_ = bf16[128,512]{1,0:T(8,128)(2,1)S(1)} collective-permute-done((bf16[128,512]{1,0:T(8,128)(2,1)S(1)}, bf16[128,512]{1,0:T(8,128)(2,1)S(1)}, u32[]{:S(2)}, u32[]{:S(2)}) %collective-permute-start.9) | collective-permute-done | bytes 131104 | tf_op jit(solution)/shard_map/ppermute | solution.py:165
  42.3 0.2 collective-permute-done.8.refs_5_
  42.5 1.5 %shard_map.59 = (f32[256,256]{1,0:T(8,128)S(1)}, s16[256,256]{1,0:T(8,128)(2,1)S(1)}, s16[256,256]{1,0:T(8,128)(2,1)S(1)}, s16[256,256]{1,0:T(8,128)(2,1)S(1)}) custom-call(bf16[1024,2048]{1,0:T(8,128)(2,1)S(1)} %get-tuple-element.16.dense, bf16[128,512]{1,0:T(8,128)(2,1)S(1)} %shard_map.58.refs_0_, bf16[128,512]{1,0:T(8,128)(2,1)S(1)} %collective-permute-done.4.refs_1_, ...), custom_call_target="tpu_custom_call" | custom-call | flops 1073741824 | bytes 6291456 | tf_op jit(solution)/shard_map/pallas_call | solution.py:193
  44.0 1.0 %collective-permute-start.11 = (s16[256,256]{1,0:T(8,128)(2,1)S(1)}, s16[256,256]{1,0:T(8,128)(2,1)S(1)}, u32[]{:S(2)}, u32[]{:S(2)}) collective-permute-start(s16[256,256]{1,0:T(8,128)(2,1)S(1)} %get-tuple-element.24), channel_id=1, source_target_pairs={{0,1},{1,0},{2,3},{3,2},{4,5},{5,4},{6,7},{7,6},{8,9},{9,8},{10,11... | collective-permute-start | bytes 393224 | tf_op jit(solution)/shard_map/ppermute | solution.py:171
  45.0 2.2 %collective-permute-start.12 = (s16[256,256]{1,0:T(8,128)(2,1)S(1)}, s16[256,256]{1,0:T(8,128)(2,1)S(1)}, u32[]{:S(2)}, u32[]{:S(2)}) collective-permute-start(s16[256,256]{1,0:T(8,128)(2,1)S(1)} %get-tuple-element.25), channel_id=1, source_target_pairs={{0,2},{1,3},{2,0},{3,1},{4,6},{5,7},{6,4},{7,5},{8,10},{9,11},{10,... | collective-permute-start | bytes 393224 | tf_op jit(solution)/shard_map/ppermute | solution.py:171
  47.2 0.3 collective-permute-start.13
  47.5 2.7 %collective-permute-done.11.refs_0_ = s16[256,256]{1,0:T(8,128)(2,1)S(1)} collective-permute-done((s16[256,256]{1,0:T(8,128)(2,1)S(1)}, s16[256,256]{1,0:T(8,128)(2,1)S(1)}, u32[]{:S(2)}, u32[]{:S(2)}) %collective-permute-start.11) | collective-permute-done | bytes 131104 | tf_op jit(solution)/shard_map/ppermute | solution.py:171
  50.2 2.7 %collective-permute-done.12.refs_1_ = s16[256,256]{1,0:T(8,128)(2,1)S(1)} collective-permute-done((s16[256,256]{1,0:T(8,128)(2,1)S(1)}, s16[256,256]{1,0:T(8,128)(2,1)S(1)}, u32[]{:S(2)}, u32[]{:S(2)}) %collective-permute-start.12) | collective-permute-done | bytes 131104 | tf_op jit(solution)/shard_map/ppermute | solution.py:171
  53.0 1.1 %collective-permute-done.13.refs_2_ = s16[256,256]{1,0:T(8,128)(2,1)S(1)} collective-permute-done((s16[256,256]{1,0:T(8,128)(2,1)S(1)}, s16[256,256]{1,0:T(8,128)(2,1)S(1)}, u32[]{:S(2)}, u32[]{:S(2)}) %collective-permute-start.13) | collective-permute-done | bytes 131104 | tf_op jit(solution)/shard_map/ppermute | solution.py:171
  54.1 0.8 %shard_map.60 = f32[256,256]{1,0:T(8,128)} custom-call(f32[256,256]{1,0:T(8,128)S(1)} %get-tuple-element.23.own, s16[256,256]{1,0:T(8,128)(2,1)S(1)} %collective-permute-done.11.refs_0_, s16[256,256]{1,0:T(8,128)(2,1)S(1)} %collective-permute-done.12.refs_1_, s16[256,256]{1,0:T(8,128)(2,1)S(1)} %collective-permute-done.13.refs_2_), custom_call_target="tpu_custom_call" | custom-call | bytes 1048576 | tf_op jit(solution)/shard_map/pallas_call | solution.py:202
  (10 shorter events, 0.0 us)
Async XLA Ops:
  0.7 1.9 %copy-start = (bf16[96,128,128]{2,1,0:T(8,128)(2,1)S(1)}, bf16[96,128,128]{2,1,0:T(8,128)(2,1)}, u32[]{:S(2)}) copy-start(bf16[96,128,128]{2,1,0:T(8,128)(2,1)} %tiles.1) | copy-start | bytes 9437188
  2.5 1.0 %copy-start.1 = (bf16[1024,256]{1,0:T(8,128)(2,1)S(1)}, bf16[1024,256]{1,0:T(8,128)(2,1)}, u32[]{:S(2)}) copy-start(bf16[1024,256]{1,0:T(8,128)(2,1)} %sketch.1) | copy-start | bytes 1572868
  3.6 0.7 %copy-start.2 = (s32[96]{0:T(128)S(1)}, s32[96]{0:T(128)}, u32[]{:S(2)}) copy-start(s32[96]{0:T(128)} %rows.1) | copy-start | bytes 1156
  4.2 0.7 %copy-start.3 = (s32[96]{0:T(128)S(1)}, s32[96]{0:T(128)}, u32[]{:S(2)}) copy-start(s32[96]{0:T(128)} %cols.1) | copy-start | bytes 1156
  9.9 2.0 %collective-permute-start = (s16[128,2048]{1,0:T(8,128)(2,1)S(1)}, s16[128,2048]{1,0:T(8,128)(2,1)S(1)}, u32[]{:S(2)}, u32[]{:S(2)}) collective-permute-start(s16[128,2048]{1,0:T(8,128)(2,1)S(1)} %get-tuple-element.18), channel_id=1, source_target_pairs={{0,4},{4,0},{8,12},{12,8},{16,20},{20,16},{24,28},{28,24},{1,5},{5... | collective-permute-start | bytes 1572872 | tf_op jit(solution)/shard_map/ppermute | solution.py:165
  12.2 7.6 %collective-permute-start.1 = (s16[128,512]{1,0:T(8,128)(2,1)S(1)}, s16[128,512]{1,0:T(8,128)(2,1)S(1)}, u32[]{:S(2)}, u32[]{:S(2)}) collective-permute-start(s16[128,512]{1,0:T(8,128)(2,1)S(1)} %get-tuple-element.20), channel_id=1, source_target_pairs={{0,8},{4,12},{8,0},{12,4},{16,24},{20,28},{24,16},{28,20},{1,9},{5... | collective-permute-start | bytes 393224 | tf_op jit(solution)/shard_map/ppermute | solution.py:168
  13.8 12.9 %collective-permute-start.2 = (s16[128,512]{1,0:T(8,128)(2,1)S(1)}, s16[128,512]{1,0:T(8,128)(2,1)S(1)}, u32[]{:S(2)}, u32[]{:S(2)}) collective-permute-start(s16[128,512]{1,0:T(8,128)(2,1)S(1)} %get-tuple-element.21), channel_id=1, source_target_pairs={{0,16},{4,20},{8,24},{12,28},{16,0},{20,4},{24,8},{28,12},{1,17},{... | collective-permute-start | bytes 393224 | tf_op jit(solution)/shard_map/ppermute | solution.py:168
  16.6 10.1 %collective-permute-start.3 = (s16[128,512]{1,0:T(8,128)(2,1)S(1)}, s16[128,512]{1,0:T(8,128)(2,1)S(1)}, u32[]{:S(2)}, u32[]{:S(2)}) collective-permute-start(s16[128,512]{1,0:T(8,128)(2,1)S(1)} %get-tuple-element.22), channel_id=1, source_target_pairs={{0,24},{4,28},{8,16},{12,20},{16,8},{20,12},{24,0},{28,4},{1,25},{... | collective-permute-start | bytes 393224 | tf_op jit(solution)/shard_map/ppermute | solution.py:168
  26.9 7.9 %collective-permute-start.6 = (bf16[128,512]{1,0:T(8,128)(2,1)S(1)}, bf16[128,512]{1,0:T(8,128)(2,1)S(1)}, u32[]{:S(2)}, u32[]{:S(2)}) collective-permute-start(bf16[128,512]{1,0:T(8,128)(2,1)S(1)} %shard_map.58.refs_0_), channel_id=1, source_target_pairs={{0,24},{4,28},{8,16},{12,20},{16,8},{20,12},{24,0},{28,4},{1,25},{... | collective-permute-start | bytes 393224 | tf_op jit(solution)/shard_map/ppermute | solution.py:168
  29.2 11.7 %collective-permute-start.5 = (bf16[128,512]{1,0:T(8,128)(2,1)S(1)}, bf16[128,512]{1,0:T(8,128)(2,1)S(1)}, u32[]{:S(2)}, u32[]{:S(2)}) collective-permute-start(bf16[128,512]{1,0:T(8,128)(2,1)S(1)} %shard_map.58.refs_0_), channel_id=1, source_target_pairs={{0,16},{4,20},{8,24},{12,28},{16,0},{20,4},{24,8},{28,12},{1,17},{... | collective-permute-start | bytes 393224 | tf_op jit(solution)/shard_map/ppermute | solution.py:168
  30.8 10.1 %collective-permute-start.4 = (bf16[128,512]{1,0:T(8,128)(2,1)S(1)}, bf16[128,512]{1,0:T(8,128)(2,1)S(1)}, u32[]{:S(2)}, u32[]{:S(2)}) collective-permute-start(bf16[128,512]{1,0:T(8,128)(2,1)S(1)} %shard_map.58.refs_0_), channel_id=1, source_target_pairs={{0,8},{4,12},{8,0},{12,4},{16,24},{20,28},{24,16},{28,20},{1,9},{5... | collective-permute-start | bytes 393224 | tf_op jit(solution)/shard_map/ppermute | solution.py:168
  31.4 10.1 %collective-permute-start.7 = (bf16[128,512]{1,0:T(8,128)(2,1)S(1)}, bf16[128,512]{1,0:T(8,128)(2,1)S(1)}, u32[]{:S(2)}, u32[]{:S(2)}) collective-permute-start(bf16[128,512]{1,0:T(8,128)(2,1)S(1)} %shard_map.58.refs_0_), channel_id=1, source_target_pairs={{0,4},{4,0},{8,12},{12,8},{16,20},{20,16},{24,28},{28,24},{1,5},{5... | collective-permute-start | bytes 393224 | tf_op jit(solution)/shard_map/ppermute | solution.py:165
  34.8 6.7 %collective-permute-start.10 = (bf16[128,512]{1,0:T(8,128)(2,1)S(1)}, bf16[128,512]{1,0:T(8,128)(2,1)S(1)}, u32[]{:S(2)}, u32[]{:S(2)}) collective-permute-start(bf16[128,512]{1,0:T(8,128)(2,1)S(1)} %collective-permute-done.6.refs_3_), channel_id=1, source_target_pairs={{0,4},{4,0},{8,12},{12,8},{16,20},{20,16},{24,28},{28,24},{1,5},{5... | collective-permute-start | bytes 393224 | tf_op jit(solution)/shard_map/ppermute | solution.py:165
  41.0 1.3 %collective-permute-start.9 = (bf16[128,512]{1,0:T(8,128)(2,1)S(1)}, bf16[128,512]{1,0:T(8,128)(2,1)S(1)}, u32[]{:S(2)}, u32[]{:S(2)}) collective-permute-start(bf16[128,512]{1,0:T(8,128)(2,1)S(1)} %collective-permute-done.5.refs_2_), channel_id=1, source_target_pairs={{0,4},{4,0},{8,12},{12,8},{16,20},{20,16},{24,28},{28,24},{1,5},{5... | collective-permute-start | bytes 393224 | tf_op jit(solution)/shard_map/ppermute | solution.py:165
  41.0 1.5 %collective-permute-start.8 = (bf16[128,512]{1,0:T(8,128)(2,1)S(1)}, bf16[128,512]{1,0:T(8,128)(2,1)S(1)}, u32[]{:S(2)}, u32[]{:S(2)}) collective-permute-start(bf16[128,512]{1,0:T(8,128)(2,1)S(1)} %collective-permute-done.4.refs_1_), channel_id=1, source_target_pairs={{0,4},{4,0},{8,12},{12,8},{16,20},{20,16},{24,28},{28,24},{1,5},{5... | collective-permute-start | bytes 393224 | tf_op jit(solution)/shard_map/ppermute | solution.py:165
  44.0 6.2 %collective-permute-start.11 = (s16[256,256]{1,0:T(8,128)(2,1)S(1)}, s16[256,256]{1,0:T(8,128)(2,1)S(1)}, u32[]{:S(2)}, u32[]{:S(2)}) collective-permute-start(s16[256,256]{1,0:T(8,128)(2,1)S(1)} %get-tuple-element.24), channel_id=1, source_target_pairs={{0,1},{1,0},{2,3},{3,2},{4,5},{5,4},{6,7},{7,6},{8,9},{9,8},{10,11... | collective-permute-start | bytes 393224 | tf_op jit(solution)/shard_map/ppermute | solution.py:171
  45.0 8.0 %collective-permute-start.12 = (s16[256,256]{1,0:T(8,128)(2,1)S(1)}, s16[256,256]{1,0:T(8,128)(2,1)S(1)}, u32[]{:S(2)}, u32[]{:S(2)}) collective-permute-start(s16[256,256]{1,0:T(8,128)(2,1)S(1)} %get-tuple-element.25), channel_id=1, source_target_pairs={{0,2},{1,3},{2,0},{3,1},{4,6},{5,7},{6,4},{7,5},{8,10},{9,11},{10,... | collective-permute-start | bytes 393224 | tf_op jit(solution)/shard_map/ppermute | solution.py:171
  47.2 6.9 %collective-permute-start.13 = (s16[256,256]{1,0:T(8,128)(2,1)S(1)}, s16[256,256]{1,0:T(8,128)(2,1)S(1)}, u32[]{:S(2)}, u32[]{:S(2)}) collective-permute-start(s16[256,256]{1,0:T(8,128)(2,1)S(1)} %get-tuple-element.26), channel_id=1, source_target_pairs={{0,3},{1,2},{2,1},{3,0},{4,7},{5,6},{6,5},{7,4},{8,11},{9,10},{10,... | collective-permute-start | bytes 393224 | tf_op jit(solution)/shard_map/ppermute | solution.py:171

commit v2 on v1

v2 whole, which is shorter than its diff:
```python
import functools

import jax
import jax.numpy as jnp
from jax import lax
from jax.experimental import pallas as pl
from jax.experimental.pallas import tpu as pltpu
from jax.sharding import PartitionSpec as P

GENE_BLOCKS = 16
CORES = 2
MIB = 1 << 20

VMEM = pl.BlockSpec(memory_space=pltpu.VMEM)
SMEM = pl.BlockSpec(memory_space=pltpu.SMEM)
HBM = pl.BlockSpec(memory_space=pltpu.HBM)
f32, bf16, i16, i32 = jnp.float32, jnp.bfloat16, jnp.int16, jnp.int32


def encode(x, out, at=()):
    peak = jnp.max(jnp.abs(x), axis=0, keepdims=True)
    expo = jnp.ceil(jnp.log2(jnp.maximum(peak, 2.0**-100)))
    expo = jnp.clip(expo, -100.0, 126.0)
    code = jnp.round(x * jnp.exp2(14.0 - expo)).astype(i32)
    top = code[:16]
    row = lax.broadcasted_iota(i32, top.shape, 0)
    word = jnp.broadcast_to(expo.astype(i32) + 128, top.shape)
    marked = (top & ~1) | ((word >> jnp.minimum(row, 7)) & 1)
    top = jnp.where(row < 8, marked, top)
    out[at + (pl.ds(0, 16),)] = top.astype(i16)
    out[at + (pl.ds(16, x.shape[0] - 16),)] = code[16:].astype(i16)


def decode(code):
    code = code.astype(i32)
    head = code[:8]
    row = lax.broadcasted_iota(i32, head.shape, 0)
    word = jnp.sum((head & 1) << row, axis=0, keepdims=True)
    scale = jnp.exp2((word - (128 + 14)).astype(f32))
    return code.astype(f32) * scale


def core_and_chip():
    place = lax.axis_index("cells")
    return lax.rem(place, CORES), lax.div(place, CORES)


def call(body, outs, in_specs, scratch=(), mib=32, flops=0, nbytes=0):
    return pl.pallas_call(
        body,
        out_shape=outs,
        in_specs=in_specs,
        out_specs=jax.tree.map(lambda _: VMEM, outs),
        scratch_shapes=list(scratch),
        compiler_params=pltpu.CompilerParams(vmem_limit_bytes=mib * MIB),
        cost_estimate=pl.CostEstimate(flops=flops, bytes_accessed=nbytes, transcendentals=0),
    )


def dense_kernel(count, rows, cols, sketch, tiles, dense, turned, theirs, place, sketch_here, load_sems, sems):
    tile = tiles.shape[1]
    core, _ = core_and_chip()
    rows_place, cols_place = place
    loads = [
        pltpu.make_async_copy(src, dst, load_sems.at[i])
        for i, (src, dst) in enumerate(((rows, rows_place), (cols, cols_place), (sketch, sketch_here)))
    ]
    for load in loads:
        load.start()

    def clear(i, _):
        dense[pl.ds(pl.multiple_of(i * 16, 16), 16), :] = jnp.zeros((16, dense.shape[1]), bf16)
        return 0

    lax.fori_loop(0, dense.shape[0] // 16, clear, 0)
    for load in loads[:2]:
        load.wait()

    def copy(s):
        r = pl.multiple_of(rows_place[s] * tile, tile)
        c = pl.multiple_of(cols_place[s] * tile, tile)
        return pltpu.make_async_copy(tiles.at[s], dense.at[pl.ds(r, tile), pl.ds(c, tile)], sems.at[s])

    def start(s, _):
        copy(s).start()
        return 0

    def wait(s, _):
        copy(s).wait()
        return 0

    lax.fori_loop(0, count[0], start, 0)
    loads[2].wait()
    turned[...] = sketch_here[...].T
    lax.fori_loop(0, count[0], wait, 0)
    half = theirs.shape[0]
    left = turned[pl.ds(pl.multiple_of((1 - core) * half, half), half), :]
    width = 512
    for j in range(dense.shape[1] // width):
        part = jnp.dot(left, dense[:, j * width : (j + 1) * width], preferred_element_type=f32)
        encode_columns(part, theirs, j * width)


def encode_columns(x, out, at):
    encode(x, out.at[:, pl.ds(at, x.shape[1])])


def own_kernel(turned, dense, mine):
    core, _ = core_and_chip()
    half = mine.shape[0]
    left = turned[pl.ds(pl.multiple_of(core * half, half), half), :]
    mine[...] = jnp.dot(left, dense[...], preferred_element_type=f32)


def pair_kernel(mine, got, out):
    width = out.shape[2]
    for j in range(out.shape[0]):
        cut = slice(j * width, (j + 1) * width)
        encode(mine[:, cut] + decode(got[:, cut]), out.at[j])


def gene_kernel(got, out):
    total = decode(got[0])
    for j in range(1, got.shape[0]):
        total = total + decode(got[j])
    for j in range(got.shape[0]):
        out[j] = total.astype(bf16)


def cell_kernel(dense, ours, theirs, out, gene):
    core, _ = core_and_chip()
    chips, half, width = ours.shape
    for j in range(chips):
        cut = slice(j * width, (j + 1) * width)
        gene[pl.ds(pl.multiple_of(core * half, half), half), cut] = ours[j]
        gene[pl.ds(pl.multiple_of((1 - core) * half, half), half), cut] = theirs[j]
    height = out.shape[1]
    for j in range(out.shape[0]):
        left = dense[j * height : (j + 1) * height, :]
        part = lax.dot_general(left, gene[...], (((1,), (1,)), ((), ())), preferred_element_type=f32)
        encode(part, out.at[j])


def last_kernel(got, out):
    total = decode(got[0])
    for j in range(1, got.shape[0]):
        total = total + decode(got[j])
    out[...] = total


def local(n_cells, n_genes, sketch, tiles, tile_rows, tile_cols, tile_counts):
    cells, rank = sketch.shape
    slots, tile, _ = tiles.shape
    genes = GENE_BLOCKS * tile
    chips = n_cells // CORES
    half = rank // CORES
    width = genes // chips
    height = cells // n_genes
    flops = 2 * cells * genes * rank
    shape = jax.ShapeDtypeStruct

    def to_core(x):
        return lax.ppermute(x, "cells", [(i, i ^ 1) for i in range(n_cells)])

    def over_chips(x):
        groups = [[chip * CORES + core for chip in range(chips)] for core in range(CORES)]
        return lax.all_to_all(x, "cells", 0, 0, axis_index_groups=groups, tiled=True)

    def over_genes(x):
        return lax.all_to_all(x, "genes", 0, 0, tiled=True)

    dense, turned, theirs = call(
        dense_kernel,
        (shape((cells, genes), bf16), shape((rank, cells), bf16), shape((half, genes), i16)),
        [SMEM] + [HBM] * 4,
        scratch=[
            (pltpu.SMEM((slots,), i32), pltpu.SMEM((slots,), i32)),
            pltpu.VMEM((cells, rank), bf16),
            pltpu.SemaphoreType.DMA((3,)),
            pltpu.SemaphoreType.DMA((slots,)),
        ],
        flops=flops // 2,
        nbytes=8 * MIB,
    )(tile_counts, *(pltpu.with_memory_space_constraint(x, pltpu.HBM) for x in (tile_rows, tile_cols, sketch, tiles)))
    got = to_core(theirs)
    mine = call(own_kernel, shape((half, genes), f32), [VMEM, VMEM], flops=flops // 2, nbytes=5 * MIB)(turned, dense)
    pieces = call(pair_kernel, shape((chips, half, width), i16), [VMEM, VMEM], nbytes=2 * MIB)(mine, got)
    chunks = call(gene_kernel, shape((chips, half, width), bf16), [VMEM], nbytes=MIB)(over_chips(pieces))
    ours = over_chips(chunks)
    theirs = to_core(ours)
    parts = call(
        cell_kernel,
        shape((n_genes, height, rank), i16),
        [VMEM] * 3,
        scratch=[pltpu.VMEM((rank, genes), bf16)],
        flops=flops,
        nbytes=6 * MIB,
    )(dense, ours, theirs)
    return call(last_kernel, shape((height, rank), f32), [VMEM], nbytes=MIB)(over_genes(parts))


def solution(mesh):
    in_specs = (
        P("cells", None),
        P(("cells", "genes"), None, None),
        P(("cells", "genes")),
        P(("cells", "genes")),
        P(("cells", "genes")),
    )
    out_specs = P(("cells", "genes"), None)
    body = functools.partial(local, mesh.shape["cells"], mesh.shape["genes"])
    return jax.shard_map(body, mesh=mesh, in_specs=in_specs, out_specs=out_specs, check_vma=False)
```

time: 54.9 us -> 61 us (1.11)
  blocking collectives: 0 us -> 49.1 us
  waiting for transfers between devices: 28.5 us -> 3.08 us
  starting transfers between devices: 13.1 us -> 0.07 us
  local copies, waits for them, and re-layouts: 4.23 us -> 0 us
  Pallas kernels: 8.43 us -> 7.75 us
    all_to_all x0 -> x3, blocking collectives: none -> 49.1 us  [the longest x2 36.8 us: over_chips(): lax.all_to_all(x, 'cells', 0, 0, axis_index_groups=groups, tiled=True)]
    ppermute x9 -> x0, waiting for transfers between devices: 26.3 us -> none  [the longest x6 19.7 us: to_chip(): lax.ppermute(x, 'cells', [(i, i ^ k * CORES) for i in range(n_cells)])]
    ppermute x9 -> x0, starting transfers between devices: 12.5 us -> none  [the longest x6 8.9 us: to_chip(): lax.ppermute(x, 'cells', [(i, i ^ k * CORES) for i in range(n_cells)])]
    unnamed x8 -> x0, local copies, waits for them, and re-layouts: 4.23 us -> none
    ppermute x5 -> x2, waiting for transfers between devices: 2.19 us -> 3.08 us  [to_core(): return lax.ppermute(x, 'cells', [(i, i ^ 1) for i in range(n_cells)])]
    pallas_call x1, Pallas kernels: 4.99 us -> 4.29 us  [local(): call(dense_kernel, (shape((cells, genes), bf16), shape((rank, cells), bf1...]
  transfers between devices with their start and end apart: 14 -> 2, of which waited for: 10 -> 2; matrix products, arithmetic and copies ran while one was open for 0% -> 0% of each run, Pallas kernels for 1% -> 1%
where the time goes in v2:
time: 61 us; the launch traced here: 60.7 us
  blocking collectives  49.1 us (80%)
  Pallas kernels  7.75 us (13%)
  waiting for transfers between devices  3.08 us (5%)
  between operations  0.69 us (1%)
    all_to_all x2, blocking collectives, over_chips(): lax.all_to_all(x, 'cells', 0, 0, axis_index_groups=groups, tiled=True)  36.8 us
    all_to_all x1, blocking collectives, over_genes(): return lax.all_to_all(x, 'genes', 0, 0, tiled=True)  12.3 us
    pallas_call x1, Pallas kernels, local(): call(dense_kernel, (shape((cells, genes), bf16), shape((rank, cells), bf1...  4.29 us
    ppermute x2, waiting for transfers between devices, to_core(): return lax.ppermute(x, 'cells', [(i, i ^ 1) for i in range(n_cells)])  3.08 us
    pallas_call x1, Pallas kernels, local(): call(cell_kernel, shape((n_genes, height, rank), i16), [VMEM] * 3, scratc...  1.42 us
  transfers between devices with their start and end apart: 2, of which 2 were waited for; matrix products, arithmetic and copies ran while one was open for 0% of the time, Pallas kernels for 1%

profile of v2, /device:TPU:0, one launch (start us, length us, event | category | flops | bytes accessed | tf_op | source)
XLA Modules:
  0.0 60.7 jit_solution(5511953565725411368)
XLA Ops:
  0.7 4.3 %shard_map.55 = (bf16[1024,2048]{1,0:T(8,128)(2,1)S(1)}, bf16[256,1024]{1,0:T(8,128)(2,1)S(1)}, s16[128,2048]{1,0:T(8,128)(2,1)S(1)}) custom-call(s32[1]{0:T(128)S(6)} %copy.6.count, s32[96]{0:T(128)} %rows.1, s32[96]{0:T(128)} %cols.1, bf16[1024,256]{1,0:T(8,128)(2,1)} %sketch.1, bf16[96,128,128]{2,1,0:T(8,128)(2,1)} %tiles.1), custom_call_target="tpu_custom_call" | custom-call | flops 536870912 | bytes 8388608 | tf_op jit(solution)/shard_map/pallas_call | solution.py:172
  4.9 0.1 collective-permute-start
  5.0 0.7 %shard_map.56.mine = f32[128,2048]{1,0:T(8,128)S(1)} custom-call(bf16[256,1024]{1,0:T(8,128)(2,1)S(1)} %get-tuple-element.9.turned, bf16[1024,2048]{1,0:T(8,128)(2,1)S(1)} %get-tuple-element.8.dense), custom_call_target="tpu_custom_call" | custom-call | flops 536870912 | bytes 5242880 | tf_op jit(solution)/shard_map/pallas_call | solution.py:186
  5.8 1.2 %collective-permute-done.got = s16[128,2048]{1,0:T(8,128)(2,1)S(1)} collective-permute-done((s16[128,2048]{1,0:T(8,128)(2,1)S(1)}, s16[128,2048]{1,0:T(8,128)(2,1)S(1)}, u32[]{:S(2)}, u32[]{:S(2)}) %collective-permute-start) | collective-permute-done | bytes 524320 | tf_op jit(solution)/shard_map/ppermute | solution.py:163
  6.9 0.3 shard_map.57
  7.3 20.2 %all_to_all.15.got = s16[4,128,512]{2,1,0:T(8,128)(2,1)S(1)} all-to-all(s16[4,128,512]{2,1,0:T(8,128)(2,1)S(1)} %shard_map.57), channel_id=1, replica_groups={{0,8,16,24},{4,12,20,28},{1,9,17,25},{5,13,21,29},{2,10,18,26},{6,14,22..., dimensions={0} | all-to-all | bytes 1048576 | tf_op jit(solution)/shard_map/all_to_all | solution.py:167
  27.5 0.2 shard_map.58
  27.6 16.6 %all_to_all.16.ours = bf16[4,128,512]{2,1,0:T(8,128)(2,1)S(1)} all-to-all(bf16[4,128,512]{2,1,0:T(8,128)(2,1)S(1)} %shard_map.58), channel_id=1, replica_groups={{0,8,16,24},{4,12,20,28},{1,9,17,25},{5,13,21,29},{2,10,18,26},{6,14,22..., dimensions={0} | all-to-all | bytes 1048576 | tf_op jit(solution)/shard_map/all_to_all | solution.py:167
  44.2 0.0 collective-permute-start.1
  44.2 1.9 %collective-permute-done.1.theirs = bf16[4,128,512]{2,1,0:T(8,128)(2,1)S(1)} collective-permute-done((bf16[4,128,512]{2,1,0:T(8,128)(2,1)S(1)}, bf16[4,128,512]{2,1,0:T(8,128)(2,1)S(1)}, u32[]{:S(2)}, u32[]{:S(2)}) %collective-permute-start.1) | collective-permute-done | bytes 524320 | tf_op jit(solution)/shard_map/ppermute | solution.py:163
  46.1 1.4 %shard_map.59 = s16[4,256,256]{2,1,0:T(8,128)(2,1)S(1)} custom-call(bf16[1024,2048]{1,0:T(8,128)(2,1)S(1)} %get-tuple-element.8.dense, bf16[4,128,512]{2,1,0:T(8,128)(2,1)S(1)} %all_to_all.16.ours, bf16[4,128,512]{2,1,0:T(8,128)(2,1)S(1)} %collective-permute-done.1.theirs), custom_call_target="tpu_custom_call" | custom-call | flops 1073741824 | bytes 6291456 | tf_op jit(solution)/shard_map/pallas_call | solution.py:191
  47.6 12.3 %all_to_all.17.got = s16[4,256,256]{2,1,0:T(8,128)(2,1)S(1)} all-to-all(s16[4,256,256]{2,1,0:T(8,128)(2,1)S(1)} %shard_map.59), channel_id=1, replica_groups=mesh['cells'=8,'genes'=4] {'genes'}, dimensions={0} | all-to-all | bytes 1048576 | tf_op jit(solution)/shard_map/all_to_all | solution.py:170
  59.9 0.8 %shard_map.60 = f32[256,256]{1,0:T(8,128)} custom-call(s16[4,256,256]{2,1,0:T(8,128)(2,1)S(1)} %all_to_all.17.got), custom_call_target="tpu_custom_call" | custom-call | bytes 1048576 | tf_op jit(solution)/shard_map/pallas_call | solution.py:199
Async XLA Ops:
  4.9 2.0 %collective-permute-start = (s16[128,2048]{1,0:T(8,128)(2,1)S(1)}, s16[128,2048]{1,0:T(8,128)(2,1)S(1)}, u32[]{:S(2)}, u32[]{:S(2)}) collective-permute-start(s16[128,2048]{1,0:T(8,128)(2,1)S(1)} %get-tuple-element.10), channel_id=1, source_target_pairs={{0,4},{4,0},{8,12},{12,8},{16,20},{20,16},{24,28},{28,24},{1,5},{5... | collective-permute-start | bytes 1572872 | tf_op jit(solution)/shard_map/ppermute | solution.py:163
  44.2 1.9 %collective-permute-start.1 = (bf16[4,128,512]{2,1,0:T(8,128)(2,1)S(1)}, bf16[4,128,512]{2,1,0:T(8,128)(2,1)S(1)}, u32[]{:S(2)}, u32[]{:S(2)}) collective-permute-start(bf16[4,128,512]{2,1,0:T(8,128)(2,1)S(1)} %all_to_all.16.ours), channel_id=1, source_target_pairs={{0,4},{4,0},{8,12},{12,8},{16,20},{20,16},{24,28},{28,24},{1,5},{5... | collective-permute-start | bytes 1572872 | tf_op jit(solution)/shard_map/ppermute | solution.py:163

commit v3 on v2

--- a/solution.py
+++ b/solution.py
@@ -9,6 +9,7 @@
 
 GENE_BLOCKS = 16
 CORES = 2
+STREAMS = 2
 MIB = 1 << 20
 
 VMEM = pl.BlockSpec(memory_space=pltpu.VMEM)
@@ -57,6 +58,12 @@
     )
 
 
+def rows_of(turned, core, rows):
+    span = rows * CORES
+    at = [pl.multiple_of(i * span + core * rows, rows) for i in range(STREAMS)]
+    return jnp.concatenate([turned[pl.ds(x, rows), :] for x in at], axis=0)
+
+
 def dense_kernel(count, rows, cols, sketch, tiles, dense, turned, theirs, place, sketch_here, load_sems, sems):
     tile = tiles.shape[1]
     core, _ = core_and_chip()
@@ -93,68 +100,93 @@
     loads[2].wait()
     turned[...] = sketch_here[...].T
     lax.fori_loop(0, count[0], wait, 0)
-    half = theirs.shape[0]
-    left = turned[pl.ds(pl.multiple_of((1 - core) * half, half), half), :]
+    left = rows_of(turned, 1 - core, theirs.shape[0] // STREAMS)
     width = 512
     for j in range(dense.shape[1] // width):
-        part = jnp.dot(left, dense[:, j * width : (j + 1) * width], preferred_element_type=f32)
-        encode_columns(part, theirs, j * width)
-
-
-def encode_columns(x, out, at):
-    encode(x, out.at[:, pl.ds(at, x.shape[1])])
+        cut = pl.ds(j * width, width)
+        encode(jnp.dot(left, dense[:, cut], preferred_element_type=f32), theirs.at[:, cut])
 
 
 def own_kernel(turned, dense, mine):
     core, _ = core_and_chip()
-    half = mine.shape[0]
-    left = turned[pl.ds(pl.multiple_of(core * half, half), half), :]
+    left = rows_of(turned, core, mine.shape[0] // STREAMS)
     mine[...] = jnp.dot(left, dense[...], preferred_element_type=f32)
 
 
-def pair_kernel(mine, got, out):
-    width = out.shape[2]
-    for j in range(out.shape[0]):
-        cut = slice(j * width, (j + 1) * width)
-        encode(mine[:, cut] + decode(got[:, cut]), out.at[j])
-
-
-def gene_kernel(got, out):
-    total = decode(got[0])
-    for j in range(1, got.shape[0]):
-        total = total + decode(got[j])
-    for j in range(got.shape[0]):
-        out[j] = total.astype(bf16)
-
-
-def cell_kernel(dense, ours, theirs, out, gene):
-    core, _ = core_and_chip()
-    chips, half, width = ours.shape
-    for j in range(chips):
-        cut = slice(j * width, (j + 1) * width)
-        gene[pl.ds(pl.multiple_of(core * half, half), half), cut] = ours[j]
-        gene[pl.ds(pl.multiple_of((1 - core) * half, half), half), cut] = theirs[j]
-    height = out.shape[1]
-    for j in range(out.shape[0]):
-        left = dense[j * height : (j + 1) * height, :]
+def halve(total, bit, keep, send):
+    _, chip = core_and_chip()
+    width = keep.shape[1]
+    ours = (chip >> bit) & 1
+    low, high = total[:, :width], total[:, width:]
+    keep[...] = jnp.where(ours == 0, low, high)
+    encode(jnp.where(ours == 0, high, low), send)
+
+
+def pair_kernel(halves, mine, got, *outs):
+    total = mine[...] + decode(got[...])
+    rows = total.shape[0] // STREAMS
+    for i in range(STREAMS):
+        part = total[i * rows : (i + 1) * rows]
+        if halves:
+            halve(part, 0, *outs[2 * i : 2 * i + 2])
+        else:
+            encode(part, outs[i])
+
+
+def add_kernel(bit, keep, got, *outs):
+    total = keep[...] + decode(got[...])
+    if len(outs) == 2:
+        halve(total, bit, *outs)
+    else:
+        encode(total, outs[0])
+
+
+def cast_kernel(code, got, out):
+    out[...] = (decode(code[...]) + decode(got[...])).astype(bf16)
+
+
+def cell_kernel(masks, dense, *refs):
+    ours, theirs = refs[: len(masks)], refs[len(masks) : 2 * len(masks)]
+    outs, gene = refs[2 * len(masks) : -1], refs[-1]
+    core, chip = core_and_chip()
+    rows, width = ours[0].shape
+    for k, mask in enumerate(masks):
+        at, size = 0, gene.shape[1]
+        for bit in range(len(masks).bit_length() - 1):
+            size //= 2
+            at = at + (((chip ^ mask) >> bit) & 1) * size
+        cut = pl.ds(pl.multiple_of(at, width), width)
+        gene[pl.ds(pl.multiple_of(core * rows, rows), rows), cut] = ours[k][...]
+        gene[pl.ds(pl.multiple_of((1 - core) * rows, rows), rows), cut] = theirs[k][...]
+    me = lax.axis_index("genes")
+    height = outs[0].shape[0]
+    for k, out in enumerate(outs):
+        left = dense[pl.ds(pl.multiple_of((me ^ k) * height, height), height), :]
         part = lax.dot_general(left, gene[...], (((1,), (1,)), ((), ())), preferred_element_type=f32)
-        encode(part, out.at[j])
-
-
-def last_kernel(got, out):
-    total = decode(got[0])
-    for j in range(1, got.shape[0]):
-        total = total + decode(got[j])
-    out[...] = total
+        if k == 0:
+            out[...] = part
+        else:
+            encode(part, out)
+
+
+def last_kernel(count, *refs):
+    out = refs[-1]
+    for i in range(STREAMS):
+        own, *got = refs[i * count : (i + 1) * count]
+        total = own[...]
+        for ref in got:
+            total = total + decode(ref[...])
+        out[:, i * own.shape[1] : (i + 1) * own.shape[1]] = total
 
 
 def local(n_cells, n_genes, sketch, tiles, tile_rows, tile_cols, tile_counts):
     cells, rank = sketch.shape
     slots, tile, _ = tiles.shape
     genes = GENE_BLOCKS * tile
-    chips = n_cells // CORES
-    half = rank // CORES
-    width = genes // chips
+    bits = (n_cells // CORES).bit_length() - 1
+    span = rank // STREAMS
+    rows = span // CORES
+    share = rows * STREAMS
     height = cells // n_genes
     flops = 2 * cells * genes * rank
     shape = jax.ShapeDtypeStruct
@@ -162,16 +194,18 @@
     def to_core(x):
         return lax.ppermute(x, "cells", [(i, i ^ 1) for i in range(n_cells)])
 
-    def over_chips(x):
-        groups = [[chip * CORES + core for chip in range(chips)] for core in range(CORES)]
-        return lax.all_to_all(x, "cells", 0, 0, axis_index_groups=groups, tiled=True)
-
-    def over_genes(x):
-        return lax.all_to_all(x, "genes", 0, 0, tiled=True)
+    def to_chip(x, bit):
+        return lax.ppermute(x, "cells", [(i, i ^ (CORES << bit)) for i in range(n_cells)])
+
+    def to_gene(x, k):
+        return lax.ppermute(x, "genes", [(i, i ^ k) for i in range(n_genes)])
+
+    def halves(width):
+        return shape((rows, width // 2), f32), shape((rows, width // 2), i16)
 
     dense, turned, theirs = call(
         dense_kernel,
-        (shape((cells, genes), bf16), shape((rank, cells), bf16), shape((half, genes), i16)),
+        (shape((cells, genes), bf16), shape((rank, cells), bf16), shape((share, genes), i16)),
         [SMEM] + [HBM] * 4,
         scratch=[
             (pltpu.SMEM((slots,), i32), pltpu.SMEM((slots,), i32)),
@@ -183,20 +217,47 @@
         nbytes=8 * MIB,
     )(tile_counts, *(pltpu.with_memory_space_constraint(x, pltpu.HBM) for x in (tile_rows, tile_cols, sketch, tiles)))
     got = to_core(theirs)
-    mine = call(own_kernel, shape((half, genes), f32), [VMEM, VMEM], flops=flops // 2, nbytes=5 * MIB)(turned, dense)
-    pieces = call(pair_kernel, shape((chips, half, width), i16), [VMEM, VMEM], nbytes=2 * MIB)(mine, got)
-    chunks = call(gene_kernel, shape((chips, half, width), bf16), [VMEM], nbytes=MIB)(over_chips(pieces))
-    ours = over_chips(chunks)
-    theirs = to_core(ours)
-    parts = call(
-        cell_kernel,
-        shape((n_genes, height, rank), i16),
-        [VMEM] * 3,
-        scratch=[pltpu.VMEM((rank, genes), bf16)],
-        flops=flops,
-        nbytes=6 * MIB,
-    )(dense, ours, theirs)
-    return call(last_kernel, shape((height, rank), f32), [VMEM], nbytes=MIB)(over_genes(parts))
+    mine = call(own_kernel, shape((share, genes), f32), [VMEM, VMEM], flops=flops // 2, nbytes=5 * MIB)(turned, dense)
+    cut = bits > 1
+    one = halves(genes) if cut else (shape((rows, genes), i16),)
+    pieces = call(functools.partial(pair_kernel, cut), one * STREAMS, [VMEM, VMEM], nbytes=2 * MIB)(mine, got)
+
+    def gene_side(i):
+        width = genes
+        if cut:
+            keep, send = pieces[2 * i : 2 * i + 2]
+            for bit in range(bits - 1):
+                width //= 2
+                got = to_chip(send, bit)
+                outs = halves(width) if bit < bits - 2 else (shape((rows, width), i16),)
+                done = call(functools.partial(add_kernel, bit + 1), outs, [VMEM, VMEM], nbytes=MIB)(keep, got)
+                keep, send = done[0], done[-1]
+            code = send
+        else:
+            code = pieces[i]
+        got = to_chip(code, bits - 1)
+        held = [call(cast_kernel, shape((rows, width), bf16), [VMEM, VMEM], nbytes=MIB)(code, got)]
+        masks = [0]
+        for bit in reversed(range(bits - 1)):
+            held += [to_chip(x, bit) for x in held]
+            masks += [mask ^ (1 << bit) for mask in masks]
+        return held, masks
+
+    parts = []
+    for i in range(STREAMS):
+        held, masks = gene_side(i)
+        partner = [to_core(x) for x in held]
+        outs = call(
+            functools.partial(cell_kernel, masks),
+            (shape((height, span), f32),) + (shape((height, span), i16),) * (n_genes - 1),
+            [VMEM] * (1 + 2 * len(held)),
+            scratch=[pltpu.VMEM((span, genes), bf16)],
+            flops=flops // STREAMS,
+            nbytes=5 * MIB,
+        )(dense, *held, *partner)
+        parts += [outs[0]] + [to_gene(outs[k], k) for k in range(1, n_genes)]
+    last = functools.partial(last_kernel, n_genes)
+    return call(last, shape((height, rank), f32), [VMEM] * len(parts), nbytes=MIB)(*parts)
 
 
 def solution(mesh):

time: 61 us -> 49.7 us (0.81)
  blocking collectives: 49.1 us -> 0 us
  waiting for transfers between devices: 3.08 us -> 23.1 us
  starting transfers between devices: 0.07 us -> 16.6 us
  Pallas kernels: 7.75 us -> 9.22 us
    all_to_all x3 -> x0, blocking collectives: 49.1 us -> none  [the longest x2 36.8 us: over_chips(): lax.all_to_all(x, 'cells', 0, 0, axis_index_groups=groups, tiled=True)]
    ppermute x0 -> x12, waiting for transfers between devices: none -> 21.9 us  [the longest x6 16.9 us: to_chip(): lax.ppermute(x, 'cells', [(i, i ^ CORES << bit) for i in range(n_cells)])]
    ppermute x0 -> x12, starting transfers between devices: none -> 16 us  [the longest x6 8.94 us: to_chip(): lax.ppermute(x, 'cells', [(i, i ^ CORES << bit) for i in range(n_cells)])]
    ppermute x2 -> x5, waiting for transfers between devices: 3.08 us -> 1.18 us  [to_core(): return lax.ppermute(x, 'cells', [(i, i ^ 1) for i in range(n_cells)])]
    pallas_call x5 -> x9, Pallas kernels: 3.47 us -> 4.93 us  [the longest x2 2.69 us: local(): call(functools.partial(cell_kernel, masks), (shape((height, span), f32),)...]
  transfers between devices with their start and end apart: 2 -> 17, of which waited for: 2 -> 10; matrix products, arithmetic and copies ran while one was open for 0% -> 0% of each run, Pallas kernels for 1% -> 8%
where the time goes in v3:
time: 49.7 us
  waiting for transfers between devices  23.1 us (46%)
  starting transfers between devices  16.6 us (33%)
  Pallas kernels  9.22 us (19%)
  between operations  0.73 us (1%)
    ppermute x6, waiting for transfers between devices, to_chip(): lax.ppermute(x, 'cells', [(i, i ^ CORES << bit) for i in range(n_cells)])  16.9 us
    ppermute x6, starting transfers between devices, to_chip(): lax.ppermute(x, 'cells', [(i, i ^ CORES << bit) for i in range(n_cells)])  8.94 us
    ppermute x6, starting transfers between devices, to_gene(): return lax.ppermute(x, 'genes', [(i, i ^ k) for i in range(n_genes)])  7.11 us
    ppermute x6, waiting for transfers between devices, to_gene(): return lax.ppermute(x, 'genes', [(i, i ^ k) for i in range(n_genes)])  5 us
    pallas_call x1, Pallas kernels, local(): call(dense_kernel, (shape((cells, genes), bf16), shape((rank, cells), bf1...  4.29 us
    pallas_call x2, Pallas kernels, local(): call(functools.partial(cell_kernel, masks), (shape((height, span), f32),)...  2.69 us
    ppermute x5, waiting for transfers between devices, to_core(): return lax.ppermute(x, 'cells', [(i, i ^ 1) for i in range(n_cells)])  1.18 us
  transfers between devices with their start and end apart: 17, of which 10 were waited for; matrix products, arithmetic and copies ran while one was open for 0% of the time, Pallas kernels for 8%

profile of v3, /device:TPU:0, one launch (start us, length us, event | category | flops | bytes accessed | tf_op | source)
XLA Modules:
  0.0 49.7 jit_solution(14001212464954008160)
XLA Ops:
  0.7 4.3 %shard_map.55 = (bf16[1024,2048]{1,0:T(8,128)(2,1)S(1)}, bf16[256,1024]{1,0:T(8,128)(2,1)S(1)}, s16[128,2048]{1,0:T(8,128)(2,1)S(1)}) custom-call(s32[1]{0:T(128)S(6)} %copy.6.count, s32[96]{0:T(128)} %rows.1, s32[96]{0:T(128)} %cols.1, bf16[1024,256]{1,0:T(8,128)(2,1)} %sketch.1, bf16[96,128,128]{2,1,0:T(8,128)(2,1)} %tiles.1), custom_call_target="tpu_custom_call" | custom-call | flops 536870912 | bytes 8388608 | tf_op jit(solution)/shard_map/pallas_call | solution.py:206
  5.0 0.7 %shard_map.56.mine = f32[128,2048]{1,0:T(8,128)S(1)} custom-call(bf16[256,1024]{1,0:T(8,128)(2,1)S(1)} %get-tuple-element.21.turned, bf16[1024,2048]{1,0:T(8,128)(2,1)S(1)} %get-tuple-element.20.dense), custom_call_target="tpu_custom_call" | custom-call | flops 536870912 | bytes 5242880 | tf_op jit(solution)/shard_map/pallas_call | solution.py:220
  5.8 1.2 %collective-permute-done.got = s16[128,2048]{1,0:T(8,128)(2,1)S(1)} collective-permute-done((s16[128,2048]{1,0:T(8,128)(2,1)S(1)}, s16[128,2048]{1,0:T(8,128)(2,1)S(1)}, u32[]{:S(2)}, u32[]{:S(2)}) %collective-permute-start) | collective-permute-done | bytes 524320 | tf_op jit(solution)/shard_map/ppermute | solution.py:195
  6.9 0.3 shard_map.57
  7.2 2.5 %collective-permute-start.1 = (s16[64,1024]{1,0:T(8,128)(2,1)S(1)}, s16[64,1024]{1,0:T(8,128)(2,1)S(1)}, u32[]{:S(2)}, u32[]{:S(2)}) collective-permute-start(s16[64,1024]{1,0:T(8,128)(2,1)S(1)} %get-tuple-element.24), channel_id=1, source_target_pairs={{0,8},{4,12},{8,0},{12,4},{16,24},{20,28},{24,16},{28,20},{1,9},{5... | collective-permute-start | bytes 393224 | tf_op jit(solution)/shard_map/ppermute | solution.py:198
  9.8 4.2 %collective-permute-done.1.got = s16[64,1024]{1,0:T(8,128)(2,1)S(1)} collective-permute-done((s16[64,1024]{1,0:T(8,128)(2,1)S(1)}, s16[64,1024]{1,0:T(8,128)(2,1)S(1)}, u32[]{:S(2)}, u32[]{:S(2)}) %collective-permute-start.1) | collective-permute-done | bytes 131104 | tf_op jit(solution)/shard_map/ppermute | solution.py:198
  14.0 0.1 shard_map.58.code
  14.1 2.8 %collective-permute-start.2 = (s16[64,1024]{1,0:T(8,128)(2,1)S(1)}, s16[64,1024]{1,0:T(8,128)(2,1)S(1)}, u32[]{:S(2)}, u32[]{:S(2)}) collective-permute-start(s16[64,1024]{1,0:T(8,128)(2,1)S(1)} %shard_map.58.code), channel_id=1, source_target_pairs={{0,16},{4,20},{8,24},{12,28},{16,0},{20,4},{24,8},{28,12},{1,17},{... | collective-permute-start | bytes 393224 | tf_op jit(solution)/shard_map/ppermute | solution.py:198
  17.0 0.1 shard_map.61.code
  17.1 2.7 %collective-permute-start.10 = (s16[64,1024]{1,0:T(8,128)(2,1)S(1)}, s16[64,1024]{1,0:T(8,128)(2,1)S(1)}, u32[]{:S(2)}, u32[]{:S(2)}) collective-permute-start(s16[64,1024]{1,0:T(8,128)(2,1)S(1)} %shard_map.61.code), channel_id=1, source_target_pairs={{0,16},{4,20},{8,24},{12,28},{16,0},{20,4},{24,8},{28,12},{1,17},{... | collective-permute-start | bytes 393224 | tf_op jit(solution)/shard_map/ppermute | solution.py:198
  19.8 6.7 %collective-permute-done.2.got = s16[64,1024]{1,0:T(8,128)(2,1)S(1)} collective-permute-done((s16[64,1024]{1,0:T(8,128)(2,1)S(1)}, s16[64,1024]{1,0:T(8,128)(2,1)S(1)}, u32[]{:S(2)}, u32[]{:S(2)}) %collective-permute-start.2) | collective-permute-done | bytes 131104 | tf_op jit(solution)/shard_map/ppermute | solution.py:198
  26.5 0.1 shard_map.59.refs_0_
  26.5 0.3 collective-permute-start.3
  26.9 1.3 %collective-permute-done.10.got = s16[64,1024]{1,0:T(8,128)(2,1)S(1)} collective-permute-done((s16[64,1024]{1,0:T(8,128)(2,1)S(1)}, s16[64,1024]{1,0:T(8,128)(2,1)S(1)}, u32[]{:S(2)}, u32[]{:S(2)}) %collective-permute-start.10) | collective-permute-done | bytes 131104 | tf_op jit(solution)/shard_map/ppermute | solution.py:198
  28.2 0.1 shard_map.62.refs_0_
  28.3 0.5 %collective-permute-start.11 = (bf16[64,1024]{1,0:T(8,128)(2,1)S(1)}, bf16[64,1024]{1,0:T(8,128)(2,1)S(1)}, u32[]{:S(2)}, u32[]{:S(2)}) collective-permute-start(bf16[64,1024]{1,0:T(8,128)(2,1)S(1)} %shard_map.62.refs_0_), channel_id=1, source_target_pairs={{0,8},{4,12},{8,0},{12,4},{16,24},{20,28},{24,16},{28,20},{1,9},{5... | collective-permute-start | bytes 393224 | tf_op jit(solution)/shard_map/ppermute | solution.py:198
  28.8 3.8 %collective-permute-done.3.refs_1_ = bf16[64,1024]{1,0:T(8,128)(2,1)S(1)} collective-permute-done((bf16[64,1024]{1,0:T(8,128)(2,1)S(1)}, bf16[64,1024]{1,0:T(8,128)(2,1)S(1)}, u32[]{:S(2)}, u32[]{:S(2)}) %collective-permute-start.3) | collective-permute-done | bytes 131104 | tf_op jit(solution)/shard_map/ppermute | solution.py:198
  32.6 0.5 %collective-permute-start.12 = (bf16[64,1024]{1,0:T(8,128)(2,1)S(1)}, bf16[64,1024]{1,0:T(8,128)(2,1)S(1)}, u32[]{:S(2)}, u32[]{:S(2)}) collective-permute-start(bf16[64,1024]{1,0:T(8,128)(2,1)S(1)} %shard_map.62.refs_0_), channel_id=1, source_target_pairs={{0,4},{4,0},{8,12},{12,8},{16,20},{20,16},{24,28},{28,24},{1,5},{5... | collective-permute-start | bytes 393224 | tf_op jit(solution)/shard_map/ppermute | solution.py:195
  33.1 0.9 %collective-permute-done.11.refs_1_ = bf16[64,1024]{1,0:T(8,128)(2,1)S(1)} collective-permute-done((bf16[64,1024]{1,0:T(8,128)(2,1)S(1)}, bf16[64,1024]{1,0:T(8,128)(2,1)S(1)}, u32[]{:S(2)}, u32[]{:S(2)}) %collective-permute-start.11) | collective-permute-done | bytes 131104 | tf_op jit(solution)/shard_map/ppermute | solution.py:198
  34.0 1.3 %shard_map.60 = (f32[256,128]{1,0:T(8,128)S(1)}, s16[256,128]{1,0:T(8,128)(2,1)S(1)}, s16[256,128]{1,0:T(8,128)(2,1)S(1)}, s16[256,128]{1,0:T(8,128)(2,1)S(1)}) custom-call(bf16[1024,2048]{1,0:T(8,128)(2,1)S(1)} %get-tuple-element.20.dense, bf16[64,1024]{1,0:T(8,128)(2,1)S(1)} %shard_map.59.refs_0_, bf16[64,1024]{1,0:T(8,128)(2,1)S(1)} %collective-permute-done.3.refs_1_, ...), custom_call_target="tpu_custom_call" | custom-call | flops 536870912 | bytes 5242880 | tf_op jit(solution)/shard_map/pallas_call | solution.py:250
  35.4 1.5 %collective-permute-start.6 = (s16[256,128]{1,0:T(8,128)(2,1)S(1)}, s16[256,128]{1,0:T(8,128)(2,1)S(1)}, u32[]{:S(2)}, u32[]{:S(2)}) collective-permute-start(s16[256,128]{1,0:T(8,128)(2,1)S(1)} %get-tuple-element.26), channel_id=1, source_target_pairs={{0,1},{1,0},{2,3},{3,2},{4,5},{5,4},{6,7},{7,6},{8,9},{9,8},{10,11... | collective-permute-start | bytes 196616 | tf_op jit(solution)/shard_map/ppermute | solution.py:201
  36.9 1.9 %collective-permute-start.7 = (s16[256,128]{1,0:T(8,128)(2,1)S(1)}, s16[256,128]{1,0:T(8,128)(2,1)S(1)}, u32[]{:S(2)}, u32[]{:S(2)}) collective-permute-start(s16[256,128]{1,0:T(8,128)(2,1)S(1)} %get-tuple-element.27), channel_id=1, source_target_pairs={{0,2},{1,3},{2,0},{3,1},{4,6},{5,7},{6,4},{7,5},{8,10},{9,11},{10,... | collective-permute-start | bytes 196616 | tf_op jit(solution)/shard_map/ppermute | solution.py:201
  38.8 0.2 collective-permute-start.8
  38.9 1.3 %shard_map.63 = (f32[256,128]{1,0:T(8,128)S(1)}, s16[256,128]{1,0:T(8,128)(2,1)S(1)}, s16[256,128]{1,0:T(8,128)(2,1)S(1)}, s16[256,128]{1,0:T(8,128)(2,1)S(1)}) custom-call(bf16[1024,2048]{1,0:T(8,128)(2,1)S(1)} %get-tuple-element.20.dense, bf16[64,1024]{1,0:T(8,128)(2,1)S(1)} %shard_map.62.refs_0_, bf16[64,1024]{1,0:T(8,128)(2,1)S(1)} %collective-permute-done.11.refs_1_, ...), custom_call_target="tpu_custom_call" | custom-call | flops 536870912 | bytes 5242880 | tf_op jit(solution)/shard_map/pallas_call | solution.py:250
  40.3 1.5 %collective-permute-start.14 = (s16[256,128]{1,0:T(8,128)(2,1)S(1)}, s16[256,128]{1,0:T(8,128)(2,1)S(1)}, u32[]{:S(2)}, u32[]{:S(2)}) collective-permute-start(s16[256,128]{1,0:T(8,128)(2,1)S(1)} %get-tuple-element.32), channel_id=1, source_target_pairs={{0,1},{1,0},{2,3},{3,2},{4,5},{5,4},{6,7},{7,6},{8,9},{9,8},{10,11... | collective-permute-start | bytes 196616 | tf_op jit(solution)/shard_map/ppermute | solution.py:201
  41.8 1.9 %collective-permute-start.15 = (s16[256,128]{1,0:T(8,128)(2,1)S(1)}, s16[256,128]{1,0:T(8,128)(2,1)S(1)}, u32[]{:S(2)}, u32[]{:S(2)}) collective-permute-start(s16[256,128]{1,0:T(8,128)(2,1)S(1)} %get-tuple-element.33), channel_id=1, source_target_pairs={{0,2},{1,3},{2,0},{3,1},{4,6},{5,7},{6,4},{7,5},{8,10},{9,11},{10,... | collective-permute-start | bytes 196616 | tf_op jit(solution)/shard_map/ppermute | solution.py:201
  43.7 0.2 collective-permute-start.16
  43.9 0.4 collective-permute-done.8.refs_3_
  44.2 0.4 collective-permute-done.14.refs_5_
  44.6 1.5 %collective-permute-done.15.refs_6_ = s16[256,128]{1,0:T(8,128)(2,1)S(1)} collective-permute-done((s16[256,128]{1,0:T(8,128)(2,1)S(1)}, s16[256,128]{1,0:T(8,128)(2,1)S(1)}, u32[]{:S(2)}, u32[]{:S(2)}) %collective-permute-start.15) | collective-permute-done | bytes 65568 | tf_op jit(solution)/shard_map/ppermute | solution.py:201
  46.1 2.8 %collective-permute-done.16.refs_7_ = s16[256,128]{1,0:T(8,128)(2,1)S(1)} collective-permute-done((s16[256,128]{1,0:T(8,128)(2,1)S(1)}, s16[256,128]{1,0:T(8,128)(2,1)S(1)}, u32[]{:S(2)}, u32[]{:S(2)}) %collective-permute-start.16) | collective-permute-done | bytes 65568 | tf_op jit(solution)/shard_map/ppermute | solution.py:201
  48.9 0.8 %shard_map.64 = f32[256,256]{1,0:T(8,128)} custom-call(f32[256,128]{1,0:T(8,128)S(1)} %get-tuple-element.25.refs_0_, s16[256,128]{1,0:T(8,128)(2,1)S(1)} %collective-permute-done.6.refs_1_, s16[256,128]{1,0:T(8,128)(2,1)S(1)} %collective-permute-done.7.refs_2_, s16[256,128]{1,0:T(8,128)(2,1)S(1)} %collective-permute-done.8.refs_3_, ...), custom_call_target="tpu_custom_call" | custom-call | bytes 1048576 | tf_op jit(solution)/shard_map/pallas_call | solution.py:260
  (12 shorter events, 0.2 us)
Async XLA Ops:
  4.9 2.0 %collective-permute-start = (s16[128,2048]{1,0:T(8,128)(2,1)S(1)}, s16[128,2048]{1,0:T(8,128)(2,1)S(1)}, u32[]{:S(2)}, u32[]{:S(2)}) collective-permute-start(s16[128,2048]{1,0:T(8,128)(2,1)S(1)} %get-tuple-element.22), channel_id=1, source_target_pairs={{0,4},{4,0},{8,12},{12,8},{16,20},{20,16},{24,28},{28,24},{1,5},{5... | collective-permute-start | bytes 1572872 | tf_op jit(solution)/shard_map/ppermute | solution.py:195
  7.2 6.8 %collective-permute-start.1 = (s16[64,1024]{1,0:T(8,128)(2,1)S(1)}, s16[64,1024]{1,0:T(8,128)(2,1)S(1)}, u32[]{:S(2)}, u32[]{:S(2)}) collective-permute-start(s16[64,1024]{1,0:T(8,128)(2,1)S(1)} %get-tuple-element.24), channel_id=1, source_target_pairs={{0,8},{4,12},{8,0},{12,4},{16,24},{20,28},{24,16},{28,20},{1,9},{5... | collective-permute-start | bytes 393224 | tf_op jit(solution)/shard_map/ppermute | solution.py:198
  9.7 7.2 %collective-permute-start.9 = (s16[64,1024]{1,0:T(8,128)(2,1)S(1)}, s16[64,1024]{1,0:T(8,128)(2,1)S(1)}, u32[]{:S(2)}, u32[]{:S(2)}) collective-permute-start(s16[64,1024]{1,0:T(8,128)(2,1)S(1)} %get-tuple-element.30), channel_id=1, source_target_pairs={{0,8},{4,12},{8,0},{12,4},{16,24},{20,28},{24,16},{28,20},{1,9},{5... | collective-permute-start | bytes 393224 | tf_op jit(solution)/shard_map/ppermute | solution.py:198
  14.1 12.3 %collective-permute-start.2 = (s16[64,1024]{1,0:T(8,128)(2,1)S(1)}, s16[64,1024]{1,0:T(8,128)(2,1)S(1)}, u32[]{:S(2)}, u32[]{:S(2)}) collective-permute-start(s16[64,1024]{1,0:T(8,128)(2,1)S(1)} %shard_map.58.code), channel_id=1, source_target_pairs={{0,16},{4,20},{8,24},{12,28},{16,0},{20,4},{24,8},{28,12},{1,17},{... | collective-permute-start | bytes 393224 | tf_op jit(solution)/shard_map/ppermute | solution.py:198
  17.1 11.1 %collective-permute-start.10 = (s16[64,1024]{1,0:T(8,128)(2,1)S(1)}, s16[64,1024]{1,0:T(8,128)(2,1)S(1)}, u32[]{:S(2)}, u32[]{:S(2)}) collective-permute-start(s16[64,1024]{1,0:T(8,128)(2,1)S(1)} %shard_map.61.code), channel_id=1, source_target_pairs={{0,16},{4,20},{8,24},{12,28},{16,0},{20,4},{24,8},{28,12},{1,17},{... | collective-permute-start | bytes 393224 | tf_op jit(solution)/shard_map/ppermute | solution.py:198
  26.5 6.1 %collective-permute-start.3 = (bf16[64,1024]{1,0:T(8,128)(2,1)S(1)}, bf16[64,1024]{1,0:T(8,128)(2,1)S(1)}, u32[]{:S(2)}, u32[]{:S(2)}) collective-permute-start(bf16[64,1024]{1,0:T(8,128)(2,1)S(1)} %shard_map.59.refs_0_), channel_id=1, source_target_pairs={{0,8},{4,12},{8,0},{12,4},{16,24},{20,28},{24,16},{28,20},{1,9},{5... | collective-permute-start | bytes 393224 | tf_op jit(solution)/shard_map/ppermute | solution.py:198
  28.3 5.7 %collective-permute-start.11 = (bf16[64,1024]{1,0:T(8,128)(2,1)S(1)}, bf16[64,1024]{1,0:T(8,128)(2,1)S(1)}, u32[]{:S(2)}, u32[]{:S(2)}) collective-permute-start(bf16[64,1024]{1,0:T(8,128)(2,1)S(1)} %shard_map.62.refs_0_), channel_id=1, source_target_pairs={{0,8},{4,12},{8,0},{12,4},{16,24},{20,28},{24,16},{28,20},{1,9},{5... | collective-permute-start | bytes 393224 | tf_op jit(solution)/shard_map/ppermute | solution.py:198
  28.8 5.2 %collective-permute-start.4 = (bf16[64,1024]{1,0:T(8,128)(2,1)S(1)}, bf16[64,1024]{1,0:T(8,128)(2,1)S(1)}, u32[]{:S(2)}, u32[]{:S(2)}) collective-permute-start(bf16[64,1024]{1,0:T(8,128)(2,1)S(1)} %shard_map.59.refs_0_), channel_id=1, source_target_pairs={{0,4},{4,0},{8,12},{12,8},{16,20},{20,16},{24,28},{28,24},{1,5},{5... | collective-permute-start | bytes 393224 | tf_op jit(solution)/shard_map/ppermute | solution.py:195
  32.6 1.4 %collective-permute-start.5 = (bf16[64,1024]{1,0:T(8,128)(2,1)S(1)}, bf16[64,1024]{1,0:T(8,128)(2,1)S(1)}, u32[]{:S(2)}, u32[]{:S(2)}) collective-permute-start(bf16[64,1024]{1,0:T(8,128)(2,1)S(1)} %collective-permute-done.3.refs_1_), channel_id=1, source_target_pairs={{0,4},{4,0},{8,12},{12,8},{16,20},{20,16},{24,28},{28,24},{1,5},{5... | collective-permute-start | bytes 393224 | tf_op jit(solution)/shard_map/ppermute | solution.py:195
  32.6 6.3 %collective-permute-start.12 = (bf16[64,1024]{1,0:T(8,128)(2,1)S(1)}, bf16[64,1024]{1,0:T(8,128)(2,1)S(1)}, u32[]{:S(2)}, u32[]{:S(2)}) collective-permute-start(bf16[64,1024]{1,0:T(8,128)(2,1)S(1)} %shard_map.62.refs_0_), channel_id=1, source_target_pairs={{0,4},{4,0},{8,12},{12,8},{16,20},{20,16},{24,28},{28,24},{1,5},{5... | collective-permute-start | bytes 393224 | tf_op jit(solution)/shard_map/ppermute | solution.py:195
  34.0 4.9 %collective-permute-start.13 = (bf16[64,1024]{1,0:T(8,128)(2,1)S(1)}, bf16[64,1024]{1,0:T(8,128)(2,1)S(1)}, u32[]{:S(2)}, u32[]{:S(2)}) collective-permute-start(bf16[64,1024]{1,0:T(8,128)(2,1)S(1)} %collective-permute-done.11.refs_1_), channel_id=1, source_target_pairs={{0,4},{4,0},{8,12},{12,8},{16,20},{20,16},{24,28},{28,24},{1,5},{5... | collective-permute-start | bytes 393224 | tf_op jit(solution)/shard_map/ppermute | solution.py:195
  35.4 8.3 %collective-permute-start.6 = (s16[256,128]{1,0:T(8,128)(2,1)S(1)}, s16[256,128]{1,0:T(8,128)(2,1)S(1)}, u32[]{:S(2)}, u32[]{:S(2)}) collective-permute-start(s16[256,128]{1,0:T(8,128)(2,1)S(1)} %get-tuple-element.26), channel_id=1, source_target_pairs={{0,1},{1,0},{2,3},{3,2},{4,5},{5,4},{6,7},{7,6},{8,9},{9,8},{10,11... | collective-permute-start | bytes 196616 | tf_op jit(solution)/shard_map/ppermute | solution.py:201
  36.9 6.9 %collective-permute-start.7 = (s16[256,128]{1,0:T(8,128)(2,1)S(1)}, s16[256,128]{1,0:T(8,128)(2,1)S(1)}, u32[]{:S(2)}, u32[]{:S(2)}) collective-permute-start(s16[256,128]{1,0:T(8,128)(2,1)S(1)} %get-tuple-element.27), channel_id=1, source_target_pairs={{0,2},{1,3},{2,0},{3,1},{4,6},{5,7},{6,4},{7,5},{8,10},{9,11},{10,... | collective-permute-start | bytes 196616 | tf_op jit(solution)/shard_map/ppermute | solution.py:201
  38.8 5.5 %collective-permute-start.8 = (s16[256,128]{1,0:T(8,128)(2,1)S(1)}, s16[256,128]{1,0:T(8,128)(2,1)S(1)}, u32[]{:S(2)}, u32[]{:S(2)}) collective-permute-start(s16[256,128]{1,0:T(8,128)(2,1)S(1)} %get-tuple-element.28), channel_id=1, source_target_pairs={{0,3},{1,2},{2,1},{3,0},{4,7},{5,6},{6,5},{7,4},{8,11},{9,10},{10,... | collective-permute-start | bytes 196616 | tf_op jit(solution)/shard_map/ppermute | solution.py:201
  40.3 4.3 %collective-permute-start.14 = (s16[256,128]{1,0:T(8,128)(2,1)S(1)}, s16[256,128]{1,0:T(8,128)(2,1)S(1)}, u32[]{:S(2)}, u32[]{:S(2)}) collective-permute-start(s16[256,128]{1,0:T(8,128)(2,1)S(1)} %get-tuple-element.32), channel_id=1, source_target_pairs={{0,1},{1,0},{2,3},{3,2},{4,5},{5,4},{6,7},{7,6},{8,9},{9,8},{10,11... | collective-permute-start | bytes 196616 | tf_op jit(solution)/shard_map/ppermute | solution.py:201
  41.8 4.3 %collective-permute-start.15 = (s16[256,128]{1,0:T(8,128)(2,1)S(1)}, s16[256,128]{1,0:T(8,128)(2,1)S(1)}, u32[]{:S(2)}, u32[]{:S(2)}) collective-permute-start(s16[256,128]{1,0:T(8,128)(2,1)S(1)} %get-tuple-element.33), channel_id=1, source_target_pairs={{0,2},{1,3},{2,0},{3,1},{4,6},{5,7},{6,4},{7,5},{8,10},{9,11},{10,... | collective-permute-start | bytes 196616 | tf_op jit(solution)/shard_map/ppermute | solution.py:201
  43.7 5.2 %collective-permute-start.16 = (s16[256,128]{1,0:T(8,128)(2,1)S(1)}, s16[256,128]{1,0:T(8,128)(2,1)S(1)}, u32[]{:S(2)}, u32[]{:S(2)}) collective-permute-start(s16[256,128]{1,0:T(8,128)(2,1)S(1)} %get-tuple-element.34), channel_id=1, source_target_pairs={{0,3},{1,2},{2,1},{3,0},{4,7},{5,6},{6,5},{7,4},{8,11},{9,10},{10,... | collective-permute-start | bytes 196616 | tf_op jit(solution)/shard_map/ppermute | solution.py:201

commit v4 on v3

--- a/solution.py
+++ b/solution.py
@@ -146,18 +146,21 @@
 
 
 def cell_kernel(masks, dense, *refs):
-    ours, theirs = refs[: len(masks)], refs[len(masks) : 2 * len(masks)]
-    outs, gene = refs[2 * len(masks) : -1], refs[-1]
+    *pieces, gene = refs
+    count = len(masks) * CORES * STREAMS
+    pieces, outs = pieces[:count], pieces[count:]
     core, chip = core_and_chip()
-    rows, width = ours[0].shape
+    rows, width = pieces[0].shape
     for k, mask in enumerate(masks):
         at, size = 0, gene.shape[1]
         for bit in range(len(masks).bit_length() - 1):
             size //= 2
             at = at + (((chip ^ mask) >> bit) & 1) * size
         cut = pl.ds(pl.multiple_of(at, width), width)
-        gene[pl.ds(pl.multiple_of(core * rows, rows), rows), cut] = ours[k][...]
-        gene[pl.ds(pl.multiple_of((1 - core) * rows, rows), rows), cut] = theirs[k][...]
+        for i in range(STREAMS):
+            for j, owner in enumerate((core, 1 - core)):
+                row = pl.multiple_of((i * CORES + owner) * rows, rows)
+                gene[pl.ds(row, rows), cut] = pieces[(i * CORES + j) * len(masks) + k][...]
     me = lax.axis_index("genes")
     height = outs[0].shape[0]
     for k, out in enumerate(outs):
@@ -169,14 +172,12 @@
             encode(part, out)
 
 
-def last_kernel(count, *refs):
-    out = refs[-1]
-    for i in range(STREAMS):
-        own, *got = refs[i * count : (i + 1) * count]
-        total = own[...]
-        for ref in got:
-            total = total + decode(ref[...])
-        out[:, i * own.shape[1] : (i + 1) * own.shape[1]] = total
+def last_kernel(own, *refs):
+    *got, out = refs
+    total = own[...]
+    for ref in got:
+        total = total + decode(ref[...])
+    out[...] = total
 
 
 def local(n_cells, n_genes, sketch, tiles, tile_rows, tile_cols, tile_counts):
@@ -222,42 +223,42 @@
     one = halves(genes) if cut else (shape((rows, genes), i16),)
     pieces = call(functools.partial(pair_kernel, cut), one * STREAMS, [VMEM, VMEM], nbytes=2 * MIB)(mine, got)
 
-    def gene_side(i):
-        width = genes
-        if cut:
-            keep, send = pieces[2 * i : 2 * i + 2]
-            for bit in range(bits - 1):
-                width //= 2
-                got = to_chip(send, bit)
-                outs = halves(width) if bit < bits - 2 else (shape((rows, width), i16),)
-                done = call(functools.partial(add_kernel, bit + 1), outs, [VMEM, VMEM], nbytes=MIB)(keep, got)
-                keep, send = done[0], done[-1]
-            code = send
-        else:
-            code = pieces[i]
+    def add_step(bit, keep, got, width):
+        outs = halves(width) if bit < bits - 2 else (shape((rows, width), i16),)
+        return call(functools.partial(add_kernel, bit + 1), outs, [VMEM, VMEM], nbytes=MIB)(keep, got)
+
+    streams = [pieces[i * len(one) : (i + 1) * len(one)] for i in range(STREAMS)]
+    width = genes
+    for bit in range(bits - 1):
+        width //= 2
+        before = None
+        for i in range(STREAMS):
+            keep, send = streams[i]
+            if before is not None:
+                send, before = lax.optimization_barrier((send, before))
+            before = to_chip(send, bit)
+            streams[i] = add_step(bit, keep, before, width)
+    held = []
+    for code in [x[-1] for x in streams]:
         got = to_chip(code, bits - 1)
-        held = [call(cast_kernel, shape((rows, width), bf16), [VMEM, VMEM], nbytes=MIB)(code, got)]
-        masks = [0]
-        for bit in reversed(range(bits - 1)):
-            held += [to_chip(x, bit) for x in held]
-            masks += [mask ^ (1 << bit) for mask in masks]
-        return held, masks
-
-    parts = []
-    for i in range(STREAMS):
-        held, masks = gene_side(i)
-        partner = [to_core(x) for x in held]
-        outs = call(
-            functools.partial(cell_kernel, masks),
-            (shape((height, span), f32),) + (shape((height, span), i16),) * (n_genes - 1),
-            [VMEM] * (1 + 2 * len(held)),
-            scratch=[pltpu.VMEM((span, genes), bf16)],
-            flops=flops // STREAMS,
-            nbytes=5 * MIB,
-        )(dense, *held, *partner)
-        parts += [outs[0]] + [to_gene(outs[k], k) for k in range(1, n_genes)]
-    last = functools.partial(last_kernel, n_genes)
-    return call(last, shape((height, rank), f32), [VMEM] * len(parts), nbytes=MIB)(*parts)
+        held.append([call(cast_kernel, shape((rows, width), bf16), [VMEM, VMEM], nbytes=MIB)(code, got)])
+    masks = [0]
+    for bit in reversed(range(bits - 1)):
+        held = [pieces + [to_chip(x, bit) for x in pieces] for pieces in held]
+        masks += [mask ^ (1 << bit) for mask in masks]
+    whole = []
+    for pieces in held:
+        whole += pieces + [to_core(x) for x in pieces]
+    parts = call(
+        functools.partial(cell_kernel, masks),
+        (shape((height, rank), f32),) + (shape((height, rank), i16),) * (n_genes - 1),
+        [VMEM] * (1 + len(whole)),
+        scratch=[pltpu.VMEM((rank, genes), bf16)],
+        flops=flops,
+        nbytes=6 * MIB,
+    )(dense, *whole)
+    got = [to_gene(parts[k], k) for k in reversed(range(1, n_genes))]
+    return call(last_kernel, shape((height, rank), f32), [VMEM] * n_genes, nbytes=MIB)(parts[0], *got)
 
 
 def solution(mesh):

time: 49.7 us -> 48.4 us (0.974)
  starting transfers between devices: 16.6 us -> 14.6 us
  waiting for transfers between devices: 23.1 us -> 24.9 us
  Pallas kernels: 9.22 us -> 7.98 us
    ppermute x6 -> x3, starting transfers between devices: 7.11 us -> 3.55 us  [to_gene(): return lax.ppermute(x, 'genes', [(i, i ^ k) for i in range(n_genes)])]
    ppermute x6, starting transfers between devices: 8.94 us -> 10.5 us  [to_chip(): lax.ppermute(x, 'cells', [(i, i ^ CORES << bit) for i in range(n_cells)])]
    ppermute x5, waiting for transfers between devices: 1.18 us -> 2.5 us  [to_core(): return lax.ppermute(x, 'cells', [(i, i ^ 1) for i in range(n_cells)])]
    pallas_call x7 -> x6, Pallas kernels: 3.91 us -> 2.67 us  [the longest x1 1.45 us: local(): call(functools.partial(cell_kernel, masks), (shape((height, rank), f32),)...]
    ppermute x6 -> x3, waiting for transfers between devices: 5 us -> 5.77 us  [to_gene(): return lax.ppermute(x, 'genes', [(i, i ^ k) for i in range(n_genes)])]
  transfers between devices with their start and end apart: 17 -> 14, of which waited for: 10 -> 10; matrix products, arithmetic and copies ran while one was open for 0% -> 0% of each run, Pallas kernels for 8% -> 2%
where the time goes in v4:
time: 48.4 us; the launch traced here: 48.2 us
  waiting for transfers between devices  24.9 us (51%)
  starting transfers between devices  14.6 us (30%)
  Pallas kernels  7.98 us (16%)
  between operations  0.74 us (2%)
    ppermute x6, waiting for transfers between devices, to_chip(): lax.ppermute(x, 'cells', [(i, i ^ CORES << bit) for i in range(n_cells)])  16.6 us
    ppermute x6, starting transfers between devices, to_chip(): lax.ppermute(x, 'cells', [(i, i ^ CORES << bit) for i in range(n_cells)])  10.5 us
    ppermute x3, waiting for transfers between devices, to_gene(): return lax.ppermute(x, 'genes', [(i, i ^ k) for i in range(n_genes)])  5.77 us
    pallas_call x1, Pallas kernels, local(): call(dense_kernel, (shape((cells, genes), bf16), shape((rank, cells), bf1...  4.29 us
    ppermute x3, starting transfers between devices, to_gene(): return lax.ppermute(x, 'genes', [(i, i ^ k) for i in range(n_genes)])  3.55 us
    ppermute x5, waiting for transfers between devices, to_core(): return lax.ppermute(x, 'cells', [(i, i ^ 1) for i in range(n_cells)])  2.5 us
    pallas_call x1, Pallas kernels, local(): call(functools.partial(cell_kernel, masks), (shape((height, rank), f32),)...  1.45 us
  transfers between devices with their start and end apart: 14, of which 10 were waited for; matrix products, arithmetic and copies ran while one was open for 0% of the time, Pallas kernels for 2%

profile of v4, /device:TPU:0, one launch (start us, length us, event | category | flops | bytes accessed | tf_op | source)
XLA Modules:
  0.0 48.2 jit_solution(4104928428571878266)
XLA Ops:
  0.7 4.3 %shard_map.55 = (bf16[1024,2048]{1,0:T(8,128)(2,1)S(1)}, bf16[256,1024]{1,0:T(8,128)(2,1)S(1)}, s16[128,2048]{1,0:T(8,128)(2,1)S(1)}) custom-call(s32[1]{0:T(128)S(6)} %copy.6.count, s32[96]{0:T(128)} %rows.1, s32[96]{0:T(128)} %cols.1, bf16[1024,256]{1,0:T(8,128)(2,1)} %sketch.1, bf16[96,128,128]{2,1,0:T(8,128)(2,1)} %tiles.1), custom_call_target="tpu_custom_call" | custom-call | flops 536870912 | bytes 8388608 | tf_op jit(solution)/shard_map/pallas_call | solution.py:207
  4.9 0.1 collective-permute-start
  5.0 0.7 %shard_map.56.mine = f32[128,2048]{1,0:T(8,128)S(1)} custom-call(bf16[256,1024]{1,0:T(8,128)(2,1)S(1)} %get-tuple-element.18.turned, bf16[1024,2048]{1,0:T(8,128)(2,1)S(1)} %get-tuple-element.17.dense), custom_call_target="tpu_custom_call" | custom-call | flops 536870912 | bytes 5242880 | tf_op jit(solution)/shard_map/pallas_call | solution.py:221
  5.8 1.2 %collective-permute-done.got = s16[128,2048]{1,0:T(8,128)(2,1)S(1)} collective-permute-done((s16[128,2048]{1,0:T(8,128)(2,1)S(1)}, s16[128,2048]{1,0:T(8,128)(2,1)S(1)}, u32[]{:S(2)}, u32[]{:S(2)}) %collective-permute-start) | collective-permute-done | bytes 524320 | tf_op jit(solution)/shard_map/ppermute | solution.py:196
  6.9 0.3 shard_map.57
  7.2 2.3 %collective-permute-start.1 = (s16[64,1024]{1,0:T(8,128)(2,1)S(1)}, s16[64,1024]{1,0:T(8,128)(2,1)S(1)}, u32[]{:S(2)}, u32[]{:S(2)}) collective-permute-start(s16[64,1024]{1,0:T(8,128)(2,1)S(1)} %get-tuple-element.21), channel_id=1, source_target_pairs={{0,8},{4,12},{8,0},{12,4},{16,24},{20,28},{24,16},{28,20},{1,9},{5... | collective-permute-start | bytes 393224 | tf_op jit(solution)/shard_map/ppermute | solution.py:199
  9.5 3.8 %collective-permute-done.1.got = s16[64,1024]{1,0:T(8,128)(2,1)S(1)} collective-permute-done((s16[64,1024]{1,0:T(8,128)(2,1)S(1)}, s16[64,1024]{1,0:T(8,128)(2,1)S(1)}, u32[]{:S(2)}, u32[]{:S(2)}) %collective-permute-start.1) | collective-permute-done | bytes 131104 | tf_op jit(solution)/shard_map/ppermute | solution.py:199
  13.3 1.7 %collective-permute-start.6 = (s16[64,1024]{1,0:T(8,128)(2,1)S(1)}, s16[64,1024]{1,0:T(8,128)(2,1)S(1)}, u32[]{:S(2)}, u32[]{:S(2)}) collective-permute-start(s16[64,1024]{1,0:T(8,128)(2,1)S(1)} %get-tuple-element.24), channel_id=1, source_target_pairs={{0,8},{4,12},{8,0},{12,4},{16,24},{20,28},{24,16},{28,20},{1,9},{5... | collective-permute-start | bytes 393224 | tf_op jit(solution)/shard_map/ppermute | solution.py:199
  15.0 0.1 shard_map.58.code
  15.1 3.1 %collective-permute-start.2 = (s16[64,1024]{1,0:T(8,128)(2,1)S(1)}, s16[64,1024]{1,0:T(8,128)(2,1)S(1)}, u32[]{:S(2)}, u32[]{:S(2)}) collective-permute-start(s16[64,1024]{1,0:T(8,128)(2,1)S(1)} %shard_map.58.code), channel_id=1, source_target_pairs={{0,16},{4,20},{8,24},{12,28},{16,0},{20,4},{24,8},{28,12},{1,17},{... | collective-permute-start | bytes 393224 | tf_op jit(solution)/shard_map/ppermute | solution.py:199
  18.3 1.4 %collective-permute-done.6.got = s16[64,1024]{1,0:T(8,128)(2,1)S(1)} collective-permute-done((s16[64,1024]{1,0:T(8,128)(2,1)S(1)}, s16[64,1024]{1,0:T(8,128)(2,1)S(1)}, u32[]{:S(2)}, u32[]{:S(2)}) %collective-permute-start.6) | collective-permute-done | bytes 131104 | tf_op jit(solution)/shard_map/ppermute | solution.py:199
  19.7 0.1 shard_map.60.code
  19.8 3.1 %collective-permute-start.7 = (s16[64,1024]{1,0:T(8,128)(2,1)S(1)}, s16[64,1024]{1,0:T(8,128)(2,1)S(1)}, u32[]{:S(2)}, u32[]{:S(2)}) collective-permute-start(s16[64,1024]{1,0:T(8,128)(2,1)S(1)} %shard_map.60.code), channel_id=1, source_target_pairs={{0,16},{4,20},{8,24},{12,28},{16,0},{20,4},{24,8},{28,12},{1,17},{... | collective-permute-start | bytes 393224 | tf_op jit(solution)/shard_map/ppermute | solution.py:199
  22.9 4.4 %collective-permute-done.2.got = s16[64,1024]{1,0:T(8,128)(2,1)S(1)} collective-permute-done((s16[64,1024]{1,0:T(8,128)(2,1)S(1)}, s16[64,1024]{1,0:T(8,128)(2,1)S(1)}, u32[]{:S(2)}, u32[]{:S(2)}) %collective-permute-start.2) | collective-permute-done | bytes 131104 | tf_op jit(solution)/shard_map/ppermute | solution.py:199
  27.3 0.1 shard_map.59.refs_0_
  27.4 0.1 collective-permute-start.3
  27.5 1.9 %collective-permute-done.7.got = s16[64,1024]{1,0:T(8,128)(2,1)S(1)} collective-permute-done((s16[64,1024]{1,0:T(8,128)(2,1)S(1)}, s16[64,1024]{1,0:T(8,128)(2,1)S(1)}, u32[]{:S(2)}, u32[]{:S(2)}) %collective-permute-start.7) | collective-permute-done | bytes 131104 | tf_op jit(solution)/shard_map/ppermute | solution.py:199
  29.5 0.1 shard_map.61.refs_4_
  29.5 0.1 collective-permute-start.8
  29.7 0.0 collective-permute-start.4
  29.7 0.5 %collective-permute-start.9 = (bf16[64,1024]{1,0:T(8,128)(2,1)S(1)}, bf16[64,1024]{1,0:T(8,128)(2,1)S(1)}, u32[]{:S(2)}, u32[]{:S(2)}) collective-permute-start(bf16[64,1024]{1,0:T(8,128)(2,1)S(1)} %shard_map.61.refs_4_), channel_id=1, source_target_pairs={{0,4},{4,0},{8,12},{12,8},{16,20},{20,16},{24,28},{28,24},{1,5},{5... | collective-permute-start | bytes 393224 | tf_op jit(solution)/shard_map/ppermute | solution.py:196
  30.2 3.2 %collective-permute-done.3.refs_1_ = bf16[64,1024]{1,0:T(8,128)(2,1)S(1)} collective-permute-done((bf16[64,1024]{1,0:T(8,128)(2,1)S(1)}, bf16[64,1024]{1,0:T(8,128)(2,1)S(1)}, u32[]{:S(2)}, u32[]{:S(2)}) %collective-permute-start.3) | collective-permute-done | bytes 131104 | tf_op jit(solution)/shard_map/ppermute | solution.py:199
  33.4 1.9 %collective-permute-done.8.refs_5_ = bf16[64,1024]{1,0:T(8,128)(2,1)S(1)} collective-permute-done((bf16[64,1024]{1,0:T(8,128)(2,1)S(1)}, bf16[64,1024]{1,0:T(8,128)(2,1)S(1)}, u32[]{:S(2)}, u32[]{:S(2)}) %collective-permute-start.8) | collective-permute-done | bytes 131104 | tf_op jit(solution)/shard_map/ppermute | solution.py:199
  35.3 0.0 collective-permute-start.10
  35.3 1.3 %collective-permute-done.10.refs_7_ = bf16[64,1024]{1,0:T(8,128)(2,1)S(1)} collective-permute-done((bf16[64,1024]{1,0:T(8,128)(2,1)S(1)}, bf16[64,1024]{1,0:T(8,128)(2,1)S(1)}, u32[]{:S(2)}, u32[]{:S(2)}) %collective-permute-start.10) | collective-permute-done | bytes 131104 | tf_op jit(solution)/shard_map/ppermute | solution.py:196
  36.6 1.5 %shard_map.62 = (f32[256,256]{1,0:T(8,128)S(1)}, s16[256,256]{1,0:T(8,128)(2,1)S(1)}, s16[256,256]{1,0:T(8,128)(2,1)S(1)}, s16[256,256]{1,0:T(8,128)(2,1)S(1)}) custom-call(bf16[1024,2048]{1,0:T(8,128)(2,1)S(1)} %get-tuple-element.17.dense, bf16[64,1024]{1,0:T(8,128)(2,1)S(1)} %shard_map.59.refs_0_, bf16[64,1024]{1,0:T(8,128)(2,1)S(1)} %collective-permute-done.3.refs_1_, ...), custom_call_target="tpu_custom_call" | custom-call | flops 1073741824 | bytes 6291456 | tf_op jit(solution)/shard_map/pallas_call | solution.py:252
  38.1 2.4 %collective-permute-start.11 = (s16[256,256]{1,0:T(8,128)(2,1)S(1)}, s16[256,256]{1,0:T(8,128)(2,1)S(1)}, u32[]{:S(2)}, u32[]{:S(2)}) collective-permute-start(s16[256,256]{1,0:T(8,128)(2,1)S(1)} %get-tuple-element.26), channel_id=1, source_target_pairs={{0,3},{1,2},{2,1},{3,0},{4,7},{5,6},{6,5},{7,4},{8,11},{9,10},{10,... | collective-permute-start | bytes 393224 | tf_op jit(solution)/shard_map/ppermute | solution.py:202
  40.5 0.6 %collective-permute-start.12 = (s16[256,256]{1,0:T(8,128)(2,1)S(1)}, s16[256,256]{1,0:T(8,128)(2,1)S(1)}, u32[]{:S(2)}, u32[]{:S(2)}) collective-permute-start(s16[256,256]{1,0:T(8,128)(2,1)S(1)} %get-tuple-element.27), channel_id=1, source_target_pairs={{0,2},{1,3},{2,0},{3,1},{4,6},{5,7},{6,4},{7,5},{8,10},{9,11},{10,... | collective-permute-start | bytes 393224 | tf_op jit(solution)/shard_map/ppermute | solution.py:202
  41.1 0.5 %collective-permute-start.13 = (s16[256,256]{1,0:T(8,128)(2,1)S(1)}, s16[256,256]{1,0:T(8,128)(2,1)S(1)}, u32[]{:S(2)}, u32[]{:S(2)}) collective-permute-start(s16[256,256]{1,0:T(8,128)(2,1)S(1)} %get-tuple-element.28), channel_id=1, source_target_pairs={{0,1},{1,0},{2,3},{3,2},{4,5},{5,4},{6,7},{7,6},{8,9},{9,8},{10,11... | collective-permute-start | bytes 393224 | tf_op jit(solution)/shard_map/ppermute | solution.py:202
  41.6 3.4 %collective-permute-done.11.refs_0_ = s16[256,256]{1,0:T(8,128)(2,1)S(1)} collective-permute-done((s16[256,256]{1,0:T(8,128)(2,1)S(1)}, s16[256,256]{1,0:T(8,128)(2,1)S(1)}, u32[]{:S(2)}, u32[]{:S(2)}) %collective-permute-start.11) | collective-permute-done | bytes 131104 | tf_op jit(solution)/shard_map/ppermute | solution.py:202
  45.0 2.4 %collective-permute-done.12.refs_1_ = s16[256,256]{1,0:T(8,128)(2,1)S(1)} collective-permute-done((s16[256,256]{1,0:T(8,128)(2,1)S(1)}, s16[256,256]{1,0:T(8,128)(2,1)S(1)}, u32[]{:S(2)}, u32[]{:S(2)}) %collective-permute-start.12) | collective-permute-done | bytes 131104 | tf_op jit(solution)/shard_map/ppermute | solution.py:202
  47.4 0.8 %shard_map.63 = f32[256,256]{1,0:T(8,128)} custom-call(f32[256,256]{1,0:T(8,128)S(1)} %get-tuple-element.25.own, s16[256,256]{1,0:T(8,128)(2,1)S(1)} %collective-permute-done.11.refs_0_, s16[256,256]{1,0:T(8,128)(2,1)S(1)} %collective-permute-done.12.refs_1_, s16[256,256]{1,0:T(8,128)(2,1)S(1)} %collective-permute-done.13.refs_2_), custom_call_target="tpu_custom_call" | custom-call | bytes 1048576 | tf_op jit(solution)/shard_map/pallas_call | solution.py:261
  (5 shorter events, 0.0 us)
Async XLA Ops:
  4.9 2.0 %collective-permute-start = (s16[128,2048]{1,0:T(8,128)(2,1)S(1)}, s16[128,2048]{1,0:T(8,128)(2,1)S(1)}, u32[]{:S(2)}, u32[]{:S(2)}) collective-permute-start(s16[128,2048]{1,0:T(8,128)(2,1)S(1)} %get-tuple-element.19), channel_id=1, source_target_pairs={{0,4},{4,0},{8,12},{12,8},{16,20},{20,16},{24,28},{28,24},{1,5},{5... | collective-permute-start | bytes 1572872 | tf_op jit(solution)/shard_map/ppermute | solution.py:196
  7.2 6.1 %collective-permute-start.1 = (s16[64,1024]{1,0:T(8,128)(2,1)S(1)}, s16[64,1024]{1,0:T(8,128)(2,1)S(1)}, u32[]{:S(2)}, u32[]{:S(2)}) collective-permute-start(s16[64,1024]{1,0:T(8,128)(2,1)S(1)} %get-tuple-element.21), channel_id=1, source_target_pairs={{0,8},{4,12},{8,0},{12,4},{16,24},{20,28},{24,16},{28,20},{1,9},{5... | collective-permute-start | bytes 393224 | tf_op jit(solution)/shard_map/ppermute | solution.py:199
  13.3 6.4 %collective-permute-start.6 = (s16[64,1024]{1,0:T(8,128)(2,1)S(1)}, s16[64,1024]{1,0:T(8,128)(2,1)S(1)}, u32[]{:S(2)}, u32[]{:S(2)}) collective-permute-start(s16[64,1024]{1,0:T(8,128)(2,1)S(1)} %get-tuple-element.24), channel_id=1, source_target_pairs={{0,8},{4,12},{8,0},{12,4},{16,24},{20,28},{24,16},{28,20},{1,9},{5... | collective-permute-start | bytes 393224 | tf_op jit(solution)/shard_map/ppermute | solution.py:199
  15.1 12.2 %collective-permute-start.2 = (s16[64,1024]{1,0:T(8,128)(2,1)S(1)}, s16[64,1024]{1,0:T(8,128)(2,1)S(1)}, u32[]{:S(2)}, u32[]{:S(2)}) collective-permute-start(s16[64,1024]{1,0:T(8,128)(2,1)S(1)} %shard_map.58.code), channel_id=1, source_target_pairs={{0,16},{4,20},{8,24},{12,28},{16,0},{20,4},{24,8},{28,12},{1,17},{... | collective-permute-start | bytes 393224 | tf_op jit(solution)/shard_map/ppermute | solution.py:199
  19.8 9.7 %collective-permute-start.7 = (s16[64,1024]{1,0:T(8,128)(2,1)S(1)}, s16[64,1024]{1,0:T(8,128)(2,1)S(1)}, u32[]{:S(2)}, u32[]{:S(2)}) collective-permute-start(s16[64,1024]{1,0:T(8,128)(2,1)S(1)} %shard_map.60.code), channel_id=1, source_target_pairs={{0,16},{4,20},{8,24},{12,28},{16,0},{20,4},{24,8},{28,12},{1,17},{... | collective-permute-start | bytes 393224 | tf_op jit(solution)/shard_map/ppermute | solution.py:199
  27.4 5.9 %collective-permute-start.3 = (bf16[64,1024]{1,0:T(8,128)(2,1)S(1)}, bf16[64,1024]{1,0:T(8,128)(2,1)S(1)}, u32[]{:S(2)}, u32[]{:S(2)}) collective-permute-start(bf16[64,1024]{1,0:T(8,128)(2,1)S(1)} %shard_map.59.refs_0_), channel_id=1, source_target_pairs={{0,8},{4,12},{8,0},{12,4},{16,24},{20,28},{24,16},{28,20},{1,9},{5... | collective-permute-start | bytes 393224 | tf_op jit(solution)/shard_map/ppermute | solution.py:199
  29.5 5.7 %collective-permute-start.8 = (bf16[64,1024]{1,0:T(8,128)(2,1)S(1)}, bf16[64,1024]{1,0:T(8,128)(2,1)S(1)}, u32[]{:S(2)}, u32[]{:S(2)}) collective-permute-start(bf16[64,1024]{1,0:T(8,128)(2,1)S(1)} %shard_map.61.refs_4_), channel_id=1, source_target_pairs={{0,8},{4,12},{8,0},{12,4},{16,24},{20,28},{24,16},{28,20},{1,9},{5... | collective-permute-start | bytes 393224 | tf_op jit(solution)/shard_map/ppermute | solution.py:199
  29.7 5.6 %collective-permute-start.4 = (bf16[64,1024]{1,0:T(8,128)(2,1)S(1)}, bf16[64,1024]{1,0:T(8,128)(2,1)S(1)}, u32[]{:S(2)}, u32[]{:S(2)}) collective-permute-start(bf16[64,1024]{1,0:T(8,128)(2,1)S(1)} %shard_map.59.refs_0_), channel_id=1, source_target_pairs={{0,4},{4,0},{8,12},{12,8},{16,20},{20,16},{24,28},{28,24},{1,5},{5... | collective-permute-start | bytes 393224 | tf_op jit(solution)/shard_map/ppermute | solution.py:196
  29.7 5.6 %collective-permute-start.9 = (bf16[64,1024]{1,0:T(8,128)(2,1)S(1)}, bf16[64,1024]{1,0:T(8,128)(2,1)S(1)}, u32[]{:S(2)}, u32[]{:S(2)}) collective-permute-start(bf16[64,1024]{1,0:T(8,128)(2,1)S(1)} %shard_map.61.refs_4_), channel_id=1, source_target_pairs={{0,4},{4,0},{8,12},{12,8},{16,20},{20,16},{24,28},{28,24},{1,5},{5... | collective-permute-start | bytes 393224 | tf_op jit(solution)/shard_map/ppermute | solution.py:196
  33.4 1.9 %collective-permute-start.5 = (bf16[64,1024]{1,0:T(8,128)(2,1)S(1)}, bf16[64,1024]{1,0:T(8,128)(2,1)S(1)}, u32[]{:S(2)}, u32[]{:S(2)}) collective-permute-start(bf16[64,1024]{1,0:T(8,128)(2,1)S(1)} %collective-permute-done.3.refs_1_), channel_id=1, source_target_pairs={{0,4},{4,0},{8,12},{12,8},{16,20},{20,16},{24,28},{28,24},{1,5},{5... | collective-permute-start | bytes 393224 | tf_op jit(solution)/shard_map/ppermute | solution.py:196
  35.3 1.3 %collective-permute-start.10 = (bf16[64,1024]{1,0:T(8,128)(2,1)S(1)}, bf16[64,1024]{1,0:T(8,128)(2,1)S(1)}, u32[]{:S(2)}, u32[]{:S(2)}) collective-permute-start(bf16[64,1024]{1,0:T(8,128)(2,1)S(1)} %collective-permute-done.8.refs_5_), channel_id=1, source_target_pairs={{0,4},{4,0},{8,12},{12,8},{16,20},{20,16},{24,28},{28,24},{1,5},{5... | collective-permute-start | bytes 393224 | tf_op jit(solution)/shard_map/ppermute | solution.py:196
  38.1 6.9 %collective-permute-start.11 = (s16[256,256]{1,0:T(8,128)(2,1)S(1)}, s16[256,256]{1,0:T(8,128)(2,1)S(1)}, u32[]{:S(2)}, u32[]{:S(2)}) collective-permute-start(s16[256,256]{1,0:T(8,128)(2,1)S(1)} %get-tuple-element.26), channel_id=1, source_target_pairs={{0,3},{1,2},{2,1},{3,0},{4,7},{5,6},{6,5},{7,4},{8,11},{9,10},{10,... | collective-permute-start | bytes 393224 | tf_op jit(solution)/shard_map/ppermute | solution.py:202
  40.5 6.9 %collective-permute-start.12 = (s16[256,256]{1,0:T(8,128)(2,1)S(1)}, s16[256,256]{1,0:T(8,128)(2,1)S(1)}, u32[]{:S(2)}, u32[]{:S(2)}) collective-permute-start(s16[256,256]{1,0:T(8,128)(2,1)S(1)} %get-tuple-element.27), channel_id=1, source_target_pairs={{0,2},{1,3},{2,0},{3,1},{4,6},{5,7},{6,4},{7,5},{8,10},{9,11},{10,... | collective-permute-start | bytes 393224 | tf_op jit(solution)/shard_map/ppermute | solution.py:202
  41.1 6.3 %collective-permute-start.13 = (s16[256,256]{1,0:T(8,128)(2,1)S(1)}, s16[256,256]{1,0:T(8,128)(2,1)S(1)}, u32[]{:S(2)}, u32[]{:S(2)}) collective-permute-start(s16[256,256]{1,0:T(8,128)(2,1)S(1)} %get-tuple-element.28), channel_id=1, source_target_pairs={{0,1},{1,0},{2,3},{3,2},{4,5},{5,4},{6,7},{7,6},{8,9},{9,8},{10,11... | collective-permute-start | bytes 393224 | tf_op jit(solution)/shard_map/ppermute | solution.py:202

commit v5 on v4

--- a/solution.py
+++ b/solution.py
@@ -122,15 +122,22 @@
     encode(jnp.where(ours == 0, high, low), send)
 
 
-def pair_kernel(halves, mine, got, *outs):
-    total = mine[...] + decode(got[...])
-    rows = total.shape[0] // STREAMS
-    for i in range(STREAMS):
-        part = total[i * rows : (i + 1) * rows]
-        if halves:
-            halve(part, 0, *outs[2 * i : 2 * i + 2])
+def pair_kernel(chips, mine, got, *refs):
+    *outs, total = refs
+    direct, rest = outs[:chips], outs[chips:]
+    _, chip = core_and_chip()
+    total[...] = mine[...] + decode(got[...])
+    rows, width = direct[0].shape
+    if len(rest) == 2:
+        halve(total[rows:, :], 0, *rest)
+    else:
+        encode(total[rows:, :], rest[0])
+    for k, out in enumerate(direct):
+        part = total[:rows, pl.ds(pl.multiple_of((chip ^ k) * width, width), width)]
+        if k == 0:
+            out[...] = part
         else:
-            encode(part, outs[i])
+            encode(part, out)
 
 
 def add_kernel(bit, keep, got, *outs):
@@ -145,39 +152,55 @@
     out[...] = (decode(code[...]) + decode(got[...])).astype(bf16)
 
 
-def cell_kernel(masks, dense, *refs):
-    *pieces, gene = refs
-    count = len(masks) * CORES * STREAMS
-    pieces, outs = pieces[:count], pieces[count:]
-    core, chip = core_and_chip()
-    rows, width = pieces[0].shape
-    for k, mask in enumerate(masks):
-        at, size = 0, gene.shape[1]
-        for bit in range(len(masks).bit_length() - 1):
-            size //= 2
-            at = at + (((chip ^ mask) >> bit) & 1) * size
-        cut = pl.ds(pl.multiple_of(at, width), width)
-        for i in range(STREAMS):
-            for j, owner in enumerate((core, 1 - core)):
-                row = pl.multiple_of((i * CORES + owner) * rows, rows)
-                gene[pl.ds(row, rows), cut] = pieces[(i * CORES + j) * len(masks) + k][...]
-    me = lax.axis_index("genes")
-    height = outs[0].shape[0]
-    for k, out in enumerate(outs):
-        left = dense[pl.ds(pl.multiple_of((me ^ k) * height, height), height), :]
-        part = lax.dot_general(left, gene[...], (((1,), (1,)), ((), ())), preferred_element_type=f32)
-        if k == 0:
-            out[...] = part
-        else:
-            encode(part, out)
-
-
-def last_kernel(own, *refs):
+def direct_cast_kernel(own, *refs):
     *got, out = refs
     total = own[...]
     for ref in got:
         total = total + decode(ref[...])
-    out[...] = total
+    out[...] = total.astype(bf16)
+
+
+def join_kernel(*refs):
+    *pieces, out = refs
+    _, chip = core_and_chip()
+    width = pieces[0].shape[1]
+    for k, piece in enumerate(pieces):
+        out[:, pl.ds(pl.multiple_of((chip ^ k) * width, width), width)] = piece[...]
+
+
+def gene_kernel(masks, first, first_theirs, *refs):
+    *pieces, gene = refs
+    core, chip = core_and_chip()
+    rows, width = pieces[0].shape
+
+    def at(stream, owner):
+        return pl.ds(pl.multiple_of((stream * CORES + owner) * rows, rows), rows)
+
+    gene[at(0, core), :] = first[...]
+    gene[at(0, 1 - core), :] = first_theirs[...]
+    for k, mask in enumerate(masks):
+        place, size = 0, gene.shape[1]
+        for bit in range(len(masks).bit_length() - 1):
+            size //= 2
+            place = place + (((chip ^ mask) >> bit) & 1) * size
+        cut = pl.ds(pl.multiple_of(place, width), width)
+        gene[at(1, core), cut] = pieces[k][...]
+        gene[at(1, 1 - core), cut] = pieces[len(masks) + k][...]
+
+
+def cell_kernel(k, dense, gene, out):
+    height = out.shape[0]
+    me = lax.axis_index("genes")
+    left = dense[pl.ds(pl.multiple_of((me ^ k) * height, height), height), :]
+    part = lax.dot_general(left, gene[...], (((1,), (1,)), ((), ())), preferred_element_type=f32)
+    if k == 0:
+        out[...] = part
+    else:
+        encode(part, out)
+
+
+def more_kernel(total, got, out):
+    out[...] = total[...] + decode(got[...])
 
 
 def local(n_cells, n_genes, sketch, tiles, tile_rows, tile_cols, tile_counts):
@@ -195,8 +218,8 @@
     def to_core(x):
         return lax.ppermute(x, "cells", [(i, i ^ 1) for i in range(n_cells)])
 
-    def to_chip(x, bit):
-        return lax.ppermute(x, "cells", [(i, i ^ (CORES << bit)) for i in range(n_cells)])
+    def to_chip(x, k):
+        return lax.ppermute(x, "cells", [(i, i ^ (CORES * k)) for i in range(n_cells)])
 
     def to_gene(x, k):
         return lax.ppermute(x, "genes", [(i, i ^ k) for i in range(n_genes)])
@@ -219,46 +242,58 @@
     )(tile_counts, *(pltpu.with_memory_space_constraint(x, pltpu.HBM) for x in (tile_rows, tile_cols, sketch, tiles)))
     got = to_core(theirs)
     mine = call(own_kernel, shape((share, genes), f32), [VMEM, VMEM], flops=flops // 2, nbytes=5 * MIB)(turned, dense)
-    cut = bits > 1
-    one = halves(genes) if cut else (shape((rows, genes), i16),)
-    pieces = call(functools.partial(pair_kernel, cut), one * STREAMS, [VMEM, VMEM], nbytes=2 * MIB)(mine, got)
-
-    def add_step(bit, keep, got, width):
-        outs = halves(width) if bit < bits - 2 else (shape((rows, width), i16),)
-        return call(functools.partial(add_kernel, bit + 1), outs, [VMEM, VMEM], nbytes=MIB)(keep, got)
-
-    streams = [pieces[i * len(one) : (i + 1) * len(one)] for i in range(STREAMS)]
+    chips = n_cells // CORES
+    chunk = genes // chips
+    one = halves(genes) if bits > 1 else (shape((rows, genes), i16),)
+    pieces = call(
+        functools.partial(pair_kernel, chips),
+        (shape((rows, chunk), f32),) + (shape((rows, chunk), i16),) * (chips - 1) + one,
+        [VMEM, VMEM],
+        scratch=[pltpu.VMEM((share, genes), f32)],
+        nbytes=3 * MIB,
+    )(mine, got)
+    direct, half = pieces[:chips], pieces[chips:]
+
     width = genes
     for bit in range(bits - 1):
         width //= 2
-        before = None
-        for i in range(STREAMS):
-            keep, send = streams[i]
-            if before is not None:
-                send, before = lax.optimization_barrier((send, before))
-            before = to_chip(send, bit)
-            streams[i] = add_step(bit, keep, before, width)
-    held = []
-    for code in [x[-1] for x in streams]:
-        got = to_chip(code, bits - 1)
-        held.append([call(cast_kernel, shape((rows, width), bf16), [VMEM, VMEM], nbytes=MIB)(code, got)])
+        outs = halves(width) if bit < bits - 2 else (shape((rows, width), i16),)
+        half = call(functools.partial(add_kernel, bit + 1), outs, [VMEM, VMEM], nbytes=MIB)(
+            half[0], to_chip(half[1], 1 << bit)
+        )
+    came = [to_chip(direct[k], k) for k in reversed(range(1, chips))]
+    summed = call(direct_cast_kernel, shape((rows, chunk), bf16), [VMEM] * chips, nbytes=MIB)(direct[0], *came)
+    crossed = to_chip(half[-1], chips // 2)
+    spread = [to_chip(summed, k) for k in reversed(range(1, chips))][::-1]
+    held = [call(cast_kernel, shape((rows, width), bf16), [VMEM, VMEM], nbytes=MIB)(half[-1], crossed)]
+    *spread, _ = lax.optimization_barrier((*spread, held[0]))
+    first = call(join_kernel, shape((rows, genes), bf16), [VMEM] * chips, nbytes=MIB)(summed, *spread)
     masks = [0]
     for bit in reversed(range(bits - 1)):
-        held = [pieces + [to_chip(x, bit) for x in pieces] for pieces in held]
+        held = held + [to_chip(x, 1 << bit) for x in held]
         masks += [mask ^ (1 << bit) for mask in masks]
-    whole = []
-    for pieces in held:
-        whole += pieces + [to_core(x) for x in pieces]
-    parts = call(
-        functools.partial(cell_kernel, masks),
-        (shape((height, rank), f32),) + (shape((height, rank), i16),) * (n_genes - 1),
-        [VMEM] * (1 + len(whole)),
-        scratch=[pltpu.VMEM((rank, genes), bf16)],
-        flops=flops,
-        nbytes=6 * MIB,
-    )(dense, *whole)
-    got = [to_gene(parts[k], k) for k in reversed(range(1, n_genes))]
-    return call(last_kernel, shape((height, rank), f32), [VMEM] * n_genes, nbytes=MIB)(parts[0], *got)
+    theirs = [to_core(x) for x in held]
+    gene = call(
+        functools.partial(gene_kernel, masks), shape((rank, genes), bf16), [VMEM] * (2 + 2 * len(held)), nbytes=2 * MIB
+    )(first, to_core(first), *held, *theirs)
+
+    def cell(k, gene):
+        kind = f32 if k == 0 else i16
+        return call(
+            functools.partial(cell_kernel, k),
+            shape((height, rank), kind),
+            [VMEM, VMEM],
+            flops=flops // n_genes,
+            nbytes=3 * MIB,
+        )(dense, gene)
+
+    got = []
+    for k in reversed(range(1, n_genes)):
+        got.append(to_gene(cell(k, gene), k))
+    total = cell(0, gene)
+    for x in got:
+        total = call(more_kernel, shape((height, rank), f32), [VMEM, VMEM], nbytes=16 * MIB)(total, x)
+    return total
 
 
 def solution(mesh):

time: 48.4 us -> 46.2 us (0.955)
  waiting for transfers between devices: 24.9 us -> 14.7 us
  starting transfers between devices: 14.6 us -> 21.6 us
  Pallas kernels: 7.98 us -> 8.73 us
    ppermute x6 -> x9, waiting for transfers between devices: 16.6 us -> 7.63 us  [to_chip(): lax.ppermute(x, 'cells', [(i, i ^ CORES * k) for i in range(n_cells)])]
    ppermute x6 -> x9, starting transfers between devices: 10.5 us -> 17.1 us  [to_chip(): lax.ppermute(x, 'cells', [(i, i ^ CORES * k) for i in range(n_cells)])]
    ppermute x3, waiting for transfers between devices: 5.77 us -> 4.82 us  [to_gene(): return lax.ppermute(x, 'genes', [(i, i ^ k) for i in range(n_genes)])]
    pallas_call x5 -> x12, Pallas kernels: 2.79 us -> 3.63 us  [the longest x4 2.03 us: cell(): call(functools.partial(cell_kernel, k), shape((height, rank), kind), [VME...]
    ppermute x5 -> x4, waiting for transfers between devices: 2.5 us -> 2.27 us  [to_core(): return lax.ppermute(x, 'cells', [(i, i ^ 1) for i in range(n_cells)])]
  transfers between devices with their start and end apart: 14 -> 16, of which waited for: 10 -> 12; matrix products, arithmetic and copies ran while one was open for 0% -> 0% of each run, Pallas kernels for 2% -> 5%
where the time goes in v5:
time: 46.2 us; the launch traced here: 45.8 us
  starting transfers between devices  21.6 us (47%)
  waiting for transfers between devices  14.7 us (32%)
  Pallas kernels  8.73 us (19%)
  between operations  0.76 us (2%)
    ppermute x9, starting transfers between devices, to_chip(): lax.ppermute(x, 'cells', [(i, i ^ CORES * k) for i in range(n_cells)])  17.1 us
    ppermute x9, waiting for transfers between devices, to_chip(): lax.ppermute(x, 'cells', [(i, i ^ CORES * k) for i in range(n_cells)])  7.63 us
    ppermute x3, waiting for transfers between devices, to_gene(): return lax.ppermute(x, 'genes', [(i, i ^ k) for i in range(n_genes)])  4.82 us
    pallas_call x1, Pallas kernels, local(): call(dense_kernel, (shape((cells, genes), bf16), shape((rank, cells), bf1...  4.29 us
    ppermute x3, starting transfers between devices, to_gene(): return lax.ppermute(x, 'genes', [(i, i ^ k) for i in range(n_genes)])  3.62 us
    ppermute x4, waiting for transfers between devices, to_core(): return lax.ppermute(x, 'cells', [(i, i ^ 1) for i in range(n_cells)])  2.27 us
    pallas_call x4, Pallas kernels, cell(): call(functools.partial(cell_kernel, k), shape((height, rank), kind), [VME...  2.03 us
  transfers between devices with their start and end apart: 16, of which 12 were waited for; matrix products, arithmetic and copies ran while one was open for 0% of the time, Pallas kernels for 5%

profile of v5, /device:TPU:0, one launch (start us, length us, event | category | flops | bytes accessed | tf_op | source)
XLA Modules:
  0.0 45.8 jit_solution(6741540345678600842)
XLA Ops:
  0.7 4.3 %shard_map.55 = (bf16[1024,2048]{1,0:T(8,128)(2,1)S(1)}, bf16[256,1024]{1,0:T(8,128)(2,1)S(1)}, s16[128,2048]{1,0:T(8,128)(2,1)S(1)}) custom-call(s32[1]{0:T(128)S(6)} %copy.6.count, s32[96]{0:T(128)} %rows.1, s32[96]{0:T(128)} %cols.1, bf16[1024,256]{1,0:T(8,128)(2,1)} %sketch.1, bf16[96,128,128]{2,1,0:T(8,128)(2,1)} %tiles.1), custom_call_target="tpu_custom_call" | custom-call | flops 536870912 | bytes 8388608 | tf_op jit(solution)/shard_map/pallas_call | solution.py:230
  4.9 0.3 collective-permute-start
  5.3 0.7 %shard_map.56.mine = f32[128,2048]{1,0:T(8,128)S(1)} custom-call(bf16[256,1024]{1,0:T(8,128)(2,1)S(1)} %get-tuple-element.18.turned, bf16[1024,2048]{1,0:T(8,128)(2,1)S(1)} %get-tuple-element.17.dense), custom_call_target="tpu_custom_call" | custom-call | flops 536870912 | bytes 5242880 | tf_op jit(solution)/shard_map/pallas_call | solution.py:244
  6.0 0.9 %collective-permute-done.got = s16[128,2048]{1,0:T(8,128)(2,1)S(1)} collective-permute-done((s16[128,2048]{1,0:T(8,128)(2,1)S(1)}, s16[128,2048]{1,0:T(8,128)(2,1)S(1)}, u32[]{:S(2)}, u32[]{:S(2)}) %collective-permute-start) | collective-permute-done | bytes 524320 | tf_op jit(solution)/shard_map/ppermute | solution.py:219
  6.9 0.5 %shard_map.57 = (f32[64,512]{1,0:T(8,128)S(1)}, s16[64,512]{1,0:T(8,128)(2,1)S(1)}, s16[64,512]{1,0:T(8,128)(2,1)S(1)}, s16[64,512]{1,0:T(8,128)(2,1)S(1)}, f32[...) custom-call(f32[128,2048]{1,0:T(8,128)S(1)} %shard_map.56.mine, s16[128,2048]{1,0:T(8,128)(2,1)S(1)} %collective-permute-done.got), custom_call_target="tpu_custom_call" | custom-call | bytes 3145728 | tf_op jit(solution)/shard_map/pallas_call | solution.py:248
  7.4 2.3 %collective-permute-start.7 = (s16[64,1024]{1,0:T(8,128)(2,1)S(1)}, s16[64,1024]{1,0:T(8,128)(2,1)S(1)}, u32[]{:S(2)}, u32[]{:S(2)}) collective-permute-start(s16[64,1024]{1,0:T(8,128)(2,1)S(1)} %get-tuple-element.25), channel_id=1, source_target_pairs={{0,8},{4,12},{8,0},{12,4},{16,24},{20,28},{24,16},{28,20},{1,9},{5... | collective-permute-start | bytes 393224 | tf_op jit(solution)/shard_map/ppermute | solution.py:222
  9.7 2.5 %collective-permute-start.1 = (s16[64,512]{1,0:T(8,128)(2,1)S(1)}, s16[64,512]{1,0:T(8,128)(2,1)S(1)}, u32[]{:S(2)}, u32[]{:S(2)}) collective-permute-start(s16[64,512]{1,0:T(8,128)(2,1)S(1)} %get-tuple-element.21), channel_id=1, source_target_pairs={{0,24},{4,28},{8,16},{12,20},{16,8},{20,12},{24,0},{28,4},{1,25},{... | collective-permute-start | bytes 196616 | tf_op jit(solution)/shard_map/ppermute | solution.py:222
  12.2 0.3 collective-permute-start.2
  12.5 1.0 %collective-permute-done.7.got = s16[64,1024]{1,0:T(8,128)(2,1)S(1)} collective-permute-done((s16[64,1024]{1,0:T(8,128)(2,1)S(1)}, s16[64,1024]{1,0:T(8,128)(2,1)S(1)}, u32[]{:S(2)}, u32[]{:S(2)}) %collective-permute-start.7) | collective-permute-done | bytes 131104 | tf_op jit(solution)/shard_map/ppermute | solution.py:222
  13.6 4.0 %collective-permute-start.8 = (s16[64,1024]{1,0:T(8,128)(2,1)S(1)}, s16[64,1024]{1,0:T(8,128)(2,1)S(1)}, u32[]{:S(2)}, u32[]{:S(2)}) collective-permute-start(s16[64,1024]{1,0:T(8,128)(2,1)S(1)} %shard_map.59.code), channel_id=1, source_target_pairs={{0,16},{4,20},{8,24},{12,28},{16,0},{20,4},{24,8},{28,12},{1,17},{... | collective-permute-start | bytes 393224 | tf_op jit(solution)/shard_map/ppermute | solution.py:222
  17.6 2.4 %collective-permute-start.3 = (s16[64,512]{1,0:T(8,128)(2,1)S(1)}, s16[64,512]{1,0:T(8,128)(2,1)S(1)}, u32[]{:S(2)}, u32[]{:S(2)}) collective-permute-start(s16[64,512]{1,0:T(8,128)(2,1)S(1)} %get-tuple-element.23), channel_id=1, source_target_pairs={{0,8},{4,12},{8,0},{12,4},{16,24},{20,28},{24,16},{28,20},{1,9},{5... | collective-permute-start | bytes 196616 | tf_op jit(solution)/shard_map/ppermute | solution.py:222
  20.0 3.0 %collective-permute-done.2.refs_1_ = s16[64,512]{1,0:T(8,128)(2,1)S(1)} collective-permute-done((s16[64,512]{1,0:T(8,128)(2,1)S(1)}, s16[64,512]{1,0:T(8,128)(2,1)S(1)}, u32[]{:S(2)}, u32[]{:S(2)}) %collective-permute-start.2) | collective-permute-done | bytes 65568 | tf_op jit(solution)/shard_map/ppermute | solution.py:222
  23.2 2.3 %collective-permute-start.6 = (bf16[64,512]{1,0:T(8,128)(2,1)S(1)}, bf16[64,512]{1,0:T(8,128)(2,1)S(1)}, u32[]{:S(2)}, u32[]{:S(2)}) collective-permute-start(bf16[64,512]{1,0:T(8,128)(2,1)S(1)} %shard_map.58.refs_0_), channel_id=1, source_target_pairs={{0,24},{4,28},{8,16},{12,20},{16,8},{20,12},{24,0},{28,4},{1,25},{... | collective-permute-start | bytes 196616 | tf_op jit(solution)/shard_map/ppermute | solution.py:222
  25.4 1.2 %collective-permute-start.5 = (bf16[64,512]{1,0:T(8,128)(2,1)S(1)}, bf16[64,512]{1,0:T(8,128)(2,1)S(1)}, u32[]{:S(2)}, u32[]{:S(2)}) collective-permute-start(bf16[64,512]{1,0:T(8,128)(2,1)S(1)} %shard_map.58.refs_0_), channel_id=1, source_target_pairs={{0,16},{4,20},{8,24},{12,28},{16,0},{20,4},{24,8},{28,12},{1,17},{... | collective-permute-start | bytes 196616 | tf_op jit(solution)/shard_map/ppermute | solution.py:222
  26.6 1.0 %collective-permute-start.4 = (bf16[64,512]{1,0:T(8,128)(2,1)S(1)}, bf16[64,512]{1,0:T(8,128)(2,1)S(1)}, u32[]{:S(2)}, u32[]{:S(2)}) collective-permute-start(bf16[64,512]{1,0:T(8,128)(2,1)S(1)} %shard_map.58.refs_0_), channel_id=1, source_target_pairs={{0,8},{4,12},{8,0},{12,4},{16,24},{20,28},{24,16},{28,20},{1,9},{5... | collective-permute-start | bytes 196616 | tf_op jit(solution)/shard_map/ppermute | solution.py:222
  27.7 1.1 %collective-permute-start.10 = (bf16[64,1024]{1,0:T(8,128)(2,1)S(1)}, bf16[64,1024]{1,0:T(8,128)(2,1)S(1)}, u32[]{:S(2)}, u32[]{:S(2)}) collective-permute-start(bf16[64,1024]{1,0:T(8,128)(2,1)S(1)} %shard_map.60.refs_0_), channel_id=1, source_target_pairs={{0,8},{4,12},{8,0},{12,4},{16,24},{20,28},{24,16},{28,20},{1,9},{5... | collective-permute-start | bytes 393224 | tf_op jit(solution)/shard_map/ppermute | solution.py:222
  28.8 1.1 %collective-permute-done.6.refs_3_ = bf16[64,512]{1,0:T(8,128)(2,1)S(1)} collective-permute-done((bf16[64,512]{1,0:T(8,128)(2,1)S(1)}, bf16[64,512]{1,0:T(8,128)(2,1)S(1)}, u32[]{:S(2)}, u32[]{:S(2)}) %collective-permute-start.6) | collective-permute-done | bytes 65568 | tf_op jit(solution)/shard_map/ppermute | solution.py:222
  29.9 1.4 %collective-permute-done.5.refs_2_ = bf16[64,512]{1,0:T(8,128)(2,1)S(1)} collective-permute-done((bf16[64,512]{1,0:T(8,128)(2,1)S(1)}, bf16[64,512]{1,0:T(8,128)(2,1)S(1)}, u32[]{:S(2)}, u32[]{:S(2)}) %collective-permute-start.5) | collective-permute-done | bytes 65568 | tf_op jit(solution)/shard_map/ppermute | solution.py:222
  31.3 0.3 collective-permute-done.4.refs_1_
  31.7 0.5 %collective-permute-start.11 = (bf16[64,1024]{1,0:T(8,128)(2,1)S(1)}, bf16[64,1024]{1,0:T(8,128)(2,1)S(1)}, u32[]{:S(2)}, u32[]{:S(2)}) collective-permute-start(bf16[64,1024]{1,0:T(8,128)(2,1)S(1)} %shard_map.60.refs_0_), channel_id=1, source_target_pairs={{0,4},{4,0},{8,12},{12,8},{16,20},{20,16},{24,28},{28,24},{1,5},{5... | collective-permute-start | bytes 393224 | tf_op jit(solution)/shard_map/ppermute | solution.py:219
  32.2 0.8 %collective-permute-done.10.refs_1_ = bf16[64,1024]{1,0:T(8,128)(2,1)S(1)} collective-permute-done((bf16[64,1024]{1,0:T(8,128)(2,1)S(1)}, bf16[64,1024]{1,0:T(8,128)(2,1)S(1)}, u32[]{:S(2)}, u32[]{:S(2)}) %collective-permute-start.10) | collective-permute-done | bytes 131104 | tf_op jit(solution)/shard_map/ppermute | solution.py:222
  33.0 0.4 collective-permute-done.11.refs_2_
  33.4 0.9 %collective-permute-done.12.refs_3_ = bf16[64,1024]{1,0:T(8,128)(2,1)S(1)} collective-permute-done((bf16[64,1024]{1,0:T(8,128)(2,1)S(1)}, bf16[64,1024]{1,0:T(8,128)(2,1)S(1)}, u32[]{:S(2)}, u32[]{:S(2)}) %collective-permute-start.12) | collective-permute-done | bytes 131104 | tf_op jit(solution)/shard_map/ppermute | solution.py:219
  34.4 0.5 %shard_map.66 = s16[256,256]{1,0:T(8,128)(2,1)S(1)} custom-call(bf16[1024,2048]{1,0:T(8,128)(2,1)S(1)} %get-tuple-element.17.dense, bf16[256,2048]{1,0:T(8,128)(2,1)S(1)} %shard_map.62.gene), custom_call_target="tpu_custom_call" | custom-call | flops 268435456 | bytes 3145728 | tf_op jit(solution)/shard_map/pallas_call | solution.py:282
  35.0 0.5 %shard_map.64 = s16[256,256]{1,0:T(8,128)(2,1)S(1)} custom-call(bf16[1024,2048]{1,0:T(8,128)(2,1)S(1)} %get-tuple-element.17.dense, bf16[256,2048]{1,0:T(8,128)(2,1)S(1)} %shard_map.62.gene), custom_call_target="tpu_custom_call" | custom-call | flops 268435456 | bytes 3145728 | tf_op jit(solution)/shard_map/pallas_call | solution.py:282
  35.5 2.5 %collective-permute-start.13 = (s16[256,256]{1,0:T(8,128)(2,1)S(1)}, s16[256,256]{1,0:T(8,128)(2,1)S(1)}, u32[]{:S(2)}, u32[]{:S(2)}) collective-permute-start(s16[256,256]{1,0:T(8,128)(2,1)S(1)} %shard_map.64), channel_id=1, source_target_pairs={{0,3},{1,2},{2,1},{3,0},{4,7},{5,6},{6,5},{7,4},{8,11},{9,10},{10,... | collective-permute-start | bytes 393224 | tf_op jit(solution)/shard_map/ppermute | solution.py:225
  38.0 0.9 %collective-permute-start.14 = (s16[256,256]{1,0:T(8,128)(2,1)S(1)}, s16[256,256]{1,0:T(8,128)(2,1)S(1)}, u32[]{:S(2)}, u32[]{:S(2)}) collective-permute-start(s16[256,256]{1,0:T(8,128)(2,1)S(1)} %shard_map.66), channel_id=1, source_target_pairs={{0,2},{1,3},{2,0},{3,1},{4,6},{5,7},{6,4},{7,5},{8,10},{9,11},{10,... | collective-permute-start | bytes 393224 | tf_op jit(solution)/shard_map/ppermute | solution.py:225
  38.8 0.5 %shard_map.68 = s16[256,256]{1,0:T(8,128)(2,1)S(1)} custom-call(bf16[1024,2048]{1,0:T(8,128)(2,1)S(1)} %get-tuple-element.17.dense, bf16[256,2048]{1,0:T(8,128)(2,1)S(1)} %shard_map.62.gene), custom_call_target="tpu_custom_call" | custom-call | flops 268435456 | bytes 3145728 | tf_op jit(solution)/shard_map/pallas_call | solution.py:282
  39.7 0.5 %shard_map.63.total = f32[256,256]{1,0:T(8,128)S(1)} custom-call(bf16[1024,2048]{1,0:T(8,128)(2,1)S(1)} %get-tuple-element.17.dense, bf16[256,2048]{1,0:T(8,128)(2,1)S(1)} %shard_map.62.gene), custom_call_target="tpu_custom_call" | custom-call | flops 268435456 | bytes 3145728 | tf_op jit(solution)/shard_map/pallas_call | solution.py:282
  40.1 2.0 %collective-permute-done.13.got = s16[256,256]{1,0:T(8,128)(2,1)S(1)} collective-permute-done((s16[256,256]{1,0:T(8,128)(2,1)S(1)}, s16[256,256]{1,0:T(8,128)(2,1)S(1)}, u32[]{:S(2)}, u32[]{:S(2)}) %collective-permute-start.13) | collective-permute-done | bytes 131104 | tf_op jit(solution)/shard_map/ppermute | solution.py:225
  42.2 2.7 %collective-permute-done.14.got = s16[256,256]{1,0:T(8,128)(2,1)S(1)} collective-permute-done((s16[256,256]{1,0:T(8,128)(2,1)S(1)}, s16[256,256]{1,0:T(8,128)(2,1)S(1)}, u32[]{:S(2)}, u32[]{:S(2)}) %collective-permute-start.14) | collective-permute-done | bytes 131104 | tf_op jit(solution)/shard_map/ppermute | solution.py:225
  45.0 0.7 %shard_map.69 = f32[256,256]{1,0:T(8,128)} custom-call(f32[256,256]{1,0:T(8,128)S(1)} %shard_map.67.total, s16[256,256]{1,0:T(8,128)(2,1)S(1)} %collective-permute-done.15.got), custom_call_target="tpu_custom_call" | custom-call | bytes 16777216 | tf_op jit(solution)/shard_map/pallas_call | solution.py:295
  (15 shorter events, 1.0 us)
Async XLA Ops:
  4.9 2.0 %collective-permute-start = (s16[128,2048]{1,0:T(8,128)(2,1)S(1)}, s16[128,2048]{1,0:T(8,128)(2,1)S(1)}, u32[]{:S(2)}, u32[]{:S(2)}) collective-permute-start(s16[128,2048]{1,0:T(8,128)(2,1)S(1)} %get-tuple-element.19), channel_id=1, source_target_pairs={{0,4},{4,0},{8,12},{12,8},{16,20},{20,16},{24,28},{28,24},{1,5},{5... | collective-permute-start | bytes 1572872 | tf_op jit(solution)/shard_map/ppermute | solution.py:219
  7.4 6.1 %collective-permute-start.7 = (s16[64,1024]{1,0:T(8,128)(2,1)S(1)}, s16[64,1024]{1,0:T(8,128)(2,1)S(1)}, u32[]{:S(2)}, u32[]{:S(2)}) collective-permute-start(s16[64,1024]{1,0:T(8,128)(2,1)S(1)} %get-tuple-element.25), channel_id=1, source_target_pairs={{0,8},{4,12},{8,0},{12,4},{16,24},{20,28},{24,16},{28,20},{1,9},{5... | collective-permute-start | bytes 393224 | tf_op jit(solution)/shard_map/ppermute | solution.py:222
  9.7 10.3 %collective-permute-start.1 = (s16[64,512]{1,0:T(8,128)(2,1)S(1)}, s16[64,512]{1,0:T(8,128)(2,1)S(1)}, u32[]{:S(2)}, u32[]{:S(2)}) collective-permute-start(s16[64,512]{1,0:T(8,128)(2,1)S(1)} %get-tuple-element.21), channel_id=1, source_target_pairs={{0,24},{4,28},{8,16},{12,20},{16,8},{20,12},{24,0},{28,4},{1,25},{... | collective-permute-start | bytes 196616 | tf_op jit(solution)/shard_map/ppermute | solution.py:222
  12.2 10.9 %collective-permute-start.2 = (s16[64,512]{1,0:T(8,128)(2,1)S(1)}, s16[64,512]{1,0:T(8,128)(2,1)S(1)}, u32[]{:S(2)}, u32[]{:S(2)}) collective-permute-start(s16[64,512]{1,0:T(8,128)(2,1)S(1)} %get-tuple-element.22), channel_id=1, source_target_pairs={{0,16},{4,20},{8,24},{12,28},{16,0},{20,4},{24,8},{28,12},{1,17},{... | collective-permute-start | bytes 196616 | tf_op jit(solution)/shard_map/ppermute | solution.py:222
  13.6 14.0 %collective-permute-start.8 = (s16[64,1024]{1,0:T(8,128)(2,1)S(1)}, s16[64,1024]{1,0:T(8,128)(2,1)S(1)}, u32[]{:S(2)}, u32[]{:S(2)}) collective-permute-start(s16[64,1024]{1,0:T(8,128)(2,1)S(1)} %shard_map.59.code), channel_id=1, source_target_pairs={{0,16},{4,20},{8,24},{12,28},{16,0},{20,4},{24,8},{28,12},{1,17},{... | collective-permute-start | bytes 393224 | tf_op jit(solution)/shard_map/ppermute | solution.py:222
  17.6 5.5 %collective-permute-start.3 = (s16[64,512]{1,0:T(8,128)(2,1)S(1)}, s16[64,512]{1,0:T(8,128)(2,1)S(1)}, u32[]{:S(2)}, u32[]{:S(2)}) collective-permute-start(s16[64,512]{1,0:T(8,128)(2,1)S(1)} %get-tuple-element.23), channel_id=1, source_target_pairs={{0,8},{4,12},{8,0},{12,4},{16,24},{20,28},{24,16},{28,20},{1,9},{5... | collective-permute-start | bytes 196616 | tf_op jit(solution)/shard_map/ppermute | solution.py:222
  23.2 6.7 %collective-permute-start.6 = (bf16[64,512]{1,0:T(8,128)(2,1)S(1)}, bf16[64,512]{1,0:T(8,128)(2,1)S(1)}, u32[]{:S(2)}, u32[]{:S(2)}) collective-permute-start(bf16[64,512]{1,0:T(8,128)(2,1)S(1)} %shard_map.58.refs_0_), channel_id=1, source_target_pairs={{0,24},{4,28},{8,16},{12,20},{16,8},{20,12},{24,0},{28,4},{1,25},{... | collective-permute-start | bytes 196616 | tf_op jit(solution)/shard_map/ppermute | solution.py:222
  25.4 5.9 %collective-permute-start.5 = (bf16[64,512]{1,0:T(8,128)(2,1)S(1)}, bf16[64,512]{1,0:T(8,128)(2,1)S(1)}, u32[]{:S(2)}, u32[]{:S(2)}) collective-permute-start(bf16[64,512]{1,0:T(8,128)(2,1)S(1)} %shard_map.58.refs_0_), channel_id=1, source_target_pairs={{0,16},{4,20},{8,24},{12,28},{16,0},{20,4},{24,8},{28,12},{1,17},{... | collective-permute-start | bytes 196616 | tf_op jit(solution)/shard_map/ppermute | solution.py:222
  26.6 5.0 %collective-permute-start.4 = (bf16[64,512]{1,0:T(8,128)(2,1)S(1)}, bf16[64,512]{1,0:T(8,128)(2,1)S(1)}, u32[]{:S(2)}, u32[]{:S(2)}) collective-permute-start(bf16[64,512]{1,0:T(8,128)(2,1)S(1)} %shard_map.58.refs_0_), channel_id=1, source_target_pairs={{0,8},{4,12},{8,0},{12,4},{16,24},{20,28},{24,16},{28,20},{1,9},{5... | collective-permute-start | bytes 196616 | tf_op jit(solution)/shard_map/ppermute | solution.py:222
  27.7 5.3 %collective-permute-start.10 = (bf16[64,1024]{1,0:T(8,128)(2,1)S(1)}, bf16[64,1024]{1,0:T(8,128)(2,1)S(1)}, u32[]{:S(2)}, u32[]{:S(2)}) collective-permute-start(bf16[64,1024]{1,0:T(8,128)(2,1)S(1)} %shard_map.60.refs_0_), channel_id=1, source_target_pairs={{0,8},{4,12},{8,0},{12,4},{16,24},{20,28},{24,16},{28,20},{1,9},{5... | collective-permute-start | bytes 393224 | tf_op jit(solution)/shard_map/ppermute | solution.py:222
  31.6 2.7 %collective-permute-start.9 = (bf16[64,2048]{1,0:T(8,128)(2,1)S(1)}, bf16[64,2048]{1,0:T(8,128)(2,1)S(1)}, u32[]{:S(2)}, u32[]{:S(2)}) collective-permute-start(bf16[64,2048]{1,0:T(8,128)(2,1)S(1)} %shard_map.61.first), channel_id=1, source_target_pairs={{0,4},{4,0},{8,12},{12,8},{16,20},{20,16},{24,28},{28,24},{1,5},{5... | collective-permute-start | bytes 786440 | tf_op jit(solution)/shard_map/ppermute | solution.py:219
  31.7 1.7 %collective-permute-start.11 = (bf16[64,1024]{1,0:T(8,128)(2,1)S(1)}, bf16[64,1024]{1,0:T(8,128)(2,1)S(1)}, u32[]{:S(2)}, u32[]{:S(2)}) collective-permute-start(bf16[64,1024]{1,0:T(8,128)(2,1)S(1)} %shard_map.60.refs_0_), channel_id=1, source_target_pairs={{0,4},{4,0},{8,12},{12,8},{16,20},{20,16},{24,28},{28,24},{1,5},{5... | collective-permute-start | bytes 393224 | tf_op jit(solution)/shard_map/ppermute | solution.py:219
  33.0 1.3 %collective-permute-start.12 = (bf16[64,1024]{1,0:T(8,128)(2,1)S(1)}, bf16[64,1024]{1,0:T(8,128)(2,1)S(1)}, u32[]{:S(2)}, u32[]{:S(2)}) collective-permute-start(bf16[64,1024]{1,0:T(8,128)(2,1)S(1)} %collective-permute-done.10.refs_1_), channel_id=1, source_target_pairs={{0,4},{4,0},{8,12},{12,8},{16,20},{20,16},{24,28},{28,24},{1,5},{5... | collective-permute-start | bytes 393224 | tf_op jit(solution)/shard_map/ppermute | solution.py:219
  35.5 6.6 %collective-permute-start.13 = (s16[256,256]{1,0:T(8,128)(2,1)S(1)}, s16[256,256]{1,0:T(8,128)(2,1)S(1)}, u32[]{:S(2)}, u32[]{:S(2)}) collective-permute-start(s16[256,256]{1,0:T(8,128)(2,1)S(1)} %shard_map.64), channel_id=1, source_target_pairs={{0,3},{1,2},{2,1},{3,0},{4,7},{5,6},{6,5},{7,4},{8,11},{9,10},{10,... | collective-permute-start | bytes 393224 | tf_op jit(solution)/shard_map/ppermute | solution.py:225
  38.0 6.9 %collective-permute-start.14 = (s16[256,256]{1,0:T(8,128)(2,1)S(1)}, s16[256,256]{1,0:T(8,128)(2,1)S(1)}, u32[]{:S(2)}, u32[]{:S(2)}) collective-permute-start(s16[256,256]{1,0:T(8,128)(2,1)S(1)} %shard_map.66), channel_id=1, source_target_pairs={{0,2},{1,3},{2,0},{3,1},{4,6},{5,7},{6,4},{7,5},{8,10},{9,11},{10,... | collective-permute-start | bytes 393224 | tf_op jit(solution)/shard_map/ppermute | solution.py:225
  39.4 5.7 %collective-permute-start.15 = (s16[256,256]{1,0:T(8,128)(2,1)S(1)}, s16[256,256]{1,0:T(8,128)(2,1)S(1)}, u32[]{:S(2)}, u32[]{:S(2)}) collective-permute-start(s16[256,256]{1,0:T(8,128)(2,1)S(1)} %shard_map.68), channel_id=1, source_target_pairs={{0,1},{1,0},{2,3},{3,2},{4,5},{5,4},{6,7},{7,6},{8,9},{9,8},{10,11... | collective-permute-start | bytes 393224 | tf_op jit(solution)/shard_map/ppermute | solution.py:225

commit v6 on v2

v6 whole, which is shorter than its diff:
```python
import functools

import jax
import jax.numpy as jnp
from jax import lax
from jax.experimental import pallas as pl
from jax.experimental.pallas import tpu as pltpu
from jax.sharding import PartitionSpec as P

GENE_BLOCKS = 16
CORES = 2
LANES = 128
PARTS = (1, 1, 1, 1)
MIB = 1 << 20

VMEM = pl.BlockSpec(memory_space=pltpu.VMEM)
SMEM = pl.BlockSpec(memory_space=pltpu.SMEM)
HBM = pl.BlockSpec(memory_space=pltpu.HBM)
f32, bf16, i16, i32 = jnp.float32, jnp.bfloat16, jnp.int16, jnp.int32


def encode(x, out, at=()):
    peak = jnp.max(jnp.abs(x), axis=0, keepdims=True)
    expo = jnp.ceil(jnp.log2(jnp.maximum(peak, 2.0**-100)))
    expo = jnp.clip(expo, -100.0, 126.0)
    code = jnp.round(x * jnp.exp2(14.0 - expo)).astype(i32)
    top = code[:16]
    row = lax.broadcasted_iota(i32, top.shape, 0)
    word = jnp.broadcast_to(expo.astype(i32) + 128, top.shape)
    marked = (top & ~1) | ((word >> jnp.minimum(row, 7)) & 1)
    top = jnp.where(row < 8, marked, top)
    out[at + (pl.ds(0, 16),)] = top.astype(i16)
    out[at + (pl.ds(16, x.shape[0] - 16),)] = code[16:].astype(i16)


def decode(code):
    code = code.astype(i32)
    head = code[:8]
    row = lax.broadcasted_iota(i32, head.shape, 0)
    word = jnp.sum((head & 1) << row, axis=0, keepdims=True)
    scale = jnp.exp2((word - (128 + 14)).astype(f32))
    return code.astype(f32) * scale


def core_and_chip():
    place = lax.axis_index("cells")
    return lax.rem(place, CORES), lax.div(place, CORES)


def call(body, outs, in_specs, scratch=(), mib=32, nbytes=0):
    return pl.pallas_call(
        body,
        out_shape=outs,
        in_specs=in_specs,
        out_specs=jax.tree.map(lambda _: VMEM, outs),
        scratch_shapes=list(scratch),
        compiler_params=pltpu.CompilerParams(vmem_limit_bytes=mib * MIB),
        cost_estimate=pl.CostEstimate(flops=0, bytes_accessed=nbytes, transcendentals=0),
    )


def block(index, size):
    return pl.ds(pl.multiple_of(index * size, size), size)


def dense_kernel(count, rows, cols, sketch, tiles, dense, turned, theirs, place, sketch_here, load_sems, sems):
    tile = tiles.shape[1]
    core, _ = core_and_chip()
    rows_place, cols_place = place
    loads = [
        pltpu.make_async_copy(src, dst, load_sems.at[i])
        for i, (src, dst) in enumerate(((rows, rows_place), (cols, cols_place), (sketch, sketch_here)))
    ]
    for load in loads:
        load.start()

    def clear(i, _):
        dense[block(i, 16), :] = jnp.zeros((16, dense.shape[1]), bf16)
        return 0

    lax.fori_loop(0, dense.shape[0] // 16, clear, 0)
    for load in loads[:2]:
        load.wait()

    def copy(s):
        to = dense.at[block(rows_place[s], tile), block(cols_place[s], tile)]
        return pltpu.make_async_copy(tiles.at[s], to, sems.at[s])

    def start(s, _):
        copy(s).start()
        return 0

    def wait(s, _):
        copy(s).wait()
        return 0

    lax.fori_loop(0, count[0], start, 0)
    loads[2].wait()
    turned[...] = sketch_here[...].T
    lax.fori_loop(0, count[0], wait, 0)
    half_kernel(1, 0, turned, dense, theirs)


def half_kernel(other, start, turned, dense, out):
    core, _ = core_and_chip()
    rows, width = out.shape
    left = turned[block(core ^ other, rows), :]
    step = min(width, 512)
    for j in range(0, width, step):
        part = jnp.dot(left, dense[:, start + j : start + j + step], preferred_element_type=f32)
        if other:
            encode(part, out.at[:, j : j + step])
        else:
            out[:, j : j + step] = part


def add_kernel(bit, mine, got, *outs):
    _, chip = core_and_chip()
    start = 0
    for keep, send in zip(outs[::2], outs[1::2]):
        width = keep.shape[1]
        ours = (chip >> bit) & 1
        cut = pl.ds(pl.multiple_of(start + (1 - ours) * width, width), width)
        encode(mine[:, cut] + decode(got[:, cut]), send)
        cut = pl.ds(pl.multiple_of(start + ours * width, width), width)
        keep[...] = mine[:, cut] + decode(got[:, cut])
        start += 2 * width


def code_kernel(mine, got, *outs):
    start = 0
    for out in outs:
        cut = slice(start, start + out.shape[1])
        encode(mine[:, cut] + decode(got[:, cut]), out)
        start += out.shape[1]


def cast_kernel(code, got, out):
    out[...] = (decode(code[...]) + decode(got[...])).astype(bf16)


def join(masks, pieces, gene):
    core, chip = core_and_chip()
    rows, width = pieces[0].shape
    for k, mask in enumerate(masks):
        place, size = 0, gene.shape[1]
        for bit in range(len(masks).bit_length() - 1):
            size //= 2
            place = place + (((chip ^ mask) >> bit) & 1) * size
        cut = pl.ds(pl.multiple_of(place, width), width)
        gene[block(core, rows), cut] = pieces[k][...]
        gene[block(1 - core, rows), cut] = pieces[len(masks) + k][...]


def gene_kernel(masks, *refs):
    join(masks, refs[:-1], refs[-1])


def product(left, gene):
    return lax.dot_general(left, gene, (((1,), (1,)), ((), ())), preferred_element_type=f32)


def part_kernel(masks, start, fresh, dense, *refs):
    *pieces, out, gene = refs
    if not fresh:
        before, *pieces = pieces
    join(masks, pieces, gene)
    step = 256
    for i in range(0, out.shape[0], step):
        part = product(dense[i : i + step, start : start + gene.shape[1]], gene[...])
        out[i : i + step, :] = part if fresh else before[i : i + step, :] + part


def cell_kernel(k, start, dense, gene, *refs):
    *before, out = refs
    cut = block(lax.axis_index("genes") ^ k, out.shape[0])
    part = product(dense[cut, start : start + gene.shape[1]], gene[...])
    if before:
        part = part + before[0][cut, :]
    if k == 0:
        out[...] = part
    else:
        encode(part, out)


def more_kernel(total, got, out):
    out[...] = total[...] + decode(got[...])


def cuts_of(genes, bits):
    for parts in (PARTS, (1, 1)):
        unit = genes // sum(parts)
        if unit >> max(bits - 1, 0) >= LANES:
            ends = [sum(parts[:i]) * unit for i in range(len(parts))]
            return tuple((at, p * unit) for at, p in zip(ends, parts))
    return ((0, genes),)


def local(n_cells, n_genes, sketch, tiles, tile_rows, tile_cols, tile_counts):
    cells, rank = sketch.shape
    slots, tile, _ = tiles.shape
    genes = GENE_BLOCKS * tile
    bits = (n_cells // CORES).bit_length() - 1
    rows = rank // CORES
    height = cells // n_genes
    shape = jax.ShapeDtypeStruct
    cuts = cuts_of(genes, bits)

    def to_core(x):
        return lax.ppermute(x, "cells", [(i, i ^ 1) for i in range(n_cells)])

    def to_chip(x, bit):
        return lax.ppermute(x, "cells", [(i, i ^ (CORES << bit)) for i in range(n_cells)])

    def to_gene(x, k):
        return lax.ppermute(x, "genes", [(i, i ^ k) for i in range(n_genes)])

    dense, turned, theirs = call(
        dense_kernel,
        (shape((cells, genes), bf16), shape((rank, cells), bf16), shape((rows, cuts[0][1]), i16)),
        [SMEM] + [HBM] * 4,
        scratch=[
            (pltpu.SMEM((slots,), i32), pltpu.SMEM((slots,), i32)),
            pltpu.VMEM((cells, rank), bf16),
            pltpu.SemaphoreType.DMA((3,)),
            pltpu.SemaphoreType.DMA((slots,)),
        ],

    )(tile_counts, *(pltpu.with_memory_space_constraint(x, pltpu.HBM) for x in (tile_rows, tile_cols, sketch, tiles)))

    def half_of(other, start, turned, width):
        body = functools.partial(half_kernel, other, start)
        return call(body, shape((rows, width), i16 if other else f32), [VMEM, VMEM])(turned, dense)

    def after(x, *others):
        return lax.optimization_barrier((x, *others))[0]

    def add_step(bit, kept, came, widths):
        if bit < bits - 1:
            outs = [shape((rows, width // 2), kind) for width in widths for kind in (f32, i16)]
            done = call(functools.partial(add_kernel, bit), tuple(outs), [VMEM, VMEM])(kept, came)
            return [done[i : i + 2] for i in range(0, len(done), 2)]
        done = call(code_kernel, tuple(shape((rows, width), i16) for width in widths), [VMEM, VMEM])(kept, came)
        return [done[i : i + 1] for i in range(len(done))]

    widths = [width for _, width in cuts]
    first, rest = widths[0], genes - widths[0]
    got = to_core(theirs)
    mine = half_of(0, 0, turned, first)
    if rest:
        got_rest = to_core(half_of(1, first, after(turned, mine), rest))
    sums = add_step(0, mine, got, widths[:1])
    if rest:
        sums += add_step(0, half_of(0, first, after(turned, *sums[0]), rest), got_rest, widths[1:])
    for bit in range(bits - 1):
        widths = [width // 2 for width in widths]
        came = [to_chip(code, bit) for _, code in sums]
        done = []
        for (kept, _), x, width in zip(sums, came, widths):
            done += add_step(bit + 1, kept, after(x, *done[-1]) if done else x, [width])
        sums = done
    held = []
    for (code,) in sums:
        came = to_chip(code, bits - 1)
        came = after(came, *held[-1]) if held else came
        held.append([call(cast_kernel, shape(code.shape, bf16), [VMEM, VMEM])(code, came)])
    masks = [0]
    for bit in reversed(range(bits - 1)):
        before = None
        for pieces in held:
            came = [to_chip(x, bit) for x in pieces]
            if before is not None:
                came = [after(x, before) for x in came]
            pieces += came
            before = came[-1]
        masks += [mask ^ (1 << bit) for mask in masks]
    sides = [pieces + [to_core(x) for x in pieces] for pieces in held]
    total = ()
    for (start, width), pieces in zip(cuts[:-1], sides):
        total = (
            call(
                functools.partial(part_kernel, masks, start, not total),
                shape((cells, rank), f32),
                [VMEM] * (1 + len(total) + len(pieces)),
                scratch=[pltpu.VMEM((rank, width), bf16)],
            )(dense, *total, *pieces),
        )
    (start, width), pieces = cuts[-1], sides[-1]
    gene = call(
        functools.partial(gene_kernel, masks), shape((rank, width), bf16), [VMEM] * len(pieces)
    )(*pieces)

    def cell(k):
        return call(
            functools.partial(cell_kernel, k, start),
            shape((height, rank), f32 if k == 0 else i16),
            [VMEM] * (2 + len(total)),
        )(dense, gene, *total)

    came = [to_gene(cell(k), k) for k in reversed(range(1, n_genes))]
    out = cell(0)
    for x in came:
        out = call(more_kernel, shape((height, rank), f32), [VMEM, VMEM], nbytes=16 * MIB)(out, x)
    return out


def solution(mesh):
    in_specs = (
        P("cells", None),
        P(("cells", "genes"), None, None),
        P(("cells", "genes")),
        P(("cells", "genes")),
        P(("cells", "genes")),
    )
    out_specs = P(("cells", "genes"), None)
    body = functools.partial(local, mesh.shape["cells"], mesh.shape["genes"])
    return jax.shard_map(body, mesh=mesh, in_specs=in_specs, out_specs=out_specs, check_vma=False)
```

time: 61 us -> 46.9 us (0.77)
  blocking collectives: 49.1 us -> 0 us
  starting transfers between devices: 0.07 us -> 23.2 us
  waiting for transfers between devices: 3.08 us -> 12.8 us
  Pallas kernels: 7.75 us -> 9.69 us
    all_to_all x3 -> x0, blocking collectives: 49.1 us -> none  [the longest x2 36.8 us: over_chips(): lax.all_to_all(x, 'cells', 0, 0, axis_index_groups=groups, tiled=True)]
    ppermute x0 -> x15, starting transfers between devices: none -> 21.1 us  [the longest x12 17.4 us: to_chip(): lax.ppermute(x, 'cells', [(i, i ^ CORES << bit) for i in range(n_cells)])]
    ppermute x0 -> x15, waiting for transfers between devices: none -> 11.4 us  [the longest x12 6.4 us: to_chip(): lax.ppermute(x, 'cells', [(i, i ^ CORES << bit) for i in range(n_cells)])]
    pallas_call x5 -> x24, Pallas kernels: 3.47 us -> 5.85 us  [the longest x3 1.53 us: half_of(): call(body, shape((rows, width), i16 if other else f32), [VMEM, VMEM])]
    ppermute x2 -> x10, starting transfers between devices: 0.07 us -> 2.11 us  [to_core(): return lax.ppermute(x, 'cells', [(i, i ^ 1) for i in range(n_cells)])]
    ppermute x2 -> x10, waiting for transfers between devices: 3.08 us -> 1.42 us  [to_core(): return lax.ppermute(x, 'cells', [(i, i ^ 1) for i in range(n_cells)])]
  transfers between devices with their start and end apart: 2 -> 25, of which waited for: 2 -> 9; matrix products, arithmetic and copies ran while one was open for 0% -> 0% of each run, Pallas kernels for 1% -> 7%
where the time goes in v6:
time: 46.9 us; the launch traced here: 46.6 us
  starting transfers between devices  23.2 us (49%)
  waiting for transfers between devices  12.8 us (27%)
  Pallas kernels  9.69 us (21%)
  between operations  0.89 us (2%)
    ppermute x12, starting transfers between devices, to_chip(): lax.ppermute(x, 'cells', [(i, i ^ CORES << bit) for i in range(n_cells)])  17.4 us
    ppermute x12, waiting for transfers between devices, to_chip(): lax.ppermute(x, 'cells', [(i, i ^ CORES << bit) for i in range(n_cells)])  6.4 us
    ppermute x3, waiting for transfers between devices, to_gene(): return lax.ppermute(x, 'genes', [(i, i ^ k) for i in range(n_genes)])  4.97 us
    pallas_call x1, Pallas kernels, local(): call(dense_kernel, (shape((cells, genes), bf16), shape((rank, cells), bf1...  3.84 us
    ppermute x3, starting transfers between devices, to_gene(): return lax.ppermute(x, 'genes', [(i, i ^ k) for i in range(n_genes)])  3.68 us
    ppermute x10, starting transfers between devices, to_core(): return lax.ppermute(x, 'cells', [(i, i ^ 1) for i in range(n_cells)])  2.11 us
    pallas_call x3, Pallas kernels, half_of(): call(body, shape((rows, width), i16 if other else f32), [VMEM, VMEM])  1.53 us
    pallas_call x3, Pallas kernels, local(): call(functools.partial(part_kernel, masks, start, not total), shape((cell...  1.5 us
  transfers between devices with their start and end apart: 25, of which 9 were waited for; matrix products, arithmetic and copies ran while one was open for 0% of the time, Pallas kernels for 7%

profile of v6, /device:TPU:0, one launch (start us, length us, event | category | flops | bytes accessed | tf_op | source)
XLA Modules:
  0.0 46.6 jit_solution(12762849483504814395)
XLA Ops:
  0.7 3.8 %shard_map.55 = (bf16[1024,2048]{1,0:T(8,128)(2,1)S(1)}, bf16[256,1024]{1,0:T(8,128)(2,1)S(1)}, s16[128,512]{1,0:T(8,128)(2,1)S(1)}) custom-call(s32[1]{0:T(128)S(6)} %copy.6.count, s32[96]{0:T(128)} %rows.1, s32[96]{0:T(128)} %cols.1, bf16[1024,256]{1,0:T(8,128)(2,1)} %sketch.1, bf16[96,128,128]{2,1,0:T(8,128)(2,1)} %tiles.1), custom_call_target="tpu_custom_call" | custom-call | tf_op jit(solution)/shard_map/pallas_call | solution.py:218
  4.8 0.6 %shard_map.59 = s16[128,1536]{1,0:T(8,128)(2,1)S(1)} custom-call(bf16[256,1024]{1,0:T(8,128)(2,1)S(1)} %get-tuple-element.33.turned, bf16[1024,2048]{1,0:T(8,128)(2,1)S(1)} %get-tuple-element.27.dense), custom_call_target="tpu_custom_call" | custom-call | tf_op jit(solution)/shard_map/pallas_call | solution.py:233
  5.6 0.5 %collective-permute-start = (s16[128,512]{1,0:T(8,128)(2,1)S(1)}, s16[128,512]{1,0:T(8,128)(2,1)S(1)}, u32[]{:S(2)}, u32[]{:S(2)}) collective-permute-start(s16[128,512]{1,0:T(8,128)(2,1)S(1)} %get-tuple-element.29), channel_id=1, source_target_pairs={{0,4},{4,0},{8,12},{12,8},{16,20},{20,16},{24,28},{28,24},{1,5},{5... | collective-permute-start | bytes 393224 | tf_op jit(solution)/shard_map/ppermute | solution.py:210
  6.0 1.4 %collective-permute-done.got = s16[128,512]{1,0:T(8,128)(2,1)S(1)} collective-permute-done((s16[128,512]{1,0:T(8,128)(2,1)S(1)}, s16[128,512]{1,0:T(8,128)(2,1)S(1)}, u32[]{:S(2)}, u32[]{:S(2)}) %collective-permute-start) | collective-permute-done | bytes 131104 | tf_op jit(solution)/shard_map/ppermute | solution.py:210
  7.5 2.5 %collective-permute-start.5 = (s16[128,256]{1,0:T(8,128)(2,1)S(1)}, s16[128,256]{1,0:T(8,128)(2,1)S(1)}, u32[]{:S(2)}, u32[]{:S(2)}) collective-permute-start(s16[128,256]{1,0:T(8,128)(2,1)S(1)} %get-tuple-element.31), channel_id=1, source_target_pairs={{0,8},{4,12},{8,0},{12,4},{16,24},{20,28},{24,16},{28,20},{1,9},{5... | collective-permute-start | bytes 196616 | tf_op jit(solution)/shard_map/ppermute | solution.py:213
  10.0 0.6 %shard_map.58.mine = f32[128,1536]{1,0:T(8,128)S(1)} custom-call(bf16[256,1024]{1,0:T(8,128)(2,1)S(1)} %get-tuple-element.33.turned, bf16[1024,2048]{1,0:T(8,128)(2,1)S(1)} %get-tuple-element.27.dense), custom_call_target="tpu_custom_call" | custom-call | tf_op jit(solution)/shard_map/pallas_call | solution.py:233
  10.9 2.0 %collective-permute-start.3 = (s16[128,256]{1,0:T(8,128)(2,1)S(1)}, s16[128,256]{1,0:T(8,128)(2,1)S(1)}, u32[]{:S(2)}, u32[]{:S(2)}) collective-permute-start(s16[128,256]{1,0:T(8,128)(2,1)S(1)} %get-tuple-element.37), channel_id=1, source_target_pairs={{0,8},{4,12},{8,0},{12,4},{16,24},{20,28},{24,16},{28,20},{1,9},{5... | collective-permute-start | bytes 196616 | tf_op jit(solution)/shard_map/ppermute | solution.py:213
  13.1 2.8 %collective-permute-start.9 = (s16[128,256]{1,0:T(8,128)(2,1)S(1)}, s16[128,256]{1,0:T(8,128)(2,1)S(1)}, u32[]{:S(2)}, u32[]{:S(2)}) collective-permute-start(s16[128,256]{1,0:T(8,128)(2,1)S(1)} %shard_map.61.code), channel_id=1, source_target_pairs={{0,16},{4,20},{8,24},{12,28},{16,0},{20,4},{24,8},{28,12},{1,17},{... | collective-permute-start | bytes 196616 | tf_op jit(solution)/shard_map/ppermute | solution.py:213
  15.9 2.5 %collective-permute-start.8 = (s16[128,256]{1,0:T(8,128)(2,1)S(1)}, s16[128,256]{1,0:T(8,128)(2,1)S(1)}, u32[]{:S(2)}, u32[]{:S(2)}) collective-permute-start(s16[128,256]{1,0:T(8,128)(2,1)S(1)} %shard_map.62.code), channel_id=1, source_target_pairs={{0,16},{4,20},{8,24},{12,28},{16,0},{20,4},{24,8},{28,12},{1,17},{... | collective-permute-start | bytes 196616 | tf_op jit(solution)/shard_map/ppermute | solution.py:213
  18.5 1.3 %collective-permute-start.7 = (s16[128,256]{1,0:T(8,128)(2,1)S(1)}, s16[128,256]{1,0:T(8,128)(2,1)S(1)}, u32[]{:S(2)}, u32[]{:S(2)}) collective-permute-start(s16[128,256]{1,0:T(8,128)(2,1)S(1)} %shard_map.63.code), channel_id=1, source_target_pairs={{0,16},{4,20},{8,24},{12,28},{16,0},{20,4},{24,8},{28,12},{1,17},{... | collective-permute-start | bytes 196616 | tf_op jit(solution)/shard_map/ppermute | solution.py:213
  19.9 1.7 %collective-permute-start.6 = (s16[128,256]{1,0:T(8,128)(2,1)S(1)}, s16[128,256]{1,0:T(8,128)(2,1)S(1)}, u32[]{:S(2)}, u32[]{:S(2)}) collective-permute-start(s16[128,256]{1,0:T(8,128)(2,1)S(1)} %shard_map.64.code), channel_id=1, source_target_pairs={{0,16},{4,20},{8,24},{12,28},{16,0},{20,4},{24,8},{28,12},{1,17},{... | collective-permute-start | bytes 196616 | tf_op jit(solution)/shard_map/ppermute | solution.py:213
  21.7 2.2 %collective-permute-start.13 = (bf16[128,256]{1,0:T(8,128)(2,1)S(1)}, bf16[128,256]{1,0:T(8,128)(2,1)S(1)}, u32[]{:S(2)}, u32[]{:S(2)}) collective-permute-start(bf16[128,256]{1,0:T(8,128)(2,1)S(1)} %shard_map.65.refs_0_), channel_id=1, source_target_pairs={{0,8},{4,12},{8,0},{12,4},{16,24},{20,28},{24,16},{28,20},{1,9},{5... | collective-permute-start | bytes 196616 | tf_op jit(solution)/shard_map/ppermute | solution.py:213
  23.9 2.6 %collective-permute-done.8.got = s16[128,256]{1,0:T(8,128)(2,1)S(1)} collective-permute-done((s16[128,256]{1,0:T(8,128)(2,1)S(1)}, s16[128,256]{1,0:T(8,128)(2,1)S(1)}, u32[]{:S(2)}, u32[]{:S(2)}) %collective-permute-start.8) | collective-permute-done | bytes 65568 | tf_op jit(solution)/shard_map/ppermute | solution.py:213
  26.7 0.9 %collective-permute-done.7.got = s16[128,256]{1,0:T(8,128)(2,1)S(1)} collective-permute-done((s16[128,256]{1,0:T(8,128)(2,1)S(1)}, s16[128,256]{1,0:T(8,128)(2,1)S(1)}, u32[]{:S(2)}, u32[]{:S(2)}) %collective-permute-start.7) | collective-permute-done | bytes 65568 | tf_op jit(solution)/shard_map/ppermute | solution.py:213
  27.6 1.2 %collective-permute-start.11 = (bf16[128,256]{1,0:T(8,128)(2,1)S(1)}, bf16[128,256]{1,0:T(8,128)(2,1)S(1)}, u32[]{:S(2)}, u32[]{:S(2)}) collective-permute-start(bf16[128,256]{1,0:T(8,128)(2,1)S(1)} %shard_map.67.refs_1_), channel_id=1, source_target_pairs={{0,8},{4,12},{8,0},{12,4},{16,24},{20,28},{24,16},{28,20},{1,9},{5... | collective-permute-start | bytes 196616 | tf_op jit(solution)/shard_map/ppermute | solution.py:213
  28.9 0.9 %collective-permute-start.10 = (bf16[128,256]{1,0:T(8,128)(2,1)S(1)}, bf16[128,256]{1,0:T(8,128)(2,1)S(1)}, u32[]{:S(2)}, u32[]{:S(2)}) collective-permute-start(bf16[128,256]{1,0:T(8,128)(2,1)S(1)} %shard_map.68.refs_0_), channel_id=1, source_target_pairs={{0,8},{4,12},{8,0},{12,4},{16,24},{20,28},{24,16},{28,20},{1,9},{5... | collective-permute-start | bytes 196616 | tf_op jit(solution)/shard_map/ppermute | solution.py:213
  29.8 0.5 %collective-permute-start.17 = (bf16[128,256]{1,0:T(8,128)(2,1)S(1)}, bf16[128,256]{1,0:T(8,128)(2,1)S(1)}, u32[]{:S(2)}, u32[]{:S(2)}) collective-permute-start(bf16[128,256]{1,0:T(8,128)(2,1)S(1)} %collective-permute-done.13.refs_1_), channel_id=1, source_target_pairs={{0,4},{4,0},{8,12},{12,8},{16,20},{20,16},{24,28},{28,24},{1,5},{5... | collective-permute-start | bytes 196616 | tf_op jit(solution)/shard_map/ppermute | solution.py:210
  30.3 1.0 %collective-permute-done.12.refs_2_ = bf16[128,256]{1,0:T(8,128)(2,1)S(1)} collective-permute-done((bf16[128,256]{1,0:T(8,128)(2,1)S(1)}, bf16[128,256]{1,0:T(8,128)(2,1)S(1)}, u32[]{:S(2)}, u32[]{:S(2)}) %collective-permute-start.12) | collective-permute-done | bytes 65568 | tf_op jit(solution)/shard_map/ppermute | solution.py:213
  31.3 0.7 %collective-permute-done.11.refs_2_ = bf16[128,256]{1,0:T(8,128)(2,1)S(1)} collective-permute-done((bf16[128,256]{1,0:T(8,128)(2,1)S(1)}, bf16[128,256]{1,0:T(8,128)(2,1)S(1)}, u32[]{:S(2)}, u32[]{:S(2)}) %collective-permute-start.11) | collective-permute-done | bytes 65568 | tf_op jit(solution)/shard_map/ppermute | solution.py:213
  32.0 1.2 %collective-permute-done.10.refs_1_ = bf16[128,256]{1,0:T(8,128)(2,1)S(1)} collective-permute-done((bf16[128,256]{1,0:T(8,128)(2,1)S(1)}, bf16[128,256]{1,0:T(8,128)(2,1)S(1)}, u32[]{:S(2)}, u32[]{:S(2)}) %collective-permute-start.10) | collective-permute-done | bytes 65568 | tf_op jit(solution)/shard_map/ppermute | solution.py:213
  33.2 0.5 %collective-permute-start.19 = (bf16[128,256]{1,0:T(8,128)(2,1)S(1)}, bf16[128,256]{1,0:T(8,128)(2,1)S(1)}, u32[]{:S(2)}, u32[]{:S(2)}) collective-permute-start(bf16[128,256]{1,0:T(8,128)(2,1)S(1)} %collective-permute-done.12.refs_2_), channel_id=1, source_target_pairs={{0,4},{4,0},{8,12},{12,8},{16,20},{20,16},{24,28},{28,24},{1,5},{5... | collective-permute-start | bytes 196616 | tf_op jit(solution)/shard_map/ppermute | solution.py:210
  33.8 0.4 collective-permute-start.21
  34.2 0.5 %shard_map.70.refs_0_ = f32[1024,256]{1,0:T(8,128)S(1)} custom-call(bf16[1024,2048]{1,0:T(8,128)(2,1)S(1)} %get-tuple-element.27.dense, bf16[128,256]{1,0:T(8,128)(2,1)S(1)} %shard_map.65.refs_0_, bf16[128,256]{1,0:T(8,128)(2,1)S(1)} %collective-permute-done.13.refs_1_, bf16[128,256]{1,0:T(8,128)(2,1)S(1)} %collective-permute-done.16.refs_2_, ...), custom_call_target="tpu_custom_call" | custom-call | tf_op jit(solution)/shard_map/pallas_call | solution.py:281
  34.8 0.5 %shard_map.71.refs_0_ = f32[1024,256]{1,0:T(8,128)S(1)} custom-call(bf16[1024,2048]{1,0:T(8,128)(2,1)S(1)} %get-tuple-element.27.dense, f32[1024,256]{1,0:T(8,128)S(1)} %shard_map.70.refs_0_, bf16[128,256]{1,0:T(8,128)(2,1)S(1)} %shard_map.66.refs_1_, bf16[128,256]{1,0:T(8,128)(2,1)S(1)} %collective-permute-done.12.refs_2_, ...), custom_call_target="tpu_custom_call" | custom-call | tf_op jit(solution)/shard_map/pallas_call | solution.py:281
  35.3 0.5 %shard_map.72.refs_0_ = f32[1024,256]{1,0:T(8,128)S(1)} custom-call(bf16[1024,2048]{1,0:T(8,128)(2,1)S(1)} %get-tuple-element.27.dense, f32[1024,256]{1,0:T(8,128)S(1)} %shard_map.71.refs_0_, bf16[128,256]{1,0:T(8,128)(2,1)S(1)} %shard_map.67.refs_1_, bf16[128,256]{1,0:T(8,128)(2,1)S(1)} %collective-permute-done.11.refs_2_, ...), custom_call_target="tpu_custom_call" | custom-call | tf_op jit(solution)/shard_map/pallas_call | solution.py:281
  36.2 2.6 %collective-permute-start.22 = (s16[256,256]{1,0:T(8,128)(2,1)S(1)}, s16[256,256]{1,0:T(8,128)(2,1)S(1)}, u32[]{:S(2)}, u32[]{:S(2)}) collective-permute-start(s16[256,256]{1,0:T(8,128)(2,1)S(1)} %shard_map.74), channel_id=1, source_target_pairs={{0,3},{1,2},{2,1},{3,0},{4,7},{5,6},{6,5},{7,4},{8,11},{9,10},{10,... | collective-permute-start | bytes 393224 | tf_op jit(solution)/shard_map/ppermute | solution.py:216
  38.8 0.3 shard_map.76
  39.1 0.8 %collective-permute-start.23 = (s16[256,256]{1,0:T(8,128)(2,1)S(1)}, s16[256,256]{1,0:T(8,128)(2,1)S(1)}, u32[]{:S(2)}, u32[]{:S(2)}) collective-permute-start(s16[256,256]{1,0:T(8,128)(2,1)S(1)} %shard_map.76), channel_id=1, source_target_pairs={{0,2},{1,3},{2,0},{3,1},{4,6},{5,7},{6,4},{7,5},{8,10},{9,11},{10,... | collective-permute-start | bytes 393224 | tf_op jit(solution)/shard_map/ppermute | solution.py:216
  39.9 0.3 shard_map.78
  40.8 2.0 %collective-permute-done.22.got = s16[256,256]{1,0:T(8,128)(2,1)S(1)} collective-permute-done((s16[256,256]{1,0:T(8,128)(2,1)S(1)}, s16[256,256]{1,0:T(8,128)(2,1)S(1)}, u32[]{:S(2)}, u32[]{:S(2)}) %collective-permute-start.22) | collective-permute-done | bytes 131104 | tf_op jit(solution)/shard_map/ppermute | solution.py:216
  42.8 2.7 %collective-permute-done.23.got = s16[256,256]{1,0:T(8,128)(2,1)S(1)} collective-permute-done((s16[256,256]{1,0:T(8,128)(2,1)S(1)}, s16[256,256]{1,0:T(8,128)(2,1)S(1)}, u32[]{:S(2)}, u32[]{:S(2)}) %collective-permute-start.23) | collective-permute-done | bytes 131104 | tf_op jit(solution)/shard_map/ppermute | solution.py:216
  45.8 0.7 %shard_map.79 = f32[256,256]{1,0:T(8,128)} custom-call(f32[256,256]{1,0:T(8,128)S(1)} %shard_map.77.total, s16[256,256]{1,0:T(8,128)(2,1)S(1)} %collective-permute-done.24.got), custom_call_target="tpu_custom_call" | custom-call | bytes 16777216 | tf_op jit(solution)/shard_map/pallas_call | solution.py:303
  (43 shorter events, 2.7 us)
Async XLA Ops:
  5.5 5.1 %collective-permute-start.1 = (s16[128,1536]{1,0:T(8,128)(2,1)S(1)}, s16[128,1536]{1,0:T(8,128)(2,1)S(1)}, u32[]{:S(2)}, u32[]{:S(2)}) collective-permute-start(s16[128,1536]{1,0:T(8,128)(2,1)S(1)} %shard_map.59), channel_id=1, source_target_pairs={{0,4},{4,0},{8,12},{12,8},{16,20},{20,16},{24,28},{28,24},{1,5},{5... | collective-permute-start | bytes 1179656 | tf_op jit(solution)/shard_map/ppermute | solution.py:210
  5.6 1.9 %collective-permute-start = (s16[128,512]{1,0:T(8,128)(2,1)S(1)}, s16[128,512]{1,0:T(8,128)(2,1)S(1)}, u32[]{:S(2)}, u32[]{:S(2)}) collective-permute-start(s16[128,512]{1,0:T(8,128)(2,1)S(1)} %get-tuple-element.29), channel_id=1, source_target_pairs={{0,4},{4,0},{8,12},{12,8},{16,20},{20,16},{24,28},{28,24},{1,5},{5... | collective-permute-start | bytes 393224 | tf_op jit(solution)/shard_map/ppermute | solution.py:210
  7.5 5.5 %collective-permute-start.5 = (s16[128,256]{1,0:T(8,128)(2,1)S(1)}, s16[128,256]{1,0:T(8,128)(2,1)S(1)}, u32[]{:S(2)}, u32[]{:S(2)}) collective-permute-start(s16[128,256]{1,0:T(8,128)(2,1)S(1)} %get-tuple-element.31), channel_id=1, source_target_pairs={{0,8},{4,12},{8,0},{12,4},{16,24},{20,28},{24,16},{28,20},{1,9},{5... | collective-permute-start | bytes 196616 | tf_op jit(solution)/shard_map/ppermute | solution.py:213
  10.8 5.0 %collective-permute-start.4 = (s16[128,256]{1,0:T(8,128)(2,1)S(1)}, s16[128,256]{1,0:T(8,128)(2,1)S(1)}, u32[]{:S(2)}, u32[]{:S(2)}) collective-permute-start(s16[128,256]{1,0:T(8,128)(2,1)S(1)} %get-tuple-element.39), channel_id=1, source_target_pairs={{0,8},{4,12},{8,0},{12,4},{16,24},{20,28},{24,16},{28,20},{1,9},{5... | collective-permute-start | bytes 196616 | tf_op jit(solution)/shard_map/ppermute | solution.py:213
  10.9 7.5 %collective-permute-start.3 = (s16[128,256]{1,0:T(8,128)(2,1)S(1)}, s16[128,256]{1,0:T(8,128)(2,1)S(1)}, u32[]{:S(2)}, u32[]{:S(2)}) collective-permute-start(s16[128,256]{1,0:T(8,128)(2,1)S(1)} %get-tuple-element.37), channel_id=1, source_target_pairs={{0,8},{4,12},{8,0},{12,4},{16,24},{20,28},{24,16},{28,20},{1,9},{5... | collective-permute-start | bytes 196616 | tf_op jit(solution)/shard_map/ppermute | solution.py:213
  12.9 6.9 %collective-permute-start.2 = (s16[128,256]{1,0:T(8,128)(2,1)S(1)}, s16[128,256]{1,0:T(8,128)(2,1)S(1)}, u32[]{:S(2)}, u32[]{:S(2)}) collective-permute-start(s16[128,256]{1,0:T(8,128)(2,1)S(1)} %get-tuple-element.35), channel_id=1, source_target_pairs={{0,8},{4,12},{8,0},{12,4},{16,24},{20,28},{24,16},{28,20},{1,9},{5... | collective-permute-start | bytes 196616 | tf_op jit(solution)/shard_map/ppermute | solution.py:213
  13.1 8.5 %collective-permute-start.9 = (s16[128,256]{1,0:T(8,128)(2,1)S(1)}, s16[128,256]{1,0:T(8,128)(2,1)S(1)}, u32[]{:S(2)}, u32[]{:S(2)}) collective-permute-start(s16[128,256]{1,0:T(8,128)(2,1)S(1)} %shard_map.61.code), channel_id=1, source_target_pairs={{0,16},{4,20},{8,24},{12,28},{16,0},{20,4},{24,8},{28,12},{1,17},{... | collective-permute-start | bytes 196616 | tf_op jit(solution)/shard_map/ppermute | solution.py:213
  15.9 10.6 %collective-permute-start.8 = (s16[128,256]{1,0:T(8,128)(2,1)S(1)}, s16[128,256]{1,0:T(8,128)(2,1)S(1)}, u32[]{:S(2)}, u32[]{:S(2)}) collective-permute-start(s16[128,256]{1,0:T(8,128)(2,1)S(1)} %shard_map.62.code), channel_id=1, source_target_pairs={{0,16},{4,20},{8,24},{12,28},{16,0},{20,4},{24,8},{28,12},{1,17},{... | collective-permute-start | bytes 196616 | tf_op jit(solution)/shard_map/ppermute | solution.py:213
  18.5 9.1 %collective-permute-start.7 = (s16[128,256]{1,0:T(8,128)(2,1)S(1)}, s16[128,256]{1,0:T(8,128)(2,1)S(1)}, u32[]{:S(2)}, u32[]{:S(2)}) collective-permute-start(s16[128,256]{1,0:T(8,128)(2,1)S(1)} %shard_map.63.code), channel_id=1, source_target_pairs={{0,16},{4,20},{8,24},{12,28},{16,0},{20,4},{24,8},{28,12},{1,17},{... | collective-permute-start | bytes 196616 | tf_op jit(solution)/shard_map/ppermute | solution.py:213
  19.9 8.9 %collective-permute-start.6 = (s16[128,256]{1,0:T(8,128)(2,1)S(1)}, s16[128,256]{1,0:T(8,128)(2,1)S(1)}, u32[]{:S(2)}, u32[]{:S(2)}) collective-permute-start(s16[128,256]{1,0:T(8,128)(2,1)S(1)} %shard_map.64.code), channel_id=1, source_target_pairs={{0,16},{4,20},{8,24},{12,28},{16,0},{20,4},{24,8},{28,12},{1,17},{... | collective-permute-start | bytes 196616 | tf_op jit(solution)/shard_map/ppermute | solution.py:213
  21.7 8.1 %collective-permute-start.13 = (bf16[128,256]{1,0:T(8,128)(2,1)S(1)}, bf16[128,256]{1,0:T(8,128)(2,1)S(1)}, u32[]{:S(2)}, u32[]{:S(2)}) collective-permute-start(bf16[128,256]{1,0:T(8,128)(2,1)S(1)} %shard_map.65.refs_0_), channel_id=1, source_target_pairs={{0,8},{4,12},{8,0},{12,4},{16,24},{20,28},{24,16},{28,20},{1,9},{5... | collective-permute-start | bytes 196616 | tf_op jit(solution)/shard_map/ppermute | solution.py:213
  26.6 4.7 %collective-permute-start.12 = (bf16[128,256]{1,0:T(8,128)(2,1)S(1)}, bf16[128,256]{1,0:T(8,128)(2,1)S(1)}, u32[]{:S(2)}, u32[]{:S(2)}) collective-permute-start(bf16[128,256]{1,0:T(8,128)(2,1)S(1)} %shard_map.66.refs_1_), channel_id=1, source_target_pairs={{0,8},{4,12},{8,0},{12,4},{16,24},{20,28},{24,16},{28,20},{1,9},{5... | collective-permute-start | bytes 196616 | tf_op jit(solution)/shard_map/ppermute | solution.py:213
  27.6 4.4 %collective-permute-start.11 = (bf16[128,256]{1,0:T(8,128)(2,1)S(1)}, bf16[128,256]{1,0:T(8,128)(2,1)S(1)}, u32[]{:S(2)}, u32[]{:S(2)}) collective-permute-start(bf16[128,256]{1,0:T(8,128)(2,1)S(1)} %shard_map.67.refs_1_), channel_id=1, source_target_pairs={{0,8},{4,12},{8,0},{12,4},{16,24},{20,28},{24,16},{28,20},{1,9},{5... | collective-permute-start | bytes 196616 | tf_op jit(solution)/shard_map/ppermute | solution.py:213
  28.9 4.3 %collective-permute-start.10 = (bf16[128,256]{1,0:T(8,128)(2,1)S(1)}, bf16[128,256]{1,0:T(8,128)(2,1)S(1)}, u32[]{:S(2)}, u32[]{:S(2)}) collective-permute-start(bf16[128,256]{1,0:T(8,128)(2,1)S(1)} %shard_map.68.refs_0_), channel_id=1, source_target_pairs={{0,8},{4,12},{8,0},{12,4},{16,24},{20,28},{24,16},{28,20},{1,9},{5... | collective-permute-start | bytes 196616 | tf_op jit(solution)/shard_map/ppermute | solution.py:213
  29.8 3.4 %collective-permute-start.16 = (bf16[128,256]{1,0:T(8,128)(2,1)S(1)}, bf16[128,256]{1,0:T(8,128)(2,1)S(1)}, u32[]{:S(2)}, u32[]{:S(2)}) collective-permute-start(bf16[128,256]{1,0:T(8,128)(2,1)S(1)} %shard_map.65.refs_0_), channel_id=1, source_target_pairs={{0,4},{4,0},{8,12},{12,8},{16,20},{20,16},{24,28},{28,24},{1,5},{5... | collective-permute-start | bytes 196616 | tf_op jit(solution)/shard_map/ppermute | solution.py:210
  29.8 3.9 %collective-permute-start.17 = (bf16[128,256]{1,0:T(8,128)(2,1)S(1)}, bf16[128,256]{1,0:T(8,128)(2,1)S(1)}, u32[]{:S(2)}, u32[]{:S(2)}) collective-permute-start(bf16[128,256]{1,0:T(8,128)(2,1)S(1)} %collective-permute-done.13.refs_1_), channel_id=1, source_target_pairs={{0,4},{4,0},{8,12},{12,8},{16,20},{20,16},{24,28},{28,24},{1,5},{5... | collective-permute-start | bytes 196616 | tf_op jit(solution)/shard_map/ppermute | solution.py:210
  31.3 2.5 %collective-permute-start.14 = (bf16[128,256]{1,0:T(8,128)(2,1)S(1)}, bf16[128,256]{1,0:T(8,128)(2,1)S(1)}, u32[]{:S(2)}, u32[]{:S(2)}) collective-permute-start(bf16[128,256]{1,0:T(8,128)(2,1)S(1)} %shard_map.68.refs_0_), channel_id=1, source_target_pairs={{0,4},{4,0},{8,12},{12,8},{16,20},{20,16},{24,28},{28,24},{1,5},{5... | collective-permute-start | bytes 196616 | tf_op jit(solution)/shard_map/ppermute | solution.py:210
  32.0 2.8 %collective-permute-start.18 = (bf16[128,256]{1,0:T(8,128)(2,1)S(1)}, bf16[128,256]{1,0:T(8,128)(2,1)S(1)}, u32[]{:S(2)}, u32[]{:S(2)}) collective-permute-start(bf16[128,256]{1,0:T(8,128)(2,1)S(1)} %shard_map.66.refs_1_), channel_id=1, source_target_pairs={{0,4},{4,0},{8,12},{12,8},{16,20},{20,16},{24,28},{28,24},{1,5},{5... | collective-permute-start | bytes 196616 | tf_op jit(solution)/shard_map/ppermute | solution.py:210
  33.2 1.5 %collective-permute-start.15 = (bf16[128,256]{1,0:T(8,128)(2,1)S(1)}, bf16[128,256]{1,0:T(8,128)(2,1)S(1)}, u32[]{:S(2)}, u32[]{:S(2)}) collective-permute-start(bf16[128,256]{1,0:T(8,128)(2,1)S(1)} %collective-permute-done.10.refs_1_), channel_id=1, source_target_pairs={{0,4},{4,0},{8,12},{12,8},{16,20},{20,16},{24,28},{28,24},{1,5},{5... | collective-permute-start | bytes 196616 | tf_op jit(solution)/shard_map/ppermute | solution.py:210
  33.2 1.6 %collective-permute-start.19 = (bf16[128,256]{1,0:T(8,128)(2,1)S(1)}, bf16[128,256]{1,0:T(8,128)(2,1)S(1)}, u32[]{:S(2)}, u32[]{:S(2)}) collective-permute-start(bf16[128,256]{1,0:T(8,128)(2,1)S(1)} %collective-permute-done.12.refs_2_), channel_id=1, source_target_pairs={{0,4},{4,0},{8,12},{12,8},{16,20},{20,16},{24,28},{28,24},{1,5},{5... | collective-permute-start | bytes 196616 | tf_op jit(solution)/shard_map/ppermute | solution.py:210
  33.7 1.6 %collective-permute-start.20 = (bf16[128,256]{1,0:T(8,128)(2,1)S(1)}, bf16[128,256]{1,0:T(8,128)(2,1)S(1)}, u32[]{:S(2)}, u32[]{:S(2)}) collective-permute-start(bf16[128,256]{1,0:T(8,128)(2,1)S(1)} %shard_map.67.refs_1_), channel_id=1, source_target_pairs={{0,4},{4,0},{8,12},{12,8},{16,20},{20,16},{24,28},{28,24},{1,5},{5... | collective-permute-start | bytes 196616 | tf_op jit(solution)/shard_map/ppermute | solution.py:210
  33.8 1.5 %collective-permute-start.21 = (bf16[128,256]{1,0:T(8,128)(2,1)S(1)}, bf16[128,256]{1,0:T(8,128)(2,1)S(1)}, u32[]{:S(2)}, u32[]{:S(2)}) collective-permute-start(bf16[128,256]{1,0:T(8,128)(2,1)S(1)} %collective-permute-done.11.refs_2_), channel_id=1, source_target_pairs={{0,4},{4,0},{8,12},{12,8},{16,20},{20,16},{24,28},{28,24},{1,5},{5... | collective-permute-start | bytes 196616 | tf_op jit(solution)/shard_map/ppermute | solution.py:210
  36.2 6.6 %collective-permute-start.22 = (s16[256,256]{1,0:T(8,128)(2,1)S(1)}, s16[256,256]{1,0:T(8,128)(2,1)S(1)}, u32[]{:S(2)}, u32[]{:S(2)}) collective-permute-start(s16[256,256]{1,0:T(8,128)(2,1)S(1)} %shard_map.74), channel_id=1, source_target_pairs={{0,3},{1,2},{2,1},{3,0},{4,7},{5,6},{6,5},{7,4},{8,11},{9,10},{10,... | collective-permute-start | bytes 393224 | tf_op jit(solution)/shard_map/ppermute | solution.py:216
  39.1 6.4 %collective-permute-start.23 = (s16[256,256]{1,0:T(8,128)(2,1)S(1)}, s16[256,256]{1,0:T(8,128)(2,1)S(1)}, u32[]{:S(2)}, u32[]{:S(2)}) collective-permute-start(s16[256,256]{1,0:T(8,128)(2,1)S(1)} %shard_map.76), channel_id=1, source_target_pairs={{0,2},{1,3},{2,0},{3,1},{4,6},{5,7},{6,4},{7,5},{8,10},{9,11},{10,... | collective-permute-start | bytes 393224 | tf_op jit(solution)/shard_map/ppermute | solution.py:216
  40.2 5.6 %collective-permute-start.24 = (s16[256,256]{1,0:T(8,128)(2,1)S(1)}, s16[256,256]{1,0:T(8,128)(2,1)S(1)}, u32[]{:S(2)}, u32[]{:S(2)}) collective-permute-start(s16[256,256]{1,0:T(8,128)(2,1)S(1)} %shard_map.78), channel_id=1, source_target_pairs={{0,1},{1,0},{2,3},{3,2},{4,5},{5,4},{6,7},{7,6},{8,9},{9,8},{10,11... | collective-permute-start | bytes 393224 | tf_op jit(solution)/shard_map/ppermute | solution.py:216

commit v7 on v6

--- a/solution.py
+++ b/solution.py
@@ -63,9 +63,9 @@
     return pl.ds(pl.multiple_of(index * size, size), size)
 
 
-def dense_kernel(count, rows, cols, sketch, tiles, dense, turned, theirs, place, sketch_here, load_sems, sems):
+def dense_kernel(count, rows, cols, sketch, tiles, dense, turned, *refs):
+    *outs, place, sketch_here, load_sems, sems = refs
     tile = tiles.shape[1]
-    core, _ = core_and_chip()
     rows_place, cols_place = place
     loads = [
         pltpu.make_async_copy(src, dst, load_sems.at[i])
@@ -98,7 +98,10 @@
     loads[2].wait()
     turned[...] = sketch_here[...].T
     lax.fori_loop(0, count[0], wait, 0)
-    half_kernel(1, 0, turned, dense, theirs)
+    start = 0
+    for out in outs:
+        half_kernel(1, start, turned, dense, out)
+        start += out.shape[1]
 
 
 def half_kernel(other, start, turned, dense, out):
@@ -135,6 +138,29 @@
         start += out.shape[1]
 
 
+def both_kernel(mine, got, *outs):
+    start = 0
+    for keep, send in zip(outs[::2], outs[1::2]):
+        cut = slice(start, start + keep.shape[1])
+        total = mine[:, cut] + decode(got[:, cut])
+        keep[...] = total
+        encode(total, send)
+        start += keep.shape[1]
+
+
+def pick_kernel(cast, got, out):
+    _, chip = core_and_chip()
+    middle = (chip == 1) | (chip == 2)
+
+    @pl.when(middle)
+    def _():
+        out[...] = cast[...]
+
+    @pl.when(jnp.logical_not(middle))
+    def _():
+        out[...] = got[...]
+
+
 def cast_kernel(code, got, out):
     out[...] = (decode(code[...]) + decode(got[...])).astype(bf16)
 
@@ -204,6 +230,8 @@
     rows = rank // CORES
     height = cells // n_genes
     shape = jax.ShapeDtypeStruct
+    chips = n_cells // CORES
+    hub = chips == 4
     cuts = cuts_of(genes, bits)
 
     def to_core(x):
@@ -215,9 +243,12 @@
     def to_gene(x, k):
         return lax.ppermute(x, "genes", [(i, i ^ k) for i in range(n_genes)])
 
-    dense, turned, theirs = call(
+    widths = [width for _, width in cuts]
+    first, rest = widths[0], genes - widths[0]
+    dense, turned, *theirs = call(
         dense_kernel,
-        (shape((cells, genes), bf16), shape((rank, cells), bf16), shape((rows, cuts[0][1]), i16)),
+        (shape((cells, genes), bf16), shape((rank, cells), bf16))
+        + tuple(shape((rows, width), i16) for width in (first, rest) if width),
         [SMEM] + [HBM] * 4,
         scratch=[
             (pltpu.SMEM((slots,), i32), pltpu.SMEM((slots,), i32)),
@@ -225,7 +256,6 @@
             pltpu.SemaphoreType.DMA((3,)),
             pltpu.SemaphoreType.DMA((slots,)),
         ],
-
     )(tile_counts, *(pltpu.with_memory_space_constraint(x, pltpu.HBM) for x in (tile_rows, tile_cols, sketch, tiles)))
 
     def half_of(other, start, turned, width):
@@ -236,6 +266,10 @@
         return lax.optimization_barrier((x, *others))[0]
 
     def add_step(bit, kept, came, widths):
+        if hub and bit == 0:
+            outs = [shape((rows, width), kind) for width in widths for kind in (f32, i16)]
+            done = call(both_kernel, tuple(outs), [VMEM, VMEM])(kept, came)
+            return [done[i : i + 2] for i in range(0, len(done), 2)]
         if bit < bits - 1:
             outs = [shape((rows, width // 2), kind) for width in widths for kind in (f32, i16)]
             done = call(functools.partial(add_kernel, bit), tuple(outs), [VMEM, VMEM])(kept, came)
@@ -243,49 +277,76 @@
         done = call(code_kernel, tuple(shape((rows, width), i16) for width in widths), [VMEM, VMEM])(kept, came)
         return [done[i : i + 1] for i in range(len(done))]
 
-    widths = [width for _, width in cuts]
-    first, rest = widths[0], genes - widths[0]
-    got = to_core(theirs)
-    mine = half_of(0, 0, turned, first)
+    def through_hubs(sums):
+        def move(x, pairs):
+            return lax.ppermute(x, "cells", [(a * CORES + i, b * CORES + i) for a, b in pairs for i in range(CORES)])
+
+        came = [move(code, ((0, 1), (3, 2))) for _, code in sums]
+        codes = []
+        for (kept, _), x in zip(sums, came):
+            x = after(x, codes[-1]) if codes else x
+            codes += call(code_kernel, (shape(x.shape, i16),), [VMEM, VMEM])(kept, x)
+        came = [move(code, ((1, 2), (2, 1))) for code in codes]
+        casts = []
+        for code, x in zip(codes, came):
+            x = after(x, casts[-1]) if casts else x
+            casts.append(call(cast_kernel, shape(x.shape, bf16), [VMEM, VMEM])(code, x))
+        came = [move(x, ((1, 0), (2, 3))) for x in casts]
+        return [(casts[0], came[0])] + [(cast, after(x, casts[-1])) for cast, x in zip(casts[1:], came[1:])]
+
+    def by_halving(sums):
+        widths = [sum_[0].shape[1] for sum_ in sums]
+        for bit in range(bits - 1):
+            came = [to_chip(code, bit) for _, code in sums]
+            done = []
+            for (kept, _), x, width in zip(sums, came, widths):
+                done += add_step(bit + 1, kept, after(x, *done[-1]) if done else x, [width])
+            sums = done
+            widths = [width // 2 for width in widths]
+        held = []
+        for (code,) in sums:
+            came = to_chip(code, bits - 1)
+            came = after(came, *held[-1]) if held else came
+            held.append([call(cast_kernel, shape(code.shape, bf16), [VMEM, VMEM])(code, came)])
+        masks = [0]
+        for bit in reversed(range(bits - 1)):
+            before = None
+            for pieces in held:
+                came = [to_chip(x, bit) for x in pieces]
+                if before is not None:
+                    came = [after(x, before) for x in came]
+                pieces += came
+                before = came[-1]
+            masks += [mask ^ (1 << bit) for mask in masks]
+        return masks, held
+
+    got = [to_core(x) for x in theirs]
+    sums = add_step(0, half_of(0, 0, turned, first), got[0], widths[:1])
     if rest:
-        got_rest = to_core(half_of(1, first, after(turned, mine), rest))
-    sums = add_step(0, mine, got, widths[:1])
-    if rest:
-        sums += add_step(0, half_of(0, first, after(turned, *sums[0]), rest), got_rest, widths[1:])
-    for bit in range(bits - 1):
-        widths = [width // 2 for width in widths]
-        came = [to_chip(code, bit) for _, code in sums]
-        done = []
-        for (kept, _), x, width in zip(sums, came, widths):
-            done += add_step(bit + 1, kept, after(x, *done[-1]) if done else x, [width])
-        sums = done
-    held = []
-    for (code,) in sums:
-        came = to_chip(code, bits - 1)
-        came = after(came, *held[-1]) if held else came
-        held.append([call(cast_kernel, shape(code.shape, bf16), [VMEM, VMEM])(code, came)])
-    masks = [0]
-    for bit in reversed(range(bits - 1)):
-        before = None
-        for pieces in held:
-            came = [to_chip(x, bit) for x in pieces]
-            if before is not None:
-                came = [after(x, before) for x in came]
-            pieces += came
-            before = came[-1]
-        masks += [mask ^ (1 << bit) for mask in masks]
-    sides = [pieces + [to_core(x) for x in pieces] for pieces in held]
-    total = ()
-    for (start, width), pieces in zip(cuts[:-1], sides):
-        total = (
+        sums += add_step(0, half_of(0, first, after(turned, *sums[0]), rest), got[1], widths[1:])
+    if hub:
+        sides = through_hubs(sums)
+        masks = [0]
+    else:
+        masks, sides = by_halving(sums)
+    totals = []
+    for i, ((start, width), pieces) in enumerate(zip(cuts, sides)):
+        if i >= 2:
+            pieces = [after(x, totals[i - 2]) for x in pieces]
+        if hub:
+            pieces = [call(pick_kernel, shape(pieces[0].shape, bf16), [VMEM, VMEM])(*pieces)]
+        pieces = pieces + [to_core(x) for x in pieces]
+        if i == len(cuts) - 1:
+            break
+        before = totals[-1:]
+        totals.append(
             call(
-                functools.partial(part_kernel, masks, start, not total),
+                functools.partial(part_kernel, masks, start, not before),
                 shape((cells, rank), f32),
-                [VMEM] * (1 + len(total) + len(pieces)),
+                [VMEM] * (1 + len(before) + len(pieces)),
                 scratch=[pltpu.VMEM((rank, width), bf16)],
-            )(dense, *total, *pieces),
+            )(dense, *before, *pieces)
         )
-    (start, width), pieces = cuts[-1], sides[-1]
     gene = call(
         functools.partial(gene_kernel, masks), shape((rank, width), bf16), [VMEM] * len(pieces)
     )(*pieces)
@@ -294,8 +355,8 @@
         return call(
             functools.partial(cell_kernel, k, start),
             shape((height, rank), f32 if k == 0 else i16),
-            [VMEM] * (2 + len(total)),
-        )(dense, gene, *total)
+            [VMEM] * (2 + len(totals[-1:])),
+        )(dense, gene, *totals[-1:])
 
     came = [to_gene(cell(k), k) for k in reversed(range(1, n_genes))]
     out = cell(0)

time: 46.9 us -> 58.1 us (1.24)
  waiting for transfers between devices: 12.8 us -> 20.5 us
  starting transfers between devices: 23.2 us -> 26.3 us
    ppermute x12, waiting for transfers between devices: 6.4 us -> 13.6 us  [move(): lax.ppermute(x, 'cells', [(a * CORES + i, b * CORES + i) for a, b in pair...]
    ppermute x12, starting transfers between devices: 17.4 us -> 21.7 us  [move(): lax.ppermute(x, 'cells', [(a * CORES + i, b * CORES + i) for a, b in pair...]
    ppermute x10 -> x6, starting transfers between devices: 2.11 us -> 0.85 us  [to_core(): return lax.ppermute(x, 'cells', [(i, i ^ 1) for i in range(n_cells)])]
    pallas_call x3 -> x2, Pallas kernels: 1.53 us -> 0.89 us  [half_of(): call(body, shape((rows, width), i16 if other else f32), [VMEM, VMEM])]
    ppermute x10 -> x6, waiting for transfers between devices: 1.42 us -> 1.92 us  [to_core(): return lax.ppermute(x, 'cells', [(i, i ^ 1) for i in range(n_cells)])]
    pallas_call x13 -> x17, Pallas kernels: 2.25 us -> 2.57 us  [the longest x3 1.47 us: local(): call(functools.partial(part_kernel, masks, start, not before), shape((cel...]
  transfers between devices with their start and end apart: 25 -> 21, of which waited for: 9 -> 9; matrix products, arithmetic and copies ran while one was open for 0% -> 0% of each run, Pallas kernels for 7% -> 8%
where the time goes in v7:
time: 58.1 us; the launch traced here: 57.6 us
  starting transfers between devices  26.3 us (45%)
  waiting for transfers between devices  20.5 us (35%)
  Pallas kernels  9.81 us (17%)
  between operations  1.05 us (2%)
    ppermute x12, starting transfers between devices, move(): lax.ppermute(x, 'cells', [(a * CORES + i, b * CORES + i) for a, b in pair...  21.7 us
    ppermute x12, waiting for transfers between devices, move(): lax.ppermute(x, 'cells', [(a * CORES + i, b * CORES + i) for a, b in pair...  13.6 us
    ppermute x3, waiting for transfers between devices, to_gene(): return lax.ppermute(x, 'genes', [(i, i ^ k) for i in range(n_genes)])  4.95 us
    pallas_call x1, Pallas kernels, local(): call(dense_kernel, (shape((cells, genes), bf16), shape((rank, cells), bf1...  4.28 us
    ppermute x3, starting transfers between devices, to_gene(): return lax.ppermute(x, 'genes', [(i, i ^ k) for i in range(n_genes)])  3.71 us
    ppermute x6, waiting for transfers between devices, to_core(): return lax.ppermute(x, 'cells', [(i, i ^ 1) for i in range(n_cells)])  1.92 us
    pallas_call x3, Pallas kernels, local(): call(functools.partial(part_kernel, masks, start, not before), shape((cel...  1.47 us
    pallas_call x4, Pallas kernels, cell(): call(functools.partial(cell_kernel, k, start), shape((height, rank), f32...  1.2 us
  transfers between devices with their start and end apart: 21, of which 9 were waited for; matrix products, arithmetic and copies ran while one was open for 0% of the time, Pallas kernels for 8%

profile of v7, /device:TPU:0, one launch (start us, length us, event | category | flops | bytes accessed | tf_op | source)
XLA Modules:
  0.0 57.6 jit_solution(1738961952240979091)
XLA Ops:
  0.7 4.3 %shard_map.55 = (bf16[1024,2048]{1,0:T(8,128)(2,1)S(1)}, bf16[256,1024]{1,0:T(8,128)(2,1)S(1)}, s16[128,512]{1,0:T(8,128)(2,1)S(1)}, s16[128,1536]{1,0:T(8,128)(2,1)S(1)}) custom-call(s32[1]{0:T(128)S(6)} %copy.6.count, s32[96]{0:T(128)} %rows.1, s32[96]{0:T(128)} %cols.1, bf16[1024,256]{1,0:T(8,128)(2,1)} %sketch.1, bf16[96,128,128]{2,1,0:T(8,128)(2,1)} %tiles.1), custom_call_target="tpu_custom_call" | custom-call | tf_op jit(solution)/shard_map/pallas_call | solution.py:248
  5.0 0.5 collective-permute-start
  5.8 1.1 %collective-permute-done.got = s16[128,512]{1,0:T(8,128)(2,1)S(1)} collective-permute-done((s16[128,512]{1,0:T(8,128)(2,1)S(1)}, s16[128,512]{1,0:T(8,128)(2,1)S(1)}, u32[]{:S(2)}, u32[]{:S(2)}) %collective-permute-start) | collective-permute-done | bytes 131104 | tf_op jit(solution)/shard_map/ppermute | solution.py:238
  7.0 4.5 %collective-permute-start.5 = (s16[128,512]{1,0:T(8,128)(2,1)S(1)}, s16[128,512]{1,0:T(8,128)(2,1)S(1)}, u32[]{:S(2)}, u32[]{:S(2)}) collective-permute-start(s16[128,512]{1,0:T(8,128)(2,1)S(1)} %get-tuple-element.35), channel_id=1, source_target_pairs={{0,8},{4,12},{24,16},{28,20},{1,9},{5,13},{25,17},{29,21},{2,10},{... | collective-permute-start | bytes 393224 | tf_op jit(solution)/shard_map/ppermute | solution.py:282
  11.6 0.6 %shard_map.58.mine = f32[128,1536]{1,0:T(8,128)S(1)} custom-call(bf16[256,1024]{1,0:T(8,128)(2,1)S(1)} %get-tuple-element.36.turned, bf16[1024,2048]{1,0:T(8,128)(2,1)S(1)} %get-tuple-element.31.dense), custom_call_target="tpu_custom_call" | custom-call | tf_op jit(solution)/shard_map/pallas_call | solution.py:263
  12.4 1.3 %collective-permute-start.4 = (s16[128,512]{1,0:T(8,128)(2,1)S(1)}, s16[128,512]{1,0:T(8,128)(2,1)S(1)}, u32[]{:S(2)}, u32[]{:S(2)}) collective-permute-start(s16[128,512]{1,0:T(8,128)(2,1)S(1)} %get-tuple-element.43), channel_id=1, source_target_pairs={{0,8},{4,12},{24,16},{28,20},{1,9},{5,13},{25,17},{29,21},{2,10},{... | collective-permute-start | bytes 393224 | tf_op jit(solution)/shard_map/ppermute | solution.py:282
  13.7 1.5 %collective-permute-done.5.got = s16[128,512]{1,0:T(8,128)(2,1)S(1)} collective-permute-done((s16[128,512]{1,0:T(8,128)(2,1)S(1)}, s16[128,512]{1,0:T(8,128)(2,1)S(1)}, u32[]{:S(2)}, u32[]{:S(2)}) %collective-permute-start.5) | collective-permute-done | bytes 131104 | tf_op jit(solution)/shard_map/ppermute | solution.py:282
  15.3 0.7 %collective-permute-start.9 = (s16[128,512]{1,0:T(8,128)(2,1)S(1)}, s16[128,512]{1,0:T(8,128)(2,1)S(1)}, u32[]{:S(2)}, u32[]{:S(2)}) collective-permute-start(s16[128,512]{1,0:T(8,128)(2,1)S(1)} %shard_map.60.code), channel_id=1, source_target_pairs={{8,16},{12,20},{16,8},{20,12},{9,17},{13,21},{17,9},{21,13},{10,18... | collective-permute-start | bytes 393224 | tf_op jit(solution)/shard_map/ppermute | solution.py:282
  16.0 6.7 %collective-permute-start.3 = (s16[128,512]{1,0:T(8,128)(2,1)S(1)}, s16[128,512]{1,0:T(8,128)(2,1)S(1)}, u32[]{:S(2)}, u32[]{:S(2)}) collective-permute-start(s16[128,512]{1,0:T(8,128)(2,1)S(1)} %get-tuple-element.41), channel_id=1, source_target_pairs={{0,8},{4,12},{24,16},{28,20},{1,9},{5,13},{25,17},{29,21},{2,10},{... | collective-permute-start | bytes 393224 | tf_op jit(solution)/shard_map/ppermute | solution.py:282
  22.7 1.3 %collective-permute-start.2 = (s16[128,512]{1,0:T(8,128)(2,1)S(1)}, s16[128,512]{1,0:T(8,128)(2,1)S(1)}, u32[]{:S(2)}, u32[]{:S(2)}) collective-permute-start(s16[128,512]{1,0:T(8,128)(2,1)S(1)} %get-tuple-element.39), channel_id=1, source_target_pairs={{0,8},{4,12},{24,16},{28,20},{1,9},{5,13},{25,17},{29,21},{2,10},{... | collective-permute-start | bytes 393224 | tf_op jit(solution)/shard_map/ppermute | solution.py:282
  24.1 0.7 %collective-permute-start.8 = (s16[128,512]{1,0:T(8,128)(2,1)S(1)}, s16[128,512]{1,0:T(8,128)(2,1)S(1)}, u32[]{:S(2)}, u32[]{:S(2)}) collective-permute-start(s16[128,512]{1,0:T(8,128)(2,1)S(1)} %shard_map.61.code), channel_id=1, source_target_pairs={{8,16},{12,20},{16,8},{20,12},{9,17},{13,21},{17,9},{21,13},{10,18... | collective-permute-start | bytes 393224 | tf_op jit(solution)/shard_map/ppermute | solution.py:282
  24.9 1.3 %collective-permute-start.10 = (bf16[128,512]{1,0:T(8,128)(2,1)S(1)}, bf16[128,512]{1,0:T(8,128)(2,1)S(1)}, u32[]{:S(2)}, u32[]{:S(2)}) collective-permute-start(bf16[128,512]{1,0:T(8,128)(2,1)S(1)} %shard_map.64.cast), channel_id=1, source_target_pairs={{8,0},{12,4},{16,24},{20,28},{9,1},{13,5},{17,25},{21,29},{10,2},{... | collective-permute-start | bytes 393224 | tf_op jit(solution)/shard_map/ppermute | solution.py:282
  26.3 0.7 %collective-permute-start.7 = (s16[128,512]{1,0:T(8,128)(2,1)S(1)}, s16[128,512]{1,0:T(8,128)(2,1)S(1)}, u32[]{:S(2)}, u32[]{:S(2)}) collective-permute-start(s16[128,512]{1,0:T(8,128)(2,1)S(1)} %shard_map.62.code), channel_id=1, source_target_pairs={{8,16},{12,20},{16,8},{20,12},{9,17},{13,21},{17,9},{21,13},{10,18... | collective-permute-start | bytes 393224 | tf_op jit(solution)/shard_map/ppermute | solution.py:282
  27.1 0.7 %collective-permute-start.6 = (s16[128,512]{1,0:T(8,128)(2,1)S(1)}, s16[128,512]{1,0:T(8,128)(2,1)S(1)}, u32[]{:S(2)}, u32[]{:S(2)}) collective-permute-start(s16[128,512]{1,0:T(8,128)(2,1)S(1)} %shard_map.63.code), channel_id=1, source_target_pairs={{8,16},{12,20},{16,8},{20,12},{9,17},{13,21},{17,9},{21,13},{10,18... | collective-permute-start | bytes 393224 | tf_op jit(solution)/shard_map/ppermute | solution.py:282
  27.9 1.3 %collective-permute-start.12 = (bf16[128,512]{1,0:T(8,128)(2,1)S(1)}, bf16[128,512]{1,0:T(8,128)(2,1)S(1)}, u32[]{:S(2)}, u32[]{:S(2)}) collective-permute-start(bf16[128,512]{1,0:T(8,128)(2,1)S(1)} %shard_map.65.cast), channel_id=1, source_target_pairs={{8,0},{12,4},{16,24},{20,28},{9,1},{13,5},{17,25},{21,29},{10,2},{... | collective-permute-start | bytes 393224 | tf_op jit(solution)/shard_map/ppermute | solution.py:282
  29.2 2.6 %collective-permute-done.10.got = bf16[128,512]{1,0:T(8,128)(2,1)S(1)} collective-permute-done((bf16[128,512]{1,0:T(8,128)(2,1)S(1)}, bf16[128,512]{1,0:T(8,128)(2,1)S(1)}, u32[]{:S(2)}, u32[]{:S(2)}) %collective-permute-start.10) | collective-permute-done | bytes 131104 | tf_op jit(solution)/shard_map/ppermute | solution.py:282
  32.0 1.3 %collective-permute-start.16 = (bf16[128,512]{1,0:T(8,128)(2,1)S(1)}, bf16[128,512]{1,0:T(8,128)(2,1)S(1)}, u32[]{:S(2)}, u32[]{:S(2)}) collective-permute-start(bf16[128,512]{1,0:T(8,128)(2,1)S(1)} %shard_map.66.cast), channel_id=1, source_target_pairs={{8,0},{12,4},{16,24},{20,28},{9,1},{13,5},{17,25},{21,29},{10,2},{... | collective-permute-start | bytes 393224 | tf_op jit(solution)/shard_map/ppermute | solution.py:282
  33.4 1.3 %collective-permute-start.14 = (bf16[128,512]{1,0:T(8,128)(2,1)S(1)}, bf16[128,512]{1,0:T(8,128)(2,1)S(1)}, u32[]{:S(2)}, u32[]{:S(2)}) collective-permute-start(bf16[128,512]{1,0:T(8,128)(2,1)S(1)} %shard_map.67.cast), channel_id=1, source_target_pairs={{8,0},{12,4},{16,24},{20,28},{9,1},{13,5},{17,25},{21,29},{10,2},{... | collective-permute-start | bytes 393224 | tf_op jit(solution)/shard_map/ppermute | solution.py:282
  34.7 4.6 %collective-permute-done.12.got = bf16[128,512]{1,0:T(8,128)(2,1)S(1)} collective-permute-done((bf16[128,512]{1,0:T(8,128)(2,1)S(1)}, bf16[128,512]{1,0:T(8,128)(2,1)S(1)}, u32[]{:S(2)}, u32[]{:S(2)}) %collective-permute-start.12) | collective-permute-done | bytes 131104 | tf_op jit(solution)/shard_map/ppermute | solution.py:282
  39.4 0.5 shard_map.69.refs_0_
  39.9 2.5 %collective-permute-done.16.got = bf16[128,512]{1,0:T(8,128)(2,1)S(1)} collective-permute-done((bf16[128,512]{1,0:T(8,128)(2,1)S(1)}, bf16[128,512]{1,0:T(8,128)(2,1)S(1)}, u32[]{:S(2)}, u32[]{:S(2)}) %collective-permute-start.16) | collective-permute-done | bytes 131104 | tf_op jit(solution)/shard_map/ppermute | solution.py:282
  42.5 2.4 %collective-permute-done.14.got = bf16[128,512]{1,0:T(8,128)(2,1)S(1)} collective-permute-done((bf16[128,512]{1,0:T(8,128)(2,1)S(1)}, bf16[128,512]{1,0:T(8,128)(2,1)S(1)}, u32[]{:S(2)}, u32[]{:S(2)}) %collective-permute-start.14) | collective-permute-done | bytes 131104 | tf_op jit(solution)/shard_map/ppermute | solution.py:282
  44.9 0.5 shard_map.71.refs_0_
  45.5 0.5 shard_map.75.refs_0_
  46.0 0.8 %collective-permute-done.15.refs_1_ = bf16[128,512]{1,0:T(8,128)(2,1)S(1)} collective-permute-done((bf16[128,512]{1,0:T(8,128)(2,1)S(1)}, bf16[128,512]{1,0:T(8,128)(2,1)S(1)}, u32[]{:S(2)}, u32[]{:S(2)}) %collective-permute-start.15) | collective-permute-done | bytes 131104 | tf_op jit(solution)/shard_map/ppermute | solution.py:238
  46.9 0.3 shard_map.77
  47.2 3.0 %collective-permute-start.18 = (s16[256,256]{1,0:T(8,128)(2,1)S(1)}, s16[256,256]{1,0:T(8,128)(2,1)S(1)}, u32[]{:S(2)}, u32[]{:S(2)}) collective-permute-start(s16[256,256]{1,0:T(8,128)(2,1)S(1)} %shard_map.77), channel_id=1, source_target_pairs={{0,3},{1,2},{2,1},{3,0},{4,7},{5,6},{6,5},{7,4},{8,11},{9,10},{10,... | collective-permute-start | bytes 393224 | tf_op jit(solution)/shard_map/ppermute | solution.py:244
  50.7 0.3 shard_map.81
  51.1 0.5 collective-permute-start.20
  51.8 2.3 %collective-permute-done.18.got = s16[256,256]{1,0:T(8,128)(2,1)S(1)} collective-permute-done((s16[256,256]{1,0:T(8,128)(2,1)S(1)}, s16[256,256]{1,0:T(8,128)(2,1)S(1)}, u32[]{:S(2)}, u32[]{:S(2)}) %collective-permute-start.18) | collective-permute-done | bytes 131104 | tf_op jit(solution)/shard_map/ppermute | solution.py:244
  54.1 2.7 %collective-permute-done.19.got = s16[256,256]{1,0:T(8,128)(2,1)S(1)} collective-permute-done((s16[256,256]{1,0:T(8,128)(2,1)S(1)}, s16[256,256]{1,0:T(8,128)(2,1)S(1)}, u32[]{:S(2)}, u32[]{:S(2)}) %collective-permute-start.19) | collective-permute-done | bytes 131104 | tf_op jit(solution)/shard_map/ppermute | solution.py:244
  56.9 0.7 %shard_map.82 = f32[256,256]{1,0:T(8,128)} custom-call(f32[256,256]{1,0:T(8,128)S(1)} %shard_map.80.total, s16[256,256]{1,0:T(8,128)(2,1)S(1)} %collective-permute-done.20.got), custom_call_target="tpu_custom_call" | custom-call | bytes 16777216 | tf_op jit(solution)/shard_map/pallas_call | solution.py:364
  (38 shorter events, 2.7 us)
Async XLA Ops:
  4.9 7.2 %collective-permute-start.1 = (s16[128,1536]{1,0:T(8,128)(2,1)S(1)}, s16[128,1536]{1,0:T(8,128)(2,1)S(1)}, u32[]{:S(2)}, u32[]{:S(2)}) collective-permute-start(s16[128,1536]{1,0:T(8,128)(2,1)S(1)} %get-tuple-element.37), channel_id=1, source_target_pairs={{0,4},{4,0},{8,12},{12,8},{16,20},{20,16},{24,28},{28,24},{1,5},{5... | collective-permute-start | bytes 1179656 | tf_op jit(solution)/shard_map/ppermute | solution.py:238
  5.0 1.9 %collective-permute-start = (s16[128,512]{1,0:T(8,128)(2,1)S(1)}, s16[128,512]{1,0:T(8,128)(2,1)S(1)}, u32[]{:S(2)}, u32[]{:S(2)}) collective-permute-start(s16[128,512]{1,0:T(8,128)(2,1)S(1)} %get-tuple-element.33), channel_id=1, source_target_pairs={{0,4},{4,0},{8,12},{12,8},{16,20},{20,16},{24,28},{28,24},{1,5},{5... | collective-permute-start | bytes 393224 | tf_op jit(solution)/shard_map/ppermute | solution.py:238
  7.0 8.2 %collective-permute-start.5 = (s16[128,512]{1,0:T(8,128)(2,1)S(1)}, s16[128,512]{1,0:T(8,128)(2,1)S(1)}, u32[]{:S(2)}, u32[]{:S(2)}) collective-permute-start(s16[128,512]{1,0:T(8,128)(2,1)S(1)} %get-tuple-element.35), channel_id=1, source_target_pairs={{0,8},{4,12},{24,16},{28,20},{1,9},{5,13},{25,17},{29,21},{2,10},{... | collective-permute-start | bytes 393224 | tf_op jit(solution)/shard_map/ppermute | solution.py:282
  12.4 11.6 %collective-permute-start.4 = (s16[128,512]{1,0:T(8,128)(2,1)S(1)}, s16[128,512]{1,0:T(8,128)(2,1)S(1)}, u32[]{:S(2)}, u32[]{:S(2)}) collective-permute-start(s16[128,512]{1,0:T(8,128)(2,1)S(1)} %get-tuple-element.43), channel_id=1, source_target_pairs={{0,8},{4,12},{24,16},{28,20},{1,9},{5,13},{25,17},{29,21},{2,10},{... | collective-permute-start | bytes 393224 | tf_op jit(solution)/shard_map/ppermute | solution.py:282
  15.3 9.5 %collective-permute-start.9 = (s16[128,512]{1,0:T(8,128)(2,1)S(1)}, s16[128,512]{1,0:T(8,128)(2,1)S(1)}, u32[]{:S(2)}, u32[]{:S(2)}) collective-permute-start(s16[128,512]{1,0:T(8,128)(2,1)S(1)} %shard_map.60.code), channel_id=1, source_target_pairs={{8,16},{12,20},{16,8},{20,12},{9,17},{13,21},{17,9},{21,13},{10,18... | collective-permute-start | bytes 393224 | tf_op jit(solution)/shard_map/ppermute | solution.py:282
  16.0 10.2 %collective-permute-start.3 = (s16[128,512]{1,0:T(8,128)(2,1)S(1)}, s16[128,512]{1,0:T(8,128)(2,1)S(1)}, u32[]{:S(2)}, u32[]{:S(2)}) collective-permute-start(s16[128,512]{1,0:T(8,128)(2,1)S(1)} %get-tuple-element.41), channel_id=1, source_target_pairs={{0,8},{4,12},{24,16},{28,20},{1,9},{5,13},{25,17},{29,21},{2,10},{... | collective-permute-start | bytes 393224 | tf_op jit(solution)/shard_map/ppermute | solution.py:282
  22.7 4.3 %collective-permute-start.2 = (s16[128,512]{1,0:T(8,128)(2,1)S(1)}, s16[128,512]{1,0:T(8,128)(2,1)S(1)}, u32[]{:S(2)}, u32[]{:S(2)}) collective-permute-start(s16[128,512]{1,0:T(8,128)(2,1)S(1)} %get-tuple-element.39), channel_id=1, source_target_pairs={{0,8},{4,12},{24,16},{28,20},{1,9},{5,13},{25,17},{29,21},{2,10},{... | collective-permute-start | bytes 393224 | tf_op jit(solution)/shard_map/ppermute | solution.py:282
  24.1 3.7 %collective-permute-start.8 = (s16[128,512]{1,0:T(8,128)(2,1)S(1)}, s16[128,512]{1,0:T(8,128)(2,1)S(1)}, u32[]{:S(2)}, u32[]{:S(2)}) collective-permute-start(s16[128,512]{1,0:T(8,128)(2,1)S(1)} %shard_map.61.code), channel_id=1, source_target_pairs={{8,16},{12,20},{16,8},{20,12},{9,17},{13,21},{17,9},{21,13},{10,18... | collective-permute-start | bytes 393224 | tf_op jit(solution)/shard_map/ppermute | solution.py:282
  24.9 6.9 %collective-permute-start.10 = (bf16[128,512]{1,0:T(8,128)(2,1)S(1)}, bf16[128,512]{1,0:T(8,128)(2,1)S(1)}, u32[]{:S(2)}, u32[]{:S(2)}) collective-permute-start(bf16[128,512]{1,0:T(8,128)(2,1)S(1)} %shard_map.64.cast), channel_id=1, source_target_pairs={{8,0},{12,4},{16,24},{20,28},{9,1},{13,5},{17,25},{21,29},{10,2},{... | collective-permute-start | bytes 393224 | tf_op jit(solution)/shard_map/ppermute | solution.py:282
  26.3 5.5 %collective-permute-start.7 = (s16[128,512]{1,0:T(8,128)(2,1)S(1)}, s16[128,512]{1,0:T(8,128)(2,1)S(1)}, u32[]{:S(2)}, u32[]{:S(2)}) collective-permute-start(s16[128,512]{1,0:T(8,128)(2,1)S(1)} %shard_map.62.code), channel_id=1, source_target_pairs={{8,16},{12,20},{16,8},{20,12},{9,17},{13,21},{17,9},{21,13},{10,18... | collective-permute-start | bytes 393224 | tf_op jit(solution)/shard_map/ppermute | solution.py:282
  27.1 6.2 %collective-permute-start.6 = (s16[128,512]{1,0:T(8,128)(2,1)S(1)}, s16[128,512]{1,0:T(8,128)(2,1)S(1)}, u32[]{:S(2)}, u32[]{:S(2)}) collective-permute-start(s16[128,512]{1,0:T(8,128)(2,1)S(1)} %shard_map.63.code), channel_id=1, source_target_pairs={{8,16},{12,20},{16,8},{20,12},{9,17},{13,21},{17,9},{21,13},{10,18... | collective-permute-start | bytes 393224 | tf_op jit(solution)/shard_map/ppermute | solution.py:282
  27.9 11.4 %collective-permute-start.12 = (bf16[128,512]{1,0:T(8,128)(2,1)S(1)}, bf16[128,512]{1,0:T(8,128)(2,1)S(1)}, u32[]{:S(2)}, u32[]{:S(2)}) collective-permute-start(bf16[128,512]{1,0:T(8,128)(2,1)S(1)} %shard_map.65.cast), channel_id=1, source_target_pairs={{8,0},{12,4},{16,24},{20,28},{9,1},{13,5},{17,25},{21,29},{10,2},{... | collective-permute-start | bytes 393224 | tf_op jit(solution)/shard_map/ppermute | solution.py:282
  31.8 7.6 %collective-permute-start.11 = (bf16[128,512]{1,0:T(8,128)(2,1)S(1)}, bf16[128,512]{1,0:T(8,128)(2,1)S(1)}, u32[]{:S(2)}, u32[]{:S(2)}) collective-permute-start(bf16[128,512]{1,0:T(8,128)(2,1)S(1)} %shard_map.68.refs_0_), channel_id=1, source_target_pairs={{0,4},{4,0},{8,12},{12,8},{16,20},{20,16},{24,28},{28,24},{1,5},{5... | collective-permute-start | bytes 393224 | tf_op jit(solution)/shard_map/ppermute | solution.py:238
  32.0 10.5 %collective-permute-start.16 = (bf16[128,512]{1,0:T(8,128)(2,1)S(1)}, bf16[128,512]{1,0:T(8,128)(2,1)S(1)}, u32[]{:S(2)}, u32[]{:S(2)}) collective-permute-start(bf16[128,512]{1,0:T(8,128)(2,1)S(1)} %shard_map.66.cast), channel_id=1, source_target_pairs={{8,0},{12,4},{16,24},{20,28},{9,1},{13,5},{17,25},{21,29},{10,2},{... | collective-permute-start | bytes 393224 | tf_op jit(solution)/shard_map/ppermute | solution.py:282
  33.4 11.5 %collective-permute-start.14 = (bf16[128,512]{1,0:T(8,128)(2,1)S(1)}, bf16[128,512]{1,0:T(8,128)(2,1)S(1)}, u32[]{:S(2)}, u32[]{:S(2)}) collective-permute-start(bf16[128,512]{1,0:T(8,128)(2,1)S(1)} %shard_map.67.cast), channel_id=1, source_target_pairs={{8,0},{12,4},{16,24},{20,28},{9,1},{13,5},{17,25},{21,29},{10,2},{... | collective-permute-start | bytes 393224 | tf_op jit(solution)/shard_map/ppermute | solution.py:282
  39.3 5.6 %collective-permute-start.13 = (bf16[128,512]{1,0:T(8,128)(2,1)S(1)}, bf16[128,512]{1,0:T(8,128)(2,1)S(1)}, u32[]{:S(2)}, u32[]{:S(2)}) collective-permute-start(bf16[128,512]{1,0:T(8,128)(2,1)S(1)} %shard_map.70.refs_1_), channel_id=1, source_target_pairs={{0,4},{4,0},{8,12},{12,8},{16,20},{20,16},{24,28},{28,24},{1,5},{5... | collective-permute-start | bytes 393224 | tf_op jit(solution)/shard_map/ppermute | solution.py:238
  42.4 3.1 %collective-permute-start.17 = (bf16[128,512]{1,0:T(8,128)(2,1)S(1)}, bf16[128,512]{1,0:T(8,128)(2,1)S(1)}, u32[]{:S(2)}, u32[]{:S(2)}) collective-permute-start(bf16[128,512]{1,0:T(8,128)(2,1)S(1)} %shard_map.74.refs_1_), channel_id=1, source_target_pairs={{0,4},{4,0},{8,12},{12,8},{16,20},{20,16},{24,28},{28,24},{1,5},{5... | collective-permute-start | bytes 393224 | tf_op jit(solution)/shard_map/ppermute | solution.py:238
  45.4 1.4 %collective-permute-start.15 = (bf16[128,512]{1,0:T(8,128)(2,1)S(1)}, bf16[128,512]{1,0:T(8,128)(2,1)S(1)}, u32[]{:S(2)}, u32[]{:S(2)}) collective-permute-start(bf16[128,512]{1,0:T(8,128)(2,1)S(1)} %shard_map.72.refs_0_), channel_id=1, source_target_pairs={{0,4},{4,0},{8,12},{12,8},{16,20},{20,16},{24,28},{28,24},{1,5},{5... | collective-permute-start | bytes 393224 | tf_op jit(solution)/shard_map/ppermute | solution.py:238
  47.2 6.9 %collective-permute-start.18 = (s16[256,256]{1,0:T(8,128)(2,1)S(1)}, s16[256,256]{1,0:T(8,128)(2,1)S(1)}, u32[]{:S(2)}, u32[]{:S(2)}) collective-permute-start(s16[256,256]{1,0:T(8,128)(2,1)S(1)} %shard_map.77), channel_id=1, source_target_pairs={{0,3},{1,2},{2,1},{3,0},{4,7},{5,6},{6,5},{7,4},{8,11},{9,10},{10,... | collective-permute-start | bytes 393224 | tf_op jit(solution)/shard_map/ppermute | solution.py:244
  50.5 6.3 %collective-permute-start.19 = (s16[256,256]{1,0:T(8,128)(2,1)S(1)}, s16[256,256]{1,0:T(8,128)(2,1)S(1)}, u32[]{:S(2)}, u32[]{:S(2)}) collective-permute-start(s16[256,256]{1,0:T(8,128)(2,1)S(1)} %shard_map.79), channel_id=1, source_target_pairs={{0,2},{1,3},{2,0},{3,1},{4,6},{5,7},{6,4},{7,5},{8,10},{9,11},{10,... | collective-permute-start | bytes 393224 | tf_op jit(solution)/shard_map/ppermute | solution.py:244
  51.1 5.8 %collective-permute-start.20 = (s16[256,256]{1,0:T(8,128)(2,1)S(1)}, s16[256,256]{1,0:T(8,128)(2,1)S(1)}, u32[]{:S(2)}, u32[]{:S(2)}) collective-permute-start(s16[256,256]{1,0:T(8,128)(2,1)S(1)} %shard_map.81), channel_id=1, source_target_pairs={{0,1},{1,0},{2,3},{3,2},{4,5},{5,4},{6,7},{7,6},{8,9},{9,8},{10,11... | collective-permute-start | bytes 393224 | tf_op jit(solution)/shard_map/ppermute | solution.py:244

commit v8 on v7

--- a/solution.py
+++ b/solution.py
@@ -10,7 +10,7 @@
 GENE_BLOCKS = 16
 CORES = 2
 LANES = 128
-PARTS = (1, 1, 1, 1)
+STREAMS = 2
 MIB = 1 << 20
 
 VMEM = pl.BlockSpec(memory_space=pltpu.VMEM)
@@ -138,27 +138,34 @@
         start += out.shape[1]
 
 
-def both_kernel(mine, got, *outs):
-    start = 0
-    for keep, send in zip(outs[::2], outs[1::2]):
-        cut = slice(start, start + keep.shape[1])
-        total = mine[:, cut] + decode(got[:, cut])
-        keep[...] = total
-        encode(total, send)
-        start += keep.shape[1]
-
-
-def pick_kernel(cast, got, out):
+def place(chip, genes, count):
+    at, size = 0, genes
+    for bit in range(count.bit_length() - 1):
+        size //= 2
+        at = at + ((chip >> bit) & 1) * size
+    return pl.ds(pl.multiple_of(at, size), size)
+
+
+def deal_kernel(mine, got, *outs):
     _, chip = core_and_chip()
-    middle = (chip == 1) | (chip == 2)
-
-    @pl.when(middle)
-    def _():
-        out[...] = cast[...]
-
-    @pl.when(jnp.logical_not(middle))
-    def _():
-        out[...] = got[...]
+    count = len(outs) // STREAMS
+    for i, out in enumerate(outs):
+        stream, k = divmod(i, count)
+        cut = place(chip ^ k, mine.shape[1] // STREAMS, count)
+        cut = pl.ds(pl.multiple_of(stream * (mine.shape[1] // STREAMS) + cut.start, cut.size), cut.size)
+        part = mine[:, cut] + decode(got[:, cut])
+        if k == 0:
+            out[...] = part
+        else:
+            encode(part, out)
+
+
+def sum_kernel(own, *refs):
+    *got, out = refs
+    total = own[...]
+    for ref in got:
+        total = total + decode(ref[...])
+    out[...] = total.astype(bf16)
 
 
 def cast_kernel(code, got, out):
@@ -167,13 +174,9 @@
 
 def join(masks, pieces, gene):
     core, chip = core_and_chip()
-    rows, width = pieces[0].shape
+    rows = pieces[0].shape[0]
     for k, mask in enumerate(masks):
-        place, size = 0, gene.shape[1]
-        for bit in range(len(masks).bit_length() - 1):
-            size //= 2
-            place = place + (((chip ^ mask) >> bit) & 1) * size
-        cut = pl.ds(pl.multiple_of(place, width), width)
+        cut = place(chip ^ mask, gene.shape[1], len(masks))
         gene[block(core, rows), cut] = pieces[k][...]
         gene[block(1 - core, rows), cut] = pieces[len(masks) + k][...]
 
@@ -214,11 +217,9 @@
 
 
 def cuts_of(genes, bits):
-    for parts in (PARTS, (1, 1)):
-        unit = genes // sum(parts)
-        if unit >> max(bits - 1, 0) >= LANES:
-            ends = [sum(parts[:i]) * unit for i in range(len(parts))]
-            return tuple((at, p * unit) for at, p in zip(ends, parts))
+    half = genes // 2
+    if half >> max(bits - 1, 0) >= LANES:
+        return ((0, half), (half, half))
     return ((0, genes),)
 
 
@@ -231,7 +232,6 @@
     height = cells // n_genes
     shape = jax.ShapeDtypeStruct
     chips = n_cells // CORES
-    hub = chips == 4
     cuts = cuts_of(genes, bits)
 
     def to_core(x):
@@ -245,10 +245,11 @@
 
     widths = [width for _, width in cuts]
     first, rest = widths[0], genes - widths[0]
+    direct = bits > 1 and rest > 0 and first // chips >= LANES
     dense, turned, *theirs = call(
         dense_kernel,
         (shape((cells, genes), bf16), shape((rank, cells), bf16))
-        + tuple(shape((rows, width), i16) for width in (first, rest) if width),
+        + tuple(shape((rows, width), i16) for width in ((genes,) if direct else (first, rest)) if width),
         [SMEM] + [HBM] * 4,
         scratch=[
             (pltpu.SMEM((slots,), i32), pltpu.SMEM((slots,), i32)),
@@ -263,13 +264,9 @@
         return call(body, shape((rows, width), i16 if other else f32), [VMEM, VMEM])(turned, dense)
 
     def after(x, *others):
-        return lax.optimization_barrier((x, *others))[0]
+        return lax.optimization_barrier((x, *others))[0] if others else x
 
     def add_step(bit, kept, came, widths):
-        if hub and bit == 0:
-            outs = [shape((rows, width), kind) for width in widths for kind in (f32, i16)]
-            done = call(both_kernel, tuple(outs), [VMEM, VMEM])(kept, came)
-            return [done[i : i + 2] for i in range(0, len(done), 2)]
         if bit < bits - 1:
             outs = [shape((rows, width // 2), kind) for width in widths for kind in (f32, i16)]
             done = call(functools.partial(add_kernel, bit), tuple(outs), [VMEM, VMEM])(kept, came)
@@ -277,22 +274,8 @@
         done = call(code_kernel, tuple(shape((rows, width), i16) for width in widths), [VMEM, VMEM])(kept, came)
         return [done[i : i + 1] for i in range(len(done))]
 
-    def through_hubs(sums):
-        def move(x, pairs):
-            return lax.ppermute(x, "cells", [(a * CORES + i, b * CORES + i) for a, b in pairs for i in range(CORES)])
-
-        came = [move(code, ((0, 1), (3, 2))) for _, code in sums]
-        codes = []
-        for (kept, _), x in zip(sums, came):
-            x = after(x, codes[-1]) if codes else x
-            codes += call(code_kernel, (shape(x.shape, i16),), [VMEM, VMEM])(kept, x)
-        came = [move(code, ((1, 2), (2, 1))) for code in codes]
-        casts = []
-        for code, x in zip(codes, came):
-            x = after(x, casts[-1]) if casts else x
-            casts.append(call(cast_kernel, shape(x.shape, bf16), [VMEM, VMEM])(code, x))
-        came = [move(x, ((1, 0), (2, 3))) for x in casts]
-        return [(casts[0], came[0])] + [(cast, after(x, casts[-1])) for cast, x in zip(casts[1:], came[1:])]
+    def to_chips(x, k):
+        return lax.ppermute(x, "cells", [(i, i ^ (k * CORES)) for i in range(n_cells)])
 
     def by_halving(sums):
         widths = [sum_[0].shape[1] for sum_ in sums]
@@ -300,7 +283,7 @@
             came = [to_chip(code, bit) for _, code in sums]
             done = []
             for (kept, _), x, width in zip(sums, came, widths):
-                done += add_step(bit + 1, kept, after(x, *done[-1]) if done else x, [width])
+                done += add_step(bit + 1, kept, after(x, *(done[-1] if done else ())), [width])
             sums = done
             widths = [width // 2 for width in widths]
         held = []
@@ -321,34 +304,41 @@
         return masks, held
 
     got = [to_core(x) for x in theirs]
-    sums = add_step(0, half_of(0, 0, turned, first), got[0], widths[:1])
-    if rest:
-        sums += add_step(0, half_of(0, first, after(turned, *sums[0]), rest), got[1], widths[1:])
-    if hub:
-        sides = through_hubs(sums)
-        masks = [0]
+    if direct:
+        width = first // chips
+        dealt = ((shape((rows, width), f32),) + (shape((rows, width), i16),) * (chips - 1)) * STREAMS
+        pieces = call(deal_kernel, dealt, [VMEM, VMEM])(half_of(0, 0, turned, genes), got[0])
+        pieces = [pieces[i * chips : (i + 1) * chips] for i in range(STREAMS)]
+        sides = []
+        for own, *codes in pieces:
+            came = [to_chips(codes[k - 1], k) for k in reversed(range(1, chips))]
+            chunk = call(sum_kernel, shape(own.shape, bf16), [VMEM] * chips)(own, *came)
+            came = [to_chips(chunk, k) for k in reversed(range(1, chips))][::-1]
+            sides.append([chunk] + came)
+        sides[0][1:] = [after(x, sides[1][0]) for x in sides[0][1:]]
+        masks = [list(range(chips))] * STREAMS
     else:
+        sums = add_step(0, half_of(0, 0, turned, first), got[0], [first])
+        if rest:
+            sums += add_step(0, half_of(0, first, after(turned, *sums[0]), rest), got[1], [rest])
         masks, sides = by_halving(sums)
+        masks = [masks] * len(sides)
     totals = []
     for i, ((start, width), pieces) in enumerate(zip(cuts, sides)):
-        if i >= 2:
-            pieces = [after(x, totals[i - 2]) for x in pieces]
-        if hub:
-            pieces = [call(pick_kernel, shape(pieces[0].shape, bf16), [VMEM, VMEM])(*pieces)]
         pieces = pieces + [to_core(x) for x in pieces]
         if i == len(cuts) - 1:
             break
         before = totals[-1:]
         totals.append(
             call(
-                functools.partial(part_kernel, masks, start, not before),
+                functools.partial(part_kernel, masks[i], start, not before),
                 shape((cells, rank), f32),
                 [VMEM] * (1 + len(before) + len(pieces)),
                 scratch=[pltpu.VMEM((rank, width), bf16)],
             )(dense, *before, *pieces)
         )
     gene = call(
-        functools.partial(gene_kernel, masks), shape((rank, width), bf16), [VMEM] * len(pieces)
+        functools.partial(gene_kernel, masks[-1]), shape((rank, width), bf16), [VMEM] * len(pieces)
     )(*pieces)
 
     def cell(k):

time: 58.1 us -> 49.4 us (0.85)
  starting transfers between devices: 26.3 us -> 20.8 us
  waiting for transfers between devices: 20.5 us -> 19 us
  Pallas kernels: 9.81 us -> 8.66 us
    ppermute x12, starting transfers between devices: 21.7 us -> 15.9 us  [to_chips(): lax.ppermute(x, 'cells', [(i, i ^ k * CORES) for i in range(n_cells)])]
    ppermute x12, waiting for transfers between devices: 13.6 us -> 12.2 us  [to_chips(): lax.ppermute(x, 'cells', [(i, i ^ k * CORES) for i in range(n_cells)])]
    pallas_call x18 -> x5, Pallas kernels: 2.6 us -> 1.32 us  [the longest x1 0.82 us: local(): call(functools.partial(part_kernel, masks[i], start, not before), shape((...]
    ppermute x6 -> x9, waiting for transfers between devices: 1.92 us -> 2.28 us  [to_core(): return lax.ppermute(x, 'cells', [(i, i ^ 1) for i in range(n_cells)])]
    ppermute x6 -> x9, starting transfers between devices: 0.85 us -> 1.17 us  [to_core(): return lax.ppermute(x, 'cells', [(i, i ^ 1) for i in range(n_cells)])]
  transfers between devices with their start and end apart: 21 -> 24, of which waited for: 9 -> 13; matrix products, arithmetic and copies ran while one was open for 0% -> 0% of each run, Pallas kernels for 8% -> 4%
where the time goes in v8:
time: 49.4 us; the launch traced here: 49.2 us
  starting transfers between devices  20.8 us (42%)
  waiting for transfers between devices  19 us (38%)
  Pallas kernels  8.66 us (18%)
  between operations  0.79 us (2%)
    ppermute x12, starting transfers between devices, to_chips(): lax.ppermute(x, 'cells', [(i, i ^ k * CORES) for i in range(n_cells)])  15.9 us
    ppermute x12, waiting for transfers between devices, to_chips(): lax.ppermute(x, 'cells', [(i, i ^ k * CORES) for i in range(n_cells)])  12.2 us
    ppermute x3, waiting for transfers between devices, to_gene(): return lax.ppermute(x, 'genes', [(i, i ^ k) for i in range(n_genes)])  4.47 us
    pallas_call x1, Pallas kernels, local(): call(dense_kernel, (shape((cells, genes), bf16), shape((rank, cells), bf1...  4.29 us
    ppermute x3, starting transfers between devices, to_gene(): return lax.ppermute(x, 'genes', [(i, i ^ k) for i in range(n_genes)])  3.69 us
    ppermute x9, waiting for transfers between devices, to_core(): return lax.ppermute(x, 'cells', [(i, i ^ 1) for i in range(n_cells)])  2.28 us
    pallas_call x4, Pallas kernels, cell(): call(functools.partial(cell_kernel, k, start), shape((height, rank), f32...  1.5 us
    ppermute x9, starting transfers between devices, to_core(): return lax.ppermute(x, 'cells', [(i, i ^ 1) for i in range(n_cells)])  1.17 us
  transfers between devices with their start and end apart: 24, of which 13 were waited for; matrix products, arithmetic and copies ran while one was open for 0% of the time, Pallas kernels for 4%

profile of v8, /device:TPU:0, one launch (start us, length us, event | category | flops | bytes accessed | tf_op | source)
XLA Modules:
  0.0 49.2 jit_solution(5197314934371152926)
XLA Ops:
  0.7 4.3 %shard_map.55 = (bf16[1024,2048]{1,0:T(8,128)(2,1)S(1)}, bf16[256,1024]{1,0:T(8,128)(2,1)S(1)}, s16[128,2048]{1,0:T(8,128)(2,1)S(1)}) custom-call(s32[1]{0:T(128)S(6)} %copy.6.count, s32[96]{0:T(128)} %rows.1, s32[96]{0:T(128)} %cols.1, bf16[1024,256]{1,0:T(8,128)(2,1)} %sketch.1, bf16[96,128,128]{2,1,0:T(8,128)(2,1)} %tiles.1), custom_call_target="tpu_custom_call" | custom-call | tf_op jit(solution)/shard_map/pallas_call | solution.py:249
  5.0 0.7 %shard_map.56.mine = f32[128,2048]{1,0:T(8,128)S(1)} custom-call(bf16[256,1024]{1,0:T(8,128)(2,1)S(1)} %get-tuple-element.20.turned, bf16[1024,2048]{1,0:T(8,128)(2,1)S(1)} %get-tuple-element.19.dense), custom_call_target="tpu_custom_call" | custom-call | tf_op jit(solution)/shard_map/pallas_call | solution.py:264
  5.8 1.2 %collective-permute-done.got = s16[128,2048]{1,0:T(8,128)(2,1)S(1)} collective-permute-done((s16[128,2048]{1,0:T(8,128)(2,1)S(1)}, s16[128,2048]{1,0:T(8,128)(2,1)S(1)}, u32[]{:S(2)}, u32[]{:S(2)}) %collective-permute-start) | collective-permute-done | bytes 524320 | tf_op jit(solution)/shard_map/ppermute | solution.py:238
  7.2 4.6 %collective-permute-start.1 = (s16[128,256]{1,0:T(8,128)(2,1)S(1)}, s16[128,256]{1,0:T(8,128)(2,1)S(1)}, u32[]{:S(2)}, u32[]{:S(2)}) collective-permute-start(s16[128,256]{1,0:T(8,128)(2,1)S(1)} %get-tuple-element.23), channel_id=1, source_target_pairs={{0,24},{4,28},{8,16},{12,20},{16,8},{20,12},{24,0},{28,4},{1,25},{... | collective-permute-start | bytes 196616 | tf_op jit(solution)/shard_map/ppermute | solution.py:278
  11.8 0.6 %collective-permute-start.3 = (s16[128,256]{1,0:T(8,128)(2,1)S(1)}, s16[128,256]{1,0:T(8,128)(2,1)S(1)}, u32[]{:S(2)}, u32[]{:S(2)}) collective-permute-start(s16[128,256]{1,0:T(8,128)(2,1)S(1)} %get-tuple-element.25), channel_id=1, source_target_pairs={{0,8},{4,12},{8,0},{12,4},{16,24},{20,28},{24,16},{28,20},{1,9},{5... | collective-permute-start | bytes 196616 | tf_op jit(solution)/shard_map/ppermute | solution.py:278
  12.5 3.7 %collective-permute-start.11 = (s16[128,256]{1,0:T(8,128)(2,1)S(1)}, s16[128,256]{1,0:T(8,128)(2,1)S(1)}, u32[]{:S(2)}, u32[]{:S(2)}) collective-permute-start(s16[128,256]{1,0:T(8,128)(2,1)S(1)} %get-tuple-element.27), channel_id=1, source_target_pairs={{0,24},{4,28},{8,16},{12,20},{16,8},{20,12},{24,0},{28,4},{1,25},{... | collective-permute-start | bytes 196616 | tf_op jit(solution)/shard_map/ppermute | solution.py:278
  16.2 0.8 %collective-permute-start.13 = (s16[128,256]{1,0:T(8,128)(2,1)S(1)}, s16[128,256]{1,0:T(8,128)(2,1)S(1)}, u32[]{:S(2)}, u32[]{:S(2)}) collective-permute-start(s16[128,256]{1,0:T(8,128)(2,1)S(1)} %get-tuple-element.29), channel_id=1, source_target_pairs={{0,8},{4,12},{8,0},{12,4},{16,24},{20,28},{24,16},{28,20},{1,9},{5... | collective-permute-start | bytes 196616 | tf_op jit(solution)/shard_map/ppermute | solution.py:278
  17.1 3.2 %collective-permute-done.2.refs_1_ = s16[128,256]{1,0:T(8,128)(2,1)S(1)} collective-permute-done((s16[128,256]{1,0:T(8,128)(2,1)S(1)}, s16[128,256]{1,0:T(8,128)(2,1)S(1)}, u32[]{:S(2)}, u32[]{:S(2)}) %collective-permute-start.2) | collective-permute-done | bytes 65568 | tf_op jit(solution)/shard_map/ppermute | solution.py:278
  20.3 0.8 %collective-permute-start.6 = (bf16[128,256]{1,0:T(8,128)(2,1)S(1)}, bf16[128,256]{1,0:T(8,128)(2,1)S(1)}, u32[]{:S(2)}, u32[]{:S(2)}) collective-permute-start(bf16[128,256]{1,0:T(8,128)(2,1)S(1)} %shard_map.58.refs_0_), channel_id=1, source_target_pairs={{0,24},{4,28},{8,16},{12,20},{16,8},{20,12},{24,0},{28,4},{1,25},{... | collective-permute-start | bytes 196616 | tf_op jit(solution)/shard_map/ppermute | solution.py:278
  21.1 3.8 %collective-permute-done.12.refs_1_ = s16[128,256]{1,0:T(8,128)(2,1)S(1)} collective-permute-done((s16[128,256]{1,0:T(8,128)(2,1)S(1)}, s16[128,256]{1,0:T(8,128)(2,1)S(1)}, u32[]{:S(2)}, u32[]{:S(2)}) %collective-permute-start.12) | collective-permute-done | bytes 65568 | tf_op jit(solution)/shard_map/ppermute | solution.py:278
  25.0 4.0 %collective-permute-start.16 = (bf16[128,256]{1,0:T(8,128)(2,1)S(1)}, bf16[128,256]{1,0:T(8,128)(2,1)S(1)}, u32[]{:S(2)}, u32[]{:S(2)}) collective-permute-start(bf16[128,256]{1,0:T(8,128)(2,1)S(1)} %shard_map.60.refs_0_), channel_id=1, source_target_pairs={{0,24},{4,28},{8,16},{12,20},{16,8},{20,12},{24,0},{28,4},{1,25},{... | collective-permute-start | bytes 196616 | tf_op jit(solution)/shard_map/ppermute | solution.py:278
  29.0 0.6 %collective-permute-start.14 = (bf16[128,256]{1,0:T(8,128)(2,1)S(1)}, bf16[128,256]{1,0:T(8,128)(2,1)S(1)}, u32[]{:S(2)}, u32[]{:S(2)}) collective-permute-start(bf16[128,256]{1,0:T(8,128)(2,1)S(1)} %shard_map.60.refs_0_), channel_id=1, source_target_pairs={{0,8},{4,12},{8,0},{12,4},{16,24},{20,28},{24,16},{28,20},{1,9},{5... | collective-permute-start | bytes 196616 | tf_op jit(solution)/shard_map/ppermute | solution.py:278
  29.7 0.9 %collective-permute-done.5.refs_2_ = bf16[128,256]{1,0:T(8,128)(2,1)S(1)} collective-permute-done((bf16[128,256]{1,0:T(8,128)(2,1)S(1)}, bf16[128,256]{1,0:T(8,128)(2,1)S(1)}, u32[]{:S(2)}, u32[]{:S(2)}) %collective-permute-start.5) | collective-permute-done | bytes 65568 | tf_op jit(solution)/shard_map/ppermute | solution.py:278
  30.5 0.6 %collective-permute-start.4 = (bf16[128,256]{1,0:T(8,128)(2,1)S(1)}, bf16[128,256]{1,0:T(8,128)(2,1)S(1)}, u32[]{:S(2)}, u32[]{:S(2)}) collective-permute-start(bf16[128,256]{1,0:T(8,128)(2,1)S(1)} %shard_map.58.refs_0_), channel_id=1, source_target_pairs={{0,8},{4,12},{8,0},{12,4},{16,24},{20,28},{24,16},{28,20},{1,9},{5... | collective-permute-start | bytes 196616 | tf_op jit(solution)/shard_map/ppermute | solution.py:278
  31.1 0.6 %collective-permute-done.16.refs_3_ = bf16[128,256]{1,0:T(8,128)(2,1)S(1)} collective-permute-done((bf16[128,256]{1,0:T(8,128)(2,1)S(1)}, bf16[128,256]{1,0:T(8,128)(2,1)S(1)}, u32[]{:S(2)}, u32[]{:S(2)}) %collective-permute-start.16) | collective-permute-done | bytes 65568 | tf_op jit(solution)/shard_map/ppermute | solution.py:278
  31.7 2.7 %collective-permute-done.15.refs_2_ = bf16[128,256]{1,0:T(8,128)(2,1)S(1)} collective-permute-done((bf16[128,256]{1,0:T(8,128)(2,1)S(1)}, bf16[128,256]{1,0:T(8,128)(2,1)S(1)}, u32[]{:S(2)}, u32[]{:S(2)}) %collective-permute-start.15) | collective-permute-done | bytes 65568 | tf_op jit(solution)/shard_map/ppermute | solution.py:278
  34.5 0.7 %collective-permute-done.14.refs_1_ = bf16[128,256]{1,0:T(8,128)(2,1)S(1)} collective-permute-done((bf16[128,256]{1,0:T(8,128)(2,1)S(1)}, bf16[128,256]{1,0:T(8,128)(2,1)S(1)}, u32[]{:S(2)}, u32[]{:S(2)}) %collective-permute-start.14) | collective-permute-done | bytes 65568 | tf_op jit(solution)/shard_map/ppermute | solution.py:278
  35.2 0.5 %collective-permute-start.20 = (bf16[128,256]{1,0:T(8,128)(2,1)S(1)}, bf16[128,256]{1,0:T(8,128)(2,1)S(1)}, u32[]{:S(2)}, u32[]{:S(2)}) collective-permute-start(bf16[128,256]{1,0:T(8,128)(2,1)S(1)} %collective-permute-done.16.refs_3_), channel_id=1, source_target_pairs={{0,4},{4,0},{8,12},{12,8},{16,20},{20,16},{24,28},{28,24},{1,5},{5... | collective-permute-start | bytes 196616 | tf_op jit(solution)/shard_map/ppermute | solution.py:238
  36.1 0.5 %collective-permute-start.19 = (bf16[128,256]{1,0:T(8,128)(2,1)S(1)}, bf16[128,256]{1,0:T(8,128)(2,1)S(1)}, u32[]{:S(2)}, u32[]{:S(2)}) collective-permute-start(bf16[128,256]{1,0:T(8,128)(2,1)S(1)} %collective-permute-done.15.refs_2_), channel_id=1, source_target_pairs={{0,4},{4,0},{8,12},{12,8},{16,20},{20,16},{24,28},{28,24},{1,5},{5... | collective-permute-start | bytes 196616 | tf_op jit(solution)/shard_map/ppermute | solution.py:238
  36.7 0.7 %collective-permute-done.8.refs_5_ = bf16[128,256]{1,0:T(8,128)(2,1)S(1)} collective-permute-done((bf16[128,256]{1,0:T(8,128)(2,1)S(1)}, bf16[128,256]{1,0:T(8,128)(2,1)S(1)}, u32[]{:S(2)}, u32[]{:S(2)}) %collective-permute-start.8) | collective-permute-done | bytes 65568 | tf_op jit(solution)/shard_map/ppermute | solution.py:238
  37.5 0.4 collective-permute-done.18.refs_5_
  37.8 0.8 %shard_map.61.refs_0_ = f32[1024,256]{1,0:T(8,128)S(1)} custom-call(bf16[1024,2048]{1,0:T(8,128)(2,1)S(1)} %get-tuple-element.19.dense, bf16[128,256]{1,0:T(8,128)(2,1)S(1)} %shard_map.60.refs_0_, bf16[128,256]{1,0:T(8,128)(2,1)S(1)} %collective-permute-done.14.refs_1_, bf16[128,256]{1,0:T(8,128)(2,1)S(1)} %collective-permute-done.15.refs_2_, ...), custom_call_target="tpu_custom_call" | custom-call | tf_op jit(solution)/shard_map/pallas_call | solution.py:333
  38.7 0.4 shard_map.63
  39.1 2.2 %collective-permute-start.21 = (s16[256,256]{1,0:T(8,128)(2,1)S(1)}, s16[256,256]{1,0:T(8,128)(2,1)S(1)}, u32[]{:S(2)}, u32[]{:S(2)}) collective-permute-start(s16[256,256]{1,0:T(8,128)(2,1)S(1)} %shard_map.63), channel_id=1, source_target_pairs={{0,3},{1,2},{2,1},{3,0},{4,7},{5,6},{6,5},{7,4},{8,11},{9,10},{10,... | collective-permute-start | bytes 393224 | tf_op jit(solution)/shard_map/ppermute | solution.py:244
  41.2 0.4 shard_map.65
  41.6 0.5 %collective-permute-start.22 = (s16[256,256]{1,0:T(8,128)(2,1)S(1)}, s16[256,256]{1,0:T(8,128)(2,1)S(1)}, u32[]{:S(2)}, u32[]{:S(2)}) collective-permute-start(s16[256,256]{1,0:T(8,128)(2,1)S(1)} %shard_map.65), channel_id=1, source_target_pairs={{0,2},{1,3},{2,0},{3,1},{4,6},{5,7},{6,4},{7,5},{8,10},{9,11},{10,... | collective-permute-start | bytes 393224 | tf_op jit(solution)/shard_map/ppermute | solution.py:244
  42.1 0.4 shard_map.67
  42.5 1.0 %collective-permute-start.23 = (s16[256,256]{1,0:T(8,128)(2,1)S(1)}, s16[256,256]{1,0:T(8,128)(2,1)S(1)}, u32[]{:S(2)}, u32[]{:S(2)}) collective-permute-start(s16[256,256]{1,0:T(8,128)(2,1)S(1)} %shard_map.67), channel_id=1, source_target_pairs={{0,1},{1,0},{2,3},{3,2},{4,5},{5,4},{6,7},{7,6},{8,9},{9,8},{10,11... | collective-permute-start | bytes 393224 | tf_op jit(solution)/shard_map/ppermute | solution.py:244
  43.5 0.3 shard_map.62.total
  43.9 1.8 %collective-permute-done.21.got = s16[256,256]{1,0:T(8,128)(2,1)S(1)} collective-permute-done((s16[256,256]{1,0:T(8,128)(2,1)S(1)}, s16[256,256]{1,0:T(8,128)(2,1)S(1)}, u32[]{:S(2)}, u32[]{:S(2)}) %collective-permute-start.21) | collective-permute-done | bytes 131104 | tf_op jit(solution)/shard_map/ppermute | solution.py:244
  45.7 2.7 %collective-permute-done.22.got = s16[256,256]{1,0:T(8,128)(2,1)S(1)} collective-permute-done((s16[256,256]{1,0:T(8,128)(2,1)S(1)}, s16[256,256]{1,0:T(8,128)(2,1)S(1)}, u32[]{:S(2)}, u32[]{:S(2)}) %collective-permute-start.22) | collective-permute-done | bytes 131104 | tf_op jit(solution)/shard_map/ppermute | solution.py:244
  48.5 0.7 %shard_map.68 = f32[256,256]{1,0:T(8,128)} custom-call(f32[256,256]{1,0:T(8,128)S(1)} %shard_map.66.total, s16[256,256]{1,0:T(8,128)(2,1)S(1)} %collective-permute-done.23.got), custom_call_target="tpu_custom_call" | custom-call | bytes 16777216 | tf_op jit(solution)/shard_map/pallas_call | solution.py:354
  (30 shorter events, 1.2 us)
Async XLA Ops:
  4.9 2.0 %collective-permute-start = (s16[128,2048]{1,0:T(8,128)(2,1)S(1)}, s16[128,2048]{1,0:T(8,128)(2,1)S(1)}, u32[]{:S(2)}, u32[]{:S(2)}) collective-permute-start(s16[128,2048]{1,0:T(8,128)(2,1)S(1)} %get-tuple-element.21), channel_id=1, source_target_pairs={{0,4},{4,0},{8,12},{12,8},{16,20},{20,16},{24,28},{28,24},{1,5},{5... | collective-permute-start | bytes 1572872 | tf_op jit(solution)/shard_map/ppermute | solution.py:238
  7.2 9.0 %collective-permute-start.1 = (s16[128,256]{1,0:T(8,128)(2,1)S(1)}, s16[128,256]{1,0:T(8,128)(2,1)S(1)}, u32[]{:S(2)}, u32[]{:S(2)}) collective-permute-start(s16[128,256]{1,0:T(8,128)(2,1)S(1)} %get-tuple-element.23), channel_id=1, source_target_pairs={{0,24},{4,28},{8,16},{12,20},{16,8},{20,12},{24,0},{28,4},{1,25},{... | collective-permute-start | bytes 196616 | tf_op jit(solution)/shard_map/ppermute | solution.py:278
  11.8 8.4 %collective-permute-start.2 = (s16[128,256]{1,0:T(8,128)(2,1)S(1)}, s16[128,256]{1,0:T(8,128)(2,1)S(1)}, u32[]{:S(2)}, u32[]{:S(2)}) collective-permute-start(s16[128,256]{1,0:T(8,128)(2,1)S(1)} %get-tuple-element.24), channel_id=1, source_target_pairs={{0,16},{4,20},{8,24},{12,28},{16,0},{20,4},{24,8},{28,12},{1,17},{... | collective-permute-start | bytes 196616 | tf_op jit(solution)/shard_map/ppermute | solution.py:278
  11.8 8.4 %collective-permute-start.3 = (s16[128,256]{1,0:T(8,128)(2,1)S(1)}, s16[128,256]{1,0:T(8,128)(2,1)S(1)}, u32[]{:S(2)}, u32[]{:S(2)}) collective-permute-start(s16[128,256]{1,0:T(8,128)(2,1)S(1)} %get-tuple-element.25), channel_id=1, source_target_pairs={{0,8},{4,12},{8,0},{12,4},{16,24},{20,28},{24,16},{28,20},{1,9},{5... | collective-permute-start | bytes 196616 | tf_op jit(solution)/shard_map/ppermute | solution.py:278
  12.5 8.6 %collective-permute-start.11 = (s16[128,256]{1,0:T(8,128)(2,1)S(1)}, s16[128,256]{1,0:T(8,128)(2,1)S(1)}, u32[]{:S(2)}, u32[]{:S(2)}) collective-permute-start(s16[128,256]{1,0:T(8,128)(2,1)S(1)} %get-tuple-element.27), channel_id=1, source_target_pairs={{0,24},{4,28},{8,16},{12,20},{16,8},{20,12},{24,0},{28,4},{1,25},{... | collective-permute-start | bytes 196616 | tf_op jit(solution)/shard_map/ppermute | solution.py:278
  16.2 8.7 %collective-permute-start.12 = (s16[128,256]{1,0:T(8,128)(2,1)S(1)}, s16[128,256]{1,0:T(8,128)(2,1)S(1)}, u32[]{:S(2)}, u32[]{:S(2)}) collective-permute-start(s16[128,256]{1,0:T(8,128)(2,1)S(1)} %get-tuple-element.28), channel_id=1, source_target_pairs={{0,16},{4,20},{8,24},{12,28},{16,0},{20,4},{24,8},{28,12},{1,17},{... | collective-permute-start | bytes 196616 | tf_op jit(solution)/shard_map/ppermute | solution.py:278
  16.2 8.7 %collective-permute-start.13 = (s16[128,256]{1,0:T(8,128)(2,1)S(1)}, s16[128,256]{1,0:T(8,128)(2,1)S(1)}, u32[]{:S(2)}, u32[]{:S(2)}) collective-permute-start(s16[128,256]{1,0:T(8,128)(2,1)S(1)} %get-tuple-element.29), channel_id=1, source_target_pairs={{0,8},{4,12},{8,0},{12,4},{16,24},{20,28},{24,16},{28,20},{1,9},{5... | collective-permute-start | bytes 196616 | tf_op jit(solution)/shard_map/ppermute | solution.py:278
  20.3 9.4 %collective-permute-start.6 = (bf16[128,256]{1,0:T(8,128)(2,1)S(1)}, bf16[128,256]{1,0:T(8,128)(2,1)S(1)}, u32[]{:S(2)}, u32[]{:S(2)}) collective-permute-start(bf16[128,256]{1,0:T(8,128)(2,1)S(1)} %shard_map.58.refs_0_), channel_id=1, source_target_pairs={{0,24},{4,28},{8,16},{12,20},{16,8},{20,12},{24,0},{28,4},{1,25},{... | collective-permute-start | bytes 196616 | tf_op jit(solution)/shard_map/ppermute | solution.py:278
  21.1 9.4 %collective-permute-start.5 = (bf16[128,256]{1,0:T(8,128)(2,1)S(1)}, bf16[128,256]{1,0:T(8,128)(2,1)S(1)}, u32[]{:S(2)}, u32[]{:S(2)}) collective-permute-start(bf16[128,256]{1,0:T(8,128)(2,1)S(1)} %shard_map.58.refs_0_), channel_id=1, source_target_pairs={{0,16},{4,20},{8,24},{12,28},{16,0},{20,4},{24,8},{28,12},{1,17},{... | collective-permute-start | bytes 196616 | tf_op jit(solution)/shard_map/ppermute | solution.py:278
  25.0 6.7 %collective-permute-start.16 = (bf16[128,256]{1,0:T(8,128)(2,1)S(1)}, bf16[128,256]{1,0:T(8,128)(2,1)S(1)}, u32[]{:S(2)}, u32[]{:S(2)}) collective-permute-start(bf16[128,256]{1,0:T(8,128)(2,1)S(1)} %shard_map.60.refs_0_), channel_id=1, source_target_pairs={{0,24},{4,28},{8,16},{12,20},{16,8},{20,12},{24,0},{28,4},{1,25},{... | collective-permute-start | bytes 196616 | tf_op jit(solution)/shard_map/ppermute | solution.py:278
  29.0 5.4 %collective-permute-start.15 = (bf16[128,256]{1,0:T(8,128)(2,1)S(1)}, bf16[128,256]{1,0:T(8,128)(2,1)S(1)}, u32[]{:S(2)}, u32[]{:S(2)}) collective-permute-start(bf16[128,256]{1,0:T(8,128)(2,1)S(1)} %shard_map.60.refs_0_), channel_id=1, source_target_pairs={{0,16},{4,20},{8,24},{12,28},{16,0},{20,4},{24,8},{28,12},{1,17},{... | collective-permute-start | bytes 196616 | tf_op jit(solution)/shard_map/ppermute | solution.py:278
  29.0 6.2 %collective-permute-start.14 = (bf16[128,256]{1,0:T(8,128)(2,1)S(1)}, bf16[128,256]{1,0:T(8,128)(2,1)S(1)}, u32[]{:S(2)}, u32[]{:S(2)}) collective-permute-start(bf16[128,256]{1,0:T(8,128)(2,1)S(1)} %shard_map.60.refs_0_), channel_id=1, source_target_pairs={{0,8},{4,12},{8,0},{12,4},{16,24},{20,28},{24,16},{28,20},{1,9},{5... | collective-permute-start | bytes 196616 | tf_op jit(solution)/shard_map/ppermute | solution.py:278
  29.7 5.5 %collective-permute-start.7 = (bf16[128,256]{1,0:T(8,128)(2,1)S(1)}, bf16[128,256]{1,0:T(8,128)(2,1)S(1)}, u32[]{:S(2)}, u32[]{:S(2)}) collective-permute-start(bf16[128,256]{1,0:T(8,128)(2,1)S(1)} %shard_map.58.refs_0_), channel_id=1, source_target_pairs={{0,4},{4,0},{8,12},{12,8},{16,20},{20,16},{24,28},{28,24},{1,5},{5... | collective-permute-start | bytes 196616 | tf_op jit(solution)/shard_map/ppermute | solution.py:238
  30.5 5.5 %collective-permute-start.4 = (bf16[128,256]{1,0:T(8,128)(2,1)S(1)}, bf16[128,256]{1,0:T(8,128)(2,1)S(1)}, u32[]{:S(2)}, u32[]{:S(2)}) collective-permute-start(bf16[128,256]{1,0:T(8,128)(2,1)S(1)} %shard_map.58.refs_0_), channel_id=1, source_target_pairs={{0,8},{4,12},{8,0},{12,4},{16,24},{20,28},{24,16},{28,20},{1,9},{5... | collective-permute-start | bytes 196616 | tf_op jit(solution)/shard_map/ppermute | solution.py:278
  31.7 4.3 %collective-permute-start.10 = (bf16[128,256]{1,0:T(8,128)(2,1)S(1)}, bf16[128,256]{1,0:T(8,128)(2,1)S(1)}, u32[]{:S(2)}, u32[]{:S(2)}) collective-permute-start(bf16[128,256]{1,0:T(8,128)(2,1)S(1)} %collective-permute-done.6.refs_3_), channel_id=1, source_target_pairs={{0,4},{4,0},{8,12},{12,8},{16,20},{20,16},{24,28},{28,24},{1,5},{5... | collective-permute-start | bytes 196616 | tf_op jit(solution)/shard_map/ppermute | solution.py:238
  34.5 2.1 %collective-permute-start.9 = (bf16[128,256]{1,0:T(8,128)(2,1)S(1)}, bf16[128,256]{1,0:T(8,128)(2,1)S(1)}, u32[]{:S(2)}, u32[]{:S(2)}) collective-permute-start(bf16[128,256]{1,0:T(8,128)(2,1)S(1)} %collective-permute-done.5.refs_2_), channel_id=1, source_target_pairs={{0,4},{4,0},{8,12},{12,8},{16,20},{20,16},{24,28},{28,24},{1,5},{5... | collective-permute-start | bytes 196616 | tf_op jit(solution)/shard_map/ppermute | solution.py:238
  35.2 2.2 %collective-permute-start.17 = (bf16[128,256]{1,0:T(8,128)(2,1)S(1)}, bf16[128,256]{1,0:T(8,128)(2,1)S(1)}, u32[]{:S(2)}, u32[]{:S(2)}) collective-permute-start(bf16[128,256]{1,0:T(8,128)(2,1)S(1)} %shard_map.60.refs_0_), channel_id=1, source_target_pairs={{0,4},{4,0},{8,12},{12,8},{16,20},{20,16},{24,28},{28,24},{1,5},{5... | collective-permute-start | bytes 196616 | tf_op jit(solution)/shard_map/ppermute | solution.py:238
  35.2 2.2 %collective-permute-start.20 = (bf16[128,256]{1,0:T(8,128)(2,1)S(1)}, bf16[128,256]{1,0:T(8,128)(2,1)S(1)}, u32[]{:S(2)}, u32[]{:S(2)}) collective-permute-start(bf16[128,256]{1,0:T(8,128)(2,1)S(1)} %collective-permute-done.16.refs_3_), channel_id=1, source_target_pairs={{0,4},{4,0},{8,12},{12,8},{16,20},{20,16},{24,28},{28,24},{1,5},{5... | collective-permute-start | bytes 196616 | tf_op jit(solution)/shard_map/ppermute | solution.py:238
  36.1 1.3 %collective-permute-start.8 = (bf16[128,256]{1,0:T(8,128)(2,1)S(1)}, bf16[128,256]{1,0:T(8,128)(2,1)S(1)}, u32[]{:S(2)}, u32[]{:S(2)}) collective-permute-start(bf16[128,256]{1,0:T(8,128)(2,1)S(1)} %collective-permute-done.4.refs_1_), channel_id=1, source_target_pairs={{0,4},{4,0},{8,12},{12,8},{16,20},{20,16},{24,28},{28,24},{1,5},{5... | collective-permute-start | bytes 196616 | tf_op jit(solution)/shard_map/ppermute | solution.py:238
  36.1 1.4 %collective-permute-start.19 = (bf16[128,256]{1,0:T(8,128)(2,1)S(1)}, bf16[128,256]{1,0:T(8,128)(2,1)S(1)}, u32[]{:S(2)}, u32[]{:S(2)}) collective-permute-start(bf16[128,256]{1,0:T(8,128)(2,1)S(1)} %collective-permute-done.15.refs_2_), channel_id=1, source_target_pairs={{0,4},{4,0},{8,12},{12,8},{16,20},{20,16},{24,28},{28,24},{1,5},{5... | collective-permute-start | bytes 196616 | tf_op jit(solution)/shard_map/ppermute | solution.py:238
  36.6 1.3 %collective-permute-start.18 = (bf16[128,256]{1,0:T(8,128)(2,1)S(1)}, bf16[128,256]{1,0:T(8,128)(2,1)S(1)}, u32[]{:S(2)}, u32[]{:S(2)}) collective-permute-start(bf16[128,256]{1,0:T(8,128)(2,1)S(1)} %collective-permute-done.14.refs_1_), channel_id=1, source_target_pairs={{0,4},{4,0},{8,12},{12,8},{16,20},{20,16},{24,28},{28,24},{1,5},{5... | collective-permute-start | bytes 196616 | tf_op jit(solution)/shard_map/ppermute | solution.py:238
  39.1 6.6 %collective-permute-start.21 = (s16[256,256]{1,0:T(8,128)(2,1)S(1)}, s16[256,256]{1,0:T(8,128)(2,1)S(1)}, u32[]{:S(2)}, u32[]{:S(2)}) collective-permute-start(s16[256,256]{1,0:T(8,128)(2,1)S(1)} %shard_map.63), channel_id=1, source_target_pairs={{0,3},{1,2},{2,1},{3,0},{4,7},{5,6},{6,5},{7,4},{8,11},{9,10},{10,... | collective-permute-start | bytes 393224 | tf_op jit(solution)/shard_map/ppermute | solution.py:244
  41.6 6.8 %collective-permute-start.22 = (s16[256,256]{1,0:T(8,128)(2,1)S(1)}, s16[256,256]{1,0:T(8,128)(2,1)S(1)}, u32[]{:S(2)}, u32[]{:S(2)}) collective-permute-start(s16[256,256]{1,0:T(8,128)(2,1)S(1)} %shard_map.65), channel_id=1, source_target_pairs={{0,2},{1,3},{2,0},{3,1},{4,6},{5,7},{6,4},{7,5},{8,10},{9,11},{10,... | collective-permute-start | bytes 393224 | tf_op jit(solution)/shard_map/ppermute | solution.py:244
  42.5 5.9 %collective-permute-start.23 = (s16[256,256]{1,0:T(8,128)(2,1)S(1)}, s16[256,256]{1,0:T(8,128)(2,1)S(1)}, u32[]{:S(2)}, u32[]{:S(2)}) collective-permute-start(s16[256,256]{1,0:T(8,128)(2,1)S(1)} %shard_map.67), channel_id=1, source_target_pairs={{0,1},{1,0},{2,3},{3,2},{4,5},{5,4},{6,7},{7,6},{8,9},{9,8},{10,11... | collective-permute-start | bytes 393224 | tf_op jit(solution)/shard_map/ppermute | solution.py:244

commit v9 on v7

--- a/solution.py
+++ b/solution.py
@@ -278,20 +278,20 @@
         return [done[i : i + 1] for i in range(len(done))]
 
     def through_hubs(sums):
-        def move(x, pairs):
-            return lax.ppermute(x, "cells", [(a * CORES + i, b * CORES + i) for a, b in pairs for i in range(CORES)])
-
-        came = [move(code, ((0, 1), (3, 2))) for _, code in sums]
+        def move(x, to):
+            return lax.ppermute(x, "cells", [(a * CORES + i, b * CORES + i) for a, b in enumerate(to) for i in range(CORES)])
+
+        came = [move(code, (1, 0, 3, 2)) for _, code in sums]
         codes = []
         for (kept, _), x in zip(sums, came):
             x = after(x, codes[-1]) if codes else x
             codes += call(code_kernel, (shape(x.shape, i16),), [VMEM, VMEM])(kept, x)
-        came = [move(code, ((1, 2), (2, 1))) for code in codes]
+        came = [move(code, (0, 2, 1, 3)) for code in codes]
         casts = []
         for code, x in zip(codes, came):
             x = after(x, casts[-1]) if casts else x
             casts.append(call(cast_kernel, shape(x.shape, bf16), [VMEM, VMEM])(code, x))
-        came = [move(x, ((1, 0), (2, 3))) for x in casts]
+        came = [move(x, (1, 0, 3, 2)) for x in casts]
         return [(casts[0], came[0])] + [(cast, after(x, casts[-1])) for cast, x in zip(casts[1:], came[1:])]
 
     def by_halving(sums):

time: 58.1 us -> 53.4 us (0.919)
  waiting for transfers between devices: 20.5 us -> 16.4 us
    ppermute x12, waiting for transfers between devices: 13.6 us -> 9.79 us  [move(): lax.ppermute(x, 'cells', [(a * CORES + i, b * CORES + i) for a, b in enum...]
where the time goes in v9:
time: 53.4 us; the launch traced here: 53.2 us
  starting transfers between devices  26 us (49%)
  waiting for transfers between devices  16.4 us (31%)
  Pallas kernels  9.81 us (18%)
  between operations  0.96 us (2%)
    ppermute x12, starting transfers between devices, move(): lax.ppermute(x, 'cells', [(a * CORES + i, b * CORES + i) for a, b in enum...  21.5 us
    ppermute x12, waiting for transfers between devices, move(): lax.ppermute(x, 'cells', [(a * CORES + i, b * CORES + i) for a, b in enum...  9.79 us
    ppermute x3, waiting for transfers between devices, to_gene(): return lax.ppermute(x, 'genes', [(i, i ^ k) for i in range(n_genes)])  4.69 us
    pallas_call x1, Pallas kernels, local(): call(dense_kernel, (shape((cells, genes), bf16), shape((rank, cells), bf1...  4.28 us
    ppermute x3, starting transfers between devices, to_gene(): return lax.ppermute(x, 'genes', [(i, i ^ k) for i in range(n_genes)])  3.67 us
    ppermute x6, waiting for transfers between devices, to_core(): return lax.ppermute(x, 'cells', [(i, i ^ 1) for i in range(n_cells)])  1.92 us
    pallas_call x3, Pallas kernels, local(): call(functools.partial(part_kernel, masks, start, not before), shape((cel...  1.48 us
    pallas_call x4, Pallas kernels, cell(): call(functools.partial(cell_kernel, k, start), shape((height, rank), f32...  1.21 us
  transfers between devices with their start and end apart: 21, of which 9 were waited for; matrix products, arithmetic and copies ran while one was open for 0% of the time, Pallas kernels for 8%

profile of v9, /device:TPU:0, one launch (start us, length us, event | category | flops | bytes accessed | tf_op | source)
XLA Modules:
  0.0 53.2 jit_solution(17720909651820024338)
XLA Ops:
  0.7 4.3 %shard_map.55 = (bf16[1024,2048]{1,0:T(8,128)(2,1)S(1)}, bf16[256,1024]{1,0:T(8,128)(2,1)S(1)}, s16[128,512]{1,0:T(8,128)(2,1)S(1)}, s16[128,1536]{1,0:T(8,128)(2,1)S(1)}) custom-call(s32[1]{0:T(128)S(6)} %copy.6.count, s32[96]{0:T(128)} %rows.1, s32[96]{0:T(128)} %cols.1, bf16[1024,256]{1,0:T(8,128)(2,1)} %sketch.1, bf16[96,128,128]{2,1,0:T(8,128)(2,1)} %tiles.1), custom_call_target="tpu_custom_call" | custom-call | tf_op jit(solution)/shard_map/pallas_call | solution.py:248
  5.0 0.5 collective-permute-start
  5.8 1.1 %collective-permute-done.got = s16[128,512]{1,0:T(8,128)(2,1)S(1)} collective-permute-done((s16[128,512]{1,0:T(8,128)(2,1)S(1)}, s16[128,512]{1,0:T(8,128)(2,1)S(1)}, u32[]{:S(2)}, u32[]{:S(2)}) %collective-permute-start) | collective-permute-done | bytes 131104 | tf_op jit(solution)/shard_map/ppermute | solution.py:238
  7.0 2.3 %collective-permute-start.5 = (s16[128,512]{1,0:T(8,128)(2,1)S(1)}, s16[128,512]{1,0:T(8,128)(2,1)S(1)}, u32[]{:S(2)}, u32[]{:S(2)}) collective-permute-start(s16[128,512]{1,0:T(8,128)(2,1)S(1)} %get-tuple-element.35), channel_id=1, source_target_pairs={{0,8},{4,12},{8,0},{12,4},{16,24},{20,28},{24,16},{28,20},{1,9},{5... | collective-permute-start | bytes 393224 | tf_op jit(solution)/shard_map/ppermute | solution.py:282
  9.3 0.6 %shard_map.58.mine = f32[128,1536]{1,0:T(8,128)S(1)} custom-call(bf16[256,1024]{1,0:T(8,128)(2,1)S(1)} %get-tuple-element.36.turned, bf16[1024,2048]{1,0:T(8,128)(2,1)S(1)} %get-tuple-element.31.dense), custom_call_target="tpu_custom_call" | custom-call | tf_op jit(solution)/shard_map/pallas_call | solution.py:263
  10.2 3.2 %collective-permute-done.5.got = s16[128,512]{1,0:T(8,128)(2,1)S(1)} collective-permute-done((s16[128,512]{1,0:T(8,128)(2,1)S(1)}, s16[128,512]{1,0:T(8,128)(2,1)S(1)}, u32[]{:S(2)}, u32[]{:S(2)}) %collective-permute-start.5) | collective-permute-done | bytes 131104 | tf_op jit(solution)/shard_map/ppermute | solution.py:282
  13.6 0.7 %collective-permute-start.9 = (s16[128,512]{1,0:T(8,128)(2,1)S(1)}, s16[128,512]{1,0:T(8,128)(2,1)S(1)}, u32[]{:S(2)}, u32[]{:S(2)}) collective-permute-start(s16[128,512]{1,0:T(8,128)(2,1)S(1)} %shard_map.60.code), channel_id=1, source_target_pairs={{0,0},{4,4},{8,16},{12,20},{16,8},{20,12},{24,24},{28,28},{1,1},{5... | collective-permute-start | bytes 393224 | tf_op jit(solution)/shard_map/ppermute | solution.py:282
  14.2 5.1 %collective-permute-start.3 = (s16[128,512]{1,0:T(8,128)(2,1)S(1)}, s16[128,512]{1,0:T(8,128)(2,1)S(1)}, u32[]{:S(2)}, u32[]{:S(2)}) collective-permute-start(s16[128,512]{1,0:T(8,128)(2,1)S(1)} %get-tuple-element.41), channel_id=1, source_target_pairs={{0,8},{4,12},{8,0},{12,4},{16,24},{20,28},{24,16},{28,20},{1,9},{5... | collective-permute-start | bytes 393224 | tf_op jit(solution)/shard_map/ppermute | solution.py:282
  19.5 0.7 %collective-permute-start.8 = (s16[128,512]{1,0:T(8,128)(2,1)S(1)}, s16[128,512]{1,0:T(8,128)(2,1)S(1)}, u32[]{:S(2)}, u32[]{:S(2)}) collective-permute-start(s16[128,512]{1,0:T(8,128)(2,1)S(1)} %shard_map.61.code), channel_id=1, source_target_pairs={{0,0},{4,4},{8,16},{12,20},{16,8},{20,12},{24,24},{28,28},{1,1},{5... | collective-permute-start | bytes 393224 | tf_op jit(solution)/shard_map/ppermute | solution.py:282
  20.3 3.7 %collective-permute-start.10 = (bf16[128,512]{1,0:T(8,128)(2,1)S(1)}, bf16[128,512]{1,0:T(8,128)(2,1)S(1)}, u32[]{:S(2)}, u32[]{:S(2)}) collective-permute-start(bf16[128,512]{1,0:T(8,128)(2,1)S(1)} %shard_map.64.cast), channel_id=1, source_target_pairs={{0,8},{4,12},{8,0},{12,4},{16,24},{20,28},{24,16},{28,20},{1,9},{5... | collective-permute-start | bytes 393224 | tf_op jit(solution)/shard_map/ppermute | solution.py:282
  24.1 0.7 %collective-permute-start.7 = (s16[128,512]{1,0:T(8,128)(2,1)S(1)}, s16[128,512]{1,0:T(8,128)(2,1)S(1)}, u32[]{:S(2)}, u32[]{:S(2)}) collective-permute-start(s16[128,512]{1,0:T(8,128)(2,1)S(1)} %shard_map.62.code), channel_id=1, source_target_pairs={{0,0},{4,4},{8,16},{12,20},{16,8},{20,12},{24,24},{28,28},{1,1},{5... | collective-permute-start | bytes 393224 | tf_op jit(solution)/shard_map/ppermute | solution.py:282
  24.7 1.5 %collective-permute-done.2.got = s16[128,512]{1,0:T(8,128)(2,1)S(1)} collective-permute-done((s16[128,512]{1,0:T(8,128)(2,1)S(1)}, s16[128,512]{1,0:T(8,128)(2,1)S(1)}, u32[]{:S(2)}, u32[]{:S(2)}) %collective-permute-start.2) | collective-permute-done | bytes 131104 | tf_op jit(solution)/shard_map/ppermute | solution.py:282
  26.3 0.7 %collective-permute-start.6 = (s16[128,512]{1,0:T(8,128)(2,1)S(1)}, s16[128,512]{1,0:T(8,128)(2,1)S(1)}, u32[]{:S(2)}, u32[]{:S(2)}) collective-permute-start(s16[128,512]{1,0:T(8,128)(2,1)S(1)} %shard_map.63.code), channel_id=1, source_target_pairs={{0,0},{4,4},{8,16},{12,20},{16,8},{20,12},{24,24},{28,28},{1,1},{5... | collective-permute-start | bytes 393224 | tf_op jit(solution)/shard_map/ppermute | solution.py:282
  27.1 4.7 %collective-permute-start.12 = (bf16[128,512]{1,0:T(8,128)(2,1)S(1)}, bf16[128,512]{1,0:T(8,128)(2,1)S(1)}, u32[]{:S(2)}, u32[]{:S(2)}) collective-permute-start(bf16[128,512]{1,0:T(8,128)(2,1)S(1)} %shard_map.65.cast), channel_id=1, source_target_pairs={{0,8},{4,12},{8,0},{12,4},{16,24},{20,28},{24,16},{28,20},{1,9},{5... | collective-permute-start | bytes 393224 | tf_op jit(solution)/shard_map/ppermute | solution.py:282
  32.0 1.0 %collective-permute-start.16 = (bf16[128,512]{1,0:T(8,128)(2,1)S(1)}, bf16[128,512]{1,0:T(8,128)(2,1)S(1)}, u32[]{:S(2)}, u32[]{:S(2)}) collective-permute-start(bf16[128,512]{1,0:T(8,128)(2,1)S(1)} %shard_map.66.cast), channel_id=1, source_target_pairs={{0,8},{4,12},{8,0},{12,4},{16,24},{20,28},{24,16},{28,20},{1,9},{5... | collective-permute-start | bytes 393224 | tf_op jit(solution)/shard_map/ppermute | solution.py:282
  33.1 1.9 %collective-permute-start.14 = (bf16[128,512]{1,0:T(8,128)(2,1)S(1)}, bf16[128,512]{1,0:T(8,128)(2,1)S(1)}, u32[]{:S(2)}, u32[]{:S(2)}) collective-permute-start(bf16[128,512]{1,0:T(8,128)(2,1)S(1)} %shard_map.67.cast), channel_id=1, source_target_pairs={{0,8},{4,12},{8,0},{12,4},{16,24},{20,28},{24,16},{28,20},{1,9},{5... | collective-permute-start | bytes 393224 | tf_op jit(solution)/shard_map/ppermute | solution.py:282
  35.0 0.6 %collective-permute-done.12.got = bf16[128,512]{1,0:T(8,128)(2,1)S(1)} collective-permute-done((bf16[128,512]{1,0:T(8,128)(2,1)S(1)}, bf16[128,512]{1,0:T(8,128)(2,1)S(1)}, u32[]{:S(2)}, u32[]{:S(2)}) %collective-permute-start.12) | collective-permute-done | bytes 131104 | tf_op jit(solution)/shard_map/ppermute | solution.py:282
  35.7 0.5 shard_map.69.refs_0_
  36.2 2.2 %collective-permute-done.16.got = bf16[128,512]{1,0:T(8,128)(2,1)S(1)} collective-permute-done((bf16[128,512]{1,0:T(8,128)(2,1)S(1)}, bf16[128,512]{1,0:T(8,128)(2,1)S(1)}, u32[]{:S(2)}, u32[]{:S(2)}) %collective-permute-start.16) | collective-permute-done | bytes 131104 | tf_op jit(solution)/shard_map/ppermute | solution.py:282
  38.5 2.2 %collective-permute-done.14.got = bf16[128,512]{1,0:T(8,128)(2,1)S(1)} collective-permute-done((bf16[128,512]{1,0:T(8,128)(2,1)S(1)}, bf16[128,512]{1,0:T(8,128)(2,1)S(1)}, u32[]{:S(2)}, u32[]{:S(2)}) %collective-permute-start.14) | collective-permute-done | bytes 131104 | tf_op jit(solution)/shard_map/ppermute | solution.py:282
  40.8 0.5 shard_map.71.refs_0_
  41.4 0.5 shard_map.75.refs_0_
  41.9 0.8 %collective-permute-done.15.refs_1_ = bf16[128,512]{1,0:T(8,128)(2,1)S(1)} collective-permute-done((bf16[128,512]{1,0:T(8,128)(2,1)S(1)}, bf16[128,512]{1,0:T(8,128)(2,1)S(1)}, u32[]{:S(2)}, u32[]{:S(2)}) %collective-permute-start.15) | collective-permute-done | bytes 131104 | tf_op jit(solution)/shard_map/ppermute | solution.py:238
  42.8 0.3 shard_map.77
  43.1 1.7 %collective-permute-start.18 = (s16[256,256]{1,0:T(8,128)(2,1)S(1)}, s16[256,256]{1,0:T(8,128)(2,1)S(1)}, u32[]{:S(2)}, u32[]{:S(2)}) collective-permute-start(s16[256,256]{1,0:T(8,128)(2,1)S(1)} %shard_map.77), channel_id=1, source_target_pairs={{0,3},{1,2},{2,1},{3,0},{4,7},{5,6},{6,5},{7,4},{8,11},{9,10},{10,... | collective-permute-start | bytes 393224 | tf_op jit(solution)/shard_map/ppermute | solution.py:244
  44.7 0.3 shard_map.79
  45.1 0.5 collective-permute-start.19
  45.6 0.3 shard_map.81
  45.9 1.5 %collective-permute-start.20 = (s16[256,256]{1,0:T(8,128)(2,1)S(1)}, s16[256,256]{1,0:T(8,128)(2,1)S(1)}, u32[]{:S(2)}, u32[]{:S(2)}) collective-permute-start(s16[256,256]{1,0:T(8,128)(2,1)S(1)} %shard_map.81), channel_id=1, source_target_pairs={{0,1},{1,0},{2,3},{3,2},{4,5},{5,4},{6,7},{7,6},{8,9},{9,8},{10,11... | collective-permute-start | bytes 393224 | tf_op jit(solution)/shard_map/ppermute | solution.py:244
  47.7 2.3 %collective-permute-done.18.got = s16[256,256]{1,0:T(8,128)(2,1)S(1)} collective-permute-done((s16[256,256]{1,0:T(8,128)(2,1)S(1)}, s16[256,256]{1,0:T(8,128)(2,1)S(1)}, u32[]{:S(2)}, u32[]{:S(2)}) %collective-permute-start.18) | collective-permute-done | bytes 131104 | tf_op jit(solution)/shard_map/ppermute | solution.py:244
  50.1 2.4 %collective-permute-done.19.got = s16[256,256]{1,0:T(8,128)(2,1)S(1)} collective-permute-done((s16[256,256]{1,0:T(8,128)(2,1)S(1)}, s16[256,256]{1,0:T(8,128)(2,1)S(1)}, u32[]{:S(2)}, u32[]{:S(2)}) %collective-permute-start.19) | collective-permute-done | bytes 131104 | tf_op jit(solution)/shard_map/ppermute | solution.py:244
  52.5 0.7 %shard_map.82 = f32[256,256]{1,0:T(8,128)} custom-call(f32[256,256]{1,0:T(8,128)S(1)} %shard_map.80.total, s16[256,256]{1,0:T(8,128)(2,1)S(1)} %collective-permute-done.20.got), custom_call_target="tpu_custom_call" | custom-call | bytes 16777216 | tf_op jit(solution)/shard_map/pallas_call | solution.py:364
  (38 shorter events, 2.3 us)
Async XLA Ops:
  4.9 5.0 %collective-permute-start.1 = (s16[128,1536]{1,0:T(8,128)(2,1)S(1)}, s16[128,1536]{1,0:T(8,128)(2,1)S(1)}, u32[]{:S(2)}, u32[]{:S(2)}) collective-permute-start(s16[128,1536]{1,0:T(8,128)(2,1)S(1)} %get-tuple-element.37), channel_id=1, source_target_pairs={{0,4},{4,0},{8,12},{12,8},{16,20},{20,16},{24,28},{28,24},{1,5},{5... | collective-permute-start | bytes 1179656 | tf_op jit(solution)/shard_map/ppermute | solution.py:238
  5.0 1.9 %collective-permute-start = (s16[128,512]{1,0:T(8,128)(2,1)S(1)}, s16[128,512]{1,0:T(8,128)(2,1)S(1)}, u32[]{:S(2)}, u32[]{:S(2)}) collective-permute-start(s16[128,512]{1,0:T(8,128)(2,1)S(1)} %get-tuple-element.33), channel_id=1, source_target_pairs={{0,4},{4,0},{8,12},{12,8},{16,20},{20,16},{24,28},{28,24},{1,5},{5... | collective-permute-start | bytes 393224 | tf_op jit(solution)/shard_map/ppermute | solution.py:238
  7.0 6.4 %collective-permute-start.5 = (s16[128,512]{1,0:T(8,128)(2,1)S(1)}, s16[128,512]{1,0:T(8,128)(2,1)S(1)}, u32[]{:S(2)}, u32[]{:S(2)}) collective-permute-start(s16[128,512]{1,0:T(8,128)(2,1)S(1)} %get-tuple-element.35), channel_id=1, source_target_pairs={{0,8},{4,12},{8,0},{12,4},{16,24},{20,28},{24,16},{28,20},{1,9},{5... | collective-permute-start | bytes 393224 | tf_op jit(solution)/shard_map/ppermute | solution.py:282
  10.2 9.2 %collective-permute-start.4 = (s16[128,512]{1,0:T(8,128)(2,1)S(1)}, s16[128,512]{1,0:T(8,128)(2,1)S(1)}, u32[]{:S(2)}, u32[]{:S(2)}) collective-permute-start(s16[128,512]{1,0:T(8,128)(2,1)S(1)} %get-tuple-element.43), channel_id=1, source_target_pairs={{0,8},{4,12},{8,0},{12,4},{16,24},{20,28},{24,16},{28,20},{1,9},{5... | collective-permute-start | bytes 393224 | tf_op jit(solution)/shard_map/ppermute | solution.py:282
  13.6 6.6 %collective-permute-start.9 = (s16[128,512]{1,0:T(8,128)(2,1)S(1)}, s16[128,512]{1,0:T(8,128)(2,1)S(1)}, u32[]{:S(2)}, u32[]{:S(2)}) collective-permute-start(s16[128,512]{1,0:T(8,128)(2,1)S(1)} %shard_map.60.code), channel_id=1, source_target_pairs={{0,0},{4,4},{8,16},{12,20},{16,8},{20,12},{24,24},{28,28},{1,1},{5... | collective-permute-start | bytes 393224 | tf_op jit(solution)/shard_map/ppermute | solution.py:282
  14.2 9.7 %collective-permute-start.3 = (s16[128,512]{1,0:T(8,128)(2,1)S(1)}, s16[128,512]{1,0:T(8,128)(2,1)S(1)}, u32[]{:S(2)}, u32[]{:S(2)}) collective-permute-start(s16[128,512]{1,0:T(8,128)(2,1)S(1)} %get-tuple-element.41), channel_id=1, source_target_pairs={{0,8},{4,12},{8,0},{12,4},{16,24},{20,28},{24,16},{28,20},{1,9},{5... | collective-permute-start | bytes 393224 | tf_op jit(solution)/shard_map/ppermute | solution.py:282
  19.3 6.9 %collective-permute-start.2 = (s16[128,512]{1,0:T(8,128)(2,1)S(1)}, s16[128,512]{1,0:T(8,128)(2,1)S(1)}, u32[]{:S(2)}, u32[]{:S(2)}) collective-permute-start(s16[128,512]{1,0:T(8,128)(2,1)S(1)} %get-tuple-element.39), channel_id=1, source_target_pairs={{0,8},{4,12},{8,0},{12,4},{16,24},{20,28},{24,16},{28,20},{1,9},{5... | collective-permute-start | bytes 393224 | tf_op jit(solution)/shard_map/ppermute | solution.py:282
  19.5 7.5 %collective-permute-start.8 = (s16[128,512]{1,0:T(8,128)(2,1)S(1)}, s16[128,512]{1,0:T(8,128)(2,1)S(1)}, u32[]{:S(2)}, u32[]{:S(2)}) collective-permute-start(s16[128,512]{1,0:T(8,128)(2,1)S(1)} %shard_map.61.code), channel_id=1, source_target_pairs={{0,0},{4,4},{8,16},{12,20},{16,8},{20,12},{24,24},{28,28},{1,1},{5... | collective-permute-start | bytes 393224 | tf_op jit(solution)/shard_map/ppermute | solution.py:282
  20.3 11.6 %collective-permute-start.10 = (bf16[128,512]{1,0:T(8,128)(2,1)S(1)}, bf16[128,512]{1,0:T(8,128)(2,1)S(1)}, u32[]{:S(2)}, u32[]{:S(2)}) collective-permute-start(bf16[128,512]{1,0:T(8,128)(2,1)S(1)} %shard_map.64.cast), channel_id=1, source_target_pairs={{0,8},{4,12},{8,0},{12,4},{16,24},{20,28},{24,16},{28,20},{1,9},{5... | collective-permute-start | bytes 393224 | tf_op jit(solution)/shard_map/ppermute | solution.py:282
  24.1 7.8 %collective-permute-start.7 = (s16[128,512]{1,0:T(8,128)(2,1)S(1)}, s16[128,512]{1,0:T(8,128)(2,1)S(1)}, u32[]{:S(2)}, u32[]{:S(2)}) collective-permute-start(s16[128,512]{1,0:T(8,128)(2,1)S(1)} %shard_map.62.code), channel_id=1, source_target_pairs={{0,0},{4,4},{8,16},{12,20},{16,8},{20,12},{24,24},{28,28},{1,1},{5... | collective-permute-start | bytes 393224 | tf_op jit(solution)/shard_map/ppermute | solution.py:282
  26.3 6.7 %collective-permute-start.6 = (s16[128,512]{1,0:T(8,128)(2,1)S(1)}, s16[128,512]{1,0:T(8,128)(2,1)S(1)}, u32[]{:S(2)}, u32[]{:S(2)}) collective-permute-start(s16[128,512]{1,0:T(8,128)(2,1)S(1)} %shard_map.63.code), channel_id=1, source_target_pairs={{0,0},{4,4},{8,16},{12,20},{16,8},{20,12},{24,24},{28,28},{1,1},{5... | collective-permute-start | bytes 393224 | tf_op jit(solution)/shard_map/ppermute | solution.py:282
  27.1 8.5 %collective-permute-start.12 = (bf16[128,512]{1,0:T(8,128)(2,1)S(1)}, bf16[128,512]{1,0:T(8,128)(2,1)S(1)}, u32[]{:S(2)}, u32[]{:S(2)}) collective-permute-start(bf16[128,512]{1,0:T(8,128)(2,1)S(1)} %shard_map.65.cast), channel_id=1, source_target_pairs={{0,8},{4,12},{8,0},{12,4},{16,24},{20,28},{24,16},{28,20},{1,9},{5... | collective-permute-start | bytes 393224 | tf_op jit(solution)/shard_map/ppermute | solution.py:282
  31.8 3.9 %collective-permute-start.11 = (bf16[128,512]{1,0:T(8,128)(2,1)S(1)}, bf16[128,512]{1,0:T(8,128)(2,1)S(1)}, u32[]{:S(2)}, u32[]{:S(2)}) collective-permute-start(bf16[128,512]{1,0:T(8,128)(2,1)S(1)} %shard_map.68.refs_0_), channel_id=1, source_target_pairs={{0,4},{4,0},{8,12},{12,8},{16,20},{20,16},{24,28},{28,24},{1,5},{5... | collective-permute-start | bytes 393224 | tf_op jit(solution)/shard_map/ppermute | solution.py:238
  32.0 6.4 %collective-permute-start.16 = (bf16[128,512]{1,0:T(8,128)(2,1)S(1)}, bf16[128,512]{1,0:T(8,128)(2,1)S(1)}, u32[]{:S(2)}, u32[]{:S(2)}) collective-permute-start(bf16[128,512]{1,0:T(8,128)(2,1)S(1)} %shard_map.66.cast), channel_id=1, source_target_pairs={{0,8},{4,12},{8,0},{12,4},{16,24},{20,28},{24,16},{28,20},{1,9},{5... | collective-permute-start | bytes 393224 | tf_op jit(solution)/shard_map/ppermute | solution.py:282
  33.1 7.7 %collective-permute-start.14 = (bf16[128,512]{1,0:T(8,128)(2,1)S(1)}, bf16[128,512]{1,0:T(8,128)(2,1)S(1)}, u32[]{:S(2)}, u32[]{:S(2)}) collective-permute-start(bf16[128,512]{1,0:T(8,128)(2,1)S(1)} %shard_map.67.cast), channel_id=1, source_target_pairs={{0,8},{4,12},{8,0},{12,4},{16,24},{20,28},{24,16},{28,20},{1,9},{5... | collective-permute-start | bytes 393224 | tf_op jit(solution)/shard_map/ppermute | solution.py:282
  35.6 5.1 %collective-permute-start.13 = (bf16[128,512]{1,0:T(8,128)(2,1)S(1)}, bf16[128,512]{1,0:T(8,128)(2,1)S(1)}, u32[]{:S(2)}, u32[]{:S(2)}) collective-permute-start(bf16[128,512]{1,0:T(8,128)(2,1)S(1)} %shard_map.70.refs_1_), channel_id=1, source_target_pairs={{0,4},{4,0},{8,12},{12,8},{16,20},{20,16},{24,28},{28,24},{1,5},{5... | collective-permute-start | bytes 393224 | tf_op jit(solution)/shard_map/ppermute | solution.py:238
  38.5 2.9 %collective-permute-start.17 = (bf16[128,512]{1,0:T(8,128)(2,1)S(1)}, bf16[128,512]{1,0:T(8,128)(2,1)S(1)}, u32[]{:S(2)}, u32[]{:S(2)}) collective-permute-start(bf16[128,512]{1,0:T(8,128)(2,1)S(1)} %shard_map.74.refs_1_), channel_id=1, source_target_pairs={{0,4},{4,0},{8,12},{12,8},{16,20},{20,16},{24,28},{28,24},{1,5},{5... | collective-permute-start | bytes 393224 | tf_op jit(solution)/shard_map/ppermute | solution.py:238
  41.3 1.4 %collective-permute-start.15 = (bf16[128,512]{1,0:T(8,128)(2,1)S(1)}, bf16[128,512]{1,0:T(8,128)(2,1)S(1)}, u32[]{:S(2)}, u32[]{:S(2)}) collective-permute-start(bf16[128,512]{1,0:T(8,128)(2,1)S(1)} %shard_map.72.refs_0_), channel_id=1, source_target_pairs={{0,4},{4,0},{8,12},{12,8},{16,20},{20,16},{24,28},{28,24},{1,5},{5... | collective-permute-start | bytes 393224 | tf_op jit(solution)/shard_map/ppermute | solution.py:238
  43.1 6.9 %collective-permute-start.18 = (s16[256,256]{1,0:T(8,128)(2,1)S(1)}, s16[256,256]{1,0:T(8,128)(2,1)S(1)}, u32[]{:S(2)}, u32[]{:S(2)}) collective-permute-start(s16[256,256]{1,0:T(8,128)(2,1)S(1)} %shard_map.77), channel_id=1, source_target_pairs={{0,3},{1,2},{2,1},{3,0},{4,7},{5,6},{6,5},{7,4},{8,11},{9,10},{10,... | collective-permute-start | bytes 393224 | tf_op jit(solution)/shard_map/ppermute | solution.py:244
  45.1 7.3 %collective-permute-start.19 = (s16[256,256]{1,0:T(8,128)(2,1)S(1)}, s16[256,256]{1,0:T(8,128)(2,1)S(1)}, u32[]{:S(2)}, u32[]{:S(2)}) collective-permute-start(s16[256,256]{1,0:T(8,128)(2,1)S(1)} %shard_map.79), channel_id=1, source_target_pairs={{0,2},{1,3},{2,0},{3,1},{4,6},{5,7},{6,4},{7,5},{8,10},{9,11},{10,... | collective-permute-start | bytes 393224 | tf_op jit(solution)/shard_map/ppermute | solution.py:244
  45.9 6.5 %collective-permute-start.20 = (s16[256,256]{1,0:T(8,128)(2,1)S(1)}, s16[256,256]{1,0:T(8,128)(2,1)S(1)}, u32[]{:S(2)}, u32[]{:S(2)}) collective-permute-start(s16[256,256]{1,0:T(8,128)(2,1)S(1)} %shard_map.81), channel_id=1, source_target_pairs={{0,1},{1,0},{2,3},{3,2},{4,5},{5,4},{6,7},{7,6},{8,9},{9,8},{10,11... | collective-permute-start | bytes 393224 | tf_op jit(solution)/shard_map/ppermute | solution.py:244

commit v10 on v9

--- a/solution.py
+++ b/solution.py
@@ -10,7 +10,7 @@
 GENE_BLOCKS = 16
 CORES = 2
 LANES = 128
-PARTS = (1, 1, 1, 1)
+PARTS = (3, 3, 2)
 MIB = 1 << 20
 
 VMEM = pl.BlockSpec(memory_space=pltpu.VMEM)
@@ -108,7 +108,7 @@
     core, _ = core_and_chip()
     rows, width = out.shape
     left = turned[block(core ^ other, rows), :]
-    step = min(width, 512)
+    step = 512 if width % 512 == 0 else 256
     for j in range(0, width, step):
         part = jnp.dot(left, dense[:, start + j : start + j + step], preferred_element_type=f32)
         if other:
@@ -138,29 +138,6 @@
         start += out.shape[1]
 
 
-def both_kernel(mine, got, *outs):
-    start = 0
-    for keep, send in zip(outs[::2], outs[1::2]):
-        cut = slice(start, start + keep.shape[1])
-        total = mine[:, cut] + decode(got[:, cut])
-        keep[...] = total
-        encode(total, send)
-        start += keep.shape[1]
-
-
-def pick_kernel(cast, got, out):
-    _, chip = core_and_chip()
-    middle = (chip == 1) | (chip == 2)
-
-    @pl.when(middle)
-    def _():
-        out[...] = cast[...]
-
-    @pl.when(jnp.logical_not(middle))
-    def _():
-        out[...] = got[...]
-
-
 def cast_kernel(code, got, out):
     out[...] = (decode(code[...]) + decode(got[...])).astype(bf16)
 
@@ -230,8 +207,6 @@
     rows = rank // CORES
     height = cells // n_genes
     shape = jax.ShapeDtypeStruct
-    chips = n_cells // CORES
-    hub = chips == 4
     cuts = cuts_of(genes, bits)
 
     def to_core(x):
@@ -266,33 +241,12 @@
         return lax.optimization_barrier((x, *others))[0]
 
     def add_step(bit, kept, came, widths):
-        if hub and bit == 0:
-            outs = [shape((rows, width), kind) for width in widths for kind in (f32, i16)]
-            done = call(both_kernel, tuple(outs), [VMEM, VMEM])(kept, came)
-            return [done[i : i + 2] for i in range(0, len(done), 2)]
         if bit < bits - 1:
             outs = [shape((rows, width // 2), kind) for width in widths for kind in (f32, i16)]
             done = call(functools.partial(add_kernel, bit), tuple(outs), [VMEM, VMEM])(kept, came)
             return [done[i : i + 2] for i in range(0, len(done), 2)]
         done = call(code_kernel, tuple(shape((rows, width), i16) for width in widths), [VMEM, VMEM])(kept, came)
         return [done[i : i + 1] for i in range(len(done))]
-
-    def through_hubs(sums):
-        def move(x, to):
-            return lax.ppermute(x, "cells", [(a * CORES + i, b * CORES + i) for a, b in enumerate(to) for i in range(CORES)])
-
-        came = [move(code, (1, 0, 3, 2)) for _, code in sums]
-        codes = []
-        for (kept, _), x in zip(sums, came):
-            x = after(x, codes[-1]) if codes else x
-            codes += call(code_kernel, (shape(x.shape, i16),), [VMEM, VMEM])(kept, x)
-        came = [move(code, (0, 2, 1, 3)) for code in codes]
-        casts = []
-        for code, x in zip(codes, came):
-            x = after(x, casts[-1]) if casts else x
-            casts.append(call(cast_kernel, shape(x.shape, bf16), [VMEM, VMEM])(code, x))
-        came = [move(x, (1, 0, 3, 2)) for x in casts]
-        return [(casts[0], came[0])] + [(cast, after(x, casts[-1])) for cast, x in zip(casts[1:], came[1:])]
 
     def by_halving(sums):
         widths = [sum_[0].shape[1] for sum_ in sums]
@@ -324,17 +278,11 @@
     sums = add_step(0, half_of(0, 0, turned, first), got[0], widths[:1])
     if rest:
         sums += add_step(0, half_of(0, first, after(turned, *sums[0]), rest), got[1], widths[1:])
-    if hub:
-        sides = through_hubs(sums)
-        masks = [0]
-    else:
-        masks, sides = by_halving(sums)
+    masks, sides = by_halving(sums)
     totals = []
     for i, ((start, width), pieces) in enumerate(zip(cuts, sides)):
         if i >= 2:
             pieces = [after(x, totals[i - 2]) for x in pieces]
-        if hub:
-            pieces = [call(pick_kernel, shape(pieces[0].shape, bf16), [VMEM, VMEM])(*pieces)]
         pieces = pieces + [to_core(x) for x in pieces]
         if i == len(cuts) - 1:
             break

time: 53.4 us -> 47.2 us (0.88)
  starting transfers between devices: 26 us -> 19 us
  waiting for transfers between devices: 16.4 us -> 17.7 us
  Pallas kernels: 9.81 us -> 9.24 us
    ppermute x12 -> x9, starting transfers between devices: 21.5 us -> 13.9 us  [to_chip(): lax.ppermute(x, 'cells', [(i, i ^ CORES << bit) for i in range(n_cells)])]
    ppermute x12 -> x9, waiting for transfers between devices: 9.79 us -> 10.7 us  [to_chip(): lax.ppermute(x, 'cells', [(i, i ^ CORES << bit) for i in range(n_cells)])]
    ppermute x6 -> x8, starting transfers between devices: 0.85 us -> 1.38 us  [to_core(): return lax.ppermute(x, 'cells', [(i, i ^ 1) for i in range(n_cells)])]
    pallas_call x14 -> x8, Pallas kernels: 1.09 us -> 0.72 us  [the longest x2 0.34 us: add_step(): call(functools.partial(add_kernel, bit), tuple(outs), [VMEM, VMEM])]
    ppermute x6 -> x8, waiting for transfers between devices: 1.92 us -> 2.27 us  [to_core(): return lax.ppermute(x, 'cells', [(i, i ^ 1) for i in range(n_cells)])]
    pallas_call x3 -> x2, Pallas kernels: 1.48 us -> 1.28 us  [local(): call(functools.partial(part_kernel, masks, start, not before), shape((cel...]
  transfers between devices with their start and end apart: 21 -> 20, of which waited for: 9 -> 12; matrix products, arithmetic and copies ran while one was open for 0% -> 0% of each run, Pallas kernels for 8% -> 7%
where the time goes in v10:
time: 47.2 us; the launch traced here: 46.8 us
  starting transfers between devices  19 us (40%)
  waiting for transfers between devices  17.7 us (38%)
  Pallas kernels  9.24 us (20%)
  between operations  0.85 us (2%)
    ppermute x9, starting transfers between devices, to_chip(): lax.ppermute(x, 'cells', [(i, i ^ CORES << bit) for i in range(n_cells)])  13.9 us
    ppermute x9, waiting for transfers between devices, to_chip(): lax.ppermute(x, 'cells', [(i, i ^ CORES << bit) for i in range(n_cells)])  10.7 us
    ppermute x3, waiting for transfers between devices, to_gene(): return lax.ppermute(x, 'genes', [(i, i ^ k) for i in range(n_genes)])  4.7 us
    pallas_call x1, Pallas kernels, local(): call(dense_kernel, (shape((cells, genes), bf16), shape((rank, cells), bf1...  4.27 us
    ppermute x3, starting transfers between devices, to_gene(): return lax.ppermute(x, 'genes', [(i, i ^ k) for i in range(n_genes)])  3.68 us
    ppermute x8, waiting for transfers between devices, to_core(): return lax.ppermute(x, 'cells', [(i, i ^ 1) for i in range(n_cells)])  2.27 us
    ppermute x8, starting transfers between devices, to_core(): return lax.ppermute(x, 'cells', [(i, i ^ 1) for i in range(n_cells)])  1.38 us
    pallas_call x2, Pallas kernels, local(): call(functools.partial(part_kernel, masks, start, not before), shape((cel...  1.28 us
  transfers between devices with their start and end apart: 20, of which 12 were waited for; matrix products, arithmetic and copies ran while one was open for 0% of the time, Pallas kernels for 7%

profile of v10, /device:TPU:0, one launch (start us, length us, event | category | flops | bytes accessed | tf_op | source)
XLA Modules:
  0.0 46.8 jit_solution(17146144845277445821)
XLA Ops:
  0.7 4.3 %shard_map.55 = (bf16[1024,2048]{1,0:T(8,128)(2,1)S(1)}, bf16[256,1024]{1,0:T(8,128)(2,1)S(1)}, s16[128,768]{1,0:T(8,128)(2,1)S(1)}, s16[128,1280]{1,0:T(8,128)(2,1)S(1)}) custom-call(s32[1]{0:T(128)S(6)} %copy.6.count, s32[96]{0:T(128)} %rows.1, s32[96]{0:T(128)} %cols.1, bf16[1024,256]{1,0:T(8,128)(2,1)} %sketch.1, bf16[96,128,128]{2,1,0:T(8,128)(2,1)} %tiles.1), custom_call_target="tpu_custom_call" | custom-call | tf_op jit(solution)/shard_map/pallas_call | solution.py:223
  5.0 0.5 %collective-permute-start = (s16[128,768]{1,0:T(8,128)(2,1)S(1)}, s16[128,768]{1,0:T(8,128)(2,1)S(1)}, u32[]{:S(2)}, u32[]{:S(2)}) collective-permute-start(s16[128,768]{1,0:T(8,128)(2,1)S(1)} %get-tuple-element.26), channel_id=1, source_target_pairs={{0,4},{4,0},{8,12},{12,8},{16,20},{20,16},{24,28},{28,24},{1,5},{5... | collective-permute-start | bytes 589832 | tf_op jit(solution)/shard_map/ppermute | solution.py:213
  5.5 0.4 shard_map.56.mine
  5.9 1.0 %collective-permute-done.got = s16[128,768]{1,0:T(8,128)(2,1)S(1)} collective-permute-done((s16[128,768]{1,0:T(8,128)(2,1)S(1)}, s16[128,768]{1,0:T(8,128)(2,1)S(1)}, u32[]{:S(2)}, u32[]{:S(2)}) %collective-permute-start) | collective-permute-done | bytes 196640 | tf_op jit(solution)/shard_map/ppermute | solution.py:213
  7.0 2.4 %collective-permute-start.4 = (s16[128,384]{1,0:T(8,128)(2,1)S(1)}, s16[128,384]{1,0:T(8,128)(2,1)S(1)}, u32[]{:S(2)}, u32[]{:S(2)}) collective-permute-start(s16[128,384]{1,0:T(8,128)(2,1)S(1)} %get-tuple-element.28), channel_id=1, source_target_pairs={{0,8},{4,12},{8,0},{12,4},{16,24},{20,28},{24,16},{28,20},{1,9},{5... | collective-permute-start | bytes 294920 | tf_op jit(solution)/shard_map/ppermute | solution.py:216
  9.5 0.5 %shard_map.58.mine = f32[128,1280]{1,0:T(8,128)S(1)} custom-call(bf16[256,1024]{1,0:T(8,128)(2,1)S(1)} %get-tuple-element.29.turned, bf16[1024,2048]{1,0:T(8,128)(2,1)S(1)} %get-tuple-element.24.dense), custom_call_target="tpu_custom_call" | custom-call | tf_op jit(solution)/shard_map/pallas_call | solution.py:238
  10.3 2.3 %collective-permute-done.4.got = s16[128,384]{1,0:T(8,128)(2,1)S(1)} collective-permute-done((s16[128,384]{1,0:T(8,128)(2,1)S(1)}, s16[128,384]{1,0:T(8,128)(2,1)S(1)}, u32[]{:S(2)}, u32[]{:S(2)}) %collective-permute-start.4) | collective-permute-done | bytes 98336 | tf_op jit(solution)/shard_map/ppermute | solution.py:216
  12.7 2.7 %collective-permute-start.7 = (s16[128,384]{1,0:T(8,128)(2,1)S(1)}, s16[128,384]{1,0:T(8,128)(2,1)S(1)}, u32[]{:S(2)}, u32[]{:S(2)}) collective-permute-start(s16[128,384]{1,0:T(8,128)(2,1)S(1)} %shard_map.60.code), channel_id=1, source_target_pairs={{0,16},{4,20},{8,24},{12,28},{16,0},{20,4},{24,8},{28,12},{1,17},{... | collective-permute-start | bytes 294920 | tf_op jit(solution)/shard_map/ppermute | solution.py:216
  15.5 2.5 %collective-permute-start.6 = (s16[128,384]{1,0:T(8,128)(2,1)S(1)}, s16[128,384]{1,0:T(8,128)(2,1)S(1)}, u32[]{:S(2)}, u32[]{:S(2)}) collective-permute-start(s16[128,384]{1,0:T(8,128)(2,1)S(1)} %shard_map.61.code), channel_id=1, source_target_pairs={{0,16},{4,20},{8,24},{12,28},{16,0},{20,4},{24,8},{28,12},{1,17},{... | collective-permute-start | bytes 294920 | tf_op jit(solution)/shard_map/ppermute | solution.py:216
  18.0 1.2 %collective-permute-start.2 = (s16[128,256]{1,0:T(8,128)(2,1)S(1)}, s16[128,256]{1,0:T(8,128)(2,1)S(1)}, u32[]{:S(2)}, u32[]{:S(2)}) collective-permute-start(s16[128,256]{1,0:T(8,128)(2,1)S(1)} %get-tuple-element.32), channel_id=1, source_target_pairs={{0,8},{4,12},{8,0},{12,4},{16,24},{20,28},{24,16},{28,20},{1,9},{5... | collective-permute-start | bytes 196616 | tf_op jit(solution)/shard_map/ppermute | solution.py:216
  19.2 2.9 %collective-permute-done.7.got = s16[128,384]{1,0:T(8,128)(2,1)S(1)} collective-permute-done((s16[128,384]{1,0:T(8,128)(2,1)S(1)}, s16[128,384]{1,0:T(8,128)(2,1)S(1)}, u32[]{:S(2)}, u32[]{:S(2)}) %collective-permute-start.7) | collective-permute-done | bytes 98336 | tf_op jit(solution)/shard_map/ppermute | solution.py:216
  22.2 1.3 %collective-permute-start.8 = (bf16[128,384]{1,0:T(8,128)(2,1)S(1)}, bf16[128,384]{1,0:T(8,128)(2,1)S(1)}, u32[]{:S(2)}, u32[]{:S(2)}) collective-permute-start(bf16[128,384]{1,0:T(8,128)(2,1)S(1)} %shard_map.63.refs_0_), channel_id=1, source_target_pairs={{0,8},{4,12},{8,0},{12,4},{16,24},{20,28},{24,16},{28,20},{1,9},{5... | collective-permute-start | bytes 294920 | tf_op jit(solution)/shard_map/ppermute | solution.py:216
  23.5 1.1 %collective-permute-done.2.got = s16[128,256]{1,0:T(8,128)(2,1)S(1)} collective-permute-done((s16[128,256]{1,0:T(8,128)(2,1)S(1)}, s16[128,256]{1,0:T(8,128)(2,1)S(1)}, u32[]{:S(2)}, u32[]{:S(2)}) %collective-permute-start.2) | collective-permute-done | bytes 65568 | tf_op jit(solution)/shard_map/ppermute | solution.py:216
  24.7 2.3 %collective-permute-start.5 = (s16[128,256]{1,0:T(8,128)(2,1)S(1)}, s16[128,256]{1,0:T(8,128)(2,1)S(1)}, u32[]{:S(2)}, u32[]{:S(2)}) collective-permute-start(s16[128,256]{1,0:T(8,128)(2,1)S(1)} %shard_map.62.code), channel_id=1, source_target_pairs={{0,16},{4,20},{8,24},{12,28},{16,0},{20,4},{24,8},{28,12},{1,17},{... | collective-permute-start | bytes 196616 | tf_op jit(solution)/shard_map/ppermute | solution.py:216
  27.3 0.3 collective-permute-done.8.refs_1_
  27.8 2.2 %collective-permute-done.5.got = s16[128,256]{1,0:T(8,128)(2,1)S(1)} collective-permute-done((s16[128,256]{1,0:T(8,128)(2,1)S(1)}, s16[128,256]{1,0:T(8,128)(2,1)S(1)}, u32[]{:S(2)}, u32[]{:S(2)}) %collective-permute-start.5) | collective-permute-done | bytes 65568 | tf_op jit(solution)/shard_map/ppermute | solution.py:216
  30.0 1.3 %collective-permute-start.11 = (bf16[128,256]{1,0:T(8,128)(2,1)S(1)}, bf16[128,256]{1,0:T(8,128)(2,1)S(1)}, u32[]{:S(2)}, u32[]{:S(2)}) collective-permute-start(bf16[128,256]{1,0:T(8,128)(2,1)S(1)} %shard_map.65.refs_0_), channel_id=1, source_target_pairs={{0,8},{4,12},{8,0},{12,4},{16,24},{20,28},{24,16},{28,20},{1,9},{5... | collective-permute-start | bytes 196616 | tf_op jit(solution)/shard_map/ppermute | solution.py:216
  31.4 1.1 %collective-permute-done.12.refs_2_ = bf16[128,384]{1,0:T(8,128)(2,1)S(1)} collective-permute-done((bf16[128,384]{1,0:T(8,128)(2,1)S(1)}, bf16[128,384]{1,0:T(8,128)(2,1)S(1)}, u32[]{:S(2)}, u32[]{:S(2)}) %collective-permute-start.12) | collective-permute-done | bytes 98336 | tf_op jit(solution)/shard_map/ppermute | solution.py:216
  32.5 0.6 %shard_map.66.refs_0_ = f32[1024,256]{1,0:T(8,128)S(1)} custom-call(bf16[1024,2048]{1,0:T(8,128)(2,1)S(1)} %get-tuple-element.24.dense, bf16[128,384]{1,0:T(8,128)(2,1)S(1)} %shard_map.63.refs_0_, bf16[128,384]{1,0:T(8,128)(2,1)S(1)} %collective-permute-done.8.refs_1_, bf16[128,384]{1,0:T(8,128)(2,1)S(1)} %collective-permute-done.9.refs_2_, ...), custom_call_target="tpu_custom_call" | custom-call | tf_op jit(solution)/shard_map/pallas_call | solution.py:291
  33.1 0.6 %collective-permute-start.13 = (bf16[128,256]{1,0:T(8,128)(2,1)S(1)}, bf16[128,256]{1,0:T(8,128)(2,1)S(1)}, u32[]{:S(2)}, u32[]{:S(2)}) collective-permute-start(bf16[128,256]{1,0:T(8,128)(2,1)S(1)} %shard_map.65.refs_0_), channel_id=1, source_target_pairs={{0,4},{4,0},{8,12},{12,8},{16,20},{20,16},{24,28},{28,24},{1,5},{5... | collective-permute-start | bytes 196616 | tf_op jit(solution)/shard_map/ppermute | solution.py:213
  33.7 0.6 %collective-permute-done.11.refs_1_ = bf16[128,256]{1,0:T(8,128)(2,1)S(1)} collective-permute-done((bf16[128,256]{1,0:T(8,128)(2,1)S(1)}, bf16[128,256]{1,0:T(8,128)(2,1)S(1)}, u32[]{:S(2)}, u32[]{:S(2)}) %collective-permute-start.11) | collective-permute-done | bytes 65568 | tf_op jit(solution)/shard_map/ppermute | solution.py:216
  34.6 1.0 %collective-permute-done.14.refs_3_ = bf16[128,256]{1,0:T(8,128)(2,1)S(1)} collective-permute-done((bf16[128,256]{1,0:T(8,128)(2,1)S(1)}, bf16[128,256]{1,0:T(8,128)(2,1)S(1)}, u32[]{:S(2)}, u32[]{:S(2)}) %collective-permute-start.14) | collective-permute-done | bytes 65568 | tf_op jit(solution)/shard_map/ppermute | solution.py:213
  35.7 0.6 %shard_map.68.refs_0_ = f32[1024,256]{1,0:T(8,128)S(1)} custom-call(bf16[1024,2048]{1,0:T(8,128)(2,1)S(1)} %get-tuple-element.24.dense, f32[1024,256]{1,0:T(8,128)S(1)} %shard_map.66.refs_0_, bf16[128,384]{1,0:T(8,128)(2,1)S(1)} %shard_map.64.refs_1_, bf16[128,384]{1,0:T(8,128)(2,1)S(1)} %collective-permute-done.12.refs_2_, ...), custom_call_target="tpu_custom_call" | custom-call | tf_op jit(solution)/shard_map/pallas_call | solution.py:291
  36.3 0.3 shard_map.70
  36.6 1.9 %collective-permute-start.17 = (s16[256,256]{1,0:T(8,128)(2,1)S(1)}, s16[256,256]{1,0:T(8,128)(2,1)S(1)}, u32[]{:S(2)}, u32[]{:S(2)}) collective-permute-start(s16[256,256]{1,0:T(8,128)(2,1)S(1)} %shard_map.70), channel_id=1, source_target_pairs={{0,3},{1,2},{2,1},{3,0},{4,7},{5,6},{6,5},{7,4},{8,11},{9,10},{10,... | collective-permute-start | bytes 393224 | tf_op jit(solution)/shard_map/ppermute | solution.py:219
  38.6 0.3 shard_map.72
  38.9 1.0 %collective-permute-start.18 = (s16[256,256]{1,0:T(8,128)(2,1)S(1)}, s16[256,256]{1,0:T(8,128)(2,1)S(1)}, u32[]{:S(2)}, u32[]{:S(2)}) collective-permute-start(s16[256,256]{1,0:T(8,128)(2,1)S(1)} %shard_map.72), channel_id=1, source_target_pairs={{0,2},{1,3},{2,0},{3,1},{4,6},{5,7},{6,4},{7,5},{8,10},{9,11},{10,... | collective-permute-start | bytes 393224 | tf_op jit(solution)/shard_map/ppermute | solution.py:219
  39.9 0.3 shard_map.74
  40.2 0.7 %collective-permute-start.19 = (s16[256,256]{1,0:T(8,128)(2,1)S(1)}, s16[256,256]{1,0:T(8,128)(2,1)S(1)}, u32[]{:S(2)}, u32[]{:S(2)}) collective-permute-start(s16[256,256]{1,0:T(8,128)(2,1)S(1)} %shard_map.74), channel_id=1, source_target_pairs={{0,1},{1,0},{2,3},{3,2},{4,5},{5,4},{6,7},{7,6},{8,9},{9,8},{10,11... | collective-permute-start | bytes 393224 | tf_op jit(solution)/shard_map/ppermute | solution.py:219
  41.2 2.1 %collective-permute-done.17.got = s16[256,256]{1,0:T(8,128)(2,1)S(1)} collective-permute-done((s16[256,256]{1,0:T(8,128)(2,1)S(1)}, s16[256,256]{1,0:T(8,128)(2,1)S(1)}, u32[]{:S(2)}, u32[]{:S(2)}) %collective-permute-start.17) | collective-permute-done | bytes 131104 | tf_op jit(solution)/shard_map/ppermute | solution.py:219
  43.3 2.6 %collective-permute-done.18.got = s16[256,256]{1,0:T(8,128)(2,1)S(1)} collective-permute-done((s16[256,256]{1,0:T(8,128)(2,1)S(1)}, s16[256,256]{1,0:T(8,128)(2,1)S(1)}, u32[]{:S(2)}, u32[]{:S(2)}) %collective-permute-start.18) | collective-permute-done | bytes 131104 | tf_op jit(solution)/shard_map/ppermute | solution.py:219
  46.0 0.7 %shard_map.75 = f32[256,256]{1,0:T(8,128)} custom-call(f32[256,256]{1,0:T(8,128)S(1)} %shard_map.73.total, s16[256,256]{1,0:T(8,128)(2,1)S(1)} %collective-permute-done.19.got), custom_call_target="tpu_custom_call" | custom-call | bytes 16777216 | tf_op jit(solution)/shard_map/pallas_call | solution.py:312
  (29 shorter events, 1.9 us)
Async XLA Ops:
  4.9 5.1 %collective-permute-start.1 = (s16[128,1280]{1,0:T(8,128)(2,1)S(1)}, s16[128,1280]{1,0:T(8,128)(2,1)S(1)}, u32[]{:S(2)}, u32[]{:S(2)}) collective-permute-start(s16[128,1280]{1,0:T(8,128)(2,1)S(1)} %get-tuple-element.30), channel_id=1, source_target_pairs={{0,4},{4,0},{8,12},{12,8},{16,20},{20,16},{24,28},{28,24},{1,5},{5... | collective-permute-start | bytes 983048 | tf_op jit(solution)/shard_map/ppermute | solution.py:213
  5.0 1.9 %collective-permute-start = (s16[128,768]{1,0:T(8,128)(2,1)S(1)}, s16[128,768]{1,0:T(8,128)(2,1)S(1)}, u32[]{:S(2)}, u32[]{:S(2)}) collective-permute-start(s16[128,768]{1,0:T(8,128)(2,1)S(1)} %get-tuple-element.26), channel_id=1, source_target_pairs={{0,4},{4,0},{8,12},{12,8},{16,20},{20,16},{24,28},{28,24},{1,5},{5... | collective-permute-start | bytes 589832 | tf_op jit(solution)/shard_map/ppermute | solution.py:213
  7.0 5.6 %collective-permute-start.4 = (s16[128,384]{1,0:T(8,128)(2,1)S(1)}, s16[128,384]{1,0:T(8,128)(2,1)S(1)}, u32[]{:S(2)}, u32[]{:S(2)}) collective-permute-start(s16[128,384]{1,0:T(8,128)(2,1)S(1)} %get-tuple-element.28), channel_id=1, source_target_pairs={{0,8},{4,12},{8,0},{12,4},{16,24},{20,28},{24,16},{28,20},{1,9},{5... | collective-permute-start | bytes 294920 | tf_op jit(solution)/shard_map/ppermute | solution.py:216
  10.2 5.2 %collective-permute-start.3 = (s16[128,384]{1,0:T(8,128)(2,1)S(1)}, s16[128,384]{1,0:T(8,128)(2,1)S(1)}, u32[]{:S(2)}, u32[]{:S(2)}) collective-permute-start(s16[128,384]{1,0:T(8,128)(2,1)S(1)} %get-tuple-element.34), channel_id=1, source_target_pairs={{0,8},{4,12},{8,0},{12,4},{16,24},{20,28},{24,16},{28,20},{1,9},{5... | collective-permute-start | bytes 294920 | tf_op jit(solution)/shard_map/ppermute | solution.py:216
  12.7 9.4 %collective-permute-start.7 = (s16[128,384]{1,0:T(8,128)(2,1)S(1)}, s16[128,384]{1,0:T(8,128)(2,1)S(1)}, u32[]{:S(2)}, u32[]{:S(2)}) collective-permute-start(s16[128,384]{1,0:T(8,128)(2,1)S(1)} %shard_map.60.code), channel_id=1, source_target_pairs={{0,16},{4,20},{8,24},{12,28},{16,0},{20,4},{24,8},{28,12},{1,17},{... | collective-permute-start | bytes 294920 | tf_op jit(solution)/shard_map/ppermute | solution.py:216
  15.5 11.5 %collective-permute-start.6 = (s16[128,384]{1,0:T(8,128)(2,1)S(1)}, s16[128,384]{1,0:T(8,128)(2,1)S(1)}, u32[]{:S(2)}, u32[]{:S(2)}) collective-permute-start(s16[128,384]{1,0:T(8,128)(2,1)S(1)} %shard_map.61.code), channel_id=1, source_target_pairs={{0,16},{4,20},{8,24},{12,28},{16,0},{20,4},{24,8},{28,12},{1,17},{... | collective-permute-start | bytes 294920 | tf_op jit(solution)/shard_map/ppermute | solution.py:216
  18.0 6.7 %collective-permute-start.2 = (s16[128,256]{1,0:T(8,128)(2,1)S(1)}, s16[128,256]{1,0:T(8,128)(2,1)S(1)}, u32[]{:S(2)}, u32[]{:S(2)}) collective-permute-start(s16[128,256]{1,0:T(8,128)(2,1)S(1)} %get-tuple-element.32), channel_id=1, source_target_pairs={{0,8},{4,12},{8,0},{12,4},{16,24},{20,28},{24,16},{28,20},{1,9},{5... | collective-permute-start | bytes 196616 | tf_op jit(solution)/shard_map/ppermute | solution.py:216
  22.2 5.4 %collective-permute-start.8 = (bf16[128,384]{1,0:T(8,128)(2,1)S(1)}, bf16[128,384]{1,0:T(8,128)(2,1)S(1)}, u32[]{:S(2)}, u32[]{:S(2)}) collective-permute-start(bf16[128,384]{1,0:T(8,128)(2,1)S(1)} %shard_map.63.refs_0_), channel_id=1, source_target_pairs={{0,8},{4,12},{8,0},{12,4},{16,24},{20,28},{24,16},{28,20},{1,9},{5... | collective-permute-start | bytes 294920 | tf_op jit(solution)/shard_map/ppermute | solution.py:216
  24.7 5.3 %collective-permute-start.5 = (s16[128,256]{1,0:T(8,128)(2,1)S(1)}, s16[128,256]{1,0:T(8,128)(2,1)S(1)}, u32[]{:S(2)}, u32[]{:S(2)}) collective-permute-start(s16[128,256]{1,0:T(8,128)(2,1)S(1)} %shard_map.62.code), channel_id=1, source_target_pairs={{0,16},{4,20},{8,24},{12,28},{16,0},{20,4},{24,8},{28,12},{1,17},{... | collective-permute-start | bytes 196616 | tf_op jit(solution)/shard_map/ppermute | solution.py:216
  27.1 5.4 %collective-permute-start.12 = (bf16[128,384]{1,0:T(8,128)(2,1)S(1)}, bf16[128,384]{1,0:T(8,128)(2,1)S(1)}, u32[]{:S(2)}, u32[]{:S(2)}) collective-permute-start(bf16[128,384]{1,0:T(8,128)(2,1)S(1)} %shard_map.64.refs_1_), channel_id=1, source_target_pairs={{0,8},{4,12},{8,0},{12,4},{16,24},{20,28},{24,16},{28,20},{1,9},{5... | collective-permute-start | bytes 294920 | tf_op jit(solution)/shard_map/ppermute | solution.py:216
  27.2 5.3 %collective-permute-start.9 = (bf16[128,384]{1,0:T(8,128)(2,1)S(1)}, bf16[128,384]{1,0:T(8,128)(2,1)S(1)}, u32[]{:S(2)}, u32[]{:S(2)}) collective-permute-start(bf16[128,384]{1,0:T(8,128)(2,1)S(1)} %shard_map.63.refs_0_), channel_id=1, source_target_pairs={{0,4},{4,0},{8,12},{12,8},{16,20},{20,16},{24,28},{28,24},{1,5},{5... | collective-permute-start | bytes 294920 | tf_op jit(solution)/shard_map/ppermute | solution.py:213
  27.6 4.9 %collective-permute-start.10 = (bf16[128,384]{1,0:T(8,128)(2,1)S(1)}, bf16[128,384]{1,0:T(8,128)(2,1)S(1)}, u32[]{:S(2)}, u32[]{:S(2)}) collective-permute-start(bf16[128,384]{1,0:T(8,128)(2,1)S(1)} %collective-permute-done.8.refs_1_), channel_id=1, source_target_pairs={{0,4},{4,0},{8,12},{12,8},{16,20},{20,16},{24,28},{28,24},{1,5},{5... | collective-permute-start | bytes 294920 | tf_op jit(solution)/shard_map/ppermute | solution.py:213
  30.0 4.3 %collective-permute-start.11 = (bf16[128,256]{1,0:T(8,128)(2,1)S(1)}, bf16[128,256]{1,0:T(8,128)(2,1)S(1)}, u32[]{:S(2)}, u32[]{:S(2)}) collective-permute-start(bf16[128,256]{1,0:T(8,128)(2,1)S(1)} %shard_map.65.refs_0_), channel_id=1, source_target_pairs={{0,8},{4,12},{8,0},{12,4},{16,24},{20,28},{24,16},{28,20},{1,9},{5... | collective-permute-start | bytes 196616 | tf_op jit(solution)/shard_map/ppermute | solution.py:216
  31.4 4.3 %collective-permute-start.15 = (bf16[128,384]{1,0:T(8,128)(2,1)S(1)}, bf16[128,384]{1,0:T(8,128)(2,1)S(1)}, u32[]{:S(2)}, u32[]{:S(2)}) collective-permute-start(bf16[128,384]{1,0:T(8,128)(2,1)S(1)} %shard_map.64.refs_1_), channel_id=1, source_target_pairs={{0,4},{4,0},{8,12},{12,8},{16,20},{20,16},{24,28},{28,24},{1,5},{5... | collective-permute-start | bytes 294920 | tf_op jit(solution)/shard_map/ppermute | solution.py:213
  32.5 3.2 %collective-permute-start.16 = (bf16[128,384]{1,0:T(8,128)(2,1)S(1)}, bf16[128,384]{1,0:T(8,128)(2,1)S(1)}, u32[]{:S(2)}, u32[]{:S(2)}) collective-permute-start(bf16[128,384]{1,0:T(8,128)(2,1)S(1)} %collective-permute-done.12.refs_2_), channel_id=1, source_target_pairs={{0,4},{4,0},{8,12},{12,8},{16,20},{20,16},{24,28},{28,24},{1,5},{5... | collective-permute-start | bytes 294920 | tf_op jit(solution)/shard_map/ppermute | solution.py:213
  33.1 1.5 %collective-permute-start.13 = (bf16[128,256]{1,0:T(8,128)(2,1)S(1)}, bf16[128,256]{1,0:T(8,128)(2,1)S(1)}, u32[]{:S(2)}, u32[]{:S(2)}) collective-permute-start(bf16[128,256]{1,0:T(8,128)(2,1)S(1)} %shard_map.65.refs_0_), channel_id=1, source_target_pairs={{0,4},{4,0},{8,12},{12,8},{16,20},{20,16},{24,28},{28,24},{1,5},{5... | collective-permute-start | bytes 196616 | tf_op jit(solution)/shard_map/ppermute | solution.py:213
  34.3 1.3 %collective-permute-start.14 = (bf16[128,256]{1,0:T(8,128)(2,1)S(1)}, bf16[128,256]{1,0:T(8,128)(2,1)S(1)}, u32[]{:S(2)}, u32[]{:S(2)}) collective-permute-start(bf16[128,256]{1,0:T(8,128)(2,1)S(1)} %collective-permute-done.11.refs_1_), channel_id=1, source_target_pairs={{0,4},{4,0},{8,12},{12,8},{16,20},{20,16},{24,28},{28,24},{1,5},{5... | collective-permute-start | bytes 196616 | tf_op jit(solution)/shard_map/ppermute | solution.py:213
  36.6 6.7 %collective-permute-start.17 = (s16[256,256]{1,0:T(8,128)(2,1)S(1)}, s16[256,256]{1,0:T(8,128)(2,1)S(1)}, u32[]{:S(2)}, u32[]{:S(2)}) collective-permute-start(s16[256,256]{1,0:T(8,128)(2,1)S(1)} %shard_map.70), channel_id=1, source_target_pairs={{0,3},{1,2},{2,1},{3,0},{4,7},{5,6},{6,5},{7,4},{8,11},{9,10},{10,... | collective-permute-start | bytes 393224 | tf_op jit(solution)/shard_map/ppermute | solution.py:219
  38.9 7.1 %collective-permute-start.18 = (s16[256,256]{1,0:T(8,128)(2,1)S(1)}, s16[256,256]{1,0:T(8,128)(2,1)S(1)}, u32[]{:S(2)}, u32[]{:S(2)}) collective-permute-start(s16[256,256]{1,0:T(8,128)(2,1)S(1)} %shard_map.72), channel_id=1, source_target_pairs={{0,2},{1,3},{2,0},{3,1},{4,6},{5,7},{6,4},{7,5},{8,10},{9,11},{10,... | collective-permute-start | bytes 393224 | tf_op jit(solution)/shard_map/ppermute | solution.py:219
  40.2 5.8 %collective-permute-start.19 = (s16[256,256]{1,0:T(8,128)(2,1)S(1)}, s16[256,256]{1,0:T(8,128)(2,1)S(1)}, u32[]{:S(2)}, u32[]{:S(2)}) collective-permute-start(s16[256,256]{1,0:T(8,128)(2,1)S(1)} %shard_map.74), channel_id=1, source_target_pairs={{0,1},{1,0},{2,3},{3,2},{4,5},{5,4},{6,7},{7,6},{8,9},{9,8},{10,11... | collective-permute-start | bytes 393224 | tf_op jit(solution)/shard_map/ppermute | solution.py:219

commit v11 on v10

--- a/solution.py
+++ b/solution.py
@@ -10,7 +10,7 @@
 GENE_BLOCKS = 16
 CORES = 2
 LANES = 128
-PARTS = (3, 3, 2)
+PARTS = (3, 5)
 MIB = 1 << 20
 
 VMEM = pl.BlockSpec(memory_space=pltpu.VMEM)
@@ -138,6 +138,10 @@
         start += out.shape[1]
 
 
+def again_kernel(code, got, out):
+    encode(decode(code[...]) + decode(got[...]), out)
+
+
 def cast_kernel(code, got, out):
     out[...] = (decode(code[...]) + decode(got[...])).astype(bf16)
 
@@ -193,9 +197,8 @@
 def cuts_of(genes, bits):
     for parts in (PARTS, (1, 1)):
         unit = genes // sum(parts)
-        if unit >> max(bits - 1, 0) >= LANES:
-            ends = [sum(parts[:i]) * unit for i in range(len(parts))]
-            return tuple((at, p * unit) for at, p in zip(ends, parts))
+        if unit * parts[1] % (LANES << max(bits - 1, 0)) == 0:
+            return ((0, parts[0] * unit), (parts[0] * unit, parts[1] * unit))
     return ((0, genes),)
 
 
@@ -272,31 +275,43 @@
                 pieces += came
                 before = came[-1]
             masks += [mask ^ (1 << bit) for mask in masks]
-        return masks, held
+        return masks, held, code
+
+    def by_doubling(code, *others):
+        for bit in reversed(range(bits)):
+            came = after(to_chip(code, bit), *others)
+            others = ()
+            body, kind = (again_kernel, i16) if bit else (cast_kernel, bf16)
+            code = call(body, shape(code.shape, kind), [VMEM, VMEM])(code, came)
+        return [code]
 
     got = [to_core(x) for x in theirs]
-    sums = add_step(0, half_of(0, 0, turned, first), got[0], widths[:1])
+    mine = half_of(0, 0, turned, first)
     if rest:
-        sums += add_step(0, half_of(0, first, after(turned, *sums[0]), rest), got[1], widths[1:])
-    masks, sides = by_halving(sums)
+        (code,) = call(code_kernel, (shape((rows, first), i16),), [VMEM, VMEM])(mine, got[0])
+        sums = add_step(0, half_of(0, first, after(turned, code), rest), got[1], [rest])
+        masks, sides, *crossing = by_halving(sums)
+        sides = [by_doubling(code, *crossing)] + sides
+        masks = [[0], masks]
+    else:
+        masks, sides, _ = by_halving(add_step(0, mine, got[0], [first]))
+        masks = [masks]
     totals = []
     for i, ((start, width), pieces) in enumerate(zip(cuts, sides)):
-        if i >= 2:
-            pieces = [after(x, totals[i - 2]) for x in pieces]
         pieces = pieces + [to_core(x) for x in pieces]
         if i == len(cuts) - 1:
             break
         before = totals[-1:]
         totals.append(
             call(
-                functools.partial(part_kernel, masks, start, not before),
+                functools.partial(part_kernel, masks[i], start, not before),
                 shape((cells, rank), f32),
                 [VMEM] * (1 + len(before) + len(pieces)),
                 scratch=[pltpu.VMEM((rank, width), bf16)],
             )(dense, *before, *pieces)
         )
     gene = call(
-        functools.partial(gene_kernel, masks), shape((rank, width), bf16), [VMEM] * len(pieces)
+        functools.partial(gene_kernel, masks[-1]), shape((rank, width), bf16), [VMEM] * len(pieces)
     )(*pieces)
 
     def cell(k):

time: 47.2 us -> 49.4 us (1.047)
  waiting for transfers between devices: 17.7 us -> 28 us
  starting transfers between devices: 19 us -> 11.2 us
    ppermute x9 -> x5, waiting for transfers between devices: 10.7 us -> 21.7 us  [to_chip(): lax.ppermute(x, 'cells', [(i, i ^ CORES << bit) for i in range(n_cells)])]
    ppermute x9 -> x5, starting transfers between devices: 13.9 us -> 6.38 us  [to_chip(): lax.ppermute(x, 'cells', [(i, i ^ CORES << bit) for i in range(n_cells)])]
    ppermute x8 -> x5, waiting for transfers between devices: 2.27 us -> 1.75 us  [to_core(): return lax.ppermute(x, 'cells', [(i, i ^ 1) for i in range(n_cells)])]
    ppermute x8 -> x5, starting transfers between devices: 1.38 us -> 1.14 us  [to_core(): return lax.ppermute(x, 'cells', [(i, i ^ 1) for i in range(n_cells)])]
    pallas_call x3 -> x5, Pallas kernels: 1.31 us -> 1.13 us  [the longest x1 0.63 us: local(): call(functools.partial(part_kernel, masks[i], start, not before), shape((...]
  transfers between devices with their start and end apart: 20 -> 13, of which waited for: 12 -> 10; matrix products, arithmetic and copies ran while one was open for 0% -> 0% of each run, Pallas kernels for 7% -> 7%
where the time goes in v11:
time: 49.4 us; the launch traced here: 49.2 us
  waiting for transfers between devices  28 us (57%)
  starting transfers between devices  11.2 us (23%)
  Pallas kernels  9.2 us (19%)
  between operations  0.81 us (2%)
    ppermute x5, waiting for transfers between devices, to_chip(): lax.ppermute(x, 'cells', [(i, i ^ CORES << bit) for i in range(n_cells)])  21.7 us
    ppermute x5, starting transfers between devices, to_chip(): lax.ppermute(x, 'cells', [(i, i ^ CORES << bit) for i in range(n_cells)])  6.38 us
    ppermute x3, waiting for transfers between devices, to_gene(): return lax.ppermute(x, 'genes', [(i, i ^ k) for i in range(n_genes)])  4.58 us
    pallas_call x1, Pallas kernels, local(): call(dense_kernel, (shape((cells, genes), bf16), shape((rank, cells), bf1...  4.27 us
    ppermute x3, starting transfers between devices, to_gene(): return lax.ppermute(x, 'genes', [(i, i ^ k) for i in range(n_genes)])  3.68 us
    ppermute x5, waiting for transfers between devices, to_core(): return lax.ppermute(x, 'cells', [(i, i ^ 1) for i in range(n_cells)])  1.75 us
    pallas_call x4, Pallas kernels, cell(): call(functools.partial(cell_kernel, k, start), shape((height, rank), f32...  1.64 us
    ppermute x5, starting transfers between devices, to_core(): return lax.ppermute(x, 'cells', [(i, i ^ 1) for i in range(n_cells)])  1.14 us
  transfers between devices with their start and end apart: 13, of which 10 were waited for; matrix products, arithmetic and copies ran while one was open for 0% of the time, Pallas kernels for 7%

profile of v11, /device:TPU:0, one launch (start us, length us, event | category | flops | bytes accessed | tf_op | source)
XLA Modules:
  0.0 49.2 jit_solution(5647393461257360466)
XLA Ops:
  0.7 4.3 %shard_map.55 = (bf16[1024,2048]{1,0:T(8,128)(2,1)S(1)}, bf16[256,1024]{1,0:T(8,128)(2,1)S(1)}, s16[128,768]{1,0:T(8,128)(2,1)S(1)}, s16[128,1280]{1,0:T(8,128)(2,1)S(1)}) custom-call(s32[1]{0:T(128)S(6)} %copy.6.count, s32[96]{0:T(128)} %rows.1, s32[96]{0:T(128)} %cols.1, bf16[1024,256]{1,0:T(8,128)(2,1)} %sketch.1, bf16[96,128,128]{2,1,0:T(8,128)(2,1)} %tiles.1), custom_call_target="tpu_custom_call" | custom-call | tf_op jit(solution)/shard_map/pallas_call | solution.py:226
  5.0 0.5 %collective-permute-start = (s16[128,768]{1,0:T(8,128)(2,1)S(1)}, s16[128,768]{1,0:T(8,128)(2,1)S(1)}, u32[]{:S(2)}, u32[]{:S(2)}) collective-permute-start(s16[128,768]{1,0:T(8,128)(2,1)S(1)} %get-tuple-element.15), channel_id=1, source_target_pairs={{0,4},{4,0},{8,12},{12,8},{16,20},{20,16},{24,28},{28,24},{1,5},{5... | collective-permute-start | bytes 589832 | tf_op jit(solution)/shard_map/ppermute | solution.py:216
  5.5 0.4 shard_map.56.mine
  5.9 1.0 %collective-permute-done.got = s16[128,768]{1,0:T(8,128)(2,1)S(1)} collective-permute-done((s16[128,768]{1,0:T(8,128)(2,1)S(1)}, s16[128,768]{1,0:T(8,128)(2,1)S(1)}, u32[]{:S(2)}, u32[]{:S(2)}) %collective-permute-start) | collective-permute-done | bytes 196640 | tf_op jit(solution)/shard_map/ppermute | solution.py:216
  6.9 0.1 shard_map.57.code
  7.0 0.5 %shard_map.58.mine = f32[128,1280]{1,0:T(8,128)S(1)} custom-call(bf16[256,1024]{1,0:T(8,128)(2,1)S(1)} %get-tuple-element.16.turned, bf16[1024,2048]{1,0:T(8,128)(2,1)S(1)} %get-tuple-element.13.dense), custom_call_target="tpu_custom_call" | custom-call | tf_op jit(solution)/shard_map/pallas_call | solution.py:241
  7.6 0.2 shard_map.59
  7.8 2.6 %collective-permute-start.2 = (s16[128,640]{1,0:T(8,128)(2,1)S(1)}, s16[128,640]{1,0:T(8,128)(2,1)S(1)}, u32[]{:S(2)}, u32[]{:S(2)}) collective-permute-start(s16[128,640]{1,0:T(8,128)(2,1)S(1)} %get-tuple-element.19), channel_id=1, source_target_pairs={{0,8},{4,12},{8,0},{12,4},{16,24},{20,28},{24,16},{28,20},{1,9},{5... | collective-permute-start | bytes 491528 | tf_op jit(solution)/shard_map/ppermute | solution.py:219
  10.4 2.5 %collective-permute-start.7 = (s16[128,768]{1,0:T(8,128)(2,1)S(1)}, s16[128,768]{1,0:T(8,128)(2,1)S(1)}, u32[]{:S(2)}, u32[]{:S(2)}) collective-permute-start(s16[128,768]{1,0:T(8,128)(2,1)S(1)} %shard_map.57.code), channel_id=1, source_target_pairs={{0,16},{4,20},{8,24},{12,28},{16,0},{20,4},{24,8},{28,12},{1,17},{... | collective-permute-start | bytes 589832 | tf_op jit(solution)/shard_map/ppermute | solution.py:219
  12.9 5.1 %collective-permute-done.2.got = s16[128,640]{1,0:T(8,128)(2,1)S(1)} collective-permute-done((s16[128,640]{1,0:T(8,128)(2,1)S(1)}, s16[128,640]{1,0:T(8,128)(2,1)S(1)}, u32[]{:S(2)}, u32[]{:S(2)}) %collective-permute-start.2) | collective-permute-done | bytes 163872 | tf_op jit(solution)/shard_map/ppermute | solution.py:219
  18.0 0.1 shard_map.60.code
  18.1 1.2 %collective-permute-start.3 = (s16[128,640]{1,0:T(8,128)(2,1)S(1)}, s16[128,640]{1,0:T(8,128)(2,1)S(1)}, u32[]{:S(2)}, u32[]{:S(2)}) collective-permute-start(s16[128,640]{1,0:T(8,128)(2,1)S(1)} %shard_map.60.code), channel_id=1, source_target_pairs={{0,16},{4,20},{8,24},{12,28},{16,0},{20,4},{24,8},{28,12},{1,17},{... | collective-permute-start | bytes 491528 | tf_op jit(solution)/shard_map/ppermute | solution.py:219
  19.3 7.6 %collective-permute-done.7.got = s16[128,768]{1,0:T(8,128)(2,1)S(1)} collective-permute-done((s16[128,768]{1,0:T(8,128)(2,1)S(1)}, s16[128,768]{1,0:T(8,128)(2,1)S(1)}, u32[]{:S(2)}, u32[]{:S(2)}) %collective-permute-start.7) | collective-permute-done | bytes 196640 | tf_op jit(solution)/shard_map/ppermute | solution.py:219
  26.9 0.2 shard_map.63.code
  27.2 2.2 %collective-permute-done.3.got = s16[128,640]{1,0:T(8,128)(2,1)S(1)} collective-permute-done((s16[128,640]{1,0:T(8,128)(2,1)S(1)}, s16[128,640]{1,0:T(8,128)(2,1)S(1)}, u32[]{:S(2)}, u32[]{:S(2)}) %collective-permute-start.3) | collective-permute-done | bytes 163872 | tf_op jit(solution)/shard_map/ppermute | solution.py:219
  29.5 5.5 %collective-permute-done.8.got = s16[128,768]{1,0:T(8,128)(2,1)S(1)} collective-permute-done((s16[128,768]{1,0:T(8,128)(2,1)S(1)}, s16[128,768]{1,0:T(8,128)(2,1)S(1)}, u32[]{:S(2)}, u32[]{:S(2)}) %collective-permute-start.8) | collective-permute-done | bytes 196640 | tf_op jit(solution)/shard_map/ppermute | solution.py:219
  35.0 0.1 shard_map.64.refs_0_
  35.2 0.5 %collective-permute-start.5 = (bf16[128,640]{1,0:T(8,128)(2,1)S(1)}, bf16[128,640]{1,0:T(8,128)(2,1)S(1)}, u32[]{:S(2)}, u32[]{:S(2)}) collective-permute-start(bf16[128,640]{1,0:T(8,128)(2,1)S(1)} %shard_map.61.refs_0_), channel_id=1, source_target_pairs={{0,4},{4,0},{8,12},{12,8},{16,20},{20,16},{24,28},{28,24},{1,5},{5... | collective-permute-start | bytes 491528 | tf_op jit(solution)/shard_map/ppermute | solution.py:216
  35.7 1.3 %collective-permute-done.4.refs_1_ = bf16[128,640]{1,0:T(8,128)(2,1)S(1)} collective-permute-done((bf16[128,640]{1,0:T(8,128)(2,1)S(1)}, bf16[128,640]{1,0:T(8,128)(2,1)S(1)}, u32[]{:S(2)}, u32[]{:S(2)}) %collective-permute-start.4) | collective-permute-done | bytes 163872 | tf_op jit(solution)/shard_map/ppermute | solution.py:219
  37.0 0.6 %shard_map.65.refs_0_ = f32[1024,256]{1,0:T(8,128)S(1)} custom-call(bf16[1024,2048]{1,0:T(8,128)(2,1)S(1)} %get-tuple-element.13.dense, bf16[128,768]{1,0:T(8,128)(2,1)S(1)} %shard_map.64.refs_0_, bf16[128,768]{1,0:T(8,128)(2,1)S(1)} %collective-permute-done.9.refs_1_), custom_call_target="tpu_custom_call" | custom-call | tf_op jit(solution)/shard_map/pallas_call | solution.py:306
  37.6 0.7 %collective-permute-done.6.refs_3_ = bf16[128,640]{1,0:T(8,128)(2,1)S(1)} collective-permute-done((bf16[128,640]{1,0:T(8,128)(2,1)S(1)}, bf16[128,640]{1,0:T(8,128)(2,1)S(1)}, u32[]{:S(2)}, u32[]{:S(2)}) %collective-permute-start.6) | collective-permute-done | bytes 163872 | tf_op jit(solution)/shard_map/ppermute | solution.py:216
  38.4 0.4 shard_map.67
  38.9 2.2 %collective-permute-start.10 = (s16[256,256]{1,0:T(8,128)(2,1)S(1)}, s16[256,256]{1,0:T(8,128)(2,1)S(1)}, u32[]{:S(2)}, u32[]{:S(2)}) collective-permute-start(s16[256,256]{1,0:T(8,128)(2,1)S(1)} %shard_map.67), channel_id=1, source_target_pairs={{0,3},{1,2},{2,1},{3,0},{4,7},{5,6},{6,5},{7,4},{8,11},{9,10},{10,... | collective-permute-start | bytes 393224 | tf_op jit(solution)/shard_map/ppermute | solution.py:222
  41.1 0.4 shard_map.69
  41.5 0.6 %collective-permute-start.11 = (s16[256,256]{1,0:T(8,128)(2,1)S(1)}, s16[256,256]{1,0:T(8,128)(2,1)S(1)}, u32[]{:S(2)}, u32[]{:S(2)}) collective-permute-start(s16[256,256]{1,0:T(8,128)(2,1)S(1)} %shard_map.69), channel_id=1, source_target_pairs={{0,2},{1,3},{2,0},{3,1},{4,6},{5,7},{6,4},{7,5},{8,10},{9,11},{10,... | collective-permute-start | bytes 393224 | tf_op jit(solution)/shard_map/ppermute | solution.py:222
  42.2 0.4 shard_map.71
  42.6 0.8 %collective-permute-start.12 = (s16[256,256]{1,0:T(8,128)(2,1)S(1)}, s16[256,256]{1,0:T(8,128)(2,1)S(1)}, u32[]{:S(2)}, u32[]{:S(2)}) collective-permute-start(s16[256,256]{1,0:T(8,128)(2,1)S(1)} %shard_map.71), channel_id=1, source_target_pairs={{0,1},{1,0},{2,3},{3,2},{4,5},{5,4},{6,7},{7,6},{8,9},{9,8},{10,11... | collective-permute-start | bytes 393224 | tf_op jit(solution)/shard_map/ppermute | solution.py:222
  43.4 0.4 shard_map.66.total
  43.8 1.7 %collective-permute-done.10.got = s16[256,256]{1,0:T(8,128)(2,1)S(1)} collective-permute-done((s16[256,256]{1,0:T(8,128)(2,1)S(1)}, s16[256,256]{1,0:T(8,128)(2,1)S(1)}, u32[]{:S(2)}, u32[]{:S(2)}) %collective-permute-start.10) | collective-permute-done | bytes 131104 | tf_op jit(solution)/shard_map/ppermute | solution.py:222
  45.5 2.7 %collective-permute-done.11.got = s16[256,256]{1,0:T(8,128)(2,1)S(1)} collective-permute-done((s16[256,256]{1,0:T(8,128)(2,1)S(1)}, s16[256,256]{1,0:T(8,128)(2,1)S(1)}, u32[]{:S(2)}, u32[]{:S(2)}) %collective-permute-start.11) | collective-permute-done | bytes 131104 | tf_op jit(solution)/shard_map/ppermute | solution.py:222
  48.2 0.2 collective-permute-done.12.got
  48.5 0.7 %shard_map.72 = f32[256,256]{1,0:T(8,128)} custom-call(f32[256,256]{1,0:T(8,128)S(1)} %shard_map.70.total, s16[256,256]{1,0:T(8,128)(2,1)S(1)} %collective-permute-done.12.got), custom_call_target="tpu_custom_call" | custom-call | bytes 16777216 | tf_op jit(solution)/shard_map/pallas_call | solution.py:327
  (12 shorter events, 0.6 us)
Async XLA Ops:
  4.9 2.6 %collective-permute-start.1 = (s16[128,1280]{1,0:T(8,128)(2,1)S(1)}, s16[128,1280]{1,0:T(8,128)(2,1)S(1)}, u32[]{:S(2)}, u32[]{:S(2)}) collective-permute-start(s16[128,1280]{1,0:T(8,128)(2,1)S(1)} %get-tuple-element.17), channel_id=1, source_target_pairs={{0,4},{4,0},{8,12},{12,8},{16,20},{20,16},{24,28},{28,24},{1,5},{5... | collective-permute-start | bytes 983048 | tf_op jit(solution)/shard_map/ppermute | solution.py:216
  5.0 1.9 %collective-permute-start = (s16[128,768]{1,0:T(8,128)(2,1)S(1)}, s16[128,768]{1,0:T(8,128)(2,1)S(1)}, u32[]{:S(2)}, u32[]{:S(2)}) collective-permute-start(s16[128,768]{1,0:T(8,128)(2,1)S(1)} %get-tuple-element.15), channel_id=1, source_target_pairs={{0,4},{4,0},{8,12},{12,8},{16,20},{20,16},{24,28},{28,24},{1,5},{5... | collective-permute-start | bytes 589832 | tf_op jit(solution)/shard_map/ppermute | solution.py:216
  7.8 10.2 %collective-permute-start.2 = (s16[128,640]{1,0:T(8,128)(2,1)S(1)}, s16[128,640]{1,0:T(8,128)(2,1)S(1)}, u32[]{:S(2)}, u32[]{:S(2)}) collective-permute-start(s16[128,640]{1,0:T(8,128)(2,1)S(1)} %get-tuple-element.19), channel_id=1, source_target_pairs={{0,8},{4,12},{8,0},{12,4},{16,24},{20,28},{24,16},{28,20},{1,9},{5... | collective-permute-start | bytes 491528 | tf_op jit(solution)/shard_map/ppermute | solution.py:219
  10.4 16.5 %collective-permute-start.7 = (s16[128,768]{1,0:T(8,128)(2,1)S(1)}, s16[128,768]{1,0:T(8,128)(2,1)S(1)}, u32[]{:S(2)}, u32[]{:S(2)}) collective-permute-start(s16[128,768]{1,0:T(8,128)(2,1)S(1)} %shard_map.57.code), channel_id=1, source_target_pairs={{0,16},{4,20},{8,24},{12,28},{16,0},{20,4},{24,8},{28,12},{1,17},{... | collective-permute-start | bytes 589832 | tf_op jit(solution)/shard_map/ppermute | solution.py:219
  18.1 11.2 %collective-permute-start.3 = (s16[128,640]{1,0:T(8,128)(2,1)S(1)}, s16[128,640]{1,0:T(8,128)(2,1)S(1)}, u32[]{:S(2)}, u32[]{:S(2)}) collective-permute-start(s16[128,640]{1,0:T(8,128)(2,1)S(1)} %shard_map.60.code), channel_id=1, source_target_pairs={{0,16},{4,20},{8,24},{12,28},{16,0},{20,4},{24,8},{28,12},{1,17},{... | collective-permute-start | bytes 491528 | tf_op jit(solution)/shard_map/ppermute | solution.py:219
  27.1 7.9 %collective-permute-start.8 = (s16[128,768]{1,0:T(8,128)(2,1)S(1)}, s16[128,768]{1,0:T(8,128)(2,1)S(1)}, u32[]{:S(2)}, u32[]{:S(2)}) collective-permute-start(s16[128,768]{1,0:T(8,128)(2,1)S(1)} %shard_map.63.code), channel_id=1, source_target_pairs={{0,8},{4,12},{8,0},{12,4},{16,24},{20,28},{24,16},{28,20},{1,9},{5... | collective-permute-start | bytes 589832 | tf_op jit(solution)/shard_map/ppermute | solution.py:219
  29.5 7.5 %collective-permute-start.4 = (bf16[128,640]{1,0:T(8,128)(2,1)S(1)}, bf16[128,640]{1,0:T(8,128)(2,1)S(1)}, u32[]{:S(2)}, u32[]{:S(2)}) collective-permute-start(bf16[128,640]{1,0:T(8,128)(2,1)S(1)} %shard_map.61.refs_0_), channel_id=1, source_target_pairs={{0,8},{4,12},{8,0},{12,4},{16,24},{20,28},{24,16},{28,20},{1,9},{5... | collective-permute-start | bytes 491528 | tf_op jit(solution)/shard_map/ppermute | solution.py:219
  35.1 1.9 %collective-permute-start.9 = (bf16[128,768]{1,0:T(8,128)(2,1)S(1)}, bf16[128,768]{1,0:T(8,128)(2,1)S(1)}, u32[]{:S(2)}, u32[]{:S(2)}) collective-permute-start(bf16[128,768]{1,0:T(8,128)(2,1)S(1)} %shard_map.64.refs_0_), channel_id=1, source_target_pairs={{0,4},{4,0},{8,12},{12,8},{16,20},{20,16},{24,28},{28,24},{1,5},{5... | collective-permute-start | bytes 589832 | tf_op jit(solution)/shard_map/ppermute | solution.py:216
  35.2 2.4 %collective-permute-start.5 = (bf16[128,640]{1,0:T(8,128)(2,1)S(1)}, bf16[128,640]{1,0:T(8,128)(2,1)S(1)}, u32[]{:S(2)}, u32[]{:S(2)}) collective-permute-start(bf16[128,640]{1,0:T(8,128)(2,1)S(1)} %shard_map.61.refs_0_), channel_id=1, source_target_pairs={{0,4},{4,0},{8,12},{12,8},{16,20},{20,16},{24,28},{28,24},{1,5},{5... | collective-permute-start | bytes 491528 | tf_op jit(solution)/shard_map/ppermute | solution.py:216
  37.0 1.4 %collective-permute-start.6 = (bf16[128,640]{1,0:T(8,128)(2,1)S(1)}, bf16[128,640]{1,0:T(8,128)(2,1)S(1)}, u32[]{:S(2)}, u32[]{:S(2)}) collective-permute-start(bf16[128,640]{1,0:T(8,128)(2,1)S(1)} %collective-permute-done.4.refs_1_), channel_id=1, source_target_pairs={{0,4},{4,0},{8,12},{12,8},{16,20},{20,16},{24,28},{28,24},{1,5},{5... | collective-permute-start | bytes 491528 | tf_op jit(solution)/shard_map/ppermute | solution.py:216
  38.9 6.6 %collective-permute-start.10 = (s16[256,256]{1,0:T(8,128)(2,1)S(1)}, s16[256,256]{1,0:T(8,128)(2,1)S(1)}, u32[]{:S(2)}, u32[]{:S(2)}) collective-permute-start(s16[256,256]{1,0:T(8,128)(2,1)S(1)} %shard_map.67), channel_id=1, source_target_pairs={{0,3},{1,2},{2,1},{3,0},{4,7},{5,6},{6,5},{7,4},{8,11},{9,10},{10,... | collective-permute-start | bytes 393224 | tf_op jit(solution)/shard_map/ppermute | solution.py:222
  41.5 6.7 %collective-permute-start.11 = (s16[256,256]{1,0:T(8,128)(2,1)S(1)}, s16[256,256]{1,0:T(8,128)(2,1)S(1)}, u32[]{:S(2)}, u32[]{:S(2)}) collective-permute-start(s16[256,256]{1,0:T(8,128)(2,1)S(1)} %shard_map.69), channel_id=1, source_target_pairs={{0,2},{1,3},{2,0},{3,1},{4,6},{5,7},{6,4},{7,5},{8,10},{9,11},{10,... | collective-permute-start | bytes 393224 | tf_op jit(solution)/shard_map/ppermute | solution.py:222
  42.6 5.9 %collective-permute-start.12 = (s16[256,256]{1,0:T(8,128)(2,1)S(1)}, s16[256,256]{1,0:T(8,128)(2,1)S(1)}, u32[]{:S(2)}, u32[]{:S(2)}) collective-permute-start(s16[256,256]{1,0:T(8,128)(2,1)S(1)} %shard_map.71), channel_id=1, source_target_pairs={{0,1},{1,0},{2,3},{3,2},{4,5},{5,4},{6,7},{7,6},{8,9},{9,8},{10,11... | collective-permute-start | bytes 393224 | tf_op jit(solution)/shard_map/ppermute | solution.py:222

commit v12 on v10

--- a/solution.py
+++ b/solution.py
@@ -10,7 +10,7 @@
 GENE_BLOCKS = 16
 CORES = 2
 LANES = 128
-PARTS = (3, 3, 2)
+PARTS = (1, 1, 1, 1)
 MIB = 1 << 20
 
 VMEM = pl.BlockSpec(memory_space=pltpu.VMEM)

time: 47.2 us -> 47.2 us (level)
  starting transfers between devices: 19 us -> 22.2 us
  waiting for transfers between devices: 17.7 us -> 14.5 us
    ppermute x9 -> x12, waiting for transfers between devices: 10.7 us -> 8.01 us  [to_chip(): lax.ppermute(x, 'cells', [(i, i ^ CORES << bit) for i in range(n_cells)])]
    ppermute x9 -> x12, starting transfers between devices: 13.9 us -> 16.2 us  [to_chip(): lax.ppermute(x, 'cells', [(i, i ^ CORES << bit) for i in range(n_cells)])]
    ppermute x8 -> x10, starting transfers between devices: 1.38 us -> 2.32 us  [to_core(): return lax.ppermute(x, 'cells', [(i, i ^ 1) for i in range(n_cells)])]
    ppermute x8 -> x10, waiting for transfers between devices: 2.27 us -> 1.77 us  [to_core(): return lax.ppermute(x, 'cells', [(i, i ^ 1) for i in range(n_cells)])]
    pallas_call x2 -> x3, Pallas kernels: 1.28 us -> 1.49 us  [local(): call(functools.partial(part_kernel, masks, start, not before), shape((cel...]
  transfers between devices with their start and end apart: 20 -> 25, of which waited for: 12 -> 14; matrix products, arithmetic and copies ran while one was open for 0% -> 0% of each run, Pallas kernels for 7% -> 9%
where the time goes in v12:
time: 47.2 us; the launch traced here: 47 us
  starting transfers between devices  22.2 us (47%)
  waiting for transfers between devices  14.5 us (31%)
  Pallas kernels  9.46 us (20%)
  between operations  0.86 us (2%)
    ppermute x12, starting transfers between devices, to_chip(): lax.ppermute(x, 'cells', [(i, i ^ CORES << bit) for i in range(n_cells)])  16.2 us
    ppermute x12, waiting for transfers between devices, to_chip(): lax.ppermute(x, 'cells', [(i, i ^ CORES << bit) for i in range(n_cells)])  8.01 us
    ppermute x3, waiting for transfers between devices, to_gene(): return lax.ppermute(x, 'genes', [(i, i ^ k) for i in range(n_genes)])  4.7 us
    pallas_call x1, Pallas kernels, local(): call(dense_kernel, (shape((cells, genes), bf16), shape((rank, cells), bf1...  4.28 us
    ppermute x3, starting transfers between devices, to_gene(): return lax.ppermute(x, 'genes', [(i, i ^ k) for i in range(n_genes)])  3.69 us
    ppermute x10, starting transfers between devices, to_core(): return lax.ppermute(x, 'cells', [(i, i ^ 1) for i in range(n_cells)])  2.32 us
    ppermute x10, waiting for transfers between devices, to_core(): return lax.ppermute(x, 'cells', [(i, i ^ 1) for i in range(n_cells)])  1.77 us
    pallas_call x3, Pallas kernels, local(): call(functools.partial(part_kernel, masks, start, not before), shape((cel...  1.49 us
  transfers between devices with their start and end apart: 25, of which 14 were waited for; matrix products, arithmetic and copies ran while one was open for 0% of the time, Pallas kernels for 9%

profile of v12, /device:TPU:0, one launch (start us, length us, event | category | flops | bytes accessed | tf_op | source)
XLA Modules:
  0.0 47.0 jit_solution(13907253481934511530)
XLA Ops:
  0.7 4.3 %shard_map.55 = (bf16[1024,2048]{1,0:T(8,128)(2,1)S(1)}, bf16[256,1024]{1,0:T(8,128)(2,1)S(1)}, s16[128,512]{1,0:T(8,128)(2,1)S(1)}, s16[128,1536]{1,0:T(8,128)(2,1)S(1)}) custom-call(s32[1]{0:T(128)S(6)} %copy.6.count, s32[96]{0:T(128)} %rows.1, s32[96]{0:T(128)} %cols.1, bf16[1024,256]{1,0:T(8,128)(2,1)} %sketch.1, bf16[96,128,128]{2,1,0:T(8,128)(2,1)} %tiles.1), custom_call_target="tpu_custom_call" | custom-call | tf_op jit(solution)/shard_map/pallas_call | solution.py:223
  5.0 0.5 %collective-permute-start = (s16[128,512]{1,0:T(8,128)(2,1)S(1)}, s16[128,512]{1,0:T(8,128)(2,1)S(1)}, u32[]{:S(2)}, u32[]{:S(2)}) collective-permute-start(s16[128,512]{1,0:T(8,128)(2,1)S(1)} %get-tuple-element.33), channel_id=1, source_target_pairs={{0,4},{4,0},{8,12},{12,8},{16,20},{20,16},{24,28},{28,24},{1,5},{5... | collective-permute-start | bytes 393224 | tf_op jit(solution)/shard_map/ppermute | solution.py:213
  5.8 1.1 %collective-permute-done.got = s16[128,512]{1,0:T(8,128)(2,1)S(1)} collective-permute-done((s16[128,512]{1,0:T(8,128)(2,1)S(1)}, s16[128,512]{1,0:T(8,128)(2,1)S(1)}, u32[]{:S(2)}, u32[]{:S(2)}) %collective-permute-start) | collective-permute-done | bytes 131104 | tf_op jit(solution)/shard_map/ppermute | solution.py:213
  7.0 2.3 %collective-permute-start.5 = (s16[128,256]{1,0:T(8,128)(2,1)S(1)}, s16[128,256]{1,0:T(8,128)(2,1)S(1)}, u32[]{:S(2)}, u32[]{:S(2)}) collective-permute-start(s16[128,256]{1,0:T(8,128)(2,1)S(1)} %get-tuple-element.35), channel_id=1, source_target_pairs={{0,8},{4,12},{8,0},{12,4},{16,24},{20,28},{24,16},{28,20},{1,9},{5... | collective-permute-start | bytes 196616 | tf_op jit(solution)/shard_map/ppermute | solution.py:216
  9.3 0.6 %shard_map.58.mine = f32[128,1536]{1,0:T(8,128)S(1)} custom-call(bf16[256,1024]{1,0:T(8,128)(2,1)S(1)} %get-tuple-element.36.turned, bf16[1024,2048]{1,0:T(8,128)(2,1)S(1)} %get-tuple-element.31.dense), custom_call_target="tpu_custom_call" | custom-call | tf_op jit(solution)/shard_map/pallas_call | solution.py:238
  10.2 1.5 %collective-permute-done.5.got = s16[128,256]{1,0:T(8,128)(2,1)S(1)} collective-permute-done((s16[128,256]{1,0:T(8,128)(2,1)S(1)}, s16[128,256]{1,0:T(8,128)(2,1)S(1)}, u32[]{:S(2)}, u32[]{:S(2)}) %collective-permute-start.5) | collective-permute-done | bytes 65568 | tf_op jit(solution)/shard_map/ppermute | solution.py:216
  11.8 3.2 %collective-permute-start.9 = (s16[128,256]{1,0:T(8,128)(2,1)S(1)}, s16[128,256]{1,0:T(8,128)(2,1)S(1)}, u32[]{:S(2)}, u32[]{:S(2)}) collective-permute-start(s16[128,256]{1,0:T(8,128)(2,1)S(1)} %shard_map.60.code), channel_id=1, source_target_pairs={{0,16},{4,20},{8,24},{12,28},{16,0},{20,4},{24,8},{28,12},{1,17},{... | collective-permute-start | bytes 196616 | tf_op jit(solution)/shard_map/ppermute | solution.py:216
  15.0 2.5 %collective-permute-start.3 = (s16[128,256]{1,0:T(8,128)(2,1)S(1)}, s16[128,256]{1,0:T(8,128)(2,1)S(1)}, u32[]{:S(2)}, u32[]{:S(2)}) collective-permute-start(s16[128,256]{1,0:T(8,128)(2,1)S(1)} %get-tuple-element.41), channel_id=1, source_target_pairs={{0,8},{4,12},{8,0},{12,4},{16,24},{20,28},{24,16},{28,20},{1,9},{5... | collective-permute-start | bytes 196616 | tf_op jit(solution)/shard_map/ppermute | solution.py:216
  17.6 0.9 %collective-permute-start.8 = (s16[128,256]{1,0:T(8,128)(2,1)S(1)}, s16[128,256]{1,0:T(8,128)(2,1)S(1)}, u32[]{:S(2)}, u32[]{:S(2)}) collective-permute-start(s16[128,256]{1,0:T(8,128)(2,1)S(1)} %shard_map.61.code), channel_id=1, source_target_pairs={{0,16},{4,20},{8,24},{12,28},{16,0},{20,4},{24,8},{28,12},{1,17},{... | collective-permute-start | bytes 196616 | tf_op jit(solution)/shard_map/ppermute | solution.py:216
  18.5 2.1 %collective-permute-start.10 = (bf16[128,256]{1,0:T(8,128)(2,1)S(1)}, bf16[128,256]{1,0:T(8,128)(2,1)S(1)}, u32[]{:S(2)}, u32[]{:S(2)}) collective-permute-start(bf16[128,256]{1,0:T(8,128)(2,1)S(1)} %shard_map.64.refs_0_), channel_id=1, source_target_pairs={{0,8},{4,12},{8,0},{12,4},{16,24},{20,28},{24,16},{28,20},{1,9},{5... | collective-permute-start | bytes 196616 | tf_op jit(solution)/shard_map/ppermute | solution.py:216
  20.6 0.4 collective-permute-done.3.got
  21.1 3.1 %collective-permute-start.7 = (s16[128,256]{1,0:T(8,128)(2,1)S(1)}, s16[128,256]{1,0:T(8,128)(2,1)S(1)}, u32[]{:S(2)}, u32[]{:S(2)}) collective-permute-start(s16[128,256]{1,0:T(8,128)(2,1)S(1)} %shard_map.62.code), channel_id=1, source_target_pairs={{0,16},{4,20},{8,24},{12,28},{16,0},{20,4},{24,8},{28,12},{1,17},{... | collective-permute-start | bytes 196616 | tf_op jit(solution)/shard_map/ppermute | solution.py:216
  24.4 0.8 %collective-permute-done.8.got = s16[128,256]{1,0:T(8,128)(2,1)S(1)} collective-permute-done((s16[128,256]{1,0:T(8,128)(2,1)S(1)}, s16[128,256]{1,0:T(8,128)(2,1)S(1)}, u32[]{:S(2)}, u32[]{:S(2)}) %collective-permute-start.8) | collective-permute-done | bytes 65568 | tf_op jit(solution)/shard_map/ppermute | solution.py:216
  25.2 0.5 collective-permute-start.13
  25.7 0.5 %collective-permute-start.12 = (bf16[128,256]{1,0:T(8,128)(2,1)S(1)}, bf16[128,256]{1,0:T(8,128)(2,1)S(1)}, u32[]{:S(2)}, u32[]{:S(2)}) collective-permute-start(bf16[128,256]{1,0:T(8,128)(2,1)S(1)} %collective-permute-done.10.refs_1_), channel_id=1, source_target_pairs={{0,4},{4,0},{8,12},{12,8},{16,20},{20,16},{24,28},{28,24},{1,5},{5... | collective-permute-start | bytes 196616 | tf_op jit(solution)/shard_map/ppermute | solution.py:213
  26.2 0.3 collective-permute-done.7.got
  26.6 1.4 %collective-permute-start.17 = (bf16[128,256]{1,0:T(8,128)(2,1)S(1)}, bf16[128,256]{1,0:T(8,128)(2,1)S(1)}, u32[]{:S(2)}, u32[]{:S(2)}) collective-permute-start(bf16[128,256]{1,0:T(8,128)(2,1)S(1)} %shard_map.66.refs_1_), channel_id=1, source_target_pairs={{0,8},{4,12},{8,0},{12,4},{16,24},{20,28},{24,16},{28,20},{1,9},{5... | collective-permute-start | bytes 196616 | tf_op jit(solution)/shard_map/ppermute | solution.py:216
  27.9 1.8 %collective-permute-done.6.got = s16[128,256]{1,0:T(8,128)(2,1)S(1)} collective-permute-done((s16[128,256]{1,0:T(8,128)(2,1)S(1)}, s16[128,256]{1,0:T(8,128)(2,1)S(1)}, u32[]{:S(2)}, u32[]{:S(2)}) %collective-permute-start.6) | collective-permute-done | bytes 65568 | tf_op jit(solution)/shard_map/ppermute | solution.py:216
  29.9 1.0 %collective-permute-done.13.refs_2_ = bf16[128,256]{1,0:T(8,128)(2,1)S(1)} collective-permute-done((bf16[128,256]{1,0:T(8,128)(2,1)S(1)}, bf16[128,256]{1,0:T(8,128)(2,1)S(1)}, u32[]{:S(2)}, u32[]{:S(2)}) %collective-permute-start.13) | collective-permute-done | bytes 65568 | tf_op jit(solution)/shard_map/ppermute | solution.py:216
  30.9 0.5 %collective-permute-start.15 = (bf16[128,256]{1,0:T(8,128)(2,1)S(1)}, bf16[128,256]{1,0:T(8,128)(2,1)S(1)}, u32[]{:S(2)}, u32[]{:S(2)}) collective-permute-start(bf16[128,256]{1,0:T(8,128)(2,1)S(1)} %collective-permute-done.13.refs_2_), channel_id=1, source_target_pairs={{0,4},{4,0},{8,12},{12,8},{16,20},{20,16},{24,28},{28,24},{1,5},{5... | collective-permute-start | bytes 196616 | tf_op jit(solution)/shard_map/ppermute | solution.py:213
  31.4 0.5 %shard_map.68.refs_0_ = f32[1024,256]{1,0:T(8,128)S(1)} custom-call(bf16[1024,2048]{1,0:T(8,128)(2,1)S(1)} %get-tuple-element.31.dense, bf16[128,256]{1,0:T(8,128)(2,1)S(1)} %shard_map.64.refs_0_, bf16[128,256]{1,0:T(8,128)(2,1)S(1)} %collective-permute-done.10.refs_1_, bf16[128,256]{1,0:T(8,128)(2,1)S(1)} %collective-permute-done.11.refs_2_, ...), custom_call_target="tpu_custom_call" | custom-call | tf_op jit(solution)/shard_map/pallas_call | solution.py:291
  32.3 1.9 %collective-permute-done.16.refs_1_ = bf16[128,256]{1,0:T(8,128)(2,1)S(1)} collective-permute-done((bf16[128,256]{1,0:T(8,128)(2,1)S(1)}, bf16[128,256]{1,0:T(8,128)(2,1)S(1)}, u32[]{:S(2)}, u32[]{:S(2)}) %collective-permute-start.16) | collective-permute-done | bytes 65568 | tf_op jit(solution)/shard_map/ppermute | solution.py:216
  34.2 0.5 %shard_map.69.refs_0_ = f32[1024,256]{1,0:T(8,128)S(1)} custom-call(bf16[1024,2048]{1,0:T(8,128)(2,1)S(1)} %get-tuple-element.31.dense, f32[1024,256]{1,0:T(8,128)S(1)} %shard_map.68.refs_0_, bf16[128,256]{1,0:T(8,128)(2,1)S(1)} %shard_map.65.refs_1_, bf16[128,256]{1,0:T(8,128)(2,1)S(1)} %collective-permute-done.13.refs_2_, ...), custom_call_target="tpu_custom_call" | custom-call | tf_op jit(solution)/shard_map/pallas_call | solution.py:291
  34.7 0.6 %collective-permute-start.18 = (bf16[128,256]{1,0:T(8,128)(2,1)S(1)}, bf16[128,256]{1,0:T(8,128)(2,1)S(1)}, u32[]{:S(2)}, u32[]{:S(2)}) collective-permute-start(bf16[128,256]{1,0:T(8,128)(2,1)S(1)} %shard_map.67.refs_0_), channel_id=1, source_target_pairs={{0,4},{4,0},{8,12},{12,8},{16,20},{20,16},{24,28},{28,24},{1,5},{5... | collective-permute-start | bytes 196616 | tf_op jit(solution)/shard_map/ppermute | solution.py:213
  35.4 0.5 %shard_map.71.refs_0_ = f32[1024,256]{1,0:T(8,128)S(1)} custom-call(bf16[1024,2048]{1,0:T(8,128)(2,1)S(1)} %get-tuple-element.31.dense, f32[1024,256]{1,0:T(8,128)S(1)} %shard_map.69.refs_0_, bf16[128,256]{1,0:T(8,128)(2,1)S(1)} %shard_map.66.refs_1_, bf16[128,256]{1,0:T(8,128)(2,1)S(1)} %collective-permute-done.17.refs_2_, ...), custom_call_target="tpu_custom_call" | custom-call | tf_op jit(solution)/shard_map/pallas_call | solution.py:291
  36.2 0.4 collective-permute-done.19.refs_3_
  36.9 2.0 %collective-permute-start.22 = (s16[256,256]{1,0:T(8,128)(2,1)S(1)}, s16[256,256]{1,0:T(8,128)(2,1)S(1)}, u32[]{:S(2)}, u32[]{:S(2)}) collective-permute-start(s16[256,256]{1,0:T(8,128)(2,1)S(1)} %shard_map.73), channel_id=1, source_target_pairs={{0,3},{1,2},{2,1},{3,0},{4,7},{5,6},{6,5},{7,4},{8,11},{9,10},{10,... | collective-permute-start | bytes 393224 | tf_op jit(solution)/shard_map/ppermute | solution.py:219
  39.2 0.8 %collective-permute-start.23 = (s16[256,256]{1,0:T(8,128)(2,1)S(1)}, s16[256,256]{1,0:T(8,128)(2,1)S(1)}, u32[]{:S(2)}, u32[]{:S(2)}) collective-permute-start(s16[256,256]{1,0:T(8,128)(2,1)S(1)} %shard_map.75), channel_id=1, source_target_pairs={{0,2},{1,3},{2,0},{3,1},{4,6},{5,7},{6,4},{7,5},{8,10},{9,11},{10,... | collective-permute-start | bytes 393224 | tf_op jit(solution)/shard_map/ppermute | solution.py:219
  40.4 0.8 %collective-permute-start.24 = (s16[256,256]{1,0:T(8,128)(2,1)S(1)}, s16[256,256]{1,0:T(8,128)(2,1)S(1)}, u32[]{:S(2)}, u32[]{:S(2)}) collective-permute-start(s16[256,256]{1,0:T(8,128)(2,1)S(1)} %shard_map.77), channel_id=1, source_target_pairs={{0,1},{1,0},{2,3},{3,2},{4,5},{5,4},{6,7},{7,6},{8,9},{9,8},{10,11... | collective-permute-start | bytes 393224 | tf_op jit(solution)/shard_map/ppermute | solution.py:219
  41.5 2.0 %collective-permute-done.22.got = s16[256,256]{1,0:T(8,128)(2,1)S(1)} collective-permute-done((s16[256,256]{1,0:T(8,128)(2,1)S(1)}, s16[256,256]{1,0:T(8,128)(2,1)S(1)}, u32[]{:S(2)}, u32[]{:S(2)}) %collective-permute-start.22) | collective-permute-done | bytes 131104 | tf_op jit(solution)/shard_map/ppermute | solution.py:219
  43.5 2.7 %collective-permute-done.23.got = s16[256,256]{1,0:T(8,128)(2,1)S(1)} collective-permute-done((s16[256,256]{1,0:T(8,128)(2,1)S(1)}, s16[256,256]{1,0:T(8,128)(2,1)S(1)}, u32[]{:S(2)}, u32[]{:S(2)}) %collective-permute-start.23) | collective-permute-done | bytes 131104 | tf_op jit(solution)/shard_map/ppermute | solution.py:219
  46.3 0.7 %shard_map.78 = f32[256,256]{1,0:T(8,128)} custom-call(f32[256,256]{1,0:T(8,128)S(1)} %shard_map.76.total, s16[256,256]{1,0:T(8,128)(2,1)S(1)} %collective-permute-done.24.got), custom_call_target="tpu_custom_call" | custom-call | bytes 16777216 | tf_op jit(solution)/shard_map/pallas_call | solution.py:312
  (42 shorter events, 3.5 us)
Async XLA Ops:
  4.9 4.9 %collective-permute-start.1 = (s16[128,1536]{1,0:T(8,128)(2,1)S(1)}, s16[128,1536]{1,0:T(8,128)(2,1)S(1)}, u32[]{:S(2)}, u32[]{:S(2)}) collective-permute-start(s16[128,1536]{1,0:T(8,128)(2,1)S(1)} %get-tuple-element.37), channel_id=1, source_target_pairs={{0,4},{4,0},{8,12},{12,8},{16,20},{20,16},{24,28},{28,24},{1,5},{5... | collective-permute-start | bytes 1179656 | tf_op jit(solution)/shard_map/ppermute | solution.py:213
  5.0 1.9 %collective-permute-start = (s16[128,512]{1,0:T(8,128)(2,1)S(1)}, s16[128,512]{1,0:T(8,128)(2,1)S(1)}, u32[]{:S(2)}, u32[]{:S(2)}) collective-permute-start(s16[128,512]{1,0:T(8,128)(2,1)S(1)} %get-tuple-element.33), channel_id=1, source_target_pairs={{0,4},{4,0},{8,12},{12,8},{16,20},{20,16},{24,28},{28,24},{1,5},{5... | collective-permute-start | bytes 393224 | tf_op jit(solution)/shard_map/ppermute | solution.py:213
  7.0 4.7 %collective-permute-start.5 = (s16[128,256]{1,0:T(8,128)(2,1)S(1)}, s16[128,256]{1,0:T(8,128)(2,1)S(1)}, u32[]{:S(2)}, u32[]{:S(2)}) collective-permute-start(s16[128,256]{1,0:T(8,128)(2,1)S(1)} %get-tuple-element.35), channel_id=1, source_target_pairs={{0,8},{4,12},{8,0},{12,4},{16,24},{20,28},{24,16},{28,20},{1,9},{5... | collective-permute-start | bytes 196616 | tf_op jit(solution)/shard_map/ppermute | solution.py:216
  10.1 7.4 %collective-permute-start.4 = (s16[128,256]{1,0:T(8,128)(2,1)S(1)}, s16[128,256]{1,0:T(8,128)(2,1)S(1)}, u32[]{:S(2)}, u32[]{:S(2)}) collective-permute-start(s16[128,256]{1,0:T(8,128)(2,1)S(1)} %get-tuple-element.43), channel_id=1, source_target_pairs={{0,8},{4,12},{8,0},{12,4},{16,24},{20,28},{24,16},{28,20},{1,9},{5... | collective-permute-start | bytes 196616 | tf_op jit(solution)/shard_map/ppermute | solution.py:216
  11.8 6.7 %collective-permute-start.9 = (s16[128,256]{1,0:T(8,128)(2,1)S(1)}, s16[128,256]{1,0:T(8,128)(2,1)S(1)}, u32[]{:S(2)}, u32[]{:S(2)}) collective-permute-start(s16[128,256]{1,0:T(8,128)(2,1)S(1)} %shard_map.60.code), channel_id=1, source_target_pairs={{0,16},{4,20},{8,24},{12,28},{16,0},{20,4},{24,8},{28,12},{1,17},{... | collective-permute-start | bytes 196616 | tf_op jit(solution)/shard_map/ppermute | solution.py:216
  15.0 6.0 %collective-permute-start.3 = (s16[128,256]{1,0:T(8,128)(2,1)S(1)}, s16[128,256]{1,0:T(8,128)(2,1)S(1)}, u32[]{:S(2)}, u32[]{:S(2)}) collective-permute-start(s16[128,256]{1,0:T(8,128)(2,1)S(1)} %get-tuple-element.41), channel_id=1, source_target_pairs={{0,8},{4,12},{8,0},{12,4},{16,24},{20,28},{24,16},{28,20},{1,9},{5... | collective-permute-start | bytes 196616 | tf_op jit(solution)/shard_map/ppermute | solution.py:216
  17.5 6.7 %collective-permute-start.2 = (s16[128,256]{1,0:T(8,128)(2,1)S(1)}, s16[128,256]{1,0:T(8,128)(2,1)S(1)}, u32[]{:S(2)}, u32[]{:S(2)}) collective-permute-start(s16[128,256]{1,0:T(8,128)(2,1)S(1)} %get-tuple-element.39), channel_id=1, source_target_pairs={{0,8},{4,12},{8,0},{12,4},{16,24},{20,28},{24,16},{28,20},{1,9},{5... | collective-permute-start | bytes 196616 | tf_op jit(solution)/shard_map/ppermute | solution.py:216
  17.6 7.6 %collective-permute-start.8 = (s16[128,256]{1,0:T(8,128)(2,1)S(1)}, s16[128,256]{1,0:T(8,128)(2,1)S(1)}, u32[]{:S(2)}, u32[]{:S(2)}) collective-permute-start(s16[128,256]{1,0:T(8,128)(2,1)S(1)} %shard_map.61.code), channel_id=1, source_target_pairs={{0,16},{4,20},{8,24},{12,28},{16,0},{20,4},{24,8},{28,12},{1,17},{... | collective-permute-start | bytes 196616 | tf_op jit(solution)/shard_map/ppermute | solution.py:216
  18.5 7.2 %collective-permute-start.10 = (bf16[128,256]{1,0:T(8,128)(2,1)S(1)}, bf16[128,256]{1,0:T(8,128)(2,1)S(1)}, u32[]{:S(2)}, u32[]{:S(2)}) collective-permute-start(bf16[128,256]{1,0:T(8,128)(2,1)S(1)} %shard_map.64.refs_0_), channel_id=1, source_target_pairs={{0,8},{4,12},{8,0},{12,4},{16,24},{20,28},{24,16},{28,20},{1,9},{5... | collective-permute-start | bytes 196616 | tf_op jit(solution)/shard_map/ppermute | solution.py:216
  21.1 5.5 %collective-permute-start.7 = (s16[128,256]{1,0:T(8,128)(2,1)S(1)}, s16[128,256]{1,0:T(8,128)(2,1)S(1)}, u32[]{:S(2)}, u32[]{:S(2)}) collective-permute-start(s16[128,256]{1,0:T(8,128)(2,1)S(1)} %shard_map.62.code), channel_id=1, source_target_pairs={{0,16},{4,20},{8,24},{12,28},{16,0},{20,4},{24,8},{28,12},{1,17},{... | collective-permute-start | bytes 196616 | tf_op jit(solution)/shard_map/ppermute | solution.py:216
  24.3 5.5 %collective-permute-start.6 = (s16[128,256]{1,0:T(8,128)(2,1)S(1)}, s16[128,256]{1,0:T(8,128)(2,1)S(1)}, u32[]{:S(2)}, u32[]{:S(2)}) collective-permute-start(s16[128,256]{1,0:T(8,128)(2,1)S(1)} %shard_map.63.code), channel_id=1, source_target_pairs={{0,16},{4,20},{8,24},{12,28},{16,0},{20,4},{24,8},{28,12},{1,17},{... | collective-permute-start | bytes 196616 | tf_op jit(solution)/shard_map/ppermute | solution.py:216
  25.2 5.7 %collective-permute-start.13 = (bf16[128,256]{1,0:T(8,128)(2,1)S(1)}, bf16[128,256]{1,0:T(8,128)(2,1)S(1)}, u32[]{:S(2)}, u32[]{:S(2)}) collective-permute-start(bf16[128,256]{1,0:T(8,128)(2,1)S(1)} %shard_map.65.refs_1_), channel_id=1, source_target_pairs={{0,8},{4,12},{8,0},{12,4},{16,24},{20,28},{24,16},{28,20},{1,9},{5... | collective-permute-start | bytes 196616 | tf_op jit(solution)/shard_map/ppermute | solution.py:216
  25.7 5.2 %collective-permute-start.11 = (bf16[128,256]{1,0:T(8,128)(2,1)S(1)}, bf16[128,256]{1,0:T(8,128)(2,1)S(1)}, u32[]{:S(2)}, u32[]{:S(2)}) collective-permute-start(bf16[128,256]{1,0:T(8,128)(2,1)S(1)} %shard_map.64.refs_0_), channel_id=1, source_target_pairs={{0,4},{4,0},{8,12},{12,8},{16,20},{20,16},{24,28},{28,24},{1,5},{5... | collective-permute-start | bytes 196616 | tf_op jit(solution)/shard_map/ppermute | solution.py:213
  25.7 5.7 %collective-permute-start.12 = (bf16[128,256]{1,0:T(8,128)(2,1)S(1)}, bf16[128,256]{1,0:T(8,128)(2,1)S(1)}, u32[]{:S(2)}, u32[]{:S(2)}) collective-permute-start(bf16[128,256]{1,0:T(8,128)(2,1)S(1)} %collective-permute-done.10.refs_1_), channel_id=1, source_target_pairs={{0,4},{4,0},{8,12},{12,8},{16,20},{20,16},{24,28},{28,24},{1,5},{5... | collective-permute-start | bytes 196616 | tf_op jit(solution)/shard_map/ppermute | solution.py:213
  26.6 5.7 %collective-permute-start.17 = (bf16[128,256]{1,0:T(8,128)(2,1)S(1)}, bf16[128,256]{1,0:T(8,128)(2,1)S(1)}, u32[]{:S(2)}, u32[]{:S(2)}) collective-permute-start(bf16[128,256]{1,0:T(8,128)(2,1)S(1)} %shard_map.66.refs_1_), channel_id=1, source_target_pairs={{0,8},{4,12},{8,0},{12,4},{16,24},{20,28},{24,16},{28,20},{1,9},{5... | collective-permute-start | bytes 196616 | tf_op jit(solution)/shard_map/ppermute | solution.py:216
  29.8 4.3 %collective-permute-start.16 = (bf16[128,256]{1,0:T(8,128)(2,1)S(1)}, bf16[128,256]{1,0:T(8,128)(2,1)S(1)}, u32[]{:S(2)}, u32[]{:S(2)}) collective-permute-start(bf16[128,256]{1,0:T(8,128)(2,1)S(1)} %shard_map.67.refs_0_), channel_id=1, source_target_pairs={{0,8},{4,12},{8,0},{12,4},{16,24},{20,28},{24,16},{28,20},{1,9},{5... | collective-permute-start | bytes 196616 | tf_op jit(solution)/shard_map/ppermute | solution.py:216
  30.9 3.3 %collective-permute-start.14 = (bf16[128,256]{1,0:T(8,128)(2,1)S(1)}, bf16[128,256]{1,0:T(8,128)(2,1)S(1)}, u32[]{:S(2)}, u32[]{:S(2)}) collective-permute-start(bf16[128,256]{1,0:T(8,128)(2,1)S(1)} %shard_map.65.refs_1_), channel_id=1, source_target_pairs={{0,4},{4,0},{8,12},{12,8},{16,20},{20,16},{24,28},{28,24},{1,5},{5... | collective-permute-start | bytes 196616 | tf_op jit(solution)/shard_map/ppermute | solution.py:213
  30.9 3.3 %collective-permute-start.15 = (bf16[128,256]{1,0:T(8,128)(2,1)S(1)}, bf16[128,256]{1,0:T(8,128)(2,1)S(1)}, u32[]{:S(2)}, u32[]{:S(2)}) collective-permute-start(bf16[128,256]{1,0:T(8,128)(2,1)S(1)} %collective-permute-done.13.refs_2_), channel_id=1, source_target_pairs={{0,4},{4,0},{8,12},{12,8},{16,20},{20,16},{24,28},{28,24},{1,5},{5... | collective-permute-start | bytes 196616 | tf_op jit(solution)/shard_map/ppermute | solution.py:213
  31.9 3.4 %collective-permute-start.20 = (bf16[128,256]{1,0:T(8,128)(2,1)S(1)}, bf16[128,256]{1,0:T(8,128)(2,1)S(1)}, u32[]{:S(2)}, u32[]{:S(2)}) collective-permute-start(bf16[128,256]{1,0:T(8,128)(2,1)S(1)} %shard_map.66.refs_1_), channel_id=1, source_target_pairs={{0,4},{4,0},{8,12},{12,8},{16,20},{20,16},{24,28},{28,24},{1,5},{5... | collective-permute-start | bytes 196616 | tf_op jit(solution)/shard_map/ppermute | solution.py:213
  34.2 1.3 %collective-permute-start.21 = (bf16[128,256]{1,0:T(8,128)(2,1)S(1)}, bf16[128,256]{1,0:T(8,128)(2,1)S(1)}, u32[]{:S(2)}, u32[]{:S(2)}) collective-permute-start(bf16[128,256]{1,0:T(8,128)(2,1)S(1)} %collective-permute-done.17.refs_2_), channel_id=1, source_target_pairs={{0,4},{4,0},{8,12},{12,8},{16,20},{20,16},{24,28},{28,24},{1,5},{5... | collective-permute-start | bytes 196616 | tf_op jit(solution)/shard_map/ppermute | solution.py:213
  34.7 1.5 %collective-permute-start.18 = (bf16[128,256]{1,0:T(8,128)(2,1)S(1)}, bf16[128,256]{1,0:T(8,128)(2,1)S(1)}, u32[]{:S(2)}, u32[]{:S(2)}) collective-permute-start(bf16[128,256]{1,0:T(8,128)(2,1)S(1)} %shard_map.67.refs_0_), channel_id=1, source_target_pairs={{0,4},{4,0},{8,12},{12,8},{16,20},{20,16},{24,28},{28,24},{1,5},{5... | collective-permute-start | bytes 196616 | tf_op jit(solution)/shard_map/ppermute | solution.py:213
  35.2 1.3 %collective-permute-start.19 = (bf16[128,256]{1,0:T(8,128)(2,1)S(1)}, bf16[128,256]{1,0:T(8,128)(2,1)S(1)}, u32[]{:S(2)}, u32[]{:S(2)}) collective-permute-start(bf16[128,256]{1,0:T(8,128)(2,1)S(1)} %collective-permute-done.16.refs_1_), channel_id=1, source_target_pairs={{0,4},{4,0},{8,12},{12,8},{16,20},{20,16},{24,28},{28,24},{1,5},{5... | collective-permute-start | bytes 196616 | tf_op jit(solution)/shard_map/ppermute | solution.py:213
  36.9 6.6 %collective-permute-start.22 = (s16[256,256]{1,0:T(8,128)(2,1)S(1)}, s16[256,256]{1,0:T(8,128)(2,1)S(1)}, u32[]{:S(2)}, u32[]{:S(2)}) collective-permute-start(s16[256,256]{1,0:T(8,128)(2,1)S(1)} %shard_map.73), channel_id=1, source_target_pairs={{0,3},{1,2},{2,1},{3,0},{4,7},{5,6},{6,5},{7,4},{8,11},{9,10},{10,... | collective-permute-start | bytes 393224 | tf_op jit(solution)/shard_map/ppermute | solution.py:219
  39.2 7.0 %collective-permute-start.23 = (s16[256,256]{1,0:T(8,128)(2,1)S(1)}, s16[256,256]{1,0:T(8,128)(2,1)S(1)}, u32[]{:S(2)}, u32[]{:S(2)}) collective-permute-start(s16[256,256]{1,0:T(8,128)(2,1)S(1)} %shard_map.75), channel_id=1, source_target_pairs={{0,2},{1,3},{2,0},{3,1},{4,6},{5,7},{6,4},{7,5},{8,10},{9,11},{10,... | collective-permute-start | bytes 393224 | tf_op jit(solution)/shard_map/ppermute | solution.py:219
  40.4 5.9 %collective-permute-start.24 = (s16[256,256]{1,0:T(8,128)(2,1)S(1)}, s16[256,256]{1,0:T(8,128)(2,1)S(1)}, u32[]{:S(2)}, u32[]{:S(2)}) collective-permute-start(s16[256,256]{1,0:T(8,128)(2,1)S(1)} %shard_map.77), channel_id=1, source_target_pairs={{0,1},{1,0},{2,3},{3,2},{4,5},{5,4},{6,7},{7,6},{8,9},{9,8},{10,11... | collective-permute-start | bytes 393224 | tf_op jit(solution)/shard_map/ppermute | solution.py:219

commit v13 on v5

--- a/solution.py
+++ b/solution.py
@@ -64,42 +64,61 @@
     return jnp.concatenate([turned[pl.ds(x, rows), :] for x in at], axis=0)
 
 
-def dense_kernel(count, rows, cols, sketch, tiles, dense, turned, theirs, place, sketch_here, load_sems, sems):
-    tile = tiles.shape[1]
+def dense_kernel(count, rows, cols, sketch, tiles, dense, turned, theirs, place, stage, sketch_here, load_sems, sems):
+    slots, tile, _ = tiles.shape
     core, _ = core_and_chip()
+    live = count[0]
     rows_place, cols_place = place
+    groups = sems.shape[0]
+    size = slots // groups
     loads = [
         pltpu.make_async_copy(src, dst, load_sems.at[i])
         for i, (src, dst) in enumerate(((rows, rows_place), (cols, cols_place), (sketch, sketch_here)))
     ]
+
+    def group(i):
+        cut = pl.ds(i * size, size)
+        return pltpu.make_async_copy(tiles.at[cut], stage.at[cut], sems.at[i])
+
     for load in loads:
         load.start()
+    for i in range(groups):
+        pl.when(live > i * size)(lambda i=i: group(i).start())
 
     def clear(i, _):
         dense[pl.ds(pl.multiple_of(i * 16, 16), 16), :] = jnp.zeros((16, dense.shape[1]), bf16)
         return 0
 
     lax.fori_loop(0, dense.shape[0] // 16, clear, 0)
+    loads[2].wait()
+    turned[...] = sketch_here[...].T
     for load in loads[:2]:
         load.wait()
 
-    def copy(s):
+    def put(s):
         r = pl.multiple_of(rows_place[s] * tile, tile)
         c = pl.multiple_of(cols_place[s] * tile, tile)
-        return pltpu.make_async_copy(tiles.at[s], dense.at[pl.ds(r, tile), pl.ds(c, tile)], sems.at[s])
-
-    def start(s, _):
-        copy(s).start()
+        dense[pl.ds(r, tile), pl.ds(c, tile)] = stage[s]
+
+    def put_one(s, _):
+        put(s)
         return 0
 
-    def wait(s, _):
-        copy(s).wait()
-        return 0
-
-    lax.fori_loop(0, count[0], start, 0)
-    loads[2].wait()
-    turned[...] = sketch_here[...].T
-    lax.fori_loop(0, count[0], wait, 0)
+    for i in range(groups):
+
+        @pl.when(live > i * size)
+        def _(i=i):
+            group(i).wait()
+
+            @pl.when(live >= (i + 1) * size)
+            def _():
+                for s in range(i * size, (i + 1) * size):
+                    put(s)
+
+            @pl.when(live < (i + 1) * size)
+            def _():
+                lax.fori_loop(i * size, live, put_one, 0)
+
     left = rows_of(turned, 1 - core, theirs.shape[0] // STREAMS)
     width = 512
     for j in range(dense.shape[1] // width):
@@ -233,9 +252,10 @@
         [SMEM] + [HBM] * 4,
         scratch=[
             (pltpu.SMEM((slots,), i32), pltpu.SMEM((slots,), i32)),
+            pltpu.VMEM((slots, tile, tile), bf16),
             pltpu.VMEM((cells, rank), bf16),
             pltpu.SemaphoreType.DMA((3,)),
-            pltpu.SemaphoreType.DMA((slots,)),
+            pltpu.SemaphoreType.DMA((slots // 16 if slots % 16 == 0 else 1,)),
         ],
         flops=flops // 2,
         nbytes=8 * MIB,
@@ -283,8 +303,6 @@
             functools.partial(cell_kernel, k),
             shape((height, rank), kind),
             [VMEM, VMEM],
-            flops=flops // n_genes,
-            nbytes=3 * MIB,
         )(dense, gene)
 
     got = []

time: 46.2 us -> 44.9 us (0.972)
  starting transfers between devices: 21.6 us -> 18.8 us
  waiting for transfers between devices: 14.7 us -> 16.8 us
  Pallas kernels: 8.73 us -> 8.24 us
    ppermute x9, starting transfers between devices: 17.1 us -> 14.2 us  [to_chip(): lax.ppermute(x, 'cells', [(i, i ^ CORES * k) for i in range(n_cells)])]
    ppermute x9, waiting for transfers between devices: 7.63 us -> 9.81 us  [to_chip(): lax.ppermute(x, 'cells', [(i, i ^ CORES * k) for i in range(n_cells)])]
    pallas_call x1, Pallas kernels: 4.29 us -> 3.8 us  [local(): call(dense_kernel, (shape((cells, genes), bf16), shape((rank, cells), bf1...]
  transfers between devices with their start and end apart: 16 -> 16, of which waited for: 12 -> 12; matrix products, arithmetic and copies ran while one was open for 0% -> 0% of each run, Pallas kernels for 5% -> 6%
where the time goes in v13:
time: 44.9 us; the launch traced here: 44.6 us
  starting transfers between devices  18.8 us (42%)
  waiting for transfers between devices  16.8 us (37%)
  Pallas kernels  8.24 us (18%)
  between operations  0.77 us (2%)
    ppermute x9, starting transfers between devices, to_chip(): lax.ppermute(x, 'cells', [(i, i ^ CORES * k) for i in range(n_cells)])  14.2 us
    ppermute x9, waiting for transfers between devices, to_chip(): lax.ppermute(x, 'cells', [(i, i ^ CORES * k) for i in range(n_cells)])  9.81 us
    ppermute x3, waiting for transfers between devices, to_gene(): return lax.ppermute(x, 'genes', [(i, i ^ k) for i in range(n_genes)])  4.44 us
    ppermute x3, starting transfers between devices, to_gene(): return lax.ppermute(x, 'genes', [(i, i ^ k) for i in range(n_genes)])  4.02 us
    pallas_call x1, Pallas kernels, local(): call(dense_kernel, (shape((cells, genes), bf16), shape((rank, cells), bf1...  3.8 us
    ppermute x4, waiting for transfers between devices, to_core(): return lax.ppermute(x, 'cells', [(i, i ^ 1) for i in range(n_cells)])  2.52 us
    pallas_call x4, Pallas kernels, cell(): call(functools.partial(cell_kernel, k), shape((height, rank), kind), [VME...  2.03 us
  transfers between devices with their start and end apart: 16, of which 12 were waited for; matrix products, arithmetic and copies ran while one was open for 0% of the time, Pallas kernels for 6%

profile of v13, /device:TPU:0, one launch (start us, length us, event | category | flops | bytes accessed | tf_op | source)
XLA Modules:
  0.0 44.6 jit_solution(4394590031262714312)
XLA Ops:
  0.7 3.8 %shard_map.55 = (bf16[1024,2048]{1,0:T(8,128)(2,1)S(1)}, bf16[256,1024]{1,0:T(8,128)(2,1)S(1)}, s16[128,2048]{1,0:T(8,128)(2,1)S(1)}) custom-call(s32[1]{0:T(128)S(6)} %copy.6.count, s32[96]{0:T(128)} %rows.1, s32[96]{0:T(128)} %cols.1, bf16[1024,256]{1,0:T(8,128)(2,1)} %sketch.1, bf16[96,128,128]{2,1,0:T(8,128)(2,1)} %tiles.1), custom_call_target="tpu_custom_call" | custom-call | flops 536870912 | bytes 8388608 | tf_op jit(solution)/shard_map/pallas_call | solution.py:249
  4.5 0.7 %shard_map.56.mine = f32[128,2048]{1,0:T(8,128)S(1)} custom-call(bf16[256,1024]{1,0:T(8,128)(2,1)S(1)} %get-tuple-element.18.turned, bf16[1024,2048]{1,0:T(8,128)(2,1)S(1)} %get-tuple-element.17.dense), custom_call_target="tpu_custom_call" | custom-call | flops 536870912 | bytes 5242880 | tf_op jit(solution)/shard_map/pallas_call | solution.py:264
  5.3 1.2 %collective-permute-done.got = s16[128,2048]{1,0:T(8,128)(2,1)S(1)} collective-permute-done((s16[128,2048]{1,0:T(8,128)(2,1)S(1)}, s16[128,2048]{1,0:T(8,128)(2,1)S(1)}, u32[]{:S(2)}, u32[]{:S(2)}) %collective-permute-start) | collective-permute-done | bytes 524320 | tf_op jit(solution)/shard_map/ppermute | solution.py:238
  6.4 0.5 %shard_map.57 = (f32[64,512]{1,0:T(8,128)S(1)}, s16[64,512]{1,0:T(8,128)(2,1)S(1)}, s16[64,512]{1,0:T(8,128)(2,1)S(1)}, s16[64,512]{1,0:T(8,128)(2,1)S(1)}, f32[...) custom-call(f32[128,2048]{1,0:T(8,128)S(1)} %shard_map.56.mine, s16[128,2048]{1,0:T(8,128)(2,1)S(1)} %collective-permute-done.got), custom_call_target="tpu_custom_call" | custom-call | bytes 3145728 | tf_op jit(solution)/shard_map/pallas_call | solution.py:268
  6.9 2.4 %collective-permute-start.7 = (s16[64,1024]{1,0:T(8,128)(2,1)S(1)}, s16[64,1024]{1,0:T(8,128)(2,1)S(1)}, u32[]{:S(2)}, u32[]{:S(2)}) collective-permute-start(s16[64,1024]{1,0:T(8,128)(2,1)S(1)} %get-tuple-element.25), channel_id=1, source_target_pairs={{0,8},{4,12},{8,0},{12,4},{16,24},{20,28},{24,16},{28,20},{1,9},{5... | collective-permute-start | bytes 393224 | tf_op jit(solution)/shard_map/ppermute | solution.py:241
  9.3 1.9 %collective-permute-start.1 = (s16[64,512]{1,0:T(8,128)(2,1)S(1)}, s16[64,512]{1,0:T(8,128)(2,1)S(1)}, u32[]{:S(2)}, u32[]{:S(2)}) collective-permute-start(s16[64,512]{1,0:T(8,128)(2,1)S(1)} %get-tuple-element.21), channel_id=1, source_target_pairs={{0,24},{4,28},{8,16},{12,20},{16,8},{20,12},{24,0},{28,4},{1,25},{... | collective-permute-start | bytes 196616 | tf_op jit(solution)/shard_map/ppermute | solution.py:241
  11.1 0.4 collective-permute-start.2
  11.5 1.6 %collective-permute-done.7.got = s16[64,1024]{1,0:T(8,128)(2,1)S(1)} collective-permute-done((s16[64,1024]{1,0:T(8,128)(2,1)S(1)}, s16[64,1024]{1,0:T(8,128)(2,1)S(1)}, u32[]{:S(2)}, u32[]{:S(2)}) %collective-permute-start.7) | collective-permute-done | bytes 131104 | tf_op jit(solution)/shard_map/ppermute | solution.py:241
  13.1 0.1 shard_map.59.code
  13.3 2.9 %collective-permute-start.8 = (s16[64,1024]{1,0:T(8,128)(2,1)S(1)}, s16[64,1024]{1,0:T(8,128)(2,1)S(1)}, u32[]{:S(2)}, u32[]{:S(2)}) collective-permute-start(s16[64,1024]{1,0:T(8,128)(2,1)S(1)} %shard_map.59.code), channel_id=1, source_target_pairs={{0,16},{4,20},{8,24},{12,28},{16,0},{20,4},{24,8},{28,12},{1,17},{... | collective-permute-start | bytes 393224 | tf_op jit(solution)/shard_map/ppermute | solution.py:241
  16.2 2.1 %collective-permute-start.3 = (s16[64,512]{1,0:T(8,128)(2,1)S(1)}, s16[64,512]{1,0:T(8,128)(2,1)S(1)}, u32[]{:S(2)}, u32[]{:S(2)}) collective-permute-start(s16[64,512]{1,0:T(8,128)(2,1)S(1)} %get-tuple-element.23), channel_id=1, source_target_pairs={{0,8},{4,12},{8,0},{12,4},{16,24},{20,28},{24,16},{28,20},{1,9},{5... | collective-permute-start | bytes 196616 | tf_op jit(solution)/shard_map/ppermute | solution.py:241
  18.3 3.6 %collective-permute-done.2.refs_1_ = s16[64,512]{1,0:T(8,128)(2,1)S(1)} collective-permute-done((s16[64,512]{1,0:T(8,128)(2,1)S(1)}, s16[64,512]{1,0:T(8,128)(2,1)S(1)}, u32[]{:S(2)}, u32[]{:S(2)}) %collective-permute-start.2) | collective-permute-done | bytes 65568 | tf_op jit(solution)/shard_map/ppermute | solution.py:241
  22.0 2.4 %collective-permute-start.6 = (bf16[64,512]{1,0:T(8,128)(2,1)S(1)}, bf16[64,512]{1,0:T(8,128)(2,1)S(1)}, u32[]{:S(2)}, u32[]{:S(2)}) collective-permute-start(bf16[64,512]{1,0:T(8,128)(2,1)S(1)} %shard_map.58.refs_0_), channel_id=1, source_target_pairs={{0,24},{4,28},{8,16},{12,20},{16,8},{20,12},{24,0},{28,4},{1,25},{... | collective-permute-start | bytes 196616 | tf_op jit(solution)/shard_map/ppermute | solution.py:241
  24.4 2.1 %collective-permute-start.4 = (bf16[64,512]{1,0:T(8,128)(2,1)S(1)}, bf16[64,512]{1,0:T(8,128)(2,1)S(1)}, u32[]{:S(2)}, u32[]{:S(2)}) collective-permute-start(bf16[64,512]{1,0:T(8,128)(2,1)S(1)} %shard_map.58.refs_0_), channel_id=1, source_target_pairs={{0,8},{4,12},{8,0},{12,4},{16,24},{20,28},{24,16},{28,20},{1,9},{5... | collective-permute-start | bytes 196616 | tf_op jit(solution)/shard_map/ppermute | solution.py:241
  26.6 2.2 %collective-permute-done.6.refs_3_ = bf16[64,512]{1,0:T(8,128)(2,1)S(1)} collective-permute-done((bf16[64,512]{1,0:T(8,128)(2,1)S(1)}, bf16[64,512]{1,0:T(8,128)(2,1)S(1)}, u32[]{:S(2)}, u32[]{:S(2)}) %collective-permute-start.6) | collective-permute-done | bytes 65568 | tf_op jit(solution)/shard_map/ppermute | solution.py:241
  28.8 1.4 %collective-permute-done.5.refs_2_ = bf16[64,512]{1,0:T(8,128)(2,1)S(1)} collective-permute-done((bf16[64,512]{1,0:T(8,128)(2,1)S(1)}, bf16[64,512]{1,0:T(8,128)(2,1)S(1)}, u32[]{:S(2)}, u32[]{:S(2)}) %collective-permute-start.5) | collective-permute-done | bytes 65568 | tf_op jit(solution)/shard_map/ppermute | solution.py:241
  30.3 0.1 collective-permute-done.4.refs_1_
  30.5 0.5 %collective-permute-start.11 = (bf16[64,1024]{1,0:T(8,128)(2,1)S(1)}, bf16[64,1024]{1,0:T(8,128)(2,1)S(1)}, u32[]{:S(2)}, u32[]{:S(2)}) collective-permute-start(bf16[64,1024]{1,0:T(8,128)(2,1)S(1)} %shard_map.60.refs_0_), channel_id=1, source_target_pairs={{0,4},{4,0},{8,12},{12,8},{16,20},{20,16},{24,28},{28,24},{1,5},{5... | collective-permute-start | bytes 393224 | tf_op jit(solution)/shard_map/ppermute | solution.py:238
  31.0 0.8 %collective-permute-done.10.refs_1_ = bf16[64,1024]{1,0:T(8,128)(2,1)S(1)} collective-permute-done((bf16[64,1024]{1,0:T(8,128)(2,1)S(1)}, bf16[64,1024]{1,0:T(8,128)(2,1)S(1)}, u32[]{:S(2)}, u32[]{:S(2)}) %collective-permute-start.10) | collective-permute-done | bytes 131104 | tf_op jit(solution)/shard_map/ppermute | solution.py:241
  31.8 0.4 collective-permute-done.11.refs_2_
  32.2 0.9 %collective-permute-done.12.refs_3_ = bf16[64,1024]{1,0:T(8,128)(2,1)S(1)} collective-permute-done((bf16[64,1024]{1,0:T(8,128)(2,1)S(1)}, bf16[64,1024]{1,0:T(8,128)(2,1)S(1)}, u32[]{:S(2)}, u32[]{:S(2)}) %collective-permute-start.12) | collective-permute-done | bytes 131104 | tf_op jit(solution)/shard_map/ppermute | solution.py:238
  33.2 0.5 %shard_map.64 = s16[256,256]{1,0:T(8,128)(2,1)S(1)} custom-call(bf16[1024,2048]{1,0:T(8,128)(2,1)S(1)} %get-tuple-element.17.dense, bf16[256,2048]{1,0:T(8,128)(2,1)S(1)} %shard_map.62.gene), custom_call_target="tpu_custom_call" | custom-call | tf_op jit(solution)/shard_map/pallas_call | solution.py:302
  33.8 3.3 %collective-permute-start.13 = (s16[256,256]{1,0:T(8,128)(2,1)S(1)}, s16[256,256]{1,0:T(8,128)(2,1)S(1)}, u32[]{:S(2)}, u32[]{:S(2)}) collective-permute-start(s16[256,256]{1,0:T(8,128)(2,1)S(1)} %shard_map.64), channel_id=1, source_target_pairs={{0,3},{1,2},{2,1},{3,0},{4,7},{5,6},{6,5},{7,4},{8,11},{9,10},{10,... | collective-permute-start | bytes 393224 | tf_op jit(solution)/shard_map/ppermute | solution.py:244
  37.1 0.5 %shard_map.66 = s16[256,256]{1,0:T(8,128)(2,1)S(1)} custom-call(bf16[1024,2048]{1,0:T(8,128)(2,1)S(1)} %get-tuple-element.17.dense, bf16[256,2048]{1,0:T(8,128)(2,1)S(1)} %shard_map.62.gene), custom_call_target="tpu_custom_call" | custom-call | tf_op jit(solution)/shard_map/pallas_call | solution.py:302
  37.6 0.5 %collective-permute-start.14 = (s16[256,256]{1,0:T(8,128)(2,1)S(1)}, s16[256,256]{1,0:T(8,128)(2,1)S(1)}, u32[]{:S(2)}, u32[]{:S(2)}) collective-permute-start(s16[256,256]{1,0:T(8,128)(2,1)S(1)} %shard_map.66), channel_id=1, source_target_pairs={{0,2},{1,3},{2,0},{3,1},{4,6},{5,7},{6,4},{7,5},{8,10},{9,11},{10,... | collective-permute-start | bytes 393224 | tf_op jit(solution)/shard_map/ppermute | solution.py:244
  38.1 0.5 %shard_map.68 = s16[256,256]{1,0:T(8,128)(2,1)S(1)} custom-call(bf16[1024,2048]{1,0:T(8,128)(2,1)S(1)} %get-tuple-element.17.dense, bf16[256,2048]{1,0:T(8,128)(2,1)S(1)} %shard_map.62.gene), custom_call_target="tpu_custom_call" | custom-call | tf_op jit(solution)/shard_map/pallas_call | solution.py:302
  38.6 0.2 collective-permute-start.15
  38.8 0.5 %shard_map.63.total = f32[256,256]{1,0:T(8,128)S(1)} custom-call(bf16[1024,2048]{1,0:T(8,128)(2,1)S(1)} %get-tuple-element.17.dense, bf16[256,2048]{1,0:T(8,128)(2,1)S(1)} %shard_map.62.gene), custom_call_target="tpu_custom_call" | custom-call | tf_op jit(solution)/shard_map/pallas_call | solution.py:302
  39.3 1.7 %collective-permute-done.13.got = s16[256,256]{1,0:T(8,128)(2,1)S(1)} collective-permute-done((s16[256,256]{1,0:T(8,128)(2,1)S(1)}, s16[256,256]{1,0:T(8,128)(2,1)S(1)}, u32[]{:S(2)}, u32[]{:S(2)}) %collective-permute-start.13) | collective-permute-done | bytes 131104 | tf_op jit(solution)/shard_map/ppermute | solution.py:244
  41.0 2.7 %collective-permute-done.14.got = s16[256,256]{1,0:T(8,128)(2,1)S(1)} collective-permute-done((s16[256,256]{1,0:T(8,128)(2,1)S(1)}, s16[256,256]{1,0:T(8,128)(2,1)S(1)}, u32[]{:S(2)}, u32[]{:S(2)}) %collective-permute-start.14) | collective-permute-done | bytes 131104 | tf_op jit(solution)/shard_map/ppermute | solution.py:244
  43.7 0.1 collective-permute-done.15.got
  43.9 0.7 %shard_map.69 = f32[256,256]{1,0:T(8,128)} custom-call(f32[256,256]{1,0:T(8,128)S(1)} %shard_map.67.total, s16[256,256]{1,0:T(8,128)(2,1)S(1)} %collective-permute-done.15.got), custom_call_target="tpu_custom_call" | custom-call | bytes 16777216 | tf_op jit(solution)/shard_map/pallas_call | solution.py:313
  (15 shorter events, 0.6 us)
Async XLA Ops:
  4.5 2.0 %collective-permute-start = (s16[128,2048]{1,0:T(8,128)(2,1)S(1)}, s16[128,2048]{1,0:T(8,128)(2,1)S(1)}, u32[]{:S(2)}, u32[]{:S(2)}) collective-permute-start(s16[128,2048]{1,0:T(8,128)(2,1)S(1)} %get-tuple-element.19), channel_id=1, source_target_pairs={{0,4},{4,0},{8,12},{12,8},{16,20},{20,16},{24,28},{28,24},{1,5},{5... | collective-permute-start | bytes 1572872 | tf_op jit(solution)/shard_map/ppermute | solution.py:238
  6.9 6.2 %collective-permute-start.7 = (s16[64,1024]{1,0:T(8,128)(2,1)S(1)}, s16[64,1024]{1,0:T(8,128)(2,1)S(1)}, u32[]{:S(2)}, u32[]{:S(2)}) collective-permute-start(s16[64,1024]{1,0:T(8,128)(2,1)S(1)} %get-tuple-element.25), channel_id=1, source_target_pairs={{0,8},{4,12},{8,0},{12,4},{16,24},{20,28},{24,16},{28,20},{1,9},{5... | collective-permute-start | bytes 393224 | tf_op jit(solution)/shard_map/ppermute | solution.py:241
  9.3 9.0 %collective-permute-start.1 = (s16[64,512]{1,0:T(8,128)(2,1)S(1)}, s16[64,512]{1,0:T(8,128)(2,1)S(1)}, u32[]{:S(2)}, u32[]{:S(2)}) collective-permute-start(s16[64,512]{1,0:T(8,128)(2,1)S(1)} %get-tuple-element.21), channel_id=1, source_target_pairs={{0,24},{4,28},{8,16},{12,20},{16,8},{20,12},{24,0},{28,4},{1,25},{... | collective-permute-start | bytes 196616 | tf_op jit(solution)/shard_map/ppermute | solution.py:241
  11.1 10.7 %collective-permute-start.2 = (s16[64,512]{1,0:T(8,128)(2,1)S(1)}, s16[64,512]{1,0:T(8,128)(2,1)S(1)}, u32[]{:S(2)}, u32[]{:S(2)}) collective-permute-start(s16[64,512]{1,0:T(8,128)(2,1)S(1)} %get-tuple-element.22), channel_id=1, source_target_pairs={{0,16},{4,20},{8,24},{12,28},{16,0},{20,4},{24,8},{28,12},{1,17},{... | collective-permute-start | bytes 196616 | tf_op jit(solution)/shard_map/ppermute | solution.py:241
  13.3 13.2 %collective-permute-start.8 = (s16[64,1024]{1,0:T(8,128)(2,1)S(1)}, s16[64,1024]{1,0:T(8,128)(2,1)S(1)}, u32[]{:S(2)}, u32[]{:S(2)}) collective-permute-start(s16[64,1024]{1,0:T(8,128)(2,1)S(1)} %shard_map.59.code), channel_id=1, source_target_pairs={{0,16},{4,20},{8,24},{12,28},{16,0},{20,4},{24,8},{28,12},{1,17},{... | collective-permute-start | bytes 393224 | tf_op jit(solution)/shard_map/ppermute | solution.py:241
  16.2 5.7 %collective-permute-start.3 = (s16[64,512]{1,0:T(8,128)(2,1)S(1)}, s16[64,512]{1,0:T(8,128)(2,1)S(1)}, u32[]{:S(2)}, u32[]{:S(2)}) collective-permute-start(s16[64,512]{1,0:T(8,128)(2,1)S(1)} %get-tuple-element.23), channel_id=1, source_target_pairs={{0,8},{4,12},{8,0},{12,4},{16,24},{20,28},{24,16},{28,20},{1,9},{5... | collective-permute-start | bytes 196616 | tf_op jit(solution)/shard_map/ppermute | solution.py:241
  22.0 6.8 %collective-permute-start.6 = (bf16[64,512]{1,0:T(8,128)(2,1)S(1)}, bf16[64,512]{1,0:T(8,128)(2,1)S(1)}, u32[]{:S(2)}, u32[]{:S(2)}) collective-permute-start(bf16[64,512]{1,0:T(8,128)(2,1)S(1)} %shard_map.58.refs_0_), channel_id=1, source_target_pairs={{0,24},{4,28},{8,16},{12,20},{16,8},{20,12},{24,0},{28,4},{1,25},{... | collective-permute-start | bytes 196616 | tf_op jit(solution)/shard_map/ppermute | solution.py:241
  24.4 5.9 %collective-permute-start.5 = (bf16[64,512]{1,0:T(8,128)(2,1)S(1)}, bf16[64,512]{1,0:T(8,128)(2,1)S(1)}, u32[]{:S(2)}, u32[]{:S(2)}) collective-permute-start(bf16[64,512]{1,0:T(8,128)(2,1)S(1)} %shard_map.58.refs_0_), channel_id=1, source_target_pairs={{0,16},{4,20},{8,24},{12,28},{16,0},{20,4},{24,8},{28,12},{1,17},{... | collective-permute-start | bytes 196616 | tf_op jit(solution)/shard_map/ppermute | solution.py:241
  24.4 6.0 %collective-permute-start.4 = (bf16[64,512]{1,0:T(8,128)(2,1)S(1)}, bf16[64,512]{1,0:T(8,128)(2,1)S(1)}, u32[]{:S(2)}, u32[]{:S(2)}) collective-permute-start(bf16[64,512]{1,0:T(8,128)(2,1)S(1)} %shard_map.58.refs_0_), channel_id=1, source_target_pairs={{0,8},{4,12},{8,0},{12,4},{16,24},{20,28},{24,16},{28,20},{1,9},{5... | collective-permute-start | bytes 196616 | tf_op jit(solution)/shard_map/ppermute | solution.py:241
  26.5 5.3 %collective-permute-start.10 = (bf16[64,1024]{1,0:T(8,128)(2,1)S(1)}, bf16[64,1024]{1,0:T(8,128)(2,1)S(1)}, u32[]{:S(2)}, u32[]{:S(2)}) collective-permute-start(bf16[64,1024]{1,0:T(8,128)(2,1)S(1)} %shard_map.60.refs_0_), channel_id=1, source_target_pairs={{0,8},{4,12},{8,0},{12,4},{16,24},{20,28},{24,16},{28,20},{1,9},{5... | collective-permute-start | bytes 393224 | tf_op jit(solution)/shard_map/ppermute | solution.py:241
  30.4 2.7 %collective-permute-start.9 = (bf16[64,2048]{1,0:T(8,128)(2,1)S(1)}, bf16[64,2048]{1,0:T(8,128)(2,1)S(1)}, u32[]{:S(2)}, u32[]{:S(2)}) collective-permute-start(bf16[64,2048]{1,0:T(8,128)(2,1)S(1)} %shard_map.61.first), channel_id=1, source_target_pairs={{0,4},{4,0},{8,12},{12,8},{16,20},{20,16},{24,28},{28,24},{1,5},{5... | collective-permute-start | bytes 786440 | tf_op jit(solution)/shard_map/ppermute | solution.py:238
  30.5 1.7 %collective-permute-start.11 = (bf16[64,1024]{1,0:T(8,128)(2,1)S(1)}, bf16[64,1024]{1,0:T(8,128)(2,1)S(1)}, u32[]{:S(2)}, u32[]{:S(2)}) collective-permute-start(bf16[64,1024]{1,0:T(8,128)(2,1)S(1)} %shard_map.60.refs_0_), channel_id=1, source_target_pairs={{0,4},{4,0},{8,12},{12,8},{16,20},{20,16},{24,28},{28,24},{1,5},{5... | collective-permute-start | bytes 393224 | tf_op jit(solution)/shard_map/ppermute | solution.py:238
  31.8 1.3 %collective-permute-start.12 = (bf16[64,1024]{1,0:T(8,128)(2,1)S(1)}, bf16[64,1024]{1,0:T(8,128)(2,1)S(1)}, u32[]{:S(2)}, u32[]{:S(2)}) collective-permute-start(bf16[64,1024]{1,0:T(8,128)(2,1)S(1)} %collective-permute-done.10.refs_1_), channel_id=1, source_target_pairs={{0,4},{4,0},{8,12},{12,8},{16,20},{20,16},{24,28},{28,24},{1,5},{5... | collective-permute-start | bytes 393224 | tf_op jit(solution)/shard_map/ppermute | solution.py:238
  33.8 7.2 %collective-permute-start.13 = (s16[256,256]{1,0:T(8,128)(2,1)S(1)}, s16[256,256]{1,0:T(8,128)(2,1)S(1)}, u32[]{:S(2)}, u32[]{:S(2)}) collective-permute-start(s16[256,256]{1,0:T(8,128)(2,1)S(1)} %shard_map.64), channel_id=1, source_target_pairs={{0,3},{1,2},{2,1},{3,0},{4,7},{5,6},{6,5},{7,4},{8,11},{9,10},{10,... | collective-permute-start | bytes 393224 | tf_op jit(solution)/shard_map/ppermute | solution.py:244
  37.6 6.1 %collective-permute-start.14 = (s16[256,256]{1,0:T(8,128)(2,1)S(1)}, s16[256,256]{1,0:T(8,128)(2,1)S(1)}, u32[]{:S(2)}, u32[]{:S(2)}) collective-permute-start(s16[256,256]{1,0:T(8,128)(2,1)S(1)} %shard_map.66), channel_id=1, source_target_pairs={{0,2},{1,3},{2,0},{3,1},{4,6},{5,7},{6,4},{7,5},{8,10},{9,11},{10,... | collective-permute-start | bytes 393224 | tf_op jit(solution)/shard_map/ppermute | solution.py:244
  38.6 5.2 %collective-permute-start.15 = (s16[256,256]{1,0:T(8,128)(2,1)S(1)}, s16[256,256]{1,0:T(8,128)(2,1)S(1)}, u32[]{:S(2)}, u32[]{:S(2)}) collective-permute-start(s16[256,256]{1,0:T(8,128)(2,1)S(1)} %shard_map.68), channel_id=1, source_target_pairs={{0,1},{1,0},{2,3},{3,2},{4,5},{5,4},{6,7},{7,6},{8,9},{9,8},{10,11... | collective-permute-start | bytes 393224 | tf_op jit(solution)/shard_map/ppermute | solution.py:244

commit v14 on v13

--- a/solution.py
+++ b/solution.py
@@ -9,7 +9,7 @@
 
 GENE_BLOCKS = 16
 CORES = 2
-STREAMS = 2
+DIRECT = (1, 2)
 MIB = 1 << 20
 
 VMEM = pl.BlockSpec(memory_space=pltpu.VMEM)
@@ -32,13 +32,15 @@
     out[at + (pl.ds(16, x.shape[0] - 16),)] = code[16:].astype(i16)
 
 
-def decode(code):
-    code = code.astype(i32)
-    head = code[:8]
+def scale_of(head):
+    head = head.astype(i32)
     row = lax.broadcasted_iota(i32, head.shape, 0)
     word = jnp.sum((head & 1) << row, axis=0, keepdims=True)
-    scale = jnp.exp2((word - (128 + 14)).astype(f32))
-    return code.astype(f32) * scale
+    return jnp.exp2((word - (128 + 14)).astype(f32))
+
+
+def decode(code):
+    return code.astype(f32) * scale_of(code[:8])
 
 
 def core_and_chip():
@@ -59,9 +61,7 @@
 
 
 def rows_of(turned, core, rows):
-    span = rows * CORES
-    at = [pl.multiple_of(i * span + core * rows, rows) for i in range(STREAMS)]
-    return jnp.concatenate([turned[pl.ds(x, rows), :] for x in at], axis=0)
+    return turned[pl.ds(pl.multiple_of(core * rows, rows), rows), :]
 
 
 def dense_kernel(count, rows, cols, sketch, tiles, dense, turned, theirs, place, stage, sketch_here, load_sems, sems):
@@ -119,7 +119,7 @@
             def _():
                 lax.fori_loop(i * size, live, put_one, 0)
 
-    left = rows_of(turned, 1 - core, theirs.shape[0] // STREAMS)
+    left = rows_of(turned, 1 - core, theirs.shape[0])
     width = 512
     for j in range(dense.shape[1] // width):
         cut = pl.ds(j * width, width)
@@ -128,7 +128,7 @@
 
 def own_kernel(turned, dense, mine):
     core, _ = core_and_chip()
-    left = rows_of(turned, core, mine.shape[0] // STREAMS)
+    left = rows_of(turned, core, mine.shape[0])
     mine[...] = jnp.dot(left, dense[...], preferred_element_type=f32)
 
 
@@ -141,18 +141,25 @@
     encode(jnp.where(ours == 0, high, low), send)
 
 
-def pair_kernel(chips, mine, got, *refs):
-    *outs, total = refs
+def pair_kernel(chips, mine, got, *outs):
     direct, rest = outs[:chips], outs[chips:]
     _, chip = core_and_chip()
-    total[...] = mine[...] + decode(got[...])
-    rows, width = direct[0].shape
+    lead = direct[0].shape[0]
+    share, genes = mine.shape
+
+    def total(rows, index, width):
+        cut = pl.ds(pl.multiple_of(index * width, width), width)
+        return mine[rows, cut] + got[rows, cut].astype(f32) * scale_of(got[:16, cut][:8])
+
     if len(rest) == 2:
-        halve(total[rows:, :], 0, *rest)
+        ours = chip & 1
+        keep, send = rest
+        encode(total(slice(lead, share), 1 - ours, genes // 2), send)
+        keep[...] = total(slice(lead, share), ours, genes // 2)
     else:
-        encode(total[rows:, :], rest[0])
+        encode(total(slice(lead, share), 0, genes), rest[0])
     for k, out in enumerate(direct):
-        part = total[:rows, pl.ds(pl.multiple_of((chip ^ k) * width, width), width)]
+        part = total(slice(0, lead), chip ^ k, out.shape[1])
         if k == 0:
             out[...] = part
         else:
@@ -191,9 +198,11 @@
     *pieces, gene = refs
     core, chip = core_and_chip()
     rows, width = pieces[0].shape
+    lead = first.shape[0]
 
     def at(stream, owner):
-        return pl.ds(pl.multiple_of((stream * CORES + owner) * rows, rows), rows)
+        start = owner * (lead + rows) + stream * lead
+        return pl.ds(pl.multiple_of(start, 16), rows if stream else lead)
 
     gene[at(0, core), :] = first[...]
     gene[at(0, 1 - core), :] = first_theirs[...]
@@ -227,9 +236,9 @@
     slots, tile, _ = tiles.shape
     genes = GENE_BLOCKS * tile
     bits = (n_cells // CORES).bit_length() - 1
-    span = rank // STREAMS
-    rows = span // CORES
-    share = rows * STREAMS
+    share = rank // CORES
+    lead = share * DIRECT[0] // DIRECT[1] // 16 * 16
+    rows = share - lead
     height = cells // n_genes
     flops = 2 * cells * genes * rank
     shape = jax.ShapeDtypeStruct
@@ -267,9 +276,8 @@
     one = halves(genes) if bits > 1 else (shape((rows, genes), i16),)
     pieces = call(
         functools.partial(pair_kernel, chips),
-        (shape((rows, chunk), f32),) + (shape((rows, chunk), i16),) * (chips - 1) + one,
+        (shape((lead, chunk), f32),) + (shape((lead, chunk), i16),) * (chips - 1) + one,
         [VMEM, VMEM],
-        scratch=[pltpu.VMEM((share, genes), f32)],
         nbytes=3 * MIB,
     )(mine, got)
     direct, half = pieces[:chips], pieces[chips:]
@@ -282,12 +290,12 @@
             half[0], to_chip(half[1], 1 << bit)
         )
     came = [to_chip(direct[k], k) for k in reversed(range(1, chips))]
-    summed = call(direct_cast_kernel, shape((rows, chunk), bf16), [VMEM] * chips, nbytes=MIB)(direct[0], *came)
+    summed = call(direct_cast_kernel, shape((lead, chunk), bf16), [VMEM] * chips, nbytes=MIB)(direct[0], *came)
     crossed = to_chip(half[-1], chips // 2)
     spread = [to_chip(summed, k) for k in reversed(range(1, chips))][::-1]
     held = [call(cast_kernel, shape((rows, width), bf16), [VMEM, VMEM], nbytes=MIB)(half[-1], crossed)]
     *spread, _ = lax.optimization_barrier((*spread, held[0]))
-    first = call(join_kernel, shape((rows, genes), bf16), [VMEM] * chips, nbytes=MIB)(summed, *spread)
+    first = call(join_kernel, shape((lead, genes), bf16), [VMEM] * chips, nbytes=MIB)(summed, *spread)
     masks = [0]
     for bit in reversed(range(bits - 1)):
         held = held + [to_chip(x, 1 << bit) for x in held]

time: 44.9 us -> 44.7 us (level)
  starting transfers between devices: 18.8 us -> 19.7 us
  waiting for transfers between devices: 16.8 us -> 16 us
    ppermute x9, waiting for transfers between devices: 9.81 us -> 9.11 us  [to_chip(): lax.ppermute(x, 'cells', [(i, i ^ CORES * k) for i in range(n_cells)])]
    ppermute x9, starting transfers between devices: 14.2 us -> 14.8 us  [to_chip(): lax.ppermute(x, 'cells', [(i, i ^ CORES * k) for i in range(n_cells)])]
  transfers between devices with their start and end apart: 16 -> 16, of which waited for: 12 -> 11; matrix products, arithmetic and copies ran while one was open for 0% -> 0% of each run, Pallas kernels for 6% -> 6%
where the time goes in v14:
time: 44.7 us; the launch traced here: 44.6 us
  starting transfers between devices  19.7 us (44%)
  waiting for transfers between devices  16 us (36%)
  Pallas kernels  8.12 us (18%)
  between operations  0.77 us (2%)
    ppermute x9, starting transfers between devices, to_chip(): lax.ppermute(x, 'cells', [(i, i ^ CORES * k) for i in range(n_cells)])  14.8 us
    ppermute x9, waiting for transfers between devices, to_chip(): lax.ppermute(x, 'cells', [(i, i ^ CORES * k) for i in range(n_cells)])  9.11 us
    ppermute x3, waiting for transfers between devices, to_gene(): return lax.ppermute(x, 'genes', [(i, i ^ k) for i in range(n_genes)])  4.33 us
    ppermute x3, starting transfers between devices, to_gene(): return lax.ppermute(x, 'genes', [(i, i ^ k) for i in range(n_genes)])  4.32 us
    pallas_call x1, Pallas kernels, local(): call(dense_kernel, (shape((cells, genes), bf16), shape((rank, cells), bf1...  3.79 us
    ppermute x4, waiting for transfers between devices, to_core(): return lax.ppermute(x, 'cells', [(i, i ^ 1) for i in range(n_cells)])  2.52 us
    pallas_call x4, Pallas kernels, cell(): call(functools.partial(cell_kernel, k), shape((height, rank), kind), [VME...  2.03 us
  transfers between devices with their start and end apart: 16, of which 11 were waited for; matrix products, arithmetic and copies ran while one was open for 0% of the time, Pallas kernels for 6%

profile of v14, /device:TPU:0, one launch (start us, length us, event | category | flops | bytes accessed | tf_op | source)
XLA Modules:
  0.0 44.6 jit_solution(16689677365678030263)
XLA Ops:
  0.7 3.8 %shard_map.55 = (bf16[1024,2048]{1,0:T(8,128)(2,1)S(1)}, bf16[256,1024]{1,0:T(8,128)(2,1)S(1)}, s16[128,2048]{1,0:T(8,128)(2,1)S(1)}) custom-call(s32[1]{0:T(128)S(6)} %copy.6.count, s32[96]{0:T(128)} %rows.1, s32[96]{0:T(128)} %cols.1, bf16[1024,256]{1,0:T(8,128)(2,1)} %sketch.1, bf16[96,128,128]{2,1,0:T(8,128)(2,1)} %tiles.1), custom_call_target="tpu_custom_call" | custom-call | flops 536870912 | bytes 8388608 | tf_op jit(solution)/shard_map/pallas_call | solution.py:258
  4.5 0.7 %shard_map.56.mine = f32[128,2048]{1,0:T(8,128)S(1)} custom-call(bf16[256,1024]{1,0:T(8,128)(2,1)S(1)} %get-tuple-element.18.turned, bf16[1024,2048]{1,0:T(8,128)(2,1)S(1)} %get-tuple-element.17.dense), custom_call_target="tpu_custom_call" | custom-call | flops 536870912 | bytes 5242880 | tf_op jit(solution)/shard_map/pallas_call | solution.py:273
  5.3 1.2 %collective-permute-done.got = s16[128,2048]{1,0:T(8,128)(2,1)S(1)} collective-permute-done((s16[128,2048]{1,0:T(8,128)(2,1)S(1)}, s16[128,2048]{1,0:T(8,128)(2,1)S(1)}, u32[]{:S(2)}, u32[]{:S(2)}) %collective-permute-start) | collective-permute-done | bytes 524320 | tf_op jit(solution)/shard_map/ppermute | solution.py:247
  6.4 0.4 shard_map.57
  6.8 2.0 %collective-permute-start.7 = (s16[64,1024]{1,0:T(8,128)(2,1)S(1)}, s16[64,1024]{1,0:T(8,128)(2,1)S(1)}, u32[]{:S(2)}, u32[]{:S(2)}) collective-permute-start(s16[64,1024]{1,0:T(8,128)(2,1)S(1)} %get-tuple-element.25), channel_id=1, source_target_pairs={{0,8},{4,12},{8,0},{12,4},{16,24},{20,28},{24,16},{28,20},{1,9},{5... | collective-permute-start | bytes 393224 | tf_op jit(solution)/shard_map/ppermute | solution.py:250
  8.8 2.2 %collective-permute-start.1 = (s16[64,512]{1,0:T(8,128)(2,1)S(1)}, s16[64,512]{1,0:T(8,128)(2,1)S(1)}, u32[]{:S(2)}, u32[]{:S(2)}) collective-permute-start(s16[64,512]{1,0:T(8,128)(2,1)S(1)} %get-tuple-element.21), channel_id=1, source_target_pairs={{0,24},{4,28},{8,16},{12,20},{16,8},{20,12},{24,0},{28,4},{1,25},{... | collective-permute-start | bytes 196616 | tf_op jit(solution)/shard_map/ppermute | solution.py:250
  11.0 0.3 collective-permute-start.2
  11.3 1.4 %collective-permute-done.7.got = s16[64,1024]{1,0:T(8,128)(2,1)S(1)} collective-permute-done((s16[64,1024]{1,0:T(8,128)(2,1)S(1)}, s16[64,1024]{1,0:T(8,128)(2,1)S(1)}, u32[]{:S(2)}, u32[]{:S(2)}) %collective-permute-start.7) | collective-permute-done | bytes 131104 | tf_op jit(solution)/shard_map/ppermute | solution.py:250
  12.7 0.1 shard_map.59.code
  12.8 3.3 %collective-permute-start.8 = (s16[64,1024]{1,0:T(8,128)(2,1)S(1)}, s16[64,1024]{1,0:T(8,128)(2,1)S(1)}, u32[]{:S(2)}, u32[]{:S(2)}) collective-permute-start(s16[64,1024]{1,0:T(8,128)(2,1)S(1)} %shard_map.59.code), channel_id=1, source_target_pairs={{0,16},{4,20},{8,24},{12,28},{16,0},{20,4},{24,8},{28,12},{1,17},{... | collective-permute-start | bytes 393224 | tf_op jit(solution)/shard_map/ppermute | solution.py:250
  16.1 2.3 %collective-permute-start.3 = (s16[64,512]{1,0:T(8,128)(2,1)S(1)}, s16[64,512]{1,0:T(8,128)(2,1)S(1)}, u32[]{:S(2)}, u32[]{:S(2)}) collective-permute-start(s16[64,512]{1,0:T(8,128)(2,1)S(1)} %get-tuple-element.23), channel_id=1, source_target_pairs={{0,8},{4,12},{8,0},{12,4},{16,24},{20,28},{24,16},{28,20},{1,9},{5... | collective-permute-start | bytes 196616 | tf_op jit(solution)/shard_map/ppermute | solution.py:250
  18.4 3.3 %collective-permute-done.2.refs_1_ = s16[64,512]{1,0:T(8,128)(2,1)S(1)} collective-permute-done((s16[64,512]{1,0:T(8,128)(2,1)S(1)}, s16[64,512]{1,0:T(8,128)(2,1)S(1)}, u32[]{:S(2)}, u32[]{:S(2)}) %collective-permute-start.2) | collective-permute-done | bytes 65568 | tf_op jit(solution)/shard_map/ppermute | solution.py:250
  21.8 2.4 %collective-permute-start.6 = (bf16[64,512]{1,0:T(8,128)(2,1)S(1)}, bf16[64,512]{1,0:T(8,128)(2,1)S(1)}, u32[]{:S(2)}, u32[]{:S(2)}) collective-permute-start(bf16[64,512]{1,0:T(8,128)(2,1)S(1)} %shard_map.58.refs_0_), channel_id=1, source_target_pairs={{0,24},{4,28},{8,16},{12,20},{16,8},{20,12},{24,0},{28,4},{1,25},{... | collective-permute-start | bytes 196616 | tf_op jit(solution)/shard_map/ppermute | solution.py:250
  24.2 0.1 collective-permute-start.5
  24.3 2.0 %collective-permute-start.4 = (bf16[64,512]{1,0:T(8,128)(2,1)S(1)}, bf16[64,512]{1,0:T(8,128)(2,1)S(1)}, u32[]{:S(2)}, u32[]{:S(2)}) collective-permute-start(bf16[64,512]{1,0:T(8,128)(2,1)S(1)} %shard_map.58.refs_0_), channel_id=1, source_target_pairs={{0,8},{4,12},{8,0},{12,4},{16,24},{20,28},{24,16},{28,20},{1,9},{5... | collective-permute-start | bytes 196616 | tf_op jit(solution)/shard_map/ppermute | solution.py:250
  26.4 0.1 collective-permute-start.10
  26.5 2.1 %collective-permute-done.6.refs_3_ = bf16[64,512]{1,0:T(8,128)(2,1)S(1)} collective-permute-done((bf16[64,512]{1,0:T(8,128)(2,1)S(1)}, bf16[64,512]{1,0:T(8,128)(2,1)S(1)}, u32[]{:S(2)}, u32[]{:S(2)}) %collective-permute-start.6) | collective-permute-done | bytes 65568 | tf_op jit(solution)/shard_map/ppermute | solution.py:250
  28.6 1.5 %collective-permute-done.5.refs_2_ = bf16[64,512]{1,0:T(8,128)(2,1)S(1)} collective-permute-done((bf16[64,512]{1,0:T(8,128)(2,1)S(1)}, bf16[64,512]{1,0:T(8,128)(2,1)S(1)}, u32[]{:S(2)}, u32[]{:S(2)}) %collective-permute-start.5) | collective-permute-done | bytes 65568 | tf_op jit(solution)/shard_map/ppermute | solution.py:250
  30.3 0.5 %collective-permute-start.11 = (bf16[64,1024]{1,0:T(8,128)(2,1)S(1)}, bf16[64,1024]{1,0:T(8,128)(2,1)S(1)}, u32[]{:S(2)}, u32[]{:S(2)}) collective-permute-start(bf16[64,1024]{1,0:T(8,128)(2,1)S(1)} %shard_map.60.refs_0_), channel_id=1, source_target_pairs={{0,4},{4,0},{8,12},{12,8},{16,20},{20,16},{24,28},{28,24},{1,5},{5... | collective-permute-start | bytes 393224 | tf_op jit(solution)/shard_map/ppermute | solution.py:247
  30.8 0.8 %collective-permute-done.10.refs_1_ = bf16[64,1024]{1,0:T(8,128)(2,1)S(1)} collective-permute-done((bf16[64,1024]{1,0:T(8,128)(2,1)S(1)}, bf16[64,1024]{1,0:T(8,128)(2,1)S(1)}, u32[]{:S(2)}, u32[]{:S(2)}) %collective-permute-start.10) | collective-permute-done | bytes 131104 | tf_op jit(solution)/shard_map/ppermute | solution.py:250
  31.6 0.4 collective-permute-done.11.refs_2_
  32.0 0.9 %collective-permute-done.12.refs_3_ = bf16[64,1024]{1,0:T(8,128)(2,1)S(1)} collective-permute-done((bf16[64,1024]{1,0:T(8,128)(2,1)S(1)}, bf16[64,1024]{1,0:T(8,128)(2,1)S(1)}, u32[]{:S(2)}, u32[]{:S(2)}) %collective-permute-start.12) | collective-permute-done | bytes 131104 | tf_op jit(solution)/shard_map/ppermute | solution.py:247
  33.0 0.5 %shard_map.64 = s16[256,256]{1,0:T(8,128)(2,1)S(1)} custom-call(bf16[1024,2048]{1,0:T(8,128)(2,1)S(1)} %get-tuple-element.17.dense, bf16[256,2048]{1,0:T(8,128)(2,1)S(1)} %shard_map.62.gene), custom_call_target="tpu_custom_call" | custom-call | tf_op jit(solution)/shard_map/pallas_call | solution.py:310
  33.5 3.6 %collective-permute-start.13 = (s16[256,256]{1,0:T(8,128)(2,1)S(1)}, s16[256,256]{1,0:T(8,128)(2,1)S(1)}, u32[]{:S(2)}, u32[]{:S(2)}) collective-permute-start(s16[256,256]{1,0:T(8,128)(2,1)S(1)} %shard_map.64), channel_id=1, source_target_pairs={{0,3},{1,2},{2,1},{3,0},{4,7},{5,6},{6,5},{7,4},{8,11},{9,10},{10,... | collective-permute-start | bytes 393224 | tf_op jit(solution)/shard_map/ppermute | solution.py:253
  37.2 0.5 %shard_map.66 = s16[256,256]{1,0:T(8,128)(2,1)S(1)} custom-call(bf16[1024,2048]{1,0:T(8,128)(2,1)S(1)} %get-tuple-element.17.dense, bf16[256,2048]{1,0:T(8,128)(2,1)S(1)} %shard_map.62.gene), custom_call_target="tpu_custom_call" | custom-call | tf_op jit(solution)/shard_map/pallas_call | solution.py:310
  37.7 0.5 %collective-permute-start.14 = (s16[256,256]{1,0:T(8,128)(2,1)S(1)}, s16[256,256]{1,0:T(8,128)(2,1)S(1)}, u32[]{:S(2)}, u32[]{:S(2)}) collective-permute-start(s16[256,256]{1,0:T(8,128)(2,1)S(1)} %shard_map.66), channel_id=1, source_target_pairs={{0,2},{1,3},{2,0},{3,1},{4,6},{5,7},{6,4},{7,5},{8,10},{9,11},{10,... | collective-permute-start | bytes 393224 | tf_op jit(solution)/shard_map/ppermute | solution.py:253
  38.2 0.5 %shard_map.68 = s16[256,256]{1,0:T(8,128)(2,1)S(1)} custom-call(bf16[1024,2048]{1,0:T(8,128)(2,1)S(1)} %get-tuple-element.17.dense, bf16[256,2048]{1,0:T(8,128)(2,1)S(1)} %shard_map.62.gene), custom_call_target="tpu_custom_call" | custom-call | tf_op jit(solution)/shard_map/pallas_call | solution.py:310
  38.7 0.2 collective-permute-start.15
  38.9 0.5 %shard_map.63.total = f32[256,256]{1,0:T(8,128)S(1)} custom-call(bf16[1024,2048]{1,0:T(8,128)(2,1)S(1)} %get-tuple-element.17.dense, bf16[256,2048]{1,0:T(8,128)(2,1)S(1)} %shard_map.62.gene), custom_call_target="tpu_custom_call" | custom-call | tf_op jit(solution)/shard_map/pallas_call | solution.py:310
  39.4 1.7 %collective-permute-done.13.got = s16[256,256]{1,0:T(8,128)(2,1)S(1)} collective-permute-done((s16[256,256]{1,0:T(8,128)(2,1)S(1)}, s16[256,256]{1,0:T(8,128)(2,1)S(1)}, u32[]{:S(2)}, u32[]{:S(2)}) %collective-permute-start.13) | collective-permute-done | bytes 131104 | tf_op jit(solution)/shard_map/ppermute | solution.py:253
  41.1 2.7 %collective-permute-done.14.got = s16[256,256]{1,0:T(8,128)(2,1)S(1)} collective-permute-done((s16[256,256]{1,0:T(8,128)(2,1)S(1)}, s16[256,256]{1,0:T(8,128)(2,1)S(1)}, u32[]{:S(2)}, u32[]{:S(2)}) %collective-permute-start.14) | collective-permute-done | bytes 131104 | tf_op jit(solution)/shard_map/ppermute | solution.py:253
  43.8 0.7 %shard_map.69 = f32[256,256]{1,0:T(8,128)} custom-call(f32[256,256]{1,0:T(8,128)S(1)} %shard_map.67.total, s16[256,256]{1,0:T(8,128)(2,1)S(1)} %collective-permute-done.15.got), custom_call_target="tpu_custom_call" | custom-call | bytes 16777216 | tf_op jit(solution)/shard_map/pallas_call | solution.py:321
  (15 shorter events, 0.6 us)
Async XLA Ops:
  4.5 2.0 %collective-permute-start = (s16[128,2048]{1,0:T(8,128)(2,1)S(1)}, s16[128,2048]{1,0:T(8,128)(2,1)S(1)}, u32[]{:S(2)}, u32[]{:S(2)}) collective-permute-start(s16[128,2048]{1,0:T(8,128)(2,1)S(1)} %get-tuple-element.19), channel_id=1, source_target_pairs={{0,4},{4,0},{8,12},{12,8},{16,20},{20,16},{24,28},{28,24},{1,5},{5... | collective-permute-start | bytes 1572872 | tf_op jit(solution)/shard_map/ppermute | solution.py:247
  6.8 5.9 %collective-permute-start.7 = (s16[64,1024]{1,0:T(8,128)(2,1)S(1)}, s16[64,1024]{1,0:T(8,128)(2,1)S(1)}, u32[]{:S(2)}, u32[]{:S(2)}) collective-permute-start(s16[64,1024]{1,0:T(8,128)(2,1)S(1)} %get-tuple-element.25), channel_id=1, source_target_pairs={{0,8},{4,12},{8,0},{12,4},{16,24},{20,28},{24,16},{28,20},{1,9},{5... | collective-permute-start | bytes 393224 | tf_op jit(solution)/shard_map/ppermute | solution.py:250
  8.8 9.6 %collective-permute-start.1 = (s16[64,512]{1,0:T(8,128)(2,1)S(1)}, s16[64,512]{1,0:T(8,128)(2,1)S(1)}, u32[]{:S(2)}, u32[]{:S(2)}) collective-permute-start(s16[64,512]{1,0:T(8,128)(2,1)S(1)} %get-tuple-element.21), channel_id=1, source_target_pairs={{0,24},{4,28},{8,16},{12,20},{16,8},{20,12},{24,0},{28,4},{1,25},{... | collective-permute-start | bytes 196616 | tf_op jit(solution)/shard_map/ppermute | solution.py:250
  11.0 10.7 %collective-permute-start.2 = (s16[64,512]{1,0:T(8,128)(2,1)S(1)}, s16[64,512]{1,0:T(8,128)(2,1)S(1)}, u32[]{:S(2)}, u32[]{:S(2)}) collective-permute-start(s16[64,512]{1,0:T(8,128)(2,1)S(1)} %get-tuple-element.22), channel_id=1, source_target_pairs={{0,16},{4,20},{8,24},{12,28},{16,0},{20,4},{24,8},{28,12},{1,17},{... | collective-permute-start | bytes 196616 | tf_op jit(solution)/shard_map/ppermute | solution.py:250
  12.8 13.5 %collective-permute-start.8 = (s16[64,1024]{1,0:T(8,128)(2,1)S(1)}, s16[64,1024]{1,0:T(8,128)(2,1)S(1)}, u32[]{:S(2)}, u32[]{:S(2)}) collective-permute-start(s16[64,1024]{1,0:T(8,128)(2,1)S(1)} %shard_map.59.code), channel_id=1, source_target_pairs={{0,16},{4,20},{8,24},{12,28},{16,0},{20,4},{24,8},{28,12},{1,17},{... | collective-permute-start | bytes 393224 | tf_op jit(solution)/shard_map/ppermute | solution.py:250
  16.1 5.6 %collective-permute-start.3 = (s16[64,512]{1,0:T(8,128)(2,1)S(1)}, s16[64,512]{1,0:T(8,128)(2,1)S(1)}, u32[]{:S(2)}, u32[]{:S(2)}) collective-permute-start(s16[64,512]{1,0:T(8,128)(2,1)S(1)} %get-tuple-element.23), channel_id=1, source_target_pairs={{0,8},{4,12},{8,0},{12,4},{16,24},{20,28},{24,16},{28,20},{1,9},{5... | collective-permute-start | bytes 196616 | tf_op jit(solution)/shard_map/ppermute | solution.py:250
  21.8 6.8 %collective-permute-start.6 = (bf16[64,512]{1,0:T(8,128)(2,1)S(1)}, bf16[64,512]{1,0:T(8,128)(2,1)S(1)}, u32[]{:S(2)}, u32[]{:S(2)}) collective-permute-start(bf16[64,512]{1,0:T(8,128)(2,1)S(1)} %shard_map.58.refs_0_), channel_id=1, source_target_pairs={{0,24},{4,28},{8,16},{12,20},{16,8},{20,12},{24,0},{28,4},{1,25},{... | collective-permute-start | bytes 196616 | tf_op jit(solution)/shard_map/ppermute | solution.py:250
  24.2 5.9 %collective-permute-start.5 = (bf16[64,512]{1,0:T(8,128)(2,1)S(1)}, bf16[64,512]{1,0:T(8,128)(2,1)S(1)}, u32[]{:S(2)}, u32[]{:S(2)}) collective-permute-start(bf16[64,512]{1,0:T(8,128)(2,1)S(1)} %shard_map.58.refs_0_), channel_id=1, source_target_pairs={{0,16},{4,20},{8,24},{12,28},{16,0},{20,4},{24,8},{28,12},{1,17},{... | collective-permute-start | bytes 196616 | tf_op jit(solution)/shard_map/ppermute | solution.py:250
  24.3 5.9 %collective-permute-start.4 = (bf16[64,512]{1,0:T(8,128)(2,1)S(1)}, bf16[64,512]{1,0:T(8,128)(2,1)S(1)}, u32[]{:S(2)}, u32[]{:S(2)}) collective-permute-start(bf16[64,512]{1,0:T(8,128)(2,1)S(1)} %shard_map.58.refs_0_), channel_id=1, source_target_pairs={{0,8},{4,12},{8,0},{12,4},{16,24},{20,28},{24,16},{28,20},{1,9},{5... | collective-permute-start | bytes 196616 | tf_op jit(solution)/shard_map/ppermute | solution.py:250
  26.4 5.2 %collective-permute-start.10 = (bf16[64,1024]{1,0:T(8,128)(2,1)S(1)}, bf16[64,1024]{1,0:T(8,128)(2,1)S(1)}, u32[]{:S(2)}, u32[]{:S(2)}) collective-permute-start(bf16[64,1024]{1,0:T(8,128)(2,1)S(1)} %shard_map.60.refs_0_), channel_id=1, source_target_pairs={{0,8},{4,12},{8,0},{12,4},{16,24},{20,28},{24,16},{28,20},{1,9},{5... | collective-permute-start | bytes 393224 | tf_op jit(solution)/shard_map/ppermute | solution.py:250
  30.2 2.7 %collective-permute-start.9 = (bf16[64,2048]{1,0:T(8,128)(2,1)S(1)}, bf16[64,2048]{1,0:T(8,128)(2,1)S(1)}, u32[]{:S(2)}, u32[]{:S(2)}) collective-permute-start(bf16[64,2048]{1,0:T(8,128)(2,1)S(1)} %shard_map.61.first), channel_id=1, source_target_pairs={{0,4},{4,0},{8,12},{12,8},{16,20},{20,16},{24,28},{28,24},{1,5},{5... | collective-permute-start | bytes 786440 | tf_op jit(solution)/shard_map/ppermute | solution.py:247
  30.3 1.7 %collective-permute-start.11 = (bf16[64,1024]{1,0:T(8,128)(2,1)S(1)}, bf16[64,1024]{1,0:T(8,128)(2,1)S(1)}, u32[]{:S(2)}, u32[]{:S(2)}) collective-permute-start(bf16[64,1024]{1,0:T(8,128)(2,1)S(1)} %shard_map.60.refs_0_), channel_id=1, source_target_pairs={{0,4},{4,0},{8,12},{12,8},{16,20},{20,16},{24,28},{28,24},{1,5},{5... | collective-permute-start | bytes 393224 | tf_op jit(solution)/shard_map/ppermute | solution.py:247
  31.6 1.3 %collective-permute-start.12 = (bf16[64,1024]{1,0:T(8,128)(2,1)S(1)}, bf16[64,1024]{1,0:T(8,128)(2,1)S(1)}, u32[]{:S(2)}, u32[]{:S(2)}) collective-permute-start(bf16[64,1024]{1,0:T(8,128)(2,1)S(1)} %collective-permute-done.10.refs_1_), channel_id=1, source_target_pairs={{0,4},{4,0},{8,12},{12,8},{16,20},{20,16},{24,28},{28,24},{1,5},{5... | collective-permute-start | bytes 393224 | tf_op jit(solution)/shard_map/ppermute | solution.py:247
  33.5 7.5 %collective-permute-start.13 = (s16[256,256]{1,0:T(8,128)(2,1)S(1)}, s16[256,256]{1,0:T(8,128)(2,1)S(1)}, u32[]{:S(2)}, u32[]{:S(2)}) collective-permute-start(s16[256,256]{1,0:T(8,128)(2,1)S(1)} %shard_map.64), channel_id=1, source_target_pairs={{0,3},{1,2},{2,1},{3,0},{4,7},{5,6},{6,5},{7,4},{8,11},{9,10},{10,... | collective-permute-start | bytes 393224 | tf_op jit(solution)/shard_map/ppermute | solution.py:253
  37.7 6.1 %collective-permute-start.14 = (s16[256,256]{1,0:T(8,128)(2,1)S(1)}, s16[256,256]{1,0:T(8,128)(2,1)S(1)}, u32[]{:S(2)}, u32[]{:S(2)}) collective-permute-start(s16[256,256]{1,0:T(8,128)(2,1)S(1)} %shard_map.66), channel_id=1, source_target_pairs={{0,2},{1,3},{2,0},{3,1},{4,6},{5,7},{6,4},{7,5},{8,10},{9,11},{10,... | collective-permute-start | bytes 393224 | tf_op jit(solution)/shard_map/ppermute | solution.py:253
  38.7 5.1 %collective-permute-start.15 = (s16[256,256]{1,0:T(8,128)(2,1)S(1)}, s16[256,256]{1,0:T(8,128)(2,1)S(1)}, u32[]{:S(2)}, u32[]{:S(2)}) collective-permute-start(s16[256,256]{1,0:T(8,128)(2,1)S(1)} %shard_map.68), channel_id=1, source_target_pairs={{0,1},{1,0},{2,3},{3,2},{4,5},{5,4},{6,7},{7,6},{8,9},{9,8},{10,11... | collective-permute-start | bytes 393224 | tf_op jit(solution)/shard_map/ppermute | solution.py:253

commit v15 on v13

--- a/solution.py
+++ b/solution.py
@@ -9,7 +9,7 @@
 
 GENE_BLOCKS = 16
 CORES = 2
-STREAMS = 2
+DIRECT = (1, 2)
 MIB = 1 << 20
 
 VMEM = pl.BlockSpec(memory_space=pltpu.VMEM)
@@ -59,9 +59,7 @@
 
 
 def rows_of(turned, core, rows):
-    span = rows * CORES
-    at = [pl.multiple_of(i * span + core * rows, rows) for i in range(STREAMS)]
-    return jnp.concatenate([turned[pl.ds(x, rows), :] for x in at], axis=0)
+    return turned[pl.ds(pl.multiple_of(core * rows, rows), rows), :]
 
 
 def dense_kernel(count, rows, cols, sketch, tiles, dense, turned, theirs, place, stage, sketch_here, load_sems, sems):
@@ -119,7 +117,7 @@
             def _():
                 lax.fori_loop(i * size, live, put_one, 0)
 
-    left = rows_of(turned, 1 - core, theirs.shape[0] // STREAMS)
+    left = rows_of(turned, 1 - core, theirs.shape[0])
     width = 512
     for j in range(dense.shape[1] // width):
         cut = pl.ds(j * width, width)
@@ -128,7 +126,7 @@
 
 def own_kernel(turned, dense, mine):
     core, _ = core_and_chip()
-    left = rows_of(turned, core, mine.shape[0] // STREAMS)
+    left = rows_of(turned, core, mine.shape[0])
     mine[...] = jnp.dot(left, dense[...], preferred_element_type=f32)
 
 
@@ -187,13 +185,48 @@
         out[:, pl.ds(pl.multiple_of((chip ^ k) * width, width), width)] = piece[...]
 
 
+def tail_kernel(code, got, chunk, out):
+    lead = chunk.shape[1]
+    out[:, :lead] = chunk[...]
+    out[:, lead:] = (decode(code[...]) + decode(got[...])).astype(bf16)
+
+
+def far_kernel(*refs):
+    *pieces, out = refs
+    width = pieces[0].shape[1]
+    for k, piece in enumerate(pieces):
+        out[:, k * width : (k + 1) * width] = piece[...]
+
+
+def tails_gene_kernel(*refs):
+    *pieces, gene = refs
+    core, chip = core_and_chip()
+    count = len(pieces) // CORES
+    for j, owner in enumerate((core, 1 - core)):
+        here, near, both = pieces[j * count : (j + 1) * count]
+        lead = both.shape[0]
+        chunk = both.shape[1] // 2
+        far = (both[:, :chunk], both[:, chunk:])
+        rows, width = here.shape[0], here.shape[1] - chunk
+        at = pl.ds(pl.multiple_of(owner * (lead + rows), 16), lead)
+        after = pl.ds(pl.multiple_of(owner * (lead + rows) + lead, 16), rows)
+        for k, piece in enumerate((here, near, *far)):
+            cut = pl.ds(pl.multiple_of((chip ^ k) * chunk, chunk), chunk)
+            gene[at, cut] = piece[:, :chunk]
+        for k, piece in enumerate((here, near)):
+            half = pl.ds(pl.multiple_of(((chip ^ k) & 1) * width, width), width)
+            gene[after, half] = piece[:, chunk:]
+
+
 def gene_kernel(masks, first, first_theirs, *refs):
     *pieces, gene = refs
     core, chip = core_and_chip()
     rows, width = pieces[0].shape
+    lead = first.shape[0]
 
     def at(stream, owner):
-        return pl.ds(pl.multiple_of((stream * CORES + owner) * rows, rows), rows)
+        start = owner * (lead + rows) + stream * lead
+        return pl.ds(pl.multiple_of(start, 16), rows if stream else lead)
 
     gene[at(0, core), :] = first[...]
     gene[at(0, 1 - core), :] = first_theirs[...]
@@ -227,9 +260,9 @@
     slots, tile, _ = tiles.shape
     genes = GENE_BLOCKS * tile
     bits = (n_cells // CORES).bit_length() - 1
-    span = rank // STREAMS
-    rows = span // CORES
-    share = rows * STREAMS
+    share = rank // CORES
+    lead = share * DIRECT[0] // DIRECT[1] // 16 * 16
+    rows = share - lead
     height = cells // n_genes
     flops = 2 * cells * genes * rank
     shape = jax.ShapeDtypeStruct
@@ -267,7 +300,7 @@
     one = halves(genes) if bits > 1 else (shape((rows, genes), i16),)
     pieces = call(
         functools.partial(pair_kernel, chips),
-        (shape((rows, chunk), f32),) + (shape((rows, chunk), i16),) * (chips - 1) + one,
+        (shape((lead, chunk), f32),) + (shape((lead, chunk), i16),) * (chips - 1) + one,
         [VMEM, VMEM],
         scratch=[pltpu.VMEM((share, genes), f32)],
         nbytes=3 * MIB,
@@ -282,20 +315,29 @@
             half[0], to_chip(half[1], 1 << bit)
         )
     came = [to_chip(direct[k], k) for k in reversed(range(1, chips))]
-    summed = call(direct_cast_kernel, shape((rows, chunk), bf16), [VMEM] * chips, nbytes=MIB)(direct[0], *came)
+    summed = call(direct_cast_kernel, shape((lead, chunk), bf16), [VMEM] * chips, flops=30000000000)(direct[0], *came)
     crossed = to_chip(half[-1], chips // 2)
-    spread = [to_chip(summed, k) for k in reversed(range(1, chips))][::-1]
-    held = [call(cast_kernel, shape((rows, width), bf16), [VMEM, VMEM], nbytes=MIB)(half[-1], crossed)]
-    *spread, _ = lax.optimization_barrier((*spread, held[0]))
-    first = call(join_kernel, shape((rows, genes), bf16), [VMEM] * chips, nbytes=MIB)(summed, *spread)
-    masks = [0]
-    for bit in reversed(range(bits - 1)):
-        held = held + [to_chip(x, 1 << bit) for x in held]
-        masks += [mask ^ (1 << bit) for mask in masks]
-    theirs = [to_core(x) for x in held]
-    gene = call(
-        functools.partial(gene_kernel, masks), shape((rank, genes), bf16), [VMEM] * (2 + 2 * len(held)), nbytes=2 * MIB
-    )(first, to_core(first), *held, *theirs)
+    if bits == 2 and lead == rows:
+        far = [to_chip(summed, k) for k in reversed(range(2, chips))][::-1]
+        tail = call(tail_kernel, shape((rows, chunk + width), bf16), [VMEM] * 3, nbytes=MIB)(half[-1], crossed, summed)
+        far = call(far_kernel, shape((lead, 2 * chunk), bf16), [VMEM] * 2, flops=30000000000, nbytes=MIB)(*far)
+        near, _ = lax.optimization_barrier((to_chip(tail, 1), far))
+        whole = [tail, near, far]
+        whole += [to_core(x) for x in whole]
+        gene = call(tails_gene_kernel, shape((rank, genes), bf16), [VMEM] * len(whole), nbytes=2 * MIB)(*whole)
+    else:
+        spread = [to_chip(summed, k) for k in reversed(range(1, chips))][::-1]
+        held = [call(cast_kernel, shape((rows, width), bf16), [VMEM, VMEM], nbytes=MIB)(half[-1], crossed)]
+        *spread, _ = lax.optimization_barrier((*spread, held[0]))
+        first = call(join_kernel, shape((lead, genes), bf16), [VMEM] * chips, nbytes=MIB)(summed, *spread)
+        masks = [0]
+        for bit in reversed(range(bits - 1)):
+            held = held + [to_chip(x, 1 << bit) for x in held]
+            masks += [mask ^ (1 << bit) for mask in masks]
+        theirs = [to_core(x) for x in held]
+        gene = call(
+            functools.partial(gene_kernel, masks), shape((rank, genes), bf16), [VMEM] * (2 + 2 * len(held)), nbytes=2 * MIB
+        )(first, to_core(first), *held, *theirs)
 
     def cell(k, gene):
         kind = f32 if k == 0 else i16

time: 44.9 us -> 46.5 us (1.036)
  waiting for transfers between devices: 16.8 us -> 20.4 us
  starting transfers between devices: 18.8 us -> 16.8 us
    ppermute x9 -> x8, waiting for transfers between devices: 9.81 us -> 14 us  [to_chip(): lax.ppermute(x, 'cells', [(i, i ^ CORES * k) for i in range(n_cells)])]
    ppermute x9 -> x8, starting transfers between devices: 14.2 us -> 12.5 us  [to_chip(): lax.ppermute(x, 'cells', [(i, i ^ CORES * k) for i in range(n_cells)])]
  transfers between devices with their start and end apart: 16 -> 15, of which waited for: 12 -> 8; matrix products, arithmetic and copies ran while one was open for 0% -> 0% of each run, Pallas kernels for 6% -> 6%
where the time goes in v15:
time: 46.5 us; the launch traced here: 46.3 us
  waiting for transfers between devices  20.4 us (44%)
  starting transfers between devices  16.8 us (36%)
  Pallas kernels  8.23 us (18%)
  between operations  0.79 us (2%)
    ppermute x8, waiting for transfers between devices, to_chip(): lax.ppermute(x, 'cells', [(i, i ^ CORES * k) for i in range(n_cells)])  14 us
    ppermute x8, starting transfers between devices, to_chip(): lax.ppermute(x, 'cells', [(i, i ^ CORES * k) for i in range(n_cells)])  12.5 us
    ppermute x3, waiting for transfers between devices, to_gene(): return lax.ppermute(x, 'genes', [(i, i ^ k) for i in range(n_genes)])  4.14 us
    pallas_call x1, Pallas kernels, local(): call(dense_kernel, (shape((cells, genes), bf16), shape((rank, cells), bf1...  3.8 us
    ppermute x3, starting transfers between devices, to_gene(): return lax.ppermute(x, 'genes', [(i, i ^ k) for i in range(n_genes)])  3.68 us
    ppermute x4, waiting for transfers between devices, to_core(): return lax.ppermute(x, 'cells', [(i, i ^ 1) for i in range(n_cells)])  2.29 us
    pallas_call x4, Pallas kernels, cell(): call(functools.partial(cell_kernel, k), shape((height, rank), kind), [VME...  2.03 us
  transfers between devices with their start and end apart: 15, of which 8 were waited for; matrix products, arithmetic and copies ran while one was open for 0% of the time, Pallas kernels for 6%

profile of v15, /device:TPU:0, one launch (start us, length us, event | category | flops | bytes accessed | tf_op | source)
XLA Modules:
  0.0 46.3 jit_solution(6670890515505277270)
XLA Ops:
  0.7 3.8 %shard_map.55 = (bf16[1024,2048]{1,0:T(8,128)(2,1)S(1)}, bf16[256,1024]{1,0:T(8,128)(2,1)S(1)}, s16[128,2048]{1,0:T(8,128)(2,1)S(1)}) custom-call(s32[1]{0:T(128)S(6)} %copy.6.count, s32[96]{0:T(128)} %rows.1, s32[96]{0:T(128)} %cols.1, bf16[1024,256]{1,0:T(8,128)(2,1)} %sketch.1, bf16[96,128,128]{2,1,0:T(8,128)(2,1)} %tiles.1), custom_call_target="tpu_custom_call" | custom-call | flops 536870912 | bytes 8388608 | tf_op jit(solution)/shard_map/pallas_call | solution.py:282
  4.5 0.1 collective-permute-start
  4.5 0.7 %shard_map.56.mine = f32[128,2048]{1,0:T(8,128)S(1)} custom-call(bf16[256,1024]{1,0:T(8,128)(2,1)S(1)} %get-tuple-element.16.turned, bf16[1024,2048]{1,0:T(8,128)(2,1)S(1)} %get-tuple-element.15.dense), custom_call_target="tpu_custom_call" | custom-call | flops 536870912 | bytes 5242880 | tf_op jit(solution)/shard_map/pallas_call | solution.py:297
  5.3 1.2 %collective-permute-done.got = s16[128,2048]{1,0:T(8,128)(2,1)S(1)} collective-permute-done((s16[128,2048]{1,0:T(8,128)(2,1)S(1)}, s16[128,2048]{1,0:T(8,128)(2,1)S(1)}, u32[]{:S(2)}, u32[]{:S(2)}) %collective-permute-start) | collective-permute-done | bytes 524320 | tf_op jit(solution)/shard_map/ppermute | solution.py:271
  6.4 0.5 %shard_map.57 = (f32[64,512]{1,0:T(8,128)S(1)}, s16[64,512]{1,0:T(8,128)(2,1)S(1)}, s16[64,512]{1,0:T(8,128)(2,1)S(1)}, s16[64,512]{1,0:T(8,128)(2,1)S(1)}, f32[...) custom-call(f32[128,2048]{1,0:T(8,128)S(1)} %shard_map.56.mine, s16[128,2048]{1,0:T(8,128)(2,1)S(1)} %collective-permute-done.got), custom_call_target="tpu_custom_call" | custom-call | bytes 3145728 | tf_op jit(solution)/shard_map/pallas_call | solution.py:301
  6.9 2.0 %collective-permute-start.1 = (s16[64,1024]{1,0:T(8,128)(2,1)S(1)}, s16[64,1024]{1,0:T(8,128)(2,1)S(1)}, u32[]{:S(2)}, u32[]{:S(2)}) collective-permute-start(s16[64,1024]{1,0:T(8,128)(2,1)S(1)} %get-tuple-element.19), channel_id=1, source_target_pairs={{0,8},{4,12},{8,0},{12,4},{16,24},{20,28},{24,16},{28,20},{1,9},{5... | collective-permute-start | bytes 393224 | tf_op jit(solution)/shard_map/ppermute | solution.py:274
  8.9 2.4 %collective-permute-start.3 = (s16[64,512]{1,0:T(8,128)(2,1)S(1)}, s16[64,512]{1,0:T(8,128)(2,1)S(1)}, u32[]{:S(2)}, u32[]{:S(2)}) collective-permute-start(s16[64,512]{1,0:T(8,128)(2,1)S(1)} %get-tuple-element.21), channel_id=1, source_target_pairs={{0,24},{4,28},{8,16},{12,20},{16,8},{20,12},{24,0},{28,4},{1,25},{... | collective-permute-start | bytes 196616 | tf_op jit(solution)/shard_map/ppermute | solution.py:274
  11.3 0.5 %collective-permute-start.4 = (s16[64,512]{1,0:T(8,128)(2,1)S(1)}, s16[64,512]{1,0:T(8,128)(2,1)S(1)}, u32[]{:S(2)}, u32[]{:S(2)}) collective-permute-start(s16[64,512]{1,0:T(8,128)(2,1)S(1)} %get-tuple-element.22), channel_id=1, source_target_pairs={{0,16},{4,20},{8,24},{12,28},{16,0},{20,4},{24,8},{28,12},{1,17},{... | collective-permute-start | bytes 196616 | tf_op jit(solution)/shard_map/ppermute | solution.py:274
  11.8 1.5 %collective-permute-start.5 = (s16[64,512]{1,0:T(8,128)(2,1)S(1)}, s16[64,512]{1,0:T(8,128)(2,1)S(1)}, u32[]{:S(2)}, u32[]{:S(2)}) collective-permute-start(s16[64,512]{1,0:T(8,128)(2,1)S(1)} %get-tuple-element.23), channel_id=1, source_target_pairs={{0,8},{4,12},{8,0},{12,4},{16,24},{20,28},{24,16},{28,20},{1,9},{5... | collective-permute-start | bytes 196616 | tf_op jit(solution)/shard_map/ppermute | solution.py:274
  13.3 0.1 shard_map.58.code
  13.4 4.1 %collective-permute-start.2 = (s16[64,1024]{1,0:T(8,128)(2,1)S(1)}, s16[64,1024]{1,0:T(8,128)(2,1)S(1)}, u32[]{:S(2)}, u32[]{:S(2)}) collective-permute-start(s16[64,1024]{1,0:T(8,128)(2,1)S(1)} %shard_map.58.code), channel_id=1, source_target_pairs={{0,16},{4,20},{8,24},{12,28},{16,0},{20,4},{24,8},{28,12},{1,17},{... | collective-permute-start | bytes 393224 | tf_op jit(solution)/shard_map/ppermute | solution.py:274
  17.6 3.2 %collective-permute-done.4.refs_1_ = s16[64,512]{1,0:T(8,128)(2,1)S(1)} collective-permute-done((s16[64,512]{1,0:T(8,128)(2,1)S(1)}, s16[64,512]{1,0:T(8,128)(2,1)S(1)}, u32[]{:S(2)}, u32[]{:S(2)}) %collective-permute-start.4) | collective-permute-done | bytes 65568 | tf_op jit(solution)/shard_map/ppermute | solution.py:274
  20.8 0.1 shard_map.59.chunk
  20.9 1.9 %collective-permute-start.8 = (bf16[64,512]{1,0:T(8,128)(2,1)S(1)}, bf16[64,512]{1,0:T(8,128)(2,1)S(1)}, u32[]{:S(2)}, u32[]{:S(2)}) collective-permute-start(bf16[64,512]{1,0:T(8,128)(2,1)S(1)} %shard_map.59.chunk), channel_id=1, source_target_pairs={{0,24},{4,28},{8,16},{12,20},{16,8},{20,12},{24,0},{28,4},{1,25},{... | collective-permute-start | bytes 196616 | tf_op jit(solution)/shard_map/ppermute | solution.py:274
  22.8 5.0 %collective-permute-done.2.got = s16[64,1024]{1,0:T(8,128)(2,1)S(1)} collective-permute-done((s16[64,1024]{1,0:T(8,128)(2,1)S(1)}, s16[64,1024]{1,0:T(8,128)(2,1)S(1)}, u32[]{:S(2)}, u32[]{:S(2)}) %collective-permute-start.2) | collective-permute-done | bytes 131104 | tf_op jit(solution)/shard_map/ppermute | solution.py:274
  27.8 0.1 shard_map.60.refs_0_
  27.9 0.1 collective-permute-start.6
  28.0 2.2 %collective-permute-done.7.refs_0_ = bf16[64,512]{1,0:T(8,128)(2,1)S(1)} collective-permute-done((bf16[64,512]{1,0:T(8,128)(2,1)S(1)}, bf16[64,512]{1,0:T(8,128)(2,1)S(1)}, u32[]{:S(2)}, u32[]{:S(2)}) %collective-permute-start.7) | collective-permute-done | bytes 65568 | tf_op jit(solution)/shard_map/ppermute | solution.py:274
  30.3 3.5 %collective-permute-done.6.refs_1_ = bf16[64,1536]{1,0:T(8,128)(2,1)S(1)} collective-permute-done((bf16[64,1536]{1,0:T(8,128)(2,1)S(1)}, bf16[64,1536]{1,0:T(8,128)(2,1)S(1)}, u32[]{:S(2)}, u32[]{:S(2)}) %collective-permute-start.6) | collective-permute-done | bytes 196640 | tf_op jit(solution)/shard_map/ppermute | solution.py:274
  33.8 0.5 %collective-permute-start.11 = (bf16[64,1024]{1,0:T(8,128)(2,1)S(1)}, bf16[64,1024]{1,0:T(8,128)(2,1)S(1)}, u32[]{:S(2)}, u32[]{:S(2)}) collective-permute-start(bf16[64,1024]{1,0:T(8,128)(2,1)S(1)} %shard_map.61.refs_2_), channel_id=1, source_target_pairs={{0,4},{4,0},{8,12},{12,8},{16,20},{20,16},{24,28},{28,24},{1,5},{5... | collective-permute-start | bytes 393224 | tf_op jit(solution)/shard_map/ppermute | solution.py:271
  34.3 1.1 %collective-permute-done.11.refs_5_ = bf16[64,1024]{1,0:T(8,128)(2,1)S(1)} collective-permute-done((bf16[64,1024]{1,0:T(8,128)(2,1)S(1)}, bf16[64,1024]{1,0:T(8,128)(2,1)S(1)}, u32[]{:S(2)}, u32[]{:S(2)}) %collective-permute-start.11) | collective-permute-done | bytes 131104 | tf_op jit(solution)/shard_map/ppermute | solution.py:271
  35.4 0.1 shard_map.62.gene
  35.5 0.5 %shard_map.64 = s16[256,256]{1,0:T(8,128)(2,1)S(1)} custom-call(bf16[1024,2048]{1,0:T(8,128)(2,1)S(1)} %get-tuple-element.15.dense, bf16[256,2048]{1,0:T(8,128)(2,1)S(1)} %shard_map.62.gene), custom_call_target="tpu_custom_call" | custom-call | tf_op jit(solution)/shard_map/pallas_call | solution.py:344
  36.0 2.3 %collective-permute-start.12 = (s16[256,256]{1,0:T(8,128)(2,1)S(1)}, s16[256,256]{1,0:T(8,128)(2,1)S(1)}, u32[]{:S(2)}, u32[]{:S(2)}) collective-permute-start(s16[256,256]{1,0:T(8,128)(2,1)S(1)} %shard_map.64), channel_id=1, source_target_pairs={{0,3},{1,2},{2,1},{3,0},{4,7},{5,6},{6,5},{7,4},{8,11},{9,10},{10,... | collective-permute-start | bytes 393224 | tf_op jit(solution)/shard_map/ppermute | solution.py:277
  38.4 0.5 %shard_map.66 = s16[256,256]{1,0:T(8,128)(2,1)S(1)} custom-call(bf16[1024,2048]{1,0:T(8,128)(2,1)S(1)} %get-tuple-element.15.dense, bf16[256,2048]{1,0:T(8,128)(2,1)S(1)} %shard_map.62.gene), custom_call_target="tpu_custom_call" | custom-call | tf_op jit(solution)/shard_map/pallas_call | solution.py:344
  38.9 0.7 %collective-permute-start.13 = (s16[256,256]{1,0:T(8,128)(2,1)S(1)}, s16[256,256]{1,0:T(8,128)(2,1)S(1)}, u32[]{:S(2)}, u32[]{:S(2)}) collective-permute-start(s16[256,256]{1,0:T(8,128)(2,1)S(1)} %shard_map.66), channel_id=1, source_target_pairs={{0,2},{1,3},{2,0},{3,1},{4,6},{5,7},{6,4},{7,5},{8,10},{9,11},{10,... | collective-permute-start | bytes 393224 | tf_op jit(solution)/shard_map/ppermute | solution.py:277
  39.6 0.5 %shard_map.68 = s16[256,256]{1,0:T(8,128)(2,1)S(1)} custom-call(bf16[1024,2048]{1,0:T(8,128)(2,1)S(1)} %get-tuple-element.15.dense, bf16[256,2048]{1,0:T(8,128)(2,1)S(1)} %shard_map.62.gene), custom_call_target="tpu_custom_call" | custom-call | tf_op jit(solution)/shard_map/pallas_call | solution.py:344
  40.1 0.7 %collective-permute-start.14 = (s16[256,256]{1,0:T(8,128)(2,1)S(1)}, s16[256,256]{1,0:T(8,128)(2,1)S(1)}, u32[]{:S(2)}, u32[]{:S(2)}) collective-permute-start(s16[256,256]{1,0:T(8,128)(2,1)S(1)} %shard_map.68), channel_id=1, source_target_pairs={{0,1},{1,0},{2,3},{3,2},{4,5},{5,4},{6,7},{7,6},{8,9},{9,8},{10,11... | collective-permute-start | bytes 393224 | tf_op jit(solution)/shard_map/ppermute | solution.py:277
  40.8 0.5 %shard_map.63.total = f32[256,256]{1,0:T(8,128)S(1)} custom-call(bf16[1024,2048]{1,0:T(8,128)(2,1)S(1)} %get-tuple-element.15.dense, bf16[256,2048]{1,0:T(8,128)(2,1)S(1)} %shard_map.62.gene), custom_call_target="tpu_custom_call" | custom-call | tf_op jit(solution)/shard_map/pallas_call | solution.py:344
  41.3 1.5 %collective-permute-done.12.got = s16[256,256]{1,0:T(8,128)(2,1)S(1)} collective-permute-done((s16[256,256]{1,0:T(8,128)(2,1)S(1)}, s16[256,256]{1,0:T(8,128)(2,1)S(1)}, u32[]{:S(2)}, u32[]{:S(2)}) %collective-permute-start.12) | collective-permute-done | bytes 131104 | tf_op jit(solution)/shard_map/ppermute | solution.py:277
  42.8 2.7 %collective-permute-done.13.got = s16[256,256]{1,0:T(8,128)(2,1)S(1)} collective-permute-done((s16[256,256]{1,0:T(8,128)(2,1)S(1)}, s16[256,256]{1,0:T(8,128)(2,1)S(1)}, u32[]{:S(2)}, u32[]{:S(2)}) %collective-permute-start.13) | collective-permute-done | bytes 131104 | tf_op jit(solution)/shard_map/ppermute | solution.py:277
  45.5 0.7 %shard_map.69 = f32[256,256]{1,0:T(8,128)} custom-call(f32[256,256]{1,0:T(8,128)S(1)} %shard_map.67.total, s16[256,256]{1,0:T(8,128)(2,1)S(1)} %collective-permute-done.14.got), custom_call_target="tpu_custom_call" | custom-call | bytes 16777216 | tf_op jit(solution)/shard_map/pallas_call | solution.py:355
  (13 shorter events, 0.2 us)
Async XLA Ops:
  4.5 2.0 %collective-permute-start = (s16[128,2048]{1,0:T(8,128)(2,1)S(1)}, s16[128,2048]{1,0:T(8,128)(2,1)S(1)}, u32[]{:S(2)}, u32[]{:S(2)}) collective-permute-start(s16[128,2048]{1,0:T(8,128)(2,1)S(1)} %get-tuple-element.17), channel_id=1, source_target_pairs={{0,4},{4,0},{8,12},{12,8},{16,20},{20,16},{24,28},{28,24},{1,5},{5... | collective-permute-start | bytes 1572872 | tf_op jit(solution)/shard_map/ppermute | solution.py:271
  6.9 6.4 %collective-permute-start.1 = (s16[64,1024]{1,0:T(8,128)(2,1)S(1)}, s16[64,1024]{1,0:T(8,128)(2,1)S(1)}, u32[]{:S(2)}, u32[]{:S(2)}) collective-permute-start(s16[64,1024]{1,0:T(8,128)(2,1)S(1)} %get-tuple-element.19), channel_id=1, source_target_pairs={{0,8},{4,12},{8,0},{12,4},{16,24},{20,28},{24,16},{28,20},{1,9},{5... | collective-permute-start | bytes 393224 | tf_op jit(solution)/shard_map/ppermute | solution.py:274
  8.9 8.7 %collective-permute-start.3 = (s16[64,512]{1,0:T(8,128)(2,1)S(1)}, s16[64,512]{1,0:T(8,128)(2,1)S(1)}, u32[]{:S(2)}, u32[]{:S(2)}) collective-permute-start(s16[64,512]{1,0:T(8,128)(2,1)S(1)} %get-tuple-element.21), channel_id=1, source_target_pairs={{0,24},{4,28},{8,16},{12,20},{16,8},{20,12},{24,0},{28,4},{1,25},{... | collective-permute-start | bytes 196616 | tf_op jit(solution)/shard_map/ppermute | solution.py:274
  11.3 9.5 %collective-permute-start.4 = (s16[64,512]{1,0:T(8,128)(2,1)S(1)}, s16[64,512]{1,0:T(8,128)(2,1)S(1)}, u32[]{:S(2)}, u32[]{:S(2)}) collective-permute-start(s16[64,512]{1,0:T(8,128)(2,1)S(1)} %get-tuple-element.22), channel_id=1, source_target_pairs={{0,16},{4,20},{8,24},{12,28},{16,0},{20,4},{24,8},{28,12},{1,17},{... | collective-permute-start | bytes 196616 | tf_op jit(solution)/shard_map/ppermute | solution.py:274
  11.8 9.0 %collective-permute-start.5 = (s16[64,512]{1,0:T(8,128)(2,1)S(1)}, s16[64,512]{1,0:T(8,128)(2,1)S(1)}, u32[]{:S(2)}, u32[]{:S(2)}) collective-permute-start(s16[64,512]{1,0:T(8,128)(2,1)S(1)} %get-tuple-element.23), channel_id=1, source_target_pairs={{0,8},{4,12},{8,0},{12,4},{16,24},{20,28},{24,16},{28,20},{1,9},{5... | collective-permute-start | bytes 196616 | tf_op jit(solution)/shard_map/ppermute | solution.py:274
  13.4 14.4 %collective-permute-start.2 = (s16[64,1024]{1,0:T(8,128)(2,1)S(1)}, s16[64,1024]{1,0:T(8,128)(2,1)S(1)}, u32[]{:S(2)}, u32[]{:S(2)}) collective-permute-start(s16[64,1024]{1,0:T(8,128)(2,1)S(1)} %shard_map.58.code), channel_id=1, source_target_pairs={{0,16},{4,20},{8,24},{12,28},{16,0},{20,4},{24,8},{28,12},{1,17},{... | collective-permute-start | bytes 393224 | tf_op jit(solution)/shard_map/ppermute | solution.py:274
  20.9 7.1 %collective-permute-start.8 = (bf16[64,512]{1,0:T(8,128)(2,1)S(1)}, bf16[64,512]{1,0:T(8,128)(2,1)S(1)}, u32[]{:S(2)}, u32[]{:S(2)}) collective-permute-start(bf16[64,512]{1,0:T(8,128)(2,1)S(1)} %shard_map.59.chunk), channel_id=1, source_target_pairs={{0,24},{4,28},{8,16},{12,20},{16,8},{20,12},{24,0},{28,4},{1,25},{... | collective-permute-start | bytes 196616 | tf_op jit(solution)/shard_map/ppermute | solution.py:274
  22.8 7.4 %collective-permute-start.7 = (bf16[64,512]{1,0:T(8,128)(2,1)S(1)}, bf16[64,512]{1,0:T(8,128)(2,1)S(1)}, u32[]{:S(2)}, u32[]{:S(2)}) collective-permute-start(bf16[64,512]{1,0:T(8,128)(2,1)S(1)} %shard_map.59.chunk), channel_id=1, source_target_pairs={{0,16},{4,20},{8,24},{12,28},{16,0},{20,4},{24,8},{28,12},{1,17},{... | collective-permute-start | bytes 196616 | tf_op jit(solution)/shard_map/ppermute | solution.py:274
  27.9 5.9 %collective-permute-start.6 = (bf16[64,1536]{1,0:T(8,128)(2,1)S(1)}, bf16[64,1536]{1,0:T(8,128)(2,1)S(1)}, u32[]{:S(2)}, u32[]{:S(2)}) collective-permute-start(bf16[64,1536]{1,0:T(8,128)(2,1)S(1)} %shard_map.60.refs_0_), channel_id=1, source_target_pairs={{0,8},{4,12},{8,0},{12,4},{16,24},{20,28},{24,16},{28,20},{1,9},{5... | collective-permute-start | bytes 589832 | tf_op jit(solution)/shard_map/ppermute | solution.py:274
  30.2 5.2 %collective-permute-start.9 = (bf16[64,1536]{1,0:T(8,128)(2,1)S(1)}, bf16[64,1536]{1,0:T(8,128)(2,1)S(1)}, u32[]{:S(2)}, u32[]{:S(2)}) collective-permute-start(bf16[64,1536]{1,0:T(8,128)(2,1)S(1)} %shard_map.60.refs_0_), channel_id=1, source_target_pairs={{0,4},{4,0},{8,12},{12,8},{16,20},{20,16},{24,28},{28,24},{1,5},{5... | collective-permute-start | bytes 589832 | tf_op jit(solution)/shard_map/ppermute | solution.py:271
  33.8 1.6 %collective-permute-start.10 = (bf16[64,1536]{1,0:T(8,128)(2,1)S(1)}, bf16[64,1536]{1,0:T(8,128)(2,1)S(1)}, u32[]{:S(2)}, u32[]{:S(2)}) collective-permute-start(bf16[64,1536]{1,0:T(8,128)(2,1)S(1)} %collective-permute-done.6.refs_1_), channel_id=1, source_target_pairs={{0,4},{4,0},{8,12},{12,8},{16,20},{20,16},{24,28},{28,24},{1,5},{5... | collective-permute-start | bytes 589832 | tf_op jit(solution)/shard_map/ppermute | solution.py:271
  33.8 1.6 %collective-permute-start.11 = (bf16[64,1024]{1,0:T(8,128)(2,1)S(1)}, bf16[64,1024]{1,0:T(8,128)(2,1)S(1)}, u32[]{:S(2)}, u32[]{:S(2)}) collective-permute-start(bf16[64,1024]{1,0:T(8,128)(2,1)S(1)} %shard_map.61.refs_2_), channel_id=1, source_target_pairs={{0,4},{4,0},{8,12},{12,8},{16,20},{20,16},{24,28},{28,24},{1,5},{5... | collective-permute-start | bytes 393224 | tf_op jit(solution)/shard_map/ppermute | solution.py:271
  36.0 6.7 %collective-permute-start.12 = (s16[256,256]{1,0:T(8,128)(2,1)S(1)}, s16[256,256]{1,0:T(8,128)(2,1)S(1)}, u32[]{:S(2)}, u32[]{:S(2)}) collective-permute-start(s16[256,256]{1,0:T(8,128)(2,1)S(1)} %shard_map.64), channel_id=1, source_target_pairs={{0,3},{1,2},{2,1},{3,0},{4,7},{5,6},{6,5},{7,4},{8,11},{9,10},{10,... | collective-permute-start | bytes 393224 | tf_op jit(solution)/shard_map/ppermute | solution.py:277
  38.9 6.6 %collective-permute-start.13 = (s16[256,256]{1,0:T(8,128)(2,1)S(1)}, s16[256,256]{1,0:T(8,128)(2,1)S(1)}, u32[]{:S(2)}, u32[]{:S(2)}) collective-permute-start(s16[256,256]{1,0:T(8,128)(2,1)S(1)} %shard_map.66), channel_id=1, source_target_pairs={{0,2},{1,3},{2,0},{3,1},{4,6},{5,7},{6,4},{7,5},{8,10},{9,11},{10,... | collective-permute-start | bytes 393224 | tf_op jit(solution)/shard_map/ppermute | solution.py:277
  40.1 5.4 %collective-permute-start.14 = (s16[256,256]{1,0:T(8,128)(2,1)S(1)}, s16[256,256]{1,0:T(8,128)(2,1)S(1)}, u32[]{:S(2)}, u32[]{:S(2)}) collective-permute-start(s16[256,256]{1,0:T(8,128)(2,1)S(1)} %shard_map.68), channel_id=1, source_target_pairs={{0,1},{1,0},{2,3},{3,2},{4,5},{5,4},{6,7},{7,6},{8,9},{9,8},{10,11... | collective-permute-start | bytes 393224 | tf_op jit(solution)/shard_map/ppermute | solution.py:277

commit v16 on v14

--- a/solution.py
+++ b/solution.py
@@ -195,7 +195,7 @@
 
 
 def gene_kernel(masks, first, first_theirs, *refs):
-    *pieces, gene = refs
+    *pieces, out, gene = refs
     core, chip = core_and_chip()
     rows, width = pieces[0].shape
     lead = first.shape[0]
@@ -214,13 +214,14 @@
         cut = pl.ds(pl.multiple_of(place, width), width)
         gene[at(1, core), cut] = pieces[k][...]
         gene[at(1, 1 - core), cut] = pieces[len(masks) + k][...]
+    out[...] = gene[...].T
 
 
 def cell_kernel(k, dense, gene, out):
     height = out.shape[0]
     me = lax.axis_index("genes")
     left = dense[pl.ds(pl.multiple_of((me ^ k) * height, height), height), :]
-    part = lax.dot_general(left, gene[...], (((1,), (1,)), ((), ())), preferred_element_type=f32)
+    part = jnp.dot(left, gene[...], preferred_element_type=f32)
     if k == 0:
         out[...] = part
     else:
@@ -264,7 +265,7 @@
             pltpu.VMEM((slots, tile, tile), bf16),
             pltpu.VMEM((cells, rank), bf16),
             pltpu.SemaphoreType.DMA((3,)),
-            pltpu.SemaphoreType.DMA((slots // 16 if slots % 16 == 0 else 1,)),
+            pltpu.SemaphoreType.DMA((slots // 8 if slots % 8 == 0 else 1,)),
         ],
         flops=flops // 2,
         nbytes=8 * MIB,
@@ -302,7 +303,11 @@
         masks += [mask ^ (1 << bit) for mask in masks]
     theirs = [to_core(x) for x in held]
     gene = call(
-        functools.partial(gene_kernel, masks), shape((rank, genes), bf16), [VMEM] * (2 + 2 * len(held)), nbytes=2 * MIB
+        functools.partial(gene_kernel, masks),
+        shape((genes, rank), bf16),
+        [VMEM] * (2 + 2 * len(held)),
+        scratch=[pltpu.VMEM((rank, genes), bf16)],
+        nbytes=2 * MIB,
     )(first, to_core(first), *held, *theirs)
 
     def cell(k, gene):

time: 44.7 us -> 45.2 us (1.011)
  starting transfers between devices: 19.7 us -> 20.8 us
  waiting for transfers between devices: 16 us -> 15 us
    ppermute x9, starting transfers between devices: 14.8 us -> 16.5 us  [to_chip(): lax.ppermute(x, 'cells', [(i, i ^ CORES * k) for i in range(n_cells)])]
    ppermute x9, waiting for transfers between devices: 9.11 us -> 7.84 us  [to_chip(): lax.ppermute(x, 'cells', [(i, i ^ CORES * k) for i in range(n_cells)])]
    ppermute x3, starting transfers between devices: 4.32 us -> 3.68 us  [to_gene(): return lax.ppermute(x, 'genes', [(i, i ^ k) for i in range(n_genes)])]
  transfers between devices with their start and end apart: 16 -> 16, of which waited for: 11 -> 12; matrix products, arithmetic and copies ran while one was open for 0% -> 0% of each run, Pallas kernels for 6% -> 6%
where the time goes in v16:
time: 45.2 us; the launch traced here: 45.1 us
  starting transfers between devices  20.8 us (46%)
  waiting for transfers between devices  15 us (33%)
  Pallas kernels  8.5 us (19%)
  between operations  0.76 us (2%)
    ppermute x9, starting transfers between devices, to_chip(): lax.ppermute(x, 'cells', [(i, i ^ CORES * k) for i in range(n_cells)])  16.5 us
    ppermute x9, waiting for transfers between devices, to_chip(): lax.ppermute(x, 'cells', [(i, i ^ CORES * k) for i in range(n_cells)])  7.84 us
    ppermute x3, waiting for transfers between devices, to_gene(): return lax.ppermute(x, 'genes', [(i, i ^ k) for i in range(n_genes)])  4.67 us
    pallas_call x1, Pallas kernels, local(): call(dense_kernel, (shape((cells, genes), bf16), shape((rank, cells), bf1...  3.95 us
    ppermute x3, starting transfers between devices, to_gene(): return lax.ppermute(x, 'genes', [(i, i ^ k) for i in range(n_genes)])  3.68 us
    ppermute x4, waiting for transfers between devices, to_core(): return lax.ppermute(x, 'cells', [(i, i ^ 1) for i in range(n_cells)])  2.52 us
    pallas_call x4, Pallas kernels, cell(): call(functools.partial(cell_kernel, k), shape((height, rank), kind), [VME...  1.91 us
  transfers between devices with their start and end apart: 16, of which 12 were waited for; matrix products, arithmetic and copies ran while one was open for 0% of the time, Pallas kernels for 6%

profile of v16, /device:TPU:0, one launch (start us, length us, event | category | flops | bytes accessed | tf_op | source)
XLA Modules:
  0.0 45.1 jit_solution(2564362826125945639)
XLA Ops:
  0.7 3.9 %shard_map.55 = (bf16[1024,2048]{1,0:T(8,128)(2,1)S(1)}, bf16[256,1024]{1,0:T(8,128)(2,1)S(1)}, s16[128,2048]{1,0:T(8,128)(2,1)S(1)}) custom-call(s32[1]{0:T(128)S(6)} %copy.6.count, s32[96]{0:T(128)} %rows.1, s32[96]{0:T(128)} %cols.1, bf16[1024,256]{1,0:T(8,128)(2,1)} %sketch.1, bf16[96,128,128]{2,1,0:T(8,128)(2,1)} %tiles.1), custom_call_target="tpu_custom_call" | custom-call | flops 536870912 | bytes 8388608 | tf_op jit(solution)/shard_map/pallas_call | solution.py:259
  4.7 0.7 %shard_map.56.mine = f32[128,2048]{1,0:T(8,128)S(1)} custom-call(bf16[256,1024]{1,0:T(8,128)(2,1)S(1)} %get-tuple-element.18.turned, bf16[1024,2048]{1,0:T(8,128)(2,1)S(1)} %get-tuple-element.17.dense), custom_call_target="tpu_custom_call" | custom-call | flops 536870912 | bytes 5242880 | tf_op jit(solution)/shard_map/pallas_call | solution.py:274
  5.4 1.2 %collective-permute-done.got = s16[128,2048]{1,0:T(8,128)(2,1)S(1)} collective-permute-done((s16[128,2048]{1,0:T(8,128)(2,1)S(1)}, s16[128,2048]{1,0:T(8,128)(2,1)S(1)}, u32[]{:S(2)}, u32[]{:S(2)}) %collective-permute-start) | collective-permute-done | bytes 524320 | tf_op jit(solution)/shard_map/ppermute | solution.py:248
  6.9 1.8 %collective-permute-start.7 = (s16[64,1024]{1,0:T(8,128)(2,1)S(1)}, s16[64,1024]{1,0:T(8,128)(2,1)S(1)}, u32[]{:S(2)}, u32[]{:S(2)}) collective-permute-start(s16[64,1024]{1,0:T(8,128)(2,1)S(1)} %get-tuple-element.25), channel_id=1, source_target_pairs={{0,8},{4,12},{8,0},{12,4},{16,24},{20,28},{24,16},{28,20},{1,9},{5... | collective-permute-start | bytes 393224 | tf_op jit(solution)/shard_map/ppermute | solution.py:251
  8.8 2.6 %collective-permute-start.1 = (s16[64,512]{1,0:T(8,128)(2,1)S(1)}, s16[64,512]{1,0:T(8,128)(2,1)S(1)}, u32[]{:S(2)}, u32[]{:S(2)}) collective-permute-start(s16[64,512]{1,0:T(8,128)(2,1)S(1)} %get-tuple-element.21), channel_id=1, source_target_pairs={{0,24},{4,28},{8,16},{12,20},{16,8},{20,12},{24,0},{28,4},{1,25},{... | collective-permute-start | bytes 196616 | tf_op jit(solution)/shard_map/ppermute | solution.py:251
  11.3 0.5 %collective-permute-start.2 = (s16[64,512]{1,0:T(8,128)(2,1)S(1)}, s16[64,512]{1,0:T(8,128)(2,1)S(1)}, u32[]{:S(2)}, u32[]{:S(2)}) collective-permute-start(s16[64,512]{1,0:T(8,128)(2,1)S(1)} %get-tuple-element.22), channel_id=1, source_target_pairs={{0,16},{4,20},{8,24},{12,28},{16,0},{20,4},{24,8},{28,12},{1,17},{... | collective-permute-start | bytes 196616 | tf_op jit(solution)/shard_map/ppermute | solution.py:251
  11.8 0.7 %collective-permute-done.7.got = s16[64,1024]{1,0:T(8,128)(2,1)S(1)} collective-permute-done((s16[64,1024]{1,0:T(8,128)(2,1)S(1)}, s16[64,1024]{1,0:T(8,128)(2,1)S(1)}, u32[]{:S(2)}, u32[]{:S(2)}) %collective-permute-start.7) | collective-permute-done | bytes 131104 | tf_op jit(solution)/shard_map/ppermute | solution.py:251
  12.7 4.1 %collective-permute-start.8 = (s16[64,1024]{1,0:T(8,128)(2,1)S(1)}, s16[64,1024]{1,0:T(8,128)(2,1)S(1)}, u32[]{:S(2)}, u32[]{:S(2)}) collective-permute-start(s16[64,1024]{1,0:T(8,128)(2,1)S(1)} %shard_map.59.code), channel_id=1, source_target_pairs={{0,16},{4,20},{8,24},{12,28},{16,0},{20,4},{24,8},{28,12},{1,17},{... | collective-permute-start | bytes 393224 | tf_op jit(solution)/shard_map/ppermute | solution.py:251
  16.8 2.4 %collective-permute-start.3 = (s16[64,512]{1,0:T(8,128)(2,1)S(1)}, s16[64,512]{1,0:T(8,128)(2,1)S(1)}, u32[]{:S(2)}, u32[]{:S(2)}) collective-permute-start(s16[64,512]{1,0:T(8,128)(2,1)S(1)} %get-tuple-element.23), channel_id=1, source_target_pairs={{0,8},{4,12},{8,0},{12,4},{16,24},{20,28},{24,16},{28,20},{1,9},{5... | collective-permute-start | bytes 196616 | tf_op jit(solution)/shard_map/ppermute | solution.py:251
  19.2 2.9 %collective-permute-done.2.refs_1_ = s16[64,512]{1,0:T(8,128)(2,1)S(1)} collective-permute-done((s16[64,512]{1,0:T(8,128)(2,1)S(1)}, s16[64,512]{1,0:T(8,128)(2,1)S(1)}, u32[]{:S(2)}, u32[]{:S(2)}) %collective-permute-start.2) | collective-permute-done | bytes 65568 | tf_op jit(solution)/shard_map/ppermute | solution.py:251
  22.3 2.3 %collective-permute-start.6 = (bf16[64,512]{1,0:T(8,128)(2,1)S(1)}, bf16[64,512]{1,0:T(8,128)(2,1)S(1)}, u32[]{:S(2)}, u32[]{:S(2)}) collective-permute-start(bf16[64,512]{1,0:T(8,128)(2,1)S(1)} %shard_map.58.refs_0_), channel_id=1, source_target_pairs={{0,24},{4,28},{8,16},{12,20},{16,8},{20,12},{24,0},{28,4},{1,25},{... | collective-permute-start | bytes 196616 | tf_op jit(solution)/shard_map/ppermute | solution.py:251
  24.6 0.7 %collective-permute-start.5 = (bf16[64,512]{1,0:T(8,128)(2,1)S(1)}, bf16[64,512]{1,0:T(8,128)(2,1)S(1)}, u32[]{:S(2)}, u32[]{:S(2)}) collective-permute-start(bf16[64,512]{1,0:T(8,128)(2,1)S(1)} %shard_map.58.refs_0_), channel_id=1, source_target_pairs={{0,16},{4,20},{8,24},{12,28},{16,0},{20,4},{24,8},{28,12},{1,17},{... | collective-permute-start | bytes 196616 | tf_op jit(solution)/shard_map/ppermute | solution.py:251
  25.2 1.5 %collective-permute-start.4 = (bf16[64,512]{1,0:T(8,128)(2,1)S(1)}, bf16[64,512]{1,0:T(8,128)(2,1)S(1)}, u32[]{:S(2)}, u32[]{:S(2)}) collective-permute-start(bf16[64,512]{1,0:T(8,128)(2,1)S(1)} %shard_map.58.refs_0_), channel_id=1, source_target_pairs={{0,8},{4,12},{8,0},{12,4},{16,24},{20,28},{24,16},{28,20},{1,9},{5... | collective-permute-start | bytes 196616 | tf_op jit(solution)/shard_map/ppermute | solution.py:251
  26.8 0.6 %collective-permute-start.10 = (bf16[64,1024]{1,0:T(8,128)(2,1)S(1)}, bf16[64,1024]{1,0:T(8,128)(2,1)S(1)}, u32[]{:S(2)}, u32[]{:S(2)}) collective-permute-start(bf16[64,1024]{1,0:T(8,128)(2,1)S(1)} %shard_map.60.refs_0_), channel_id=1, source_target_pairs={{0,8},{4,12},{8,0},{12,4},{16,24},{20,28},{24,16},{28,20},{1,9},{5... | collective-permute-start | bytes 393224 | tf_op jit(solution)/shard_map/ppermute | solution.py:251
  27.4 1.7 %collective-permute-done.6.refs_3_ = bf16[64,512]{1,0:T(8,128)(2,1)S(1)} collective-permute-done((bf16[64,512]{1,0:T(8,128)(2,1)S(1)}, bf16[64,512]{1,0:T(8,128)(2,1)S(1)}, u32[]{:S(2)}, u32[]{:S(2)}) %collective-permute-start.6) | collective-permute-done | bytes 65568 | tf_op jit(solution)/shard_map/ppermute | solution.py:251
  29.1 1.4 %collective-permute-done.5.refs_2_ = bf16[64,512]{1,0:T(8,128)(2,1)S(1)} collective-permute-done((bf16[64,512]{1,0:T(8,128)(2,1)S(1)}, bf16[64,512]{1,0:T(8,128)(2,1)S(1)}, u32[]{:S(2)}, u32[]{:S(2)}) %collective-permute-start.5) | collective-permute-done | bytes 65568 | tf_op jit(solution)/shard_map/ppermute | solution.py:251
  30.9 0.5 %collective-permute-start.11 = (bf16[64,1024]{1,0:T(8,128)(2,1)S(1)}, bf16[64,1024]{1,0:T(8,128)(2,1)S(1)}, u32[]{:S(2)}, u32[]{:S(2)}) collective-permute-start(bf16[64,1024]{1,0:T(8,128)(2,1)S(1)} %shard_map.60.refs_0_), channel_id=1, source_target_pairs={{0,4},{4,0},{8,12},{12,8},{16,20},{20,16},{24,28},{28,24},{1,5},{5... | collective-permute-start | bytes 393224 | tf_op jit(solution)/shard_map/ppermute | solution.py:248
  31.4 0.8 %collective-permute-done.10.refs_1_ = bf16[64,1024]{1,0:T(8,128)(2,1)S(1)} collective-permute-done((bf16[64,1024]{1,0:T(8,128)(2,1)S(1)}, bf16[64,1024]{1,0:T(8,128)(2,1)S(1)}, u32[]{:S(2)}, u32[]{:S(2)}) %collective-permute-start.10) | collective-permute-done | bytes 131104 | tf_op jit(solution)/shard_map/ppermute | solution.py:251
  32.2 0.4 collective-permute-done.11.refs_2_
  32.6 0.9 %collective-permute-done.12.refs_3_ = bf16[64,1024]{1,0:T(8,128)(2,1)S(1)} collective-permute-done((bf16[64,1024]{1,0:T(8,128)(2,1)S(1)}, bf16[64,1024]{1,0:T(8,128)(2,1)S(1)}, u32[]{:S(2)}, u32[]{:S(2)}) %collective-permute-start.12) | collective-permute-done | bytes 131104 | tf_op jit(solution)/shard_map/ppermute | solution.py:248
  33.5 0.4 shard_map.62.gene
  34.0 0.5 %shard_map.64 = s16[256,256]{1,0:T(8,128)(2,1)S(1)} custom-call(bf16[1024,2048]{1,0:T(8,128)(2,1)S(1)} %get-tuple-element.17.dense, bf16[2048,256]{1,0:T(8,128)(2,1)S(1)} %shard_map.62.gene), custom_call_target="tpu_custom_call" | custom-call | tf_op jit(solution)/shard_map/pallas_call | solution.py:315
  34.5 2.7 %collective-permute-start.13 = (s16[256,256]{1,0:T(8,128)(2,1)S(1)}, s16[256,256]{1,0:T(8,128)(2,1)S(1)}, u32[]{:S(2)}, u32[]{:S(2)}) collective-permute-start(s16[256,256]{1,0:T(8,128)(2,1)S(1)} %shard_map.64), channel_id=1, source_target_pairs={{0,3},{1,2},{2,1},{3,0},{4,7},{5,6},{6,5},{7,4},{8,11},{9,10},{10,... | collective-permute-start | bytes 393224 | tf_op jit(solution)/shard_map/ppermute | solution.py:254
  37.2 0.5 %shard_map.66 = s16[256,256]{1,0:T(8,128)(2,1)S(1)} custom-call(bf16[1024,2048]{1,0:T(8,128)(2,1)S(1)} %get-tuple-element.17.dense, bf16[2048,256]{1,0:T(8,128)(2,1)S(1)} %shard_map.62.gene), custom_call_target="tpu_custom_call" | custom-call | tf_op jit(solution)/shard_map/pallas_call | solution.py:315
  37.7 0.6 %collective-permute-start.14 = (s16[256,256]{1,0:T(8,128)(2,1)S(1)}, s16[256,256]{1,0:T(8,128)(2,1)S(1)}, u32[]{:S(2)}, u32[]{:S(2)}) collective-permute-start(s16[256,256]{1,0:T(8,128)(2,1)S(1)} %shard_map.66), channel_id=1, source_target_pairs={{0,2},{1,3},{2,0},{3,1},{4,6},{5,7},{6,4},{7,5},{8,10},{9,11},{10,... | collective-permute-start | bytes 393224 | tf_op jit(solution)/shard_map/ppermute | solution.py:254
  38.3 0.5 %shard_map.68 = s16[256,256]{1,0:T(8,128)(2,1)S(1)} custom-call(bf16[1024,2048]{1,0:T(8,128)(2,1)S(1)} %get-tuple-element.17.dense, bf16[2048,256]{1,0:T(8,128)(2,1)S(1)} %shard_map.62.gene), custom_call_target="tpu_custom_call" | custom-call | tf_op jit(solution)/shard_map/pallas_call | solution.py:315
  38.8 0.4 collective-permute-start.15
  39.2 0.4 shard_map.63.total
  39.6 1.5 %collective-permute-done.13.got = s16[256,256]{1,0:T(8,128)(2,1)S(1)} collective-permute-done((s16[256,256]{1,0:T(8,128)(2,1)S(1)}, s16[256,256]{1,0:T(8,128)(2,1)S(1)}, u32[]{:S(2)}, u32[]{:S(2)}) %collective-permute-start.13) | collective-permute-done | bytes 131104 | tf_op jit(solution)/shard_map/ppermute | solution.py:254
  41.1 2.7 %collective-permute-done.14.got = s16[256,256]{1,0:T(8,128)(2,1)S(1)} collective-permute-done((s16[256,256]{1,0:T(8,128)(2,1)S(1)}, s16[256,256]{1,0:T(8,128)(2,1)S(1)}, u32[]{:S(2)}, u32[]{:S(2)}) %collective-permute-start.14) | collective-permute-done | bytes 131104 | tf_op jit(solution)/shard_map/ppermute | solution.py:254
  43.9 0.5 %collective-permute-done.15.got = s16[256,256]{1,0:T(8,128)(2,1)S(1)} collective-permute-done((s16[256,256]{1,0:T(8,128)(2,1)S(1)}, s16[256,256]{1,0:T(8,128)(2,1)S(1)}, u32[]{:S(2)}, u32[]{:S(2)}) %collective-permute-start.15) | collective-permute-done | bytes 131104 | tf_op jit(solution)/shard_map/ppermute | solution.py:254
  44.4 0.7 %shard_map.69 = f32[256,256]{1,0:T(8,128)} custom-call(f32[256,256]{1,0:T(8,128)S(1)} %shard_map.67.total, s16[256,256]{1,0:T(8,128)(2,1)S(1)} %collective-permute-done.15.got), custom_call_target="tpu_custom_call" | custom-call | bytes 16777216 | tf_op jit(solution)/shard_map/pallas_call | solution.py:326
  (15 shorter events, 1.2 us)
Async XLA Ops:
  4.6 2.0 %collective-permute-start = (s16[128,2048]{1,0:T(8,128)(2,1)S(1)}, s16[128,2048]{1,0:T(8,128)(2,1)S(1)}, u32[]{:S(2)}, u32[]{:S(2)}) collective-permute-start(s16[128,2048]{1,0:T(8,128)(2,1)S(1)} %get-tuple-element.19), channel_id=1, source_target_pairs={{0,4},{4,0},{8,12},{12,8},{16,20},{20,16},{24,28},{28,24},{1,5},{5... | collective-permute-start | bytes 1572872 | tf_op jit(solution)/shard_map/ppermute | solution.py:248
  6.9 5.6 %collective-permute-start.7 = (s16[64,1024]{1,0:T(8,128)(2,1)S(1)}, s16[64,1024]{1,0:T(8,128)(2,1)S(1)}, u32[]{:S(2)}, u32[]{:S(2)}) collective-permute-start(s16[64,1024]{1,0:T(8,128)(2,1)S(1)} %get-tuple-element.25), channel_id=1, source_target_pairs={{0,8},{4,12},{8,0},{12,4},{16,24},{20,28},{24,16},{28,20},{1,9},{5... | collective-permute-start | bytes 393224 | tf_op jit(solution)/shard_map/ppermute | solution.py:251
  8.8 10.5 %collective-permute-start.1 = (s16[64,512]{1,0:T(8,128)(2,1)S(1)}, s16[64,512]{1,0:T(8,128)(2,1)S(1)}, u32[]{:S(2)}, u32[]{:S(2)}) collective-permute-start(s16[64,512]{1,0:T(8,128)(2,1)S(1)} %get-tuple-element.21), channel_id=1, source_target_pairs={{0,24},{4,28},{8,16},{12,20},{16,8},{20,12},{24,0},{28,4},{1,25},{... | collective-permute-start | bytes 196616 | tf_op jit(solution)/shard_map/ppermute | solution.py:251
  11.3 10.8 %collective-permute-start.2 = (s16[64,512]{1,0:T(8,128)(2,1)S(1)}, s16[64,512]{1,0:T(8,128)(2,1)S(1)}, u32[]{:S(2)}, u32[]{:S(2)}) collective-permute-start(s16[64,512]{1,0:T(8,128)(2,1)S(1)} %get-tuple-element.22), channel_id=1, source_target_pairs={{0,16},{4,20},{8,24},{12,28},{16,0},{20,4},{24,8},{28,12},{1,17},{... | collective-permute-start | bytes 196616 | tf_op jit(solution)/shard_map/ppermute | solution.py:251
  12.7 14.0 %collective-permute-start.8 = (s16[64,1024]{1,0:T(8,128)(2,1)S(1)}, s16[64,1024]{1,0:T(8,128)(2,1)S(1)}, u32[]{:S(2)}, u32[]{:S(2)}) collective-permute-start(s16[64,1024]{1,0:T(8,128)(2,1)S(1)} %shard_map.59.code), channel_id=1, source_target_pairs={{0,16},{4,20},{8,24},{12,28},{16,0},{20,4},{24,8},{28,12},{1,17},{... | collective-permute-start | bytes 393224 | tf_op jit(solution)/shard_map/ppermute | solution.py:251
  16.8 5.4 %collective-permute-start.3 = (s16[64,512]{1,0:T(8,128)(2,1)S(1)}, s16[64,512]{1,0:T(8,128)(2,1)S(1)}, u32[]{:S(2)}, u32[]{:S(2)}) collective-permute-start(s16[64,512]{1,0:T(8,128)(2,1)S(1)} %get-tuple-element.23), channel_id=1, source_target_pairs={{0,8},{4,12},{8,0},{12,4},{16,24},{20,28},{24,16},{28,20},{1,9},{5... | collective-permute-start | bytes 196616 | tf_op jit(solution)/shard_map/ppermute | solution.py:251
  22.3 6.8 %collective-permute-start.6 = (bf16[64,512]{1,0:T(8,128)(2,1)S(1)}, bf16[64,512]{1,0:T(8,128)(2,1)S(1)}, u32[]{:S(2)}, u32[]{:S(2)}) collective-permute-start(bf16[64,512]{1,0:T(8,128)(2,1)S(1)} %shard_map.58.refs_0_), channel_id=1, source_target_pairs={{0,24},{4,28},{8,16},{12,20},{16,8},{20,12},{24,0},{28,4},{1,25},{... | collective-permute-start | bytes 196616 | tf_op jit(solution)/shard_map/ppermute | solution.py:251
  24.6 5.9 %collective-permute-start.5 = (bf16[64,512]{1,0:T(8,128)(2,1)S(1)}, bf16[64,512]{1,0:T(8,128)(2,1)S(1)}, u32[]{:S(2)}, u32[]{:S(2)}) collective-permute-start(bf16[64,512]{1,0:T(8,128)(2,1)S(1)} %shard_map.58.refs_0_), channel_id=1, source_target_pairs={{0,16},{4,20},{8,24},{12,28},{16,0},{20,4},{24,8},{28,12},{1,17},{... | collective-permute-start | bytes 196616 | tf_op jit(solution)/shard_map/ppermute | solution.py:251
  25.2 5.5 %collective-permute-start.4 = (bf16[64,512]{1,0:T(8,128)(2,1)S(1)}, bf16[64,512]{1,0:T(8,128)(2,1)S(1)}, u32[]{:S(2)}, u32[]{:S(2)}) collective-permute-start(bf16[64,512]{1,0:T(8,128)(2,1)S(1)} %shard_map.58.refs_0_), channel_id=1, source_target_pairs={{0,8},{4,12},{8,0},{12,4},{16,24},{20,28},{24,16},{28,20},{1,9},{5... | collective-permute-start | bytes 196616 | tf_op jit(solution)/shard_map/ppermute | solution.py:251
  26.8 5.4 %collective-permute-start.10 = (bf16[64,1024]{1,0:T(8,128)(2,1)S(1)}, bf16[64,1024]{1,0:T(8,128)(2,1)S(1)}, u32[]{:S(2)}, u32[]{:S(2)}) collective-permute-start(bf16[64,1024]{1,0:T(8,128)(2,1)S(1)} %shard_map.60.refs_0_), channel_id=1, source_target_pairs={{0,8},{4,12},{8,0},{12,4},{16,24},{20,28},{24,16},{28,20},{1,9},{5... | collective-permute-start | bytes 393224 | tf_op jit(solution)/shard_map/ppermute | solution.py:251
  30.8 2.7 %collective-permute-start.9 = (bf16[64,2048]{1,0:T(8,128)(2,1)S(1)}, bf16[64,2048]{1,0:T(8,128)(2,1)S(1)}, u32[]{:S(2)}, u32[]{:S(2)}) collective-permute-start(bf16[64,2048]{1,0:T(8,128)(2,1)S(1)} %shard_map.61.first), channel_id=1, source_target_pairs={{0,4},{4,0},{8,12},{12,8},{16,20},{20,16},{24,28},{28,24},{1,5},{5... | collective-permute-start | bytes 786440 | tf_op jit(solution)/shard_map/ppermute | solution.py:248
  30.9 1.7 %collective-permute-start.11 = (bf16[64,1024]{1,0:T(8,128)(2,1)S(1)}, bf16[64,1024]{1,0:T(8,128)(2,1)S(1)}, u32[]{:S(2)}, u32[]{:S(2)}) collective-permute-start(bf16[64,1024]{1,0:T(8,128)(2,1)S(1)} %shard_map.60.refs_0_), channel_id=1, source_target_pairs={{0,4},{4,0},{8,12},{12,8},{16,20},{20,16},{24,28},{28,24},{1,5},{5... | collective-permute-start | bytes 393224 | tf_op jit(solution)/shard_map/ppermute | solution.py:248
  32.2 1.3 %collective-permute-start.12 = (bf16[64,1024]{1,0:T(8,128)(2,1)S(1)}, bf16[64,1024]{1,0:T(8,128)(2,1)S(1)}, u32[]{:S(2)}, u32[]{:S(2)}) collective-permute-start(bf16[64,1024]{1,0:T(8,128)(2,1)S(1)} %collective-permute-done.10.refs_1_), channel_id=1, source_target_pairs={{0,4},{4,0},{8,12},{12,8},{16,20},{20,16},{24,28},{28,24},{1,5},{5... | collective-permute-start | bytes 393224 | tf_op jit(solution)/shard_map/ppermute | solution.py:248
  34.5 6.6 %collective-permute-start.13 = (s16[256,256]{1,0:T(8,128)(2,1)S(1)}, s16[256,256]{1,0:T(8,128)(2,1)S(1)}, u32[]{:S(2)}, u32[]{:S(2)}) collective-permute-start(s16[256,256]{1,0:T(8,128)(2,1)S(1)} %shard_map.64), channel_id=1, source_target_pairs={{0,3},{1,2},{2,1},{3,0},{4,7},{5,6},{6,5},{7,4},{8,11},{9,10},{10,... | collective-permute-start | bytes 393224 | tf_op jit(solution)/shard_map/ppermute | solution.py:254
  37.7 6.1 %collective-permute-start.14 = (s16[256,256]{1,0:T(8,128)(2,1)S(1)}, s16[256,256]{1,0:T(8,128)(2,1)S(1)}, u32[]{:S(2)}, u32[]{:S(2)}) collective-permute-start(s16[256,256]{1,0:T(8,128)(2,1)S(1)} %shard_map.66), channel_id=1, source_target_pairs={{0,2},{1,3},{2,0},{3,1},{4,6},{5,7},{6,4},{7,5},{8,10},{9,11},{10,... | collective-permute-start | bytes 393224 | tf_op jit(solution)/shard_map/ppermute | solution.py:254
  38.8 5.6 %collective-permute-start.15 = (s16[256,256]{1,0:T(8,128)(2,1)S(1)}, s16[256,256]{1,0:T(8,128)(2,1)S(1)}, u32[]{:S(2)}, u32[]{:S(2)}) collective-permute-start(s16[256,256]{1,0:T(8,128)(2,1)S(1)} %shard_map.68), channel_id=1, source_target_pairs={{0,1},{1,0},{2,3},{3,2},{4,5},{5,4},{6,7},{7,6},{8,9},{9,8},{10,11... | collective-permute-start | bytes 393224 | tf_op jit(solution)/shard_map/ppermute | solution.py:254

commit v17 on v14

--- a/solution.py
+++ b/solution.py
@@ -86,10 +86,10 @@
         pl.when(live > i * size)(lambda i=i: group(i).start())
 
     def clear(i, _):
-        dense[pl.ds(pl.multiple_of(i * 16, 16), 16), :] = jnp.zeros((16, dense.shape[1]), bf16)
+        dense[pl.ds(pl.multiple_of(i * 64, 64), 64), :] = jnp.zeros((64, dense.shape[1]), bf16)
         return 0
 
-    lax.fori_loop(0, dense.shape[0] // 16, clear, 0)
+    lax.fori_loop(0, dense.shape[0] // 64, clear, 0)
     loads[2].wait()
     turned[...] = sketch_here[...].T
     for load in loads[:2]:
@@ -120,7 +120,7 @@
                 lax.fori_loop(i * size, live, put_one, 0)
 
     left = rows_of(turned, 1 - core, theirs.shape[0])
-    width = 512
+    width = 1024
     for j in range(dense.shape[1] // width):
         cut = pl.ds(j * width, width)
         encode(jnp.dot(left, dense[:, cut], preferred_element_type=f32), theirs.at[:, cut])

time: 44.7 us -> 44.9 us (level)
  starting transfers between devices: 19.7 us -> 20.2 us
    ppermute x9, starting transfers between devices: 14.8 us -> 15.3 us  [to_chip(): lax.ppermute(x, 'cells', [(i, i ^ CORES * k) for i in range(n_cells)])]
    ppermute x9, waiting for transfers between devices: 9.11 us -> 8.63 us  [to_chip(): lax.ppermute(x, 'cells', [(i, i ^ CORES * k) for i in range(n_cells)])]
  transfers between devices with their start and end apart: 16 -> 16, of which waited for: 11 -> 12; matrix products, arithmetic and copies ran while one was open for 0% -> 0% of each run, Pallas kernels for 6% -> 6%
where the time goes in v17:
time: 44.9 us; the launch traced here: 44.8 us
  starting transfers between devices  20.2 us (45%)
  waiting for transfers between devices  15.7 us (35%)
  Pallas kernels  8.13 us (18%)
  between operations  0.77 us (2%)
    ppermute x9, starting transfers between devices, to_chip(): lax.ppermute(x, 'cells', [(i, i ^ CORES * k) for i in range(n_cells)])  15.3 us
    ppermute x9, waiting for transfers between devices, to_chip(): lax.ppermute(x, 'cells', [(i, i ^ CORES * k) for i in range(n_cells)])  8.63 us
    ppermute x3, waiting for transfers between devices, to_gene(): return lax.ppermute(x, 'genes', [(i, i ^ k) for i in range(n_genes)])  4.6 us
    ppermute x3, starting transfers between devices, to_gene(): return lax.ppermute(x, 'genes', [(i, i ^ k) for i in range(n_genes)])  4.22 us
    pallas_call x1, Pallas kernels, local(): call(dense_kernel, (shape((cells, genes), bf16), shape((rank, cells), bf1...  3.81 us
    ppermute x4, waiting for transfers between devices, to_core(): return lax.ppermute(x, 'cells', [(i, i ^ 1) for i in range(n_cells)])  2.52 us
    pallas_call x4, Pallas kernels, cell(): call(functools.partial(cell_kernel, k), shape((height, rank), kind), [VME...  2.03 us
  transfers between devices with their start and end apart: 16, of which 12 were waited for; matrix products, arithmetic and copies ran while one was open for 0% of the time, Pallas kernels for 6%

profile of v17, /device:TPU:0, one launch (start us, length us, event | category | flops | bytes accessed | tf_op | source)
XLA Modules:
  0.0 44.8 jit_solution(7049307391063037849)
XLA Ops:
  0.7 3.8 %shard_map.55 = (bf16[1024,2048]{1,0:T(8,128)(2,1)S(1)}, bf16[256,1024]{1,0:T(8,128)(2,1)S(1)}, s16[128,2048]{1,0:T(8,128)(2,1)S(1)}) custom-call(s32[1]{0:T(128)S(6)} %copy.6.count, s32[96]{0:T(128)} %rows.1, s32[96]{0:T(128)} %cols.1, bf16[1024,256]{1,0:T(8,128)(2,1)} %sketch.1, bf16[96,128,128]{2,1,0:T(8,128)(2,1)} %tiles.1), custom_call_target="tpu_custom_call" | custom-call | flops 536870912 | bytes 8388608 | tf_op jit(solution)/shard_map/pallas_call | solution.py:258
  4.5 0.7 %shard_map.56.mine = f32[128,2048]{1,0:T(8,128)S(1)} custom-call(bf16[256,1024]{1,0:T(8,128)(2,1)S(1)} %get-tuple-element.18.turned, bf16[1024,2048]{1,0:T(8,128)(2,1)S(1)} %get-tuple-element.17.dense), custom_call_target="tpu_custom_call" | custom-call | flops 536870912 | bytes 5242880 | tf_op jit(solution)/shard_map/pallas_call | solution.py:273
  5.3 1.2 %collective-permute-done.got = s16[128,2048]{1,0:T(8,128)(2,1)S(1)} collective-permute-done((s16[128,2048]{1,0:T(8,128)(2,1)S(1)}, s16[128,2048]{1,0:T(8,128)(2,1)S(1)}, u32[]{:S(2)}, u32[]{:S(2)}) %collective-permute-start) | collective-permute-done | bytes 524320 | tf_op jit(solution)/shard_map/ppermute | solution.py:247
  6.4 0.4 shard_map.57
  6.8 2.0 %collective-permute-start.7 = (s16[64,1024]{1,0:T(8,128)(2,1)S(1)}, s16[64,1024]{1,0:T(8,128)(2,1)S(1)}, u32[]{:S(2)}, u32[]{:S(2)}) collective-permute-start(s16[64,1024]{1,0:T(8,128)(2,1)S(1)} %get-tuple-element.25), channel_id=1, source_target_pairs={{0,8},{4,12},{8,0},{12,4},{16,24},{20,28},{24,16},{28,20},{1,9},{5... | collective-permute-start | bytes 393224 | tf_op jit(solution)/shard_map/ppermute | solution.py:250
  8.8 2.2 %collective-permute-start.1 = (s16[64,512]{1,0:T(8,128)(2,1)S(1)}, s16[64,512]{1,0:T(8,128)(2,1)S(1)}, u32[]{:S(2)}, u32[]{:S(2)}) collective-permute-start(s16[64,512]{1,0:T(8,128)(2,1)S(1)} %get-tuple-element.21), channel_id=1, source_target_pairs={{0,24},{4,28},{8,16},{12,20},{16,8},{20,12},{24,0},{28,4},{1,25},{... | collective-permute-start | bytes 196616 | tf_op jit(solution)/shard_map/ppermute | solution.py:250
  11.0 0.4 collective-permute-start.2
  11.4 1.2 %collective-permute-done.7.got = s16[64,1024]{1,0:T(8,128)(2,1)S(1)} collective-permute-done((s16[64,1024]{1,0:T(8,128)(2,1)S(1)}, s16[64,1024]{1,0:T(8,128)(2,1)S(1)}, u32[]{:S(2)}, u32[]{:S(2)}) %collective-permute-start.7) | collective-permute-done | bytes 131104 | tf_op jit(solution)/shard_map/ppermute | solution.py:250
  12.8 3.3 %collective-permute-start.8 = (s16[64,1024]{1,0:T(8,128)(2,1)S(1)}, s16[64,1024]{1,0:T(8,128)(2,1)S(1)}, u32[]{:S(2)}, u32[]{:S(2)}) collective-permute-start(s16[64,1024]{1,0:T(8,128)(2,1)S(1)} %shard_map.59.code), channel_id=1, source_target_pairs={{0,16},{4,20},{8,24},{12,28},{16,0},{20,4},{24,8},{28,12},{1,17},{... | collective-permute-start | bytes 393224 | tf_op jit(solution)/shard_map/ppermute | solution.py:250
  16.1 2.6 %collective-permute-start.3 = (s16[64,512]{1,0:T(8,128)(2,1)S(1)}, s16[64,512]{1,0:T(8,128)(2,1)S(1)}, u32[]{:S(2)}, u32[]{:S(2)}) collective-permute-start(s16[64,512]{1,0:T(8,128)(2,1)S(1)} %get-tuple-element.23), channel_id=1, source_target_pairs={{0,8},{4,12},{8,0},{12,4},{16,24},{20,28},{24,16},{28,20},{1,9},{5... | collective-permute-start | bytes 196616 | tf_op jit(solution)/shard_map/ppermute | solution.py:250
  18.7 3.1 %collective-permute-done.2.refs_1_ = s16[64,512]{1,0:T(8,128)(2,1)S(1)} collective-permute-done((s16[64,512]{1,0:T(8,128)(2,1)S(1)}, s16[64,512]{1,0:T(8,128)(2,1)S(1)}, u32[]{:S(2)}, u32[]{:S(2)}) %collective-permute-start.2) | collective-permute-done | bytes 65568 | tf_op jit(solution)/shard_map/ppermute | solution.py:250
  21.9 2.4 %collective-permute-start.6 = (bf16[64,512]{1,0:T(8,128)(2,1)S(1)}, bf16[64,512]{1,0:T(8,128)(2,1)S(1)}, u32[]{:S(2)}, u32[]{:S(2)}) collective-permute-start(bf16[64,512]{1,0:T(8,128)(2,1)S(1)} %shard_map.58.refs_0_), channel_id=1, source_target_pairs={{0,24},{4,28},{8,16},{12,20},{16,8},{20,12},{24,0},{28,4},{1,25},{... | collective-permute-start | bytes 196616 | tf_op jit(solution)/shard_map/ppermute | solution.py:250
  24.3 0.3 collective-permute-start.5
  24.6 1.8 %collective-permute-start.4 = (bf16[64,512]{1,0:T(8,128)(2,1)S(1)}, bf16[64,512]{1,0:T(8,128)(2,1)S(1)}, u32[]{:S(2)}, u32[]{:S(2)}) collective-permute-start(bf16[64,512]{1,0:T(8,128)(2,1)S(1)} %shard_map.58.refs_0_), channel_id=1, source_target_pairs={{0,8},{4,12},{8,0},{12,4},{16,24},{20,28},{24,16},{28,20},{1,9},{5... | collective-permute-start | bytes 196616 | tf_op jit(solution)/shard_map/ppermute | solution.py:250
  26.4 0.3 collective-permute-start.10
  26.8 1.9 %collective-permute-done.6.refs_3_ = bf16[64,512]{1,0:T(8,128)(2,1)S(1)} collective-permute-done((bf16[64,512]{1,0:T(8,128)(2,1)S(1)}, bf16[64,512]{1,0:T(8,128)(2,1)S(1)}, u32[]{:S(2)}, u32[]{:S(2)}) %collective-permute-start.6) | collective-permute-done | bytes 65568 | tf_op jit(solution)/shard_map/ppermute | solution.py:250
  28.6 1.5 %collective-permute-done.5.refs_2_ = bf16[64,512]{1,0:T(8,128)(2,1)S(1)} collective-permute-done((bf16[64,512]{1,0:T(8,128)(2,1)S(1)}, bf16[64,512]{1,0:T(8,128)(2,1)S(1)}, u32[]{:S(2)}, u32[]{:S(2)}) %collective-permute-start.5) | collective-permute-done | bytes 65568 | tf_op jit(solution)/shard_map/ppermute | solution.py:250
  30.4 0.5 %collective-permute-start.11 = (bf16[64,1024]{1,0:T(8,128)(2,1)S(1)}, bf16[64,1024]{1,0:T(8,128)(2,1)S(1)}, u32[]{:S(2)}, u32[]{:S(2)}) collective-permute-start(bf16[64,1024]{1,0:T(8,128)(2,1)S(1)} %shard_map.60.refs_0_), channel_id=1, source_target_pairs={{0,4},{4,0},{8,12},{12,8},{16,20},{20,16},{24,28},{28,24},{1,5},{5... | collective-permute-start | bytes 393224 | tf_op jit(solution)/shard_map/ppermute | solution.py:247
  30.9 0.8 %collective-permute-done.10.refs_1_ = bf16[64,1024]{1,0:T(8,128)(2,1)S(1)} collective-permute-done((bf16[64,1024]{1,0:T(8,128)(2,1)S(1)}, bf16[64,1024]{1,0:T(8,128)(2,1)S(1)}, u32[]{:S(2)}, u32[]{:S(2)}) %collective-permute-start.10) | collective-permute-done | bytes 131104 | tf_op jit(solution)/shard_map/ppermute | solution.py:250
  31.7 0.4 collective-permute-done.11.refs_2_
  32.1 0.9 %collective-permute-done.12.refs_3_ = bf16[64,1024]{1,0:T(8,128)(2,1)S(1)} collective-permute-done((bf16[64,1024]{1,0:T(8,128)(2,1)S(1)}, bf16[64,1024]{1,0:T(8,128)(2,1)S(1)}, u32[]{:S(2)}, u32[]{:S(2)}) %collective-permute-start.12) | collective-permute-done | bytes 131104 | tf_op jit(solution)/shard_map/ppermute | solution.py:247
  33.1 0.5 %shard_map.64 = s16[256,256]{1,0:T(8,128)(2,1)S(1)} custom-call(bf16[1024,2048]{1,0:T(8,128)(2,1)S(1)} %get-tuple-element.17.dense, bf16[256,2048]{1,0:T(8,128)(2,1)S(1)} %shard_map.62.gene), custom_call_target="tpu_custom_call" | custom-call | tf_op jit(solution)/shard_map/pallas_call | solution.py:310
  33.6 3.4 %collective-permute-start.13 = (s16[256,256]{1,0:T(8,128)(2,1)S(1)}, s16[256,256]{1,0:T(8,128)(2,1)S(1)}, u32[]{:S(2)}, u32[]{:S(2)}) collective-permute-start(s16[256,256]{1,0:T(8,128)(2,1)S(1)} %shard_map.64), channel_id=1, source_target_pairs={{0,3},{1,2},{2,1},{3,0},{4,7},{5,6},{6,5},{7,4},{8,11},{9,10},{10,... | collective-permute-start | bytes 393224 | tf_op jit(solution)/shard_map/ppermute | solution.py:253
  37.0 0.5 %shard_map.66 = s16[256,256]{1,0:T(8,128)(2,1)S(1)} custom-call(bf16[1024,2048]{1,0:T(8,128)(2,1)S(1)} %get-tuple-element.17.dense, bf16[256,2048]{1,0:T(8,128)(2,1)S(1)} %shard_map.62.gene), custom_call_target="tpu_custom_call" | custom-call | tf_op jit(solution)/shard_map/pallas_call | solution.py:310
  37.5 0.6 %collective-permute-start.14 = (s16[256,256]{1,0:T(8,128)(2,1)S(1)}, s16[256,256]{1,0:T(8,128)(2,1)S(1)}, u32[]{:S(2)}, u32[]{:S(2)}) collective-permute-start(s16[256,256]{1,0:T(8,128)(2,1)S(1)} %shard_map.66), channel_id=1, source_target_pairs={{0,2},{1,3},{2,0},{3,1},{4,6},{5,7},{6,4},{7,5},{8,10},{9,11},{10,... | collective-permute-start | bytes 393224 | tf_op jit(solution)/shard_map/ppermute | solution.py:253
  38.1 0.5 %shard_map.68 = s16[256,256]{1,0:T(8,128)(2,1)S(1)} custom-call(bf16[1024,2048]{1,0:T(8,128)(2,1)S(1)} %get-tuple-element.17.dense, bf16[256,2048]{1,0:T(8,128)(2,1)S(1)} %shard_map.62.gene), custom_call_target="tpu_custom_call" | custom-call | tf_op jit(solution)/shard_map/pallas_call | solution.py:310
  38.6 0.3 collective-permute-start.15
  38.9 0.5 %shard_map.63.total = f32[256,256]{1,0:T(8,128)S(1)} custom-call(bf16[1024,2048]{1,0:T(8,128)(2,1)S(1)} %get-tuple-element.17.dense, bf16[256,2048]{1,0:T(8,128)(2,1)S(1)} %shard_map.62.gene), custom_call_target="tpu_custom_call" | custom-call | tf_op jit(solution)/shard_map/pallas_call | solution.py:310
  39.4 1.5 %collective-permute-done.13.got = s16[256,256]{1,0:T(8,128)(2,1)S(1)} collective-permute-done((s16[256,256]{1,0:T(8,128)(2,1)S(1)}, s16[256,256]{1,0:T(8,128)(2,1)S(1)}, u32[]{:S(2)}, u32[]{:S(2)}) %collective-permute-start.13) | collective-permute-done | bytes 131104 | tf_op jit(solution)/shard_map/ppermute | solution.py:253
  41.0 2.7 %collective-permute-done.14.got = s16[256,256]{1,0:T(8,128)(2,1)S(1)} collective-permute-done((s16[256,256]{1,0:T(8,128)(2,1)S(1)}, s16[256,256]{1,0:T(8,128)(2,1)S(1)}, u32[]{:S(2)}, u32[]{:S(2)}) %collective-permute-start.14) | collective-permute-done | bytes 131104 | tf_op jit(solution)/shard_map/ppermute | solution.py:253
  43.7 0.4 collective-permute-done.15.got
  44.1 0.7 %shard_map.69 = f32[256,256]{1,0:T(8,128)} custom-call(f32[256,256]{1,0:T(8,128)S(1)} %shard_map.67.total, s16[256,256]{1,0:T(8,128)(2,1)S(1)} %collective-permute-done.15.got), custom_call_target="tpu_custom_call" | custom-call | bytes 16777216 | tf_op jit(solution)/shard_map/pallas_call | solution.py:321
  (15 shorter events, 0.8 us)
Async XLA Ops:
  4.5 2.0 %collective-permute-start = (s16[128,2048]{1,0:T(8,128)(2,1)S(1)}, s16[128,2048]{1,0:T(8,128)(2,1)S(1)}, u32[]{:S(2)}, u32[]{:S(2)}) collective-permute-start(s16[128,2048]{1,0:T(8,128)(2,1)S(1)} %get-tuple-element.19), channel_id=1, source_target_pairs={{0,4},{4,0},{8,12},{12,8},{16,20},{20,16},{24,28},{28,24},{1,5},{5... | collective-permute-start | bytes 1572872 | tf_op jit(solution)/shard_map/ppermute | solution.py:247
  6.8 5.8 %collective-permute-start.7 = (s16[64,1024]{1,0:T(8,128)(2,1)S(1)}, s16[64,1024]{1,0:T(8,128)(2,1)S(1)}, u32[]{:S(2)}, u32[]{:S(2)}) collective-permute-start(s16[64,1024]{1,0:T(8,128)(2,1)S(1)} %get-tuple-element.25), channel_id=1, source_target_pairs={{0,8},{4,12},{8,0},{12,4},{16,24},{20,28},{24,16},{28,20},{1,9},{5... | collective-permute-start | bytes 393224 | tf_op jit(solution)/shard_map/ppermute | solution.py:250
  8.8 9.9 %collective-permute-start.1 = (s16[64,512]{1,0:T(8,128)(2,1)S(1)}, s16[64,512]{1,0:T(8,128)(2,1)S(1)}, u32[]{:S(2)}, u32[]{:S(2)}) collective-permute-start(s16[64,512]{1,0:T(8,128)(2,1)S(1)} %get-tuple-element.21), channel_id=1, source_target_pairs={{0,24},{4,28},{8,16},{12,20},{16,8},{20,12},{24,0},{28,4},{1,25},{... | collective-permute-start | bytes 196616 | tf_op jit(solution)/shard_map/ppermute | solution.py:250
  11.0 10.8 %collective-permute-start.2 = (s16[64,512]{1,0:T(8,128)(2,1)S(1)}, s16[64,512]{1,0:T(8,128)(2,1)S(1)}, u32[]{:S(2)}, u32[]{:S(2)}) collective-permute-start(s16[64,512]{1,0:T(8,128)(2,1)S(1)} %get-tuple-element.22), channel_id=1, source_target_pairs={{0,16},{4,20},{8,24},{12,28},{16,0},{20,4},{24,8},{28,12},{1,17},{... | collective-permute-start | bytes 196616 | tf_op jit(solution)/shard_map/ppermute | solution.py:250
  12.8 13.6 %collective-permute-start.8 = (s16[64,1024]{1,0:T(8,128)(2,1)S(1)}, s16[64,1024]{1,0:T(8,128)(2,1)S(1)}, u32[]{:S(2)}, u32[]{:S(2)}) collective-permute-start(s16[64,1024]{1,0:T(8,128)(2,1)S(1)} %shard_map.59.code), channel_id=1, source_target_pairs={{0,16},{4,20},{8,24},{12,28},{16,0},{20,4},{24,8},{28,12},{1,17},{... | collective-permute-start | bytes 393224 | tf_op jit(solution)/shard_map/ppermute | solution.py:250
  16.1 5.7 %collective-permute-start.3 = (s16[64,512]{1,0:T(8,128)(2,1)S(1)}, s16[64,512]{1,0:T(8,128)(2,1)S(1)}, u32[]{:S(2)}, u32[]{:S(2)}) collective-permute-start(s16[64,512]{1,0:T(8,128)(2,1)S(1)} %get-tuple-element.23), channel_id=1, source_target_pairs={{0,8},{4,12},{8,0},{12,4},{16,24},{20,28},{24,16},{28,20},{1,9},{5... | collective-permute-start | bytes 196616 | tf_op jit(solution)/shard_map/ppermute | solution.py:250
  21.9 6.7 %collective-permute-start.6 = (bf16[64,512]{1,0:T(8,128)(2,1)S(1)}, bf16[64,512]{1,0:T(8,128)(2,1)S(1)}, u32[]{:S(2)}, u32[]{:S(2)}) collective-permute-start(bf16[64,512]{1,0:T(8,128)(2,1)S(1)} %shard_map.58.refs_0_), channel_id=1, source_target_pairs={{0,24},{4,28},{8,16},{12,20},{16,8},{20,12},{24,0},{28,4},{1,25},{... | collective-permute-start | bytes 196616 | tf_op jit(solution)/shard_map/ppermute | solution.py:250
  24.3 5.9 %collective-permute-start.5 = (bf16[64,512]{1,0:T(8,128)(2,1)S(1)}, bf16[64,512]{1,0:T(8,128)(2,1)S(1)}, u32[]{:S(2)}, u32[]{:S(2)}) collective-permute-start(bf16[64,512]{1,0:T(8,128)(2,1)S(1)} %shard_map.58.refs_0_), channel_id=1, source_target_pairs={{0,16},{4,20},{8,24},{12,28},{16,0},{20,4},{24,8},{28,12},{1,17},{... | collective-permute-start | bytes 196616 | tf_op jit(solution)/shard_map/ppermute | solution.py:250
  24.6 5.7 %collective-permute-start.4 = (bf16[64,512]{1,0:T(8,128)(2,1)S(1)}, bf16[64,512]{1,0:T(8,128)(2,1)S(1)}, u32[]{:S(2)}, u32[]{:S(2)}) collective-permute-start(bf16[64,512]{1,0:T(8,128)(2,1)S(1)} %shard_map.58.refs_0_), channel_id=1, source_target_pairs={{0,8},{4,12},{8,0},{12,4},{16,24},{20,28},{24,16},{28,20},{1,9},{5... | collective-permute-start | bytes 196616 | tf_op jit(solution)/shard_map/ppermute | solution.py:250
  26.4 5.2 %collective-permute-start.10 = (bf16[64,1024]{1,0:T(8,128)(2,1)S(1)}, bf16[64,1024]{1,0:T(8,128)(2,1)S(1)}, u32[]{:S(2)}, u32[]{:S(2)}) collective-permute-start(bf16[64,1024]{1,0:T(8,128)(2,1)S(1)} %shard_map.60.refs_0_), channel_id=1, source_target_pairs={{0,8},{4,12},{8,0},{12,4},{16,24},{20,28},{24,16},{28,20},{1,9},{5... | collective-permute-start | bytes 393224 | tf_op jit(solution)/shard_map/ppermute | solution.py:250
  30.3 2.7 %collective-permute-start.9 = (bf16[64,2048]{1,0:T(8,128)(2,1)S(1)}, bf16[64,2048]{1,0:T(8,128)(2,1)S(1)}, u32[]{:S(2)}, u32[]{:S(2)}) collective-permute-start(bf16[64,2048]{1,0:T(8,128)(2,1)S(1)} %shard_map.61.first), channel_id=1, source_target_pairs={{0,4},{4,0},{8,12},{12,8},{16,20},{20,16},{24,28},{28,24},{1,5},{5... | collective-permute-start | bytes 786440 | tf_op jit(solution)/shard_map/ppermute | solution.py:247
  30.4 1.7 %collective-permute-start.11 = (bf16[64,1024]{1,0:T(8,128)(2,1)S(1)}, bf16[64,1024]{1,0:T(8,128)(2,1)S(1)}, u32[]{:S(2)}, u32[]{:S(2)}) collective-permute-start(bf16[64,1024]{1,0:T(8,128)(2,1)S(1)} %shard_map.60.refs_0_), channel_id=1, source_target_pairs={{0,4},{4,0},{8,12},{12,8},{16,20},{20,16},{24,28},{28,24},{1,5},{5... | collective-permute-start | bytes 393224 | tf_op jit(solution)/shard_map/ppermute | solution.py:247
  31.7 1.3 %collective-permute-start.12 = (bf16[64,1024]{1,0:T(8,128)(2,1)S(1)}, bf16[64,1024]{1,0:T(8,128)(2,1)S(1)}, u32[]{:S(2)}, u32[]{:S(2)}) collective-permute-start(bf16[64,1024]{1,0:T(8,128)(2,1)S(1)} %collective-permute-done.10.refs_1_), channel_id=1, source_target_pairs={{0,4},{4,0},{8,12},{12,8},{16,20},{20,16},{24,28},{28,24},{1,5},{5... | collective-permute-start | bytes 393224 | tf_op jit(solution)/shard_map/ppermute | solution.py:247
  33.6 7.3 %collective-permute-start.13 = (s16[256,256]{1,0:T(8,128)(2,1)S(1)}, s16[256,256]{1,0:T(8,128)(2,1)S(1)}, u32[]{:S(2)}, u32[]{:S(2)}) collective-permute-start(s16[256,256]{1,0:T(8,128)(2,1)S(1)} %shard_map.64), channel_id=1, source_target_pairs={{0,3},{1,2},{2,1},{3,0},{4,7},{5,6},{6,5},{7,4},{8,11},{9,10},{10,... | collective-permute-start | bytes 393224 | tf_op jit(solution)/shard_map/ppermute | solution.py:253
  37.5 6.1 %collective-permute-start.14 = (s16[256,256]{1,0:T(8,128)(2,1)S(1)}, s16[256,256]{1,0:T(8,128)(2,1)S(1)}, u32[]{:S(2)}, u32[]{:S(2)}) collective-permute-start(s16[256,256]{1,0:T(8,128)(2,1)S(1)} %shard_map.66), channel_id=1, source_target_pairs={{0,2},{1,3},{2,0},{3,1},{4,6},{5,7},{6,4},{7,5},{8,10},{9,11},{10,... | collective-permute-start | bytes 393224 | tf_op jit(solution)/shard_map/ppermute | solution.py:253
  38.6 5.5 %collective-permute-start.15 = (s16[256,256]{1,0:T(8,128)(2,1)S(1)}, s16[256,256]{1,0:T(8,128)(2,1)S(1)}, u32[]{:S(2)}, u32[]{:S(2)}) collective-permute-start(s16[256,256]{1,0:T(8,128)(2,1)S(1)} %shard_map.68), channel_id=1, source_target_pairs={{0,1},{1,0},{2,3},{3,2},{4,5},{5,4},{6,7},{7,6},{8,9},{9,8},{10,11... | collective-permute-start | bytes 393224 | tf_op jit(solution)/shard_map/ppermute | solution.py:253

commit v18 on v14

--- a/solution.py
+++ b/solution.py
@@ -314,7 +314,7 @@
         )(dense, gene)
 
     got = []
-    for k in reversed(range(1, n_genes)):
+    for k in (n_genes - 1, *range(1, n_genes - 1)):
         got.append(to_gene(cell(k, gene), k))
     total = cell(0, gene)
     for x in got:

time: 44.7 us -> 45.2 us (1.011)
  starting transfers between devices: 19.7 us -> 21.2 us
  waiting for transfers between devices: 16 us -> 15.1 us
    ppermute x9, starting transfers between devices: 14.8 us -> 16.9 us  [to_chip(): lax.ppermute(x, 'cells', [(i, i ^ CORES * k) for i in range(n_cells)])]
    ppermute x9, waiting for transfers between devices: 9.11 us -> 8.14 us  [to_chip(): lax.ppermute(x, 'cells', [(i, i ^ CORES * k) for i in range(n_cells)])]
    ppermute x3, starting transfers between devices: 4.32 us -> 3.68 us  [to_gene(): return lax.ppermute(x, 'genes', [(i, i ^ k) for i in range(n_genes)])]
  transfers between devices with their start and end apart: 16 -> 16, of which waited for: 11 -> 12; matrix products, arithmetic and copies ran while one was open for 0% -> 0% of each run, Pallas kernels for 6% -> 6%
where the time goes in v18:
time: 45.2 us; the launch traced here: 45.3 us
  starting transfers between devices  21.2 us (47%)
  waiting for transfers between devices  15.1 us (33%)
  Pallas kernels  8.11 us (18%)
  between operations  0.77 us (2%)
    ppermute x9, starting transfers between devices, to_chip(): lax.ppermute(x, 'cells', [(i, i ^ CORES * k) for i in range(n_cells)])  16.9 us
    ppermute x9, waiting for transfers between devices, to_chip(): lax.ppermute(x, 'cells', [(i, i ^ CORES * k) for i in range(n_cells)])  8.14 us
    ppermute x3, waiting for transfers between devices, to_gene(): return lax.ppermute(x, 'genes', [(i, i ^ k) for i in range(n_genes)])  4.48 us
    pallas_call x1, Pallas kernels, local(): call(dense_kernel, (shape((cells, genes), bf16), shape((rank, cells), bf1...  3.79 us
    ppermute x3, starting transfers between devices, to_gene(): return lax.ppermute(x, 'genes', [(i, i ^ k) for i in range(n_genes)])  3.68 us
    ppermute x4, waiting for transfers between devices, to_core(): return lax.ppermute(x, 'cells', [(i, i ^ 1) for i in range(n_cells)])  2.52 us
    pallas_call x4, Pallas kernels, cell(): call(functools.partial(cell_kernel, k), shape((height, rank), kind), [VME...  2.03 us
  transfers between devices with their start and end apart: 16, of which 12 were waited for; matrix products, arithmetic and copies ran while one was open for 0% of the time, Pallas kernels for 6%

profile of v18, /device:TPU:0, one launch (start us, length us, event | category | flops | bytes accessed | tf_op | source)
XLA Modules:
  0.0 45.3 jit_solution(8575446595452048255)
XLA Ops:
  0.7 3.8 %shard_map.55 = (bf16[1024,2048]{1,0:T(8,128)(2,1)S(1)}, bf16[256,1024]{1,0:T(8,128)(2,1)S(1)}, s16[128,2048]{1,0:T(8,128)(2,1)S(1)}) custom-call(s32[1]{0:T(128)S(6)} %copy.6.count, s32[96]{0:T(128)} %rows.1, s32[96]{0:T(128)} %cols.1, bf16[1024,256]{1,0:T(8,128)(2,1)} %sketch.1, bf16[96,128,128]{2,1,0:T(8,128)(2,1)} %tiles.1), custom_call_target="tpu_custom_call" | custom-call | flops 536870912 | bytes 8388608 | tf_op jit(solution)/shard_map/pallas_call | solution.py:258
  4.5 0.7 %shard_map.56.mine = f32[128,2048]{1,0:T(8,128)S(1)} custom-call(bf16[256,1024]{1,0:T(8,128)(2,1)S(1)} %get-tuple-element.18.turned, bf16[1024,2048]{1,0:T(8,128)(2,1)S(1)} %get-tuple-element.17.dense), custom_call_target="tpu_custom_call" | custom-call | flops 536870912 | bytes 5242880 | tf_op jit(solution)/shard_map/pallas_call | solution.py:273
  5.3 1.2 %collective-permute-done.got = s16[128,2048]{1,0:T(8,128)(2,1)S(1)} collective-permute-done((s16[128,2048]{1,0:T(8,128)(2,1)S(1)}, s16[128,2048]{1,0:T(8,128)(2,1)S(1)}, u32[]{:S(2)}, u32[]{:S(2)}) %collective-permute-start) | collective-permute-done | bytes 524320 | tf_op jit(solution)/shard_map/ppermute | solution.py:247
  6.4 0.4 shard_map.57
  6.8 2.0 %collective-permute-start.7 = (s16[64,1024]{1,0:T(8,128)(2,1)S(1)}, s16[64,1024]{1,0:T(8,128)(2,1)S(1)}, u32[]{:S(2)}, u32[]{:S(2)}) collective-permute-start(s16[64,1024]{1,0:T(8,128)(2,1)S(1)} %get-tuple-element.25), channel_id=1, source_target_pairs={{0,8},{4,12},{8,0},{12,4},{16,24},{20,28},{24,16},{28,20},{1,9},{5... | collective-permute-start | bytes 393224 | tf_op jit(solution)/shard_map/ppermute | solution.py:250
  8.7 3.0 %collective-permute-start.1 = (s16[64,512]{1,0:T(8,128)(2,1)S(1)}, s16[64,512]{1,0:T(8,128)(2,1)S(1)}, u32[]{:S(2)}, u32[]{:S(2)}) collective-permute-start(s16[64,512]{1,0:T(8,128)(2,1)S(1)} %get-tuple-element.21), channel_id=1, source_target_pairs={{0,24},{4,28},{8,16},{12,20},{16,8},{20,12},{24,0},{28,4},{1,25},{... | collective-permute-start | bytes 196616 | tf_op jit(solution)/shard_map/ppermute | solution.py:250
  11.8 0.5 %collective-permute-start.2 = (s16[64,512]{1,0:T(8,128)(2,1)S(1)}, s16[64,512]{1,0:T(8,128)(2,1)S(1)}, u32[]{:S(2)}, u32[]{:S(2)}) collective-permute-start(s16[64,512]{1,0:T(8,128)(2,1)S(1)} %get-tuple-element.22), channel_id=1, source_target_pairs={{0,16},{4,20},{8,24},{12,28},{16,0},{20,4},{24,8},{28,12},{1,17},{... | collective-permute-start | bytes 196616 | tf_op jit(solution)/shard_map/ppermute | solution.py:250
  12.3 0.4 collective-permute-done.7.got
  12.8 4.3 %collective-permute-start.8 = (s16[64,1024]{1,0:T(8,128)(2,1)S(1)}, s16[64,1024]{1,0:T(8,128)(2,1)S(1)}, u32[]{:S(2)}, u32[]{:S(2)}) collective-permute-start(s16[64,1024]{1,0:T(8,128)(2,1)S(1)} %shard_map.59.code), channel_id=1, source_target_pairs={{0,16},{4,20},{8,24},{12,28},{16,0},{20,4},{24,8},{28,12},{1,17},{... | collective-permute-start | bytes 393224 | tf_op jit(solution)/shard_map/ppermute | solution.py:250
  17.0 2.4 %collective-permute-start.3 = (s16[64,512]{1,0:T(8,128)(2,1)S(1)}, s16[64,512]{1,0:T(8,128)(2,1)S(1)}, u32[]{:S(2)}, u32[]{:S(2)}) collective-permute-start(s16[64,512]{1,0:T(8,128)(2,1)S(1)} %get-tuple-element.23), channel_id=1, source_target_pairs={{0,8},{4,12},{8,0},{12,4},{16,24},{20,28},{24,16},{28,20},{1,9},{5... | collective-permute-start | bytes 196616 | tf_op jit(solution)/shard_map/ppermute | solution.py:250
  19.5 3.1 %collective-permute-done.2.refs_1_ = s16[64,512]{1,0:T(8,128)(2,1)S(1)} collective-permute-done((s16[64,512]{1,0:T(8,128)(2,1)S(1)}, s16[64,512]{1,0:T(8,128)(2,1)S(1)}, u32[]{:S(2)}, u32[]{:S(2)}) %collective-permute-start.2) | collective-permute-done | bytes 65568 | tf_op jit(solution)/shard_map/ppermute | solution.py:250
  22.7 2.3 %collective-permute-start.6 = (bf16[64,512]{1,0:T(8,128)(2,1)S(1)}, bf16[64,512]{1,0:T(8,128)(2,1)S(1)}, u32[]{:S(2)}, u32[]{:S(2)}) collective-permute-start(bf16[64,512]{1,0:T(8,128)(2,1)S(1)} %shard_map.58.refs_0_), channel_id=1, source_target_pairs={{0,24},{4,28},{8,16},{12,20},{16,8},{20,12},{24,0},{28,4},{1,25},{... | collective-permute-start | bytes 196616 | tf_op jit(solution)/shard_map/ppermute | solution.py:250
  25.0 0.4 collective-permute-start.5
  25.3 1.8 %collective-permute-start.4 = (bf16[64,512]{1,0:T(8,128)(2,1)S(1)}, bf16[64,512]{1,0:T(8,128)(2,1)S(1)}, u32[]{:S(2)}, u32[]{:S(2)}) collective-permute-start(bf16[64,512]{1,0:T(8,128)(2,1)S(1)} %shard_map.58.refs_0_), channel_id=1, source_target_pairs={{0,8},{4,12},{8,0},{12,4},{16,24},{20,28},{24,16},{28,20},{1,9},{5... | collective-permute-start | bytes 196616 | tf_op jit(solution)/shard_map/ppermute | solution.py:250
  27.3 0.3 collective-permute-start.10
  27.5 1.8 %collective-permute-done.6.refs_3_ = bf16[64,512]{1,0:T(8,128)(2,1)S(1)} collective-permute-done((bf16[64,512]{1,0:T(8,128)(2,1)S(1)}, bf16[64,512]{1,0:T(8,128)(2,1)S(1)}, u32[]{:S(2)}, u32[]{:S(2)}) %collective-permute-start.6) | collective-permute-done | bytes 65568 | tf_op jit(solution)/shard_map/ppermute | solution.py:250
  29.3 1.5 %collective-permute-done.5.refs_2_ = bf16[64,512]{1,0:T(8,128)(2,1)S(1)} collective-permute-done((bf16[64,512]{1,0:T(8,128)(2,1)S(1)}, bf16[64,512]{1,0:T(8,128)(2,1)S(1)}, u32[]{:S(2)}, u32[]{:S(2)}) %collective-permute-start.5) | collective-permute-done | bytes 65568 | tf_op jit(solution)/shard_map/ppermute | solution.py:250
  30.8 0.6 %collective-permute-done.4.refs_1_ = bf16[64,512]{1,0:T(8,128)(2,1)S(1)} collective-permute-done((bf16[64,512]{1,0:T(8,128)(2,1)S(1)}, bf16[64,512]{1,0:T(8,128)(2,1)S(1)}, u32[]{:S(2)}, u32[]{:S(2)}) %collective-permute-start.4) | collective-permute-done | bytes 65568 | tf_op jit(solution)/shard_map/ppermute | solution.py:250
  31.5 0.5 %collective-permute-start.11 = (bf16[64,1024]{1,0:T(8,128)(2,1)S(1)}, bf16[64,1024]{1,0:T(8,128)(2,1)S(1)}, u32[]{:S(2)}, u32[]{:S(2)}) collective-permute-start(bf16[64,1024]{1,0:T(8,128)(2,1)S(1)} %shard_map.60.refs_0_), channel_id=1, source_target_pairs={{0,4},{4,0},{8,12},{12,8},{16,20},{20,16},{24,28},{28,24},{1,5},{5... | collective-permute-start | bytes 393224 | tf_op jit(solution)/shard_map/ppermute | solution.py:247
  32.0 0.8 %collective-permute-done.10.refs_1_ = bf16[64,1024]{1,0:T(8,128)(2,1)S(1)} collective-permute-done((bf16[64,1024]{1,0:T(8,128)(2,1)S(1)}, bf16[64,1024]{1,0:T(8,128)(2,1)S(1)}, u32[]{:S(2)}, u32[]{:S(2)}) %collective-permute-start.10) | collective-permute-done | bytes 131104 | tf_op jit(solution)/shard_map/ppermute | solution.py:250
  32.8 0.4 collective-permute-done.11.refs_2_
  33.2 0.9 %collective-permute-done.12.refs_3_ = bf16[64,1024]{1,0:T(8,128)(2,1)S(1)} collective-permute-done((bf16[64,1024]{1,0:T(8,128)(2,1)S(1)}, bf16[64,1024]{1,0:T(8,128)(2,1)S(1)}, u32[]{:S(2)}, u32[]{:S(2)}) %collective-permute-start.12) | collective-permute-done | bytes 131104 | tf_op jit(solution)/shard_map/ppermute | solution.py:247
  34.2 0.5 %shard_map.64 = s16[256,256]{1,0:T(8,128)(2,1)S(1)} custom-call(bf16[1024,2048]{1,0:T(8,128)(2,1)S(1)} %get-tuple-element.17.dense, bf16[256,2048]{1,0:T(8,128)(2,1)S(1)} %shard_map.62.gene), custom_call_target="tpu_custom_call" | custom-call | tf_op jit(solution)/shard_map/pallas_call | solution.py:310
  34.7 2.2 %collective-permute-start.13 = (s16[256,256]{1,0:T(8,128)(2,1)S(1)}, s16[256,256]{1,0:T(8,128)(2,1)S(1)}, u32[]{:S(2)}, u32[]{:S(2)}) collective-permute-start(s16[256,256]{1,0:T(8,128)(2,1)S(1)} %shard_map.64), channel_id=1, source_target_pairs={{0,3},{1,2},{2,1},{3,0},{4,7},{5,6},{6,5},{7,4},{8,11},{9,10},{10,... | collective-permute-start | bytes 393224 | tf_op jit(solution)/shard_map/ppermute | solution.py:253
  36.9 0.5 %shard_map.66 = s16[256,256]{1,0:T(8,128)(2,1)S(1)} custom-call(bf16[1024,2048]{1,0:T(8,128)(2,1)S(1)} %get-tuple-element.17.dense, bf16[256,2048]{1,0:T(8,128)(2,1)S(1)} %shard_map.62.gene), custom_call_target="tpu_custom_call" | custom-call | tf_op jit(solution)/shard_map/pallas_call | solution.py:310
  37.4 1.2 %collective-permute-start.14 = (s16[256,256]{1,0:T(8,128)(2,1)S(1)}, s16[256,256]{1,0:T(8,128)(2,1)S(1)}, u32[]{:S(2)}, u32[]{:S(2)}) collective-permute-start(s16[256,256]{1,0:T(8,128)(2,1)S(1)} %shard_map.66), channel_id=1, source_target_pairs={{0,1},{1,0},{2,3},{3,2},{4,5},{5,4},{6,7},{7,6},{8,9},{9,8},{10,11... | collective-permute-start | bytes 393224 | tf_op jit(solution)/shard_map/ppermute | solution.py:253
  38.6 0.5 %shard_map.68 = s16[256,256]{1,0:T(8,128)(2,1)S(1)} custom-call(bf16[1024,2048]{1,0:T(8,128)(2,1)S(1)} %get-tuple-element.17.dense, bf16[256,2048]{1,0:T(8,128)(2,1)S(1)} %shard_map.62.gene), custom_call_target="tpu_custom_call" | custom-call | tf_op jit(solution)/shard_map/pallas_call | solution.py:310
  39.1 0.3 collective-permute-start.15
  39.5 0.5 %shard_map.63.total = f32[256,256]{1,0:T(8,128)S(1)} custom-call(bf16[1024,2048]{1,0:T(8,128)(2,1)S(1)} %get-tuple-element.17.dense, bf16[256,2048]{1,0:T(8,128)(2,1)S(1)} %shard_map.62.gene), custom_call_target="tpu_custom_call" | custom-call | tf_op jit(solution)/shard_map/pallas_call | solution.py:310
  39.9 2.1 %collective-permute-done.13.got = s16[256,256]{1,0:T(8,128)(2,1)S(1)} collective-permute-done((s16[256,256]{1,0:T(8,128)(2,1)S(1)}, s16[256,256]{1,0:T(8,128)(2,1)S(1)}, u32[]{:S(2)}, u32[]{:S(2)}) %collective-permute-start.13) | collective-permute-done | bytes 131104 | tf_op jit(solution)/shard_map/ppermute | solution.py:253
  42.1 2.3 %collective-permute-done.14.got = s16[256,256]{1,0:T(8,128)(2,1)S(1)} collective-permute-done((s16[256,256]{1,0:T(8,128)(2,1)S(1)}, s16[256,256]{1,0:T(8,128)(2,1)S(1)}, u32[]{:S(2)}, u32[]{:S(2)}) %collective-permute-start.14) | collective-permute-done | bytes 131104 | tf_op jit(solution)/shard_map/ppermute | solution.py:253
  44.5 0.7 %shard_map.69 = f32[256,256]{1,0:T(8,128)} custom-call(f32[256,256]{1,0:T(8,128)S(1)} %shard_map.67.total, s16[256,256]{1,0:T(8,128)(2,1)S(1)} %collective-permute-done.15.got), custom_call_target="tpu_custom_call" | custom-call | bytes 16777216 | tf_op jit(solution)/shard_map/pallas_call | solution.py:321
  (15 shorter events, 0.7 us)
Async XLA Ops:
  4.4 2.0 %collective-permute-start = (s16[128,2048]{1,0:T(8,128)(2,1)S(1)}, s16[128,2048]{1,0:T(8,128)(2,1)S(1)}, u32[]{:S(2)}, u32[]{:S(2)}) collective-permute-start(s16[128,2048]{1,0:T(8,128)(2,1)S(1)} %get-tuple-element.19), channel_id=1, source_target_pairs={{0,4},{4,0},{8,12},{12,8},{16,20},{20,16},{24,28},{28,24},{1,5},{5... | collective-permute-start | bytes 1572872 | tf_op jit(solution)/shard_map/ppermute | solution.py:247
  6.8 5.9 %collective-permute-start.7 = (s16[64,1024]{1,0:T(8,128)(2,1)S(1)}, s16[64,1024]{1,0:T(8,128)(2,1)S(1)}, u32[]{:S(2)}, u32[]{:S(2)}) collective-permute-start(s16[64,1024]{1,0:T(8,128)(2,1)S(1)} %get-tuple-element.25), channel_id=1, source_target_pairs={{0,8},{4,12},{8,0},{12,4},{16,24},{20,28},{24,16},{28,20},{1,9},{5... | collective-permute-start | bytes 393224 | tf_op jit(solution)/shard_map/ppermute | solution.py:250
  8.7 10.7 %collective-permute-start.1 = (s16[64,512]{1,0:T(8,128)(2,1)S(1)}, s16[64,512]{1,0:T(8,128)(2,1)S(1)}, u32[]{:S(2)}, u32[]{:S(2)}) collective-permute-start(s16[64,512]{1,0:T(8,128)(2,1)S(1)} %get-tuple-element.21), channel_id=1, source_target_pairs={{0,24},{4,28},{8,16},{12,20},{16,8},{20,12},{24,0},{28,4},{1,25},{... | collective-permute-start | bytes 196616 | tf_op jit(solution)/shard_map/ppermute | solution.py:250
  11.8 10.8 %collective-permute-start.2 = (s16[64,512]{1,0:T(8,128)(2,1)S(1)}, s16[64,512]{1,0:T(8,128)(2,1)S(1)}, u32[]{:S(2)}, u32[]{:S(2)}) collective-permute-start(s16[64,512]{1,0:T(8,128)(2,1)S(1)} %get-tuple-element.22), channel_id=1, source_target_pairs={{0,16},{4,20},{8,24},{12,28},{16,0},{20,4},{24,8},{28,12},{1,17},{... | collective-permute-start | bytes 196616 | tf_op jit(solution)/shard_map/ppermute | solution.py:250
  12.8 14.4 %collective-permute-start.8 = (s16[64,1024]{1,0:T(8,128)(2,1)S(1)}, s16[64,1024]{1,0:T(8,128)(2,1)S(1)}, u32[]{:S(2)}, u32[]{:S(2)}) collective-permute-start(s16[64,1024]{1,0:T(8,128)(2,1)S(1)} %shard_map.59.code), channel_id=1, source_target_pairs={{0,16},{4,20},{8,24},{12,28},{16,0},{20,4},{24,8},{28,12},{1,17},{... | collective-permute-start | bytes 393224 | tf_op jit(solution)/shard_map/ppermute | solution.py:250
  17.0 5.6 %collective-permute-start.3 = (s16[64,512]{1,0:T(8,128)(2,1)S(1)}, s16[64,512]{1,0:T(8,128)(2,1)S(1)}, u32[]{:S(2)}, u32[]{:S(2)}) collective-permute-start(s16[64,512]{1,0:T(8,128)(2,1)S(1)} %get-tuple-element.23), channel_id=1, source_target_pairs={{0,8},{4,12},{8,0},{12,4},{16,24},{20,28},{24,16},{28,20},{1,9},{5... | collective-permute-start | bytes 196616 | tf_op jit(solution)/shard_map/ppermute | solution.py:250
  22.7 6.6 %collective-permute-start.6 = (bf16[64,512]{1,0:T(8,128)(2,1)S(1)}, bf16[64,512]{1,0:T(8,128)(2,1)S(1)}, u32[]{:S(2)}, u32[]{:S(2)}) collective-permute-start(bf16[64,512]{1,0:T(8,128)(2,1)S(1)} %shard_map.58.refs_0_), channel_id=1, source_target_pairs={{0,24},{4,28},{8,16},{12,20},{16,8},{20,12},{24,0},{28,4},{1,25},{... | collective-permute-start | bytes 196616 | tf_op jit(solution)/shard_map/ppermute | solution.py:250
  25.0 5.8 %collective-permute-start.5 = (bf16[64,512]{1,0:T(8,128)(2,1)S(1)}, bf16[64,512]{1,0:T(8,128)(2,1)S(1)}, u32[]{:S(2)}, u32[]{:S(2)}) collective-permute-start(bf16[64,512]{1,0:T(8,128)(2,1)S(1)} %shard_map.58.refs_0_), channel_id=1, source_target_pairs={{0,16},{4,20},{8,24},{12,28},{16,0},{20,4},{24,8},{28,12},{1,17},{... | collective-permute-start | bytes 196616 | tf_op jit(solution)/shard_map/ppermute | solution.py:250
  25.3 6.0 %collective-permute-start.4 = (bf16[64,512]{1,0:T(8,128)(2,1)S(1)}, bf16[64,512]{1,0:T(8,128)(2,1)S(1)}, u32[]{:S(2)}, u32[]{:S(2)}) collective-permute-start(bf16[64,512]{1,0:T(8,128)(2,1)S(1)} %shard_map.58.refs_0_), channel_id=1, source_target_pairs={{0,8},{4,12},{8,0},{12,4},{16,24},{20,28},{24,16},{28,20},{1,9},{5... | collective-permute-start | bytes 196616 | tf_op jit(solution)/shard_map/ppermute | solution.py:250
  27.3 5.5 %collective-permute-start.10 = (bf16[64,1024]{1,0:T(8,128)(2,1)S(1)}, bf16[64,1024]{1,0:T(8,128)(2,1)S(1)}, u32[]{:S(2)}, u32[]{:S(2)}) collective-permute-start(bf16[64,1024]{1,0:T(8,128)(2,1)S(1)} %shard_map.60.refs_0_), channel_id=1, source_target_pairs={{0,8},{4,12},{8,0},{12,4},{16,24},{20,28},{24,16},{28,20},{1,9},{5... | collective-permute-start | bytes 393224 | tf_op jit(solution)/shard_map/ppermute | solution.py:250
  31.4 2.7 %collective-permute-start.9 = (bf16[64,2048]{1,0:T(8,128)(2,1)S(1)}, bf16[64,2048]{1,0:T(8,128)(2,1)S(1)}, u32[]{:S(2)}, u32[]{:S(2)}) collective-permute-start(bf16[64,2048]{1,0:T(8,128)(2,1)S(1)} %shard_map.61.first), channel_id=1, source_target_pairs={{0,4},{4,0},{8,12},{12,8},{16,20},{20,16},{24,28},{28,24},{1,5},{5... | collective-permute-start | bytes 786440 | tf_op jit(solution)/shard_map/ppermute | solution.py:247
  31.5 1.7 %collective-permute-start.11 = (bf16[64,1024]{1,0:T(8,128)(2,1)S(1)}, bf16[64,1024]{1,0:T(8,128)(2,1)S(1)}, u32[]{:S(2)}, u32[]{:S(2)}) collective-permute-start(bf16[64,1024]{1,0:T(8,128)(2,1)S(1)} %shard_map.60.refs_0_), channel_id=1, source_target_pairs={{0,4},{4,0},{8,12},{12,8},{16,20},{20,16},{24,28},{28,24},{1,5},{5... | collective-permute-start | bytes 393224 | tf_op jit(solution)/shard_map/ppermute | solution.py:247
  32.8 1.3 %collective-permute-start.12 = (bf16[64,1024]{1,0:T(8,128)(2,1)S(1)}, bf16[64,1024]{1,0:T(8,128)(2,1)S(1)}, u32[]{:S(2)}, u32[]{:S(2)}) collective-permute-start(bf16[64,1024]{1,0:T(8,128)(2,1)S(1)} %collective-permute-done.10.refs_1_), channel_id=1, source_target_pairs={{0,4},{4,0},{8,12},{12,8},{16,20},{20,16},{24,28},{28,24},{1,5},{5... | collective-permute-start | bytes 393224 | tf_op jit(solution)/shard_map/ppermute | solution.py:247
  34.7 7.3 %collective-permute-start.13 = (s16[256,256]{1,0:T(8,128)(2,1)S(1)}, s16[256,256]{1,0:T(8,128)(2,1)S(1)}, u32[]{:S(2)}, u32[]{:S(2)}) collective-permute-start(s16[256,256]{1,0:T(8,128)(2,1)S(1)} %shard_map.64), channel_id=1, source_target_pairs={{0,3},{1,2},{2,1},{3,0},{4,7},{5,6},{6,5},{7,4},{8,11},{9,10},{10,... | collective-permute-start | bytes 393224 | tf_op jit(solution)/shard_map/ppermute | solution.py:253
  37.4 6.9 %collective-permute-start.14 = (s16[256,256]{1,0:T(8,128)(2,1)S(1)}, s16[256,256]{1,0:T(8,128)(2,1)S(1)}, u32[]{:S(2)}, u32[]{:S(2)}) collective-permute-start(s16[256,256]{1,0:T(8,128)(2,1)S(1)} %shard_map.66), channel_id=1, source_target_pairs={{0,1},{1,0},{2,3},{3,2},{4,5},{5,4},{6,7},{7,6},{8,9},{9,8},{10,11... | collective-permute-start | bytes 393224 | tf_op jit(solution)/shard_map/ppermute | solution.py:253
  39.1 5.4 %collective-permute-start.15 = (s16[256,256]{1,0:T(8,128)(2,1)S(1)}, s16[256,256]{1,0:T(8,128)(2,1)S(1)}, u32[]{:S(2)}, u32[]{:S(2)}) collective-permute-start(s16[256,256]{1,0:T(8,128)(2,1)S(1)} %shard_map.68), channel_id=1, source_target_pairs={{0,2},{1,3},{2,0},{3,1},{4,6},{5,7},{6,4},{7,5},{8,10},{9,11},{10,... | collective-permute-start | bytes 393224 | tf_op jit(solution)/shard_map/ppermute | solution.py:253
